TPU v7x, 32 devices: a whole 2x2x4 slice. The times are simulated.
32 devices in a mesh: member: 2 (over x), horiz: 16 (over z, y, core).
Axes of the slice: x: 2, y: 2, z: 4, core: 2. Of those that a mesh axis runs over, the one named last changes fastest.
Arguments:
- perturbation: float32 [16, 80, 4, 1920], P('member', 'horiz'), parts along dimension 0, may hold values from -36 to 36
- base_state: float32 [8, 80, 4, 1920], P(None, 'horiz'), may hold values from -6 to 6
- target_state: float32 [8, 80, 4, 1920], P(None, 'horiz'), may hold values from -6 to 6
- cost_weight: float32 [80, 1920], P('horiz'), may hold values from 0.5 to 6
- diffusivity: float32 [80, 1920], P('horiz'), may hold values from 0.04 to 0.2
- chan_mix: float32 [8, 4, 4], replicated, may hold values from -3 to 3
- coupler_mix: float32 [4, 4], replicated, may hold values from -3 to 3
- owner_mix: float32 [16, 80, 80], P('horiz'), may hold values from -0.625 to 0.625
- air_temp: float32 [2, 16, 80, 128], P(None, 'horiz'), may hold values from -6 to 6
- wind_speed: float32 [2, 16, 80, 128], P(None, 'horiz'), may hold values from 2 to 12
- wet_list: int32 [16, 75], P('horiz'), may hold values from -1 to 74, as said below
- wet_owner: int32 [16, 75], P('horiz'), may hold values from -1 to 15, as said below
- remap_src: int32 [240], P('horiz'), may hold values from 0 to 79, as said below
- remap_tgt: int32 [240], P('horiz'), may hold values from 0 to 31, as said below
- remap_weight: float32 [240], P('horiz'), may hold values from 0.2 to 0.8
Outputs:
- new_perturbation: float32 [16, 80, 4, 1920], P('member', 'horiz'), parts along dimension 0
There are 2 independent parts, one for each index of `member`. A program takes and returns all parts, laid end to end along the dimension named above; an argument that names none is the same for every part. Nothing has to cross between parts.
Inputs may be any that keep to these rules, and one draw needn't show every extreme that they name: Each row of wet_list names distinct tiles, valid entries first and -1 after them; wet_owner is -1 exactly where wet_list is. Every device lists at least 37 wet tiles and some device lists all 75. Within one device's list no owner appears more than 5 times, and some owner appears exactly 5 times in every device's list. `wet_owner`: see wet_list. `remap_src`: the source row of each entry is one of the rows of the device that holds the entry. `remap_tgt`: each entry's latitude row differs from (2 times its source row) // 5 by at most 1.
All inputs are finite; a program needn't handle non-finite values.
Results may differ from a plain program's by a relative error of at most 0.0001.
Values sent between devices are 32-bit elements; how exact they have to be, the bound alone decides.
No kernel may reach another device: no remote copies, remote signals or barrier semaphores. Data moves between devices by JAX's collectives and lax.ppermute only.
A program may use at most 64 MiB of HBM per device.

v0:
```python
import functools

import jax
import jax.numpy as jnp
from jax import lax
from jax.experimental import pallas as pl
from jax.experimental.pallas import tpu as pltpu
from jax.sharding import PartitionSpec as P

LAT_DEV = 2
NEAR_LAT = LAT_DEV + 2
CHANNELS = 4
LEVELS = 8
WIDTH = 128
SUBLANES = 8

KAPPA_V = 0.1
TIME_STEP = 0.3
FLUX_RATE = 0.05
FEEDBACK = 0.5
ASCENT = 0.5
EPSILON = 1e-06
HIGHEST = lax.Precision.HIGHEST
VMEM_BYTES = 32 * 1024 * 1024


class Sizes:
    def __init__(self, devices, capacity, rows, cells):
        self.devices = devices
        self.capacity = capacity
        self.slots = devices * capacity
        self.rows = rows
        self.cells = cells
        self.row_tiles = cells // WIDTH
        self.tiles = rows * self.row_tiles
        self.row_width = CHANNELS * self.row_tiles
        self.pitch = -(-self.row_tiles // SUBLANES) * SUBLANES
        self.own_rows = CHANNELS * capacity
        self.chunk = -(-(self.own_rows + 2 * capacity) // SUBLANES) * SUBLANES
        self.slot_lines = -(-self.slots // WIDTH)
        self.facts = -(-(self.slot_lines + 1) // SUBLANES) * SUBLANES
        self.lat_lines = LAT_DEV * self.pitch
        self.whole = (rows, CHANNELS, LEVELS, cells)
        self.edge = (CHANNELS, LEVELS, cells)
        self.surface = (CHANNELS * (self.tiles + 1), WIDTH)
        self.narrow = (CHANNELS * self.slots, WIDTH)
        self.wide = (devices * self.chunk, WIDTH)
        self.slope = (NEAR_LAT * self.pitch, WIDTH)
        self.lats = (self.lat_lines, WIDTH)
        self.told = (self.lat_lines + self.facts, WIDTH)
        self.bulk_at = NEAR_LAT * rows
        self.tables = (3 * self.slot_lines, WIDTH)
        self.weights = (3 * self.facts, WIDTH)
        self.near = (-(-(self.tiles + 1) // SUBLANES) * SUBLANES, WIDTH)
        self.by_slot = (CHANNELS, self.slots, WIDTH)


class Shipped:
    def __init__(self, block, home, sems):
        self.block, self.home, self.sems = block, home, sems
        self.by_row = False
        self.started = False

    def __getitem__(self, at):
        return self.block[at]

    def __setitem__(self, at, value):
        self.block[at] = value

    def row(self, index):
        self.by_row = True
        self.started = True
        return pltpu.make_async_copy(
            self.block.at[index], self.home.at[index], self.sems.at[index]
        )

    def all(self):
        return pltpu.make_async_copy(self.block, self.home, self.sems.at[0])

    def start(self):
        self.started = True
        self.all().start()

    def finish(self, rows):
        if self.by_row:
            for index in range(rows):
                self.row(index).wait()
        else:
            self.all().wait()


def cols(tile):
    return slice(tile * WIDTH, (tile + 1) * WIDTH)


def lanes_sum(left_here, left_before, right_here, right_after, lane):
    return jnp.where(lane == 0, left_before, left_here) + jnp.where(
        lane == WIDTH - 1, right_after, right_here
    )


def levels_sum(field, sub):
    return jnp.where(sub == 0, 0.0, pltpu.roll(field, 1, 0)) + jnp.where(
        sub == LEVELS - 1, 0.0, pltpu.roll(field, LEVELS - 1, 0)
    )


def row_tiles_of(sz, ref, row):
    return ref[pl.ds(row * sz.row_width, sz.row_tiles, stride=CHANNELS), :]


def put_row_tiles(sz, ref, row, value):
    ref[pl.ds(row * sz.row_width, sz.row_tiles, stride=CHANNELS), :] = value


def near_row(sz, ref, row):
    return ref[row * sz.row_tiles : (row + 1) * sz.row_tiles, :]


def load_surface_row(sz, target, row, source, base):
    for tile in range(sz.row_tiles):
        for channel in range(CHANNELS):
            at = base + tile * CHANNELS + channel
            target[row, channel, 0:1, cols(tile)] = source[pl.ds(at, 1), :]


def as_column(row, size):
    shape = (size, row.shape[1])
    diagonal = lax.broadcasted_iota(jnp.int32, shape, 0) == lax.broadcasted_iota(jnp.int32, shape, 1)
    return jnp.sum(jnp.where(diagonal, row, 0.0), axis=1, keepdims=True)


def setup_kernel(sz, entries, remap_entries, arrive, wet, remap, mix_rows, diffusivity, weight, *outs):
    table, facts, mix, diffusivity_rows, weight_rows, diffusivity_tiles, weight_tiles = outs
    arrive_all(arrive)
    for source, by_row, by_tile in (
        (diffusivity, diffusivity_rows, diffusivity_tiles),
        (weight, weight_rows, weight_tiles),
    ):
        for row in range(sz.rows):
            for tile in range(sz.row_tiles):
                line = source[row : row + 1, cols(tile)]
                by_row[row, 0:1, cols(tile)] = line
                at = (row * sz.row_tiles + tile) * CHANNELS
                by_tile[at : at + CHANNELS, :] = jnp.broadcast_to(line, (CHANNELS, WIDTH))
        by_row.start()
        by_tile.start()
    for index in range(CHANNELS * CHANNELS):
        column = as_column(mix_rows[index : index + 1, :], LEVELS)
        mix[index] = jnp.broadcast_to(column, (LEVELS, WIDTH))
    mix.start()
    tiles, owners = wet[0:1, :], wet[1:2, :]
    size = -(-entries // SUBLANES) * SUBLANES
    shape = (size, wet.shape[1])
    tile_here, owner_here = as_column(tiles, size), as_column(owners, size)
    earlier = lax.broadcasted_iota(jnp.int32, shape, 1) < lax.broadcasted_iota(jnp.int32, shape, 0)
    same = (owner_here == owners) & earlier
    rank = jnp.sum(jnp.where(same, 1.0, 0.0), axis=1, keepdims=True)
    slot = jnp.where(owner_here >= 0.0, owner_here * sz.capacity + rank, -1.0)
    facts[...] = jnp.zeros((sz.facts, WIDTH), jnp.float32)
    for line in range(sz.slot_lines):
        place = lax.broadcasted_iota(jnp.int32, (size, WIDTH), 1) + line * WIDTH
        match = slot.astype(jnp.int32) == place
        told = jnp.sum(jnp.where(match, sz.tiles - tile_here, 0.0), axis=0, keepdims=True)
        facts[line : line + 1, :] = told
        table[line : line + 1, :] = sz.tiles - told.astype(jnp.int32)
    size = -(-remap_entries // SUBLANES) * SUBLANES
    at, amount = as_column(remap[0:1, :], size), as_column(remap[1:2, :], size)
    place = lax.broadcasted_iota(jnp.int32, (size, WIDTH), 1)
    facts[sz.slot_lines : sz.slot_lines + 1, :] = jnp.sum(
        jnp.where(at.astype(jnp.int32) == place, amount, 0.0), axis=0, keepdims=True
    )


def gather_levels(block, rows_at, channel, tile):
    sub = lax.broadcasted_iota(jnp.int32, (LEVELS, WIDTH), 0)
    total = None
    for level in range(LEVELS):
        line = block[(level, *rows_at, slice(channel, channel + 1), cols(tile))]
        line = jnp.broadcast_to(line, (LEVELS, WIDTH))
        total = line if total is None else jnp.where(sub == level, line, total)
    return total


def edges_kernel(sz, arrive, low_start, high_start, low_base, high_base, low, high):
    arrive_all(arrive)
    for start, base, edge in ((low_start, low_base, low), (high_start, high_base, high)):
        for channel in range(CHANNELS):
            for tile in range(sz.row_tiles):
                edge[channel, :, cols(tile)] = gather_levels(
                    start, (), channel, tile
                ) + gather_levels(base, (), channel, tile)


def load_kernel(sz, arrive, perturbation, base, field, start, start_block, base_block, in_sems):
    def arrivals(row):
        return [
            pltpu.make_async_copy(source.at[:, row], block.at[row], in_sems.at[index, row])
            for index, (source, block) in enumerate(
                ((perturbation, start_block), (base, base_block))
            )
        ]

    for row in range(sz.rows):
        for arrival in arrivals(row):
            arrival.start()

    def one_row(row, carry):
        for arrival in arrivals(row):
            arrival.wait()
        for channel in range(CHANNELS):
            for tile in range(sz.row_tiles):
                here = gather_levels(start_block.at[row], (), channel, tile)
                start[row, channel, :, cols(tile)] = here
                field[row, channel, :, cols(tile)] = here + gather_levels(
                    base_block.at[row], (), channel, tile
                )
        start.row(row).start()
        return carry

    lax.fori_loop(0, sz.rows, one_row, 0)


class Remap:
    def __init__(self, sz, weights):
        self.sz, self.weights = sz, weights

    def weight(self, which, lat, row):
        line = which * self.sz.facts + self.sz.slot_lines
        return self.weights[line, lat * self.sz.rows + row]

    def own(self, lat, row):
        return self.weight(0, lat, row)

    def of_low(self, lat, row):
        return self.weight(1, lat + LAT_DEV, row)

    def of_high(self, lat, row):
        return self.weight(2, lat - LAT_DEV, row)


def tile_at(sz, tables, which, slot):
    return tables[which * sz.slot_lines + slot // WIDTH, slot % WIDTH]


def sum_of(weights, values):
    total = weights[0] * values[0]
    for weight, value in zip(weights[1:], values[1:]):
        total = total + weight * value
    return total


def own_sums(sz, remap, own, factor):
    return [
        factor * sum_of([remap.own(lat, row) for row in range(sz.rows)], own)
        for lat in range(NEAR_LAT)
    ]


def send_sums(sz, sums, send_low, send_high):
    for lat in range(NEAR_LAT):
        send = send_low if lat < LAT_DEV else send_high
        at = (lat % LAT_DEV) * sz.pitch
        send[at : at + sz.row_tiles, :] = sums[lat]


def lat_rows(sz, ref, lat):
    return ref[lat * sz.pitch : lat * sz.pitch + sz.row_tiles, :]


def told_sums(sz, from_low, from_high):
    return [
        lat_rows(sz, from_low if lat < LAT_DEV else from_high, lat % LAT_DEV)
        for lat in range(NEAR_LAT)
    ]


def forward_kernel(sz, first, last, arrive, *refs):
    refs = list(refs)
    low, high, diffusivity, mix, tables, facts, field = refs[:7]
    refs = refs[7:]
    if first:
        told_facts = refs[0]
        refs = refs[1:]
    else:
        surface, low_surface, high_surface = refs[:3]
        refs = refs[3:]
    if last:
        weight, target = refs[:2]
        refs = refs[2:]
    out, drive, new_surface, packed, tell_low, tell_high, edge_low, edge_high, padded = refs[:9]
    remap = Remap(sz, facts)
    if not first:
        in_sems = refs[9]

    def arrivals(row):
        copies = [pltpu.make_async_copy(field.at[row], padded.at[row + 1], in_sems.at[0, row])]
        if last:
            copies.append(
                pltpu.make_async_copy(target.at[:, row], refs[10].at[row], in_sems.at[1, row])
            )
        return copies

    if not first:
        for row in range(sz.rows):
            for arrival in arrivals(row):
                arrival.start()
    arrive_all(arrive)
    padded[0] = low[...]
    padded[sz.rows + 1] = high[...]
    if not first:
        load_surface_row(sz, padded, 0, low_surface, 0)
        load_surface_row(sz, padded, sz.rows + 1, high_surface, 0)

    def ready(row):
        if first:
            padded[row + 1] = field[row]
        else:
            for arrival in arrivals(row):
                arrival.wait()
            load_surface_row(sz, padded, row + 1, surface, row * sz.row_width)

    ready(0)
    lane = lax.broadcasted_iota(jnp.int32, (LEVELS, WIDTH), 1)
    sub = lax.broadcasted_iota(jnp.int32, (LEVELS, WIDTH), 0)
    count = sz.row_tiles

    def one_row(row, carry):
        @pl.when(row < sz.rows - 1)
        def _():
            ready(row + 1)

        here = [[padded[row + 1, c, :, cols(t)] for t in range(count)] for c in range(CHANNELS)]
        for t in range(count):
            coeff = jnp.broadcast_to(diffusivity[row, 0:1, cols(t)], (LEVELS, WIDTH))
            if last:
                scale = weight[row, 0:1, cols(t)]
                scale = jnp.broadcast_to(scale * scale, (LEVELS, WIDTH))
            for c in range(CHANNELS):
                mixed = mix[c * CHANNELS] * here[0][t]
                for k in range(1, CHANNELS):
                    mixed = mixed + mix[c * CHANNELS + k] * here[k][t]
                bent = jnp.tanh(mixed)
                drive[row, c, :, cols(t)] = bent
                field_here = here[c][t]
                around = lanes_sum(
                    pltpu.roll(field_here, 1, 1),
                    pltpu.roll(here[c][(t - 1) % count], 1, 1),
                    pltpu.roll(field_here, WIDTH - 1, 1),
                    pltpu.roll(here[c][(t + 1) % count], WIDTH - 1, 1),
                    lane,
                )
                around = around + (padded[row, c, :, cols(t)] + padded[row + 2, c, :, cols(t)])
                stepped = (
                    field_here
                    + coeff * (around - 4.0 * field_here)
                    + KAPPA_V * (levels_sum(field_here, sub) - 2.0 * field_here)
                    + TIME_STEP * bent
                )
                new_surface[pl.ds((row * count + t) * CHANNELS + c, 1), :] = stepped[0:1, :]
                if last:
                    stepped = scale * (stepped - gather_levels(refs[10].at[row], (), c, t))
                out[row, c, :, cols(t)] = stepped
        drive.row(row).start()
        out.row(row).start()
        return carry

    lax.fori_loop(0, sz.rows, one_row, 0)
    new_surface[CHANNELS * sz.tiles :, :] = jnp.zeros((CHANNELS, WIDTH), jnp.float32)
    new_surface.start()
    pack_slots(sz, tables, new_surface, packed)
    packed.start()
    own = [row_tiles_of(sz, new_surface.block, row) for row in range(sz.rows)]
    send_sums(sz, own_sums(sz, remap, own, 1.0), tell_low, tell_high)
    blank = told_facts[...] if first else jnp.zeros((sz.facts, WIDTH), jnp.float32)
    for tell in (tell_low, tell_high):
        tell[sz.lat_lines :, :] = blank
        tell.start()
    store_edges(sz, out, diffusivity if last else None, edge_low, edge_high)


def pack_slots(sz, tables, surface, packed):
    for slot in range(sz.slots):
        at = pl.multiple_of(tile_at(sz, tables, 0, slot) * CHANNELS, CHANNELS)
        packed[slot * CHANNELS : (slot + 1) * CHANNELS, :] = surface[pl.ds(at, CHANNELS), :]


def store_edges(sz, field, diffusivity, send_low, send_high):
    for row, send in ((0, send_low), (sz.rows - 1, send_high)):
        for channel in range(CHANNELS):
            for tile in range(sz.row_tiles):
                value = field[row, channel, :, cols(tile)]
                if diffusivity is not None:
                    value = value * jnp.broadcast_to(
                        diffusivity[row, 0:1, cols(tile)], (LEVELS, WIDTH)
                    )
                send[channel, :, cols(tile)] = value
        send.start()


def owner_kernel(sz, decode, arrive, arrived, mixing, air, wind, facts, *refs):
    slots = sz.slots
    if decode:
        told_low, told_high, own_table, own_facts, tables, weights = refs[:6]
        refs = refs[6:]
    flux, mixed_slope, flux_slope, flat, first = refs
    arrive_all(arrive)
    if decode:
        lines = sz.slot_lines
        tables[0:lines, :] = own_table[...]
        weights[0 : sz.facts, :] = own_facts[...]
        for which, told in ((1, told_low), (2, told_high)):
            got = told[sz.lat_lines : sz.lat_lines + lines, :]
            tables[which * lines : (which + 1) * lines, :] = sz.tiles - got.astype(jnp.int32)
            at = which * sz.facts
            weights[at : at + sz.facts, :] = told[sz.lat_lines :, :]
        tables.start()
        weights.start()

    def bulk(row, column):
        return facts[sz.slot_lines, sz.bulk_at + row * CHANNELS + column]

    values = [arrived[pl.ds(c, slots, stride=CHANNELS), :] for c in range(CHANNELS)]
    mixed = jnp.tanh(
        jnp.dot(
            mixing[...],
            jnp.concatenate(values, axis=1),
            precision=HIGHEST,
            preferred_element_type=jnp.float32,
        )
    )
    contrast = []
    for c in range(CHANNELS):
        mixed_here = mixed[:, cols(c)]
        mixed_slope[c] = 1.0 - mixed_here * mixed_here
        contrast.append((air[...] - values[0] if c == 0 else values[c]) + mixed_here)
    mixed_slope.start()
    rate = FLUX_RATE * wind[...]
    for c in range(CHANNELS):
        forcing = bulk(c, 0) * contrast[0]
        for k in range(1, CHANNELS):
            forcing = forcing + bulk(c, k) * contrast[k]
        bent = jnp.tanh(forcing)
        flux_slope[c] = rate * (1.0 - bent * bent)
        one = rate * bent
        flat[pl.ds(c, slots, stride=CHANNELS), :] = one
        if c == 0:
            first[...] = one
    flux_slope.start()
    cap = sz.capacity
    gap = jnp.zeros((sz.chunk - sz.own_rows, WIDTH), jnp.float32)
    for d in range(sz.devices):
        at = d * sz.chunk
        flux[at : at + sz.own_rows, :] = flat[d * sz.own_rows : (d + 1) * sz.own_rows, :]
        at = at + sz.own_rows
        flux[at : (d + 1) * sz.chunk, :] = gap
        if d > 0:
            flux[at : at + cap, :] = first[(d - 1) * cap : d * cap, :]
        if d < sz.devices - 1:
            flux[at + cap : at + 2 * cap, :] = first[(d + 1) * cap : (d + 2) * cap, :]


def owner_back_kernel(sz, arrive, arrived, mixing, mixed_slope, flux_slope, facts, back, flat, extra):
    slots, cap = sz.slots, sz.capacity

    def bulk(row, column):
        return facts[sz.slot_lines, sz.bulk_at + row * CHANNELS + column]

    for d in range(sz.devices):
        at = d * sz.chunk
        flat[d * sz.own_rows : (d + 1) * sz.own_rows, :] = arrived[at : at + sz.own_rows, :]
        more = jnp.zeros((cap, WIDTH), jnp.float32)
        if d < sz.devices - 1:
            at = (d + 1) * sz.chunk + sz.own_rows
            more = more + arrived[at : at + cap, :]
        if d > 0:
            at = (d - 1) * sz.chunk + sz.own_rows + cap
            more = more + arrived[at : at + cap, :]
        extra[d * cap : (d + 1) * cap, :] = more
    arrive_all(arrive)
    forced = []
    for c in range(CHANNELS):
        got = flat[pl.ds(c, slots, stride=CHANNELS), :]
        if c == 0:
            got = got + extra[...]
        forced.append(flux_slope[c] * got)
    direct = []
    for k in range(CHANNELS):
        total = bulk(0, k) * forced[0]
        for c in range(1, CHANNELS):
            total = total + bulk(c, k) * forced[c]
        direct.append(total)
    through = lax.dot_general(
        mixing[...],
        jnp.concatenate([direct[k] * mixed_slope[k] for k in range(CHANNELS)], axis=1),
        (((0,), (0,)), ((), ())),
        precision=HIGHEST,
        preferred_element_type=jnp.float32,
    )
    for k in range(CHANNELS):
        sign = -1.0 if k == 0 else 1.0
        back.block[pl.ds(k, slots, stride=CHANNELS), :] = through[:, cols(k)] + sign * direct[k]


def spread_back(sz, surface, slope, remap, tables, packed, near_low, near_high, tell_low, tell_high):
    rows, count, cap = sz.rows, sz.row_tiles, sz.capacity
    block = surface.block
    own = [row_tiles_of(sz, block, row) for row in range(rows)]
    sums = own_sums(sz, remap, own, FEEDBACK)
    send_sums(sz, sums, tell_low, tell_high)
    tell_low.start()
    tell_high.start()
    lats = [lat_rows(sz, slope, lat) * sums[lat] for lat in range(NEAR_LAT)]
    every = range(NEAR_LAT)
    for row in range(rows):
        added = sum_of([remap.own(lat, row) for lat in every], lats)
        put_row_tiles(sz, block, row, own[row] + added)
        at = row * count
        near_low[at : at + count, :] = sum_of(
            [remap.of_low(lat, row) for lat in range(LAT_DEV)], lats[:LAT_DEV]
        )
        near_high[at : at + count, :] = sum_of(
            [remap.of_high(lat, row) for lat in range(LAT_DEV, NEAR_LAT)], lats[LAT_DEV:]
        )
    rest = sz.near[0] - sz.tiles
    near_low[sz.tiles :, :] = jnp.zeros((rest, WIDTH), jnp.float32)
    near_high[sz.tiles :, :] = jnp.zeros((rest, WIDTH), jnp.float32)
    surface.start()
    gap = jnp.zeros((sz.chunk - sz.own_rows, WIDTH), jnp.float32)
    for owner in range(sz.devices):
        packed[owner * sz.chunk + sz.own_rows : (owner + 1) * sz.chunk, :] = gap
    for slot in range(sz.slots):
        owner, rank = slot // cap, slot % cap
        at = owner * sz.chunk + rank * CHANNELS
        tile = pl.multiple_of(tile_at(sz, tables, 0, slot) * CHANNELS, CHANNELS)
        packed[at : at + CHANNELS, :] = surface[pl.ds(tile, CHANNELS), :]
        at = owner * sz.chunk + sz.own_rows + rank
        packed[at : at + 1, :] = near_low[pl.ds(tile_at(sz, tables, 1, slot), 1), :]
        at = at + cap
        packed[at : at + 1, :] = near_high[pl.ds(tile_at(sz, tables, 2, slot), 1), :]


def surface_kernel(sz, last, arrive, *refs):
    refs = list(refs)
    flux, from_low, from_high, before, tables, weights = refs[:6]
    refs = refs[6:]
    if last:
        target, weight = refs[:2]
        surface, slope, packed, tell_low, tell_high, near_low, near_high = refs[2:]
        block = surface.block
    else:
        surface, send_low, send_high, slope, near_low, near_high = refs
        block = surface
    remap = Remap(sz, weights)
    arrive_all(arrive)
    rows, cap = sz.rows, sz.capacity
    block[...] = before[...]
    near_low[...] = jnp.zeros(sz.near, jnp.float32)
    near_high[...] = jnp.zeros(sz.near, jnp.float32)
    for slot in range(sz.slots):
        owner, rank = slot // cap, slot % cap
        at = owner * sz.chunk + rank * CHANNELS
        tile = pl.multiple_of(tile_at(sz, tables, 0, slot) * CHANNELS, CHANNELS)
        block[pl.ds(tile, CHANNELS), :] = (
            before[pl.ds(tile, CHANNELS), :] + flux[at : at + CHANNELS, :]
        )
        at = owner * sz.chunk + sz.own_rows + rank
        near_low[pl.ds(tile_at(sz, tables, 1, slot), 1), :] = flux[at : at + 1, :]
        at = at + cap
        near_high[pl.ds(tile_at(sz, tables, 2, slot), 1), :] = flux[at : at + 1, :]
    block[CHANNELS * sz.tiles :, :] = jnp.zeros((CHANNELS, WIDTH), jnp.float32)
    own = [row_tiles_of(sz, block, row) for row in range(rows)]
    sums = own_sums(sz, remap, own, 1.0)
    told = told_sums(sz, from_low, from_high)
    air = []
    for lat in range(NEAR_LAT):
        if lat < LAT_DEV:
            near, weights = near_low, [remap.of_low(lat, row) for row in range(rows)]
        else:
            near, weights = near_high, [remap.of_high(lat, row) for row in range(rows)]
        more = sum_of(weights, [near_row(sz, near, row) for row in range(rows)])
        one = jnp.tanh(sums[lat] + told[lat] + more)
        slope[lat * sz.pitch : lat * sz.pitch + sz.row_tiles, :] = 1.0 - one * one
        air.append(one)
    slope.start()
    for row in range(rows):
        weights = [remap.own(lat, row) for lat in range(NEAR_LAT)]
        put_row_tiles(sz, block, row, own[row] + FEEDBACK * sum_of(weights, air))
    if last:
        for row in range(rows):
            for tile in range(sz.row_tiles):
                at = row * sz.row_width + tile * CHANNELS
                scale = weight[at : at + CHANNELS, :]
                off = block[at : at + CHANNELS, :] - target[row, :, cols(tile)]
                block[at : at + CHANNELS, :] = scale * scale * off
        spread_back(
            sz, surface, slope, remap, tables, packed, near_low, near_high, tell_low, tell_high
        )
    else:
        send_low[...] = surface[0 : sz.row_width, :]
        send_high[...] = surface[(rows - 1) * sz.row_width : rows * sz.row_width, :]


def merge_kernel(
    sz, arrive, back, from_low, from_high, before, slope, tables, facts, diffusivity, surface, send_low, send_high
):
    rows, width = sz.rows, sz.row_width
    remap = Remap(sz, facts)
    arrive_all(arrive)
    surface[...] = before[...]
    for slot in range(sz.slots):
        tile = pl.multiple_of(tile_at(sz, tables, 0, slot) * CHANNELS, CHANNELS)
        surface[pl.ds(tile, CHANNELS), :] = (
            before[pl.ds(tile, CHANNELS), :] + back[slot * CHANNELS : (slot + 1) * CHANNELS, :]
        )
    surface[CHANNELS * sz.tiles :, :] = jnp.zeros((CHANNELS, WIDTH), jnp.float32)
    told = told_sums(sz, from_low, from_high)
    lats = [lat_rows(sz, slope, lat) * told[lat] for lat in range(NEAR_LAT)]
    for row in range(rows):
        own = row_tiles_of(sz, surface, row)
        weights = [remap.own(lat, row) for lat in range(NEAR_LAT)]
        put_row_tiles(sz, surface, row, own + sum_of(weights, lats))
    send_low[...] = diffusivity[0:width, :] * surface[0:width, :]
    end = rows * width
    send_high[...] = diffusivity[end - width : end, :] * surface[end - width : end, :]


def backward_kernel(sz, last, arrive, *refs):
    refs = list(refs)
    surface, low, high, low_surface, high_surface, diffusivity, mix = refs[:7]
    field, drive = refs[7:9]
    refs = refs[9:]
    if last:
        perturbation, out, sums = refs[:3]
        local, bent_all, padded, in_sems, start_all = refs[3:]
    else:
        tables, weights, slope = refs[:3]
        out, new_surface, packed, tell_low, tell_high, edge_low, edge_high = refs[3:10]
        local, bent_all, padded, in_sems, near_low, near_high = refs[10:]
        remap = Remap(sz, weights)
    count = sz.row_tiles

    def arrivals(row):
        copies = [
            pltpu.make_async_copy(field.at[row], local.at[row], in_sems.at[0, row]),
            pltpu.make_async_copy(drive.at[row], bent_all.at[row], in_sems.at[1, row]),
        ]
        if last:
            copies.append(
                pltpu.make_async_copy(perturbation.at[row], start_all.at[row], in_sems.at[2, row])
            )
        return copies

    for row in range(sz.rows):
        for arrival in arrivals(row):
            arrival.start()
    arrive_all(arrive)

    def ready(row):
        for arrival in arrivals(row):
            arrival.wait()
        load_surface_row(sz, local, row, surface, row * sz.row_width)
        for t in range(count):
            coeff = jnp.broadcast_to(diffusivity[row, 0:1, cols(t)], (LEVELS, WIDTH))
            for c in range(CHANNELS):
                padded[row + 1, c, :, cols(t)] = coeff * local[row, c, :, cols(t)]

    padded[0] = low[...]
    padded[sz.rows + 1] = high[...]
    load_surface_row(sz, padded, 0, low_surface, 0)
    load_surface_row(sz, padded, sz.rows + 1, high_surface, 0)
    ready(0)
    lane = lax.broadcasted_iota(jnp.int32, (LEVELS, WIDTH), 1)
    sub = lax.broadcasted_iota(jnp.int32, (LEVELS, WIDTH), 0)

    def one_row(row, carry):
        @pl.when(row < sz.rows - 1)
        def _():
            ready(row + 1)

        scaled = [[padded[row + 1, c, :, cols(t)] for t in range(count)] for c in range(CHANNELS)]
        for t in range(count):
            here, bent = [], []
            for c in range(CHANNELS):
                value = local[row, c, :, cols(t)]
                one = bent_all[row, c, :, cols(t)]
                here.append(value)
                bent.append((1.0 - one * one) * value)
            for c in range(CHANNELS):
                mixed = mix[c] * bent[0]
                for k in range(1, CHANNELS):
                    mixed = mixed + mix[k * CHANNELS + c] * bent[k]
                around = lanes_sum(
                    pltpu.roll(scaled[c][t], 1, 1),
                    pltpu.roll(scaled[c][(t - 1) % count], 1, 1),
                    pltpu.roll(scaled[c][t], WIDTH - 1, 1),
                    pltpu.roll(scaled[c][(t + 1) % count], WIDTH - 1, 1),
                    lane,
                )
                around = around + (padded[row, c, :, cols(t)] + padded[row + 2, c, :, cols(t)])
                stepped = (
                    here[c]
                    + (around - 4.0 * scaled[c][t])
                    + KAPPA_V * (levels_sum(here[c], sub) - 2.0 * here[c])
                    + TIME_STEP * mixed
                )
                out[row, c, :, cols(t)] = stepped
                if last:
                    start = start_all[row, c, :, cols(t)]
                    carry = (
                        carry[0] + start * start,
                        carry[1] + start * stepped,
                        carry[2] + stepped * stepped,
                    )
                else:
                    new_surface[pl.ds((row * count + t) * CHANNELS + c, 1), :] = stepped[0:1, :]
        out.row(row).start()
        return carry

    blank = jnp.zeros((LEVELS, WIDTH), jnp.float32)
    totals = lax.fori_loop(0, sz.rows, one_row, (blank, blank, blank) if last else 0)
    if last:
        place = lax.broadcasted_iota(jnp.int32, sums.block.shape, 1)
        held = jnp.zeros(sums.block.shape, jnp.float32)
        for index in range(3):
            total = jnp.sum(jnp.sum(totals[index], axis=0, keepdims=True), axis=1, keepdims=True)
            held = jnp.where(place == index, total, held)
        sums[...] = held
    else:
        new_surface[CHANNELS * sz.tiles :, :] = jnp.zeros((CHANNELS, WIDTH), jnp.float32)
        spread_back(
            sz, new_surface, slope, remap, tables, packed, near_low, near_high, tell_low, tell_high
        )
        packed.start()
        store_edges(sz, out, diffusivity, edge_low, edge_high)


def final_kernel(cell_total, arrive, everyones, perturbation, gradient, out):
    sums = jnp.sum(everyones[...], axis=0, keepdims=True) / cell_total
    place = lax.broadcasted_iota(jnp.int32, sums.shape, 1)
    means = [
        jnp.broadcast_to(
            jnp.sum(jnp.where(place == index, sums, 0.0), axis=1, keepdims=True), (1, WIDTH)
        )
        for index in range(3)
    ]
    scale = lax.rsqrt(means[2] + EPSILON)
    mean_sq = means[0] + 2.0 * ASCENT * scale * means[1] + ASCENT * ASCENT * scale * scale * means[2]
    shrink = lax.rsqrt(mean_sq + EPSILON)
    step = jnp.broadcast_to(ASCENT * scale * shrink, (CHANNELS, WIDTH))
    shrink = jnp.broadcast_to(shrink, (CHANNELS, WIDTH))
    levels, rows, _, cells = perturbation.shape

    def one_level(level, carry):
        for row in range(rows):
            for tile in range(cells // WIDTH):
                start = perturbation[level, row, :, cols(tile)]
                slope = gradient[level, row, :, cols(tile)]
                out[level, row, :, cols(tile)] = shrink * start + step * slope
        out.row(level).start()
        return carry

    lax.fori_loop(0, levels, one_level, 0)


class Operand:
    def __init__(self, array, space, fetch=None, at=()):
        self.array, self.space, self.fetch, self.at = array, space, fetch, at

    def block(self):
        whole = self.array.shape
        taken = [size for size, index in zip(whole, self.at) if isinstance(index, slice)]
        return self.fetch((*taken, *whole[len(self.at) :]), self.array.dtype)


def near_by(*arrays):
    return [Operand(array, pltpu.VMEM) for array in arrays]


def far_off(*arrays):
    return [
        Operand(pltpu.with_memory_space_constraint(array, pltpu.HBM), pltpu.HBM)
        for array in arrays
    ]


def fetched(*arrays, at=(), into=pltpu.VMEM):
    return [
        Operand(pltpu.with_memory_space_constraint(array, pltpu.HBM), pltpu.HBM, into, at)
        for array in arrays
    ]


def scalars(*arrays):
    return fetched(*arrays, into=pltpu.SMEM)


def call(kernel, name, inputs, kept=(), shipped=(), scratch=()):
    n_in, n_kept, n_out = len(inputs), len(kept), len(shipped)
    brought = [index for index, item in enumerate(inputs) if item.fetch is not None]

    def as_shape(item):
        return item if isinstance(item, jax.ShapeDtypeStruct) else jax.ShapeDtypeStruct(item, jnp.float32)

    kept = [as_shape(item) for item in kept]
    shipped = [as_shape(item) for item in shipped]

    def run(*refs):
        ins = list(refs[:n_in])
        kept_refs = refs[n_in : n_in + n_kept]
        homes = refs[n_in + n_kept : n_in + n_kept + n_out]
        rest = refs[n_in + n_kept + n_out :]
        outs = [
            Shipped(block, home, sems)
            for block, home, sems in zip(rest[:n_out], homes, rest[n_out : 2 * n_out])
        ]
        rest = rest[2 * n_out :]
        if brought:
            blocks, arrive_sems = rest[: len(brought)], rest[len(brought)]
            rest = rest[len(brought) + 1 :]
            copies = []
            for place, (index, block) in enumerate(zip(brought, blocks)):
                source = ins[index]
                if inputs[index].at:
                    source = source.at[inputs[index].at]
                copies.append(pltpu.make_async_copy(source, block, arrive_sems.at[place]))
                ins[index] = block
            for copy in copies:
                copy.start()
            arrive = [copy.wait for copy in copies]
        else:
            arrive = []
        kernel(arrive, *ins, *kept_refs, *outs, *rest)
        for out in outs:
            if not out.started:
                out.start()
        for out in outs:
            out.finish(out.block.shape[0])

    spaces = [pltpu.VMEM] * n_kept + [pltpu.HBM] * n_out
    blocks = [pltpu.VMEM(item.shape, item.dtype) for item in shipped]
    sems = [
        pltpu.SemaphoreType.DMA((item.shape[0] if len(item.shape) > 3 else 1,)) for item in shipped
    ]
    arriving = [inputs[index].block() for index in brought]
    if brought:
        arriving.append(pltpu.SemaphoreType.DMA((len(brought),)))
    more = [
        item if not isinstance(item, tuple) else pltpu.VMEM(item, jnp.float32) for item in scratch
    ]
    return pl.pallas_call(
        run,
        name=name,
        in_specs=[pl.BlockSpec(memory_space=item.space) for item in inputs],
        out_specs=[pl.BlockSpec(memory_space=space) for space in spaces],
        out_shape=kept + [pltpu.HBM(item.shape, item.dtype) for item in shipped],
        scratch_shapes=blocks + sems + arriving + more,
        compiler_params=pltpu.CompilerParams(vmem_limit_bytes=VMEM_BYTES),
    )(*[item.array for item in inputs])


def arrive_all(arrive):
    for wait in arrive:
        wait()


def swap(low, high):
    count = lax.axis_size("horiz")
    upward = [(i, i + 1) for i in range(count - 1)]
    downward = [(target, source) for source, target in upward]
    return lax.ppermute(high, "horiz", upward), lax.ppermute(low, "horiz", downward)


def exchange(array, devices):
    rows = array.shape[0] // devices
    split = array.reshape(devices, rows // CHANNELS, CHANNELS, WIDTH)
    moved = lax.all_to_all(split, "horiz", split_axis=0, concat_axis=0, tiled=True)
    return moved.reshape(array.shape)


def body(
    perturbation,
    base_state,
    target_state,
    cost_weight,
    diffusivity,
    chan_mix,
    coupler_mix,
    owner_mix,
    air_temp,
    wind_speed,
    wet_list,
    wet_owner,
    remap_src,
    remap_tgt,
    remap_weight,
):
    devices = lax.axis_size("horiz")
    hours = air_temp.shape[0]
    sz = Sizes(devices, air_temp.shape[2] // devices, base_state.shape[1], base_state.shape[3])
    rows = sz.rows
    native_row = (LEVELS, CHANNELS, sz.cells)

    edge_inputs = []
    for array in (perturbation, base_state):
        for row in (0, rows - 1):
            edge_inputs += fetched(array, at=(slice(None), row))
    edges = swap(
        *call(functools.partial(edges_kernel, sz), "edges", edge_inputs, kept=[sz.edge, sz.edge])
    )
    me = lax.axis_index("horiz").astype(jnp.int32)

    def lined(first_row, second_row):
        size = -(-first_row.shape[0] // WIDTH) * WIDTH
        pair = jnp.stack([first_row.astype(jnp.float32), second_row.astype(jnp.float32)])
        return jnp.pad(pair, ((0, 0), (0, size - pair.shape[1])), constant_values=-1.0)

    places = jnp.arange(CHANNELS * CHANNELS, dtype=jnp.int32) + sz.bulk_at
    remap_at = (remap_tgt - (me * LAT_DEV - 1)) * rows + remap_src - me * rows
    remap_lines = lined(
        jnp.concatenate([remap_at, places]),
        jnp.concatenate([remap_weight, coupler_mix.reshape(-1)]),
    )
    mix_rows = chan_mix.transpose(1, 2, 0).reshape(CHANNELS * CHANNELS, LEVELS)
    row_lines = (rows, 1, sz.cells)
    tiles_lines = (CHANNELS * sz.tiles, WIDTH)
    table, facts, mix, diffusivity_rows, weight_rows, diffusivity_tiles, weight_tiles = call(
        functools.partial(setup_kernel, sz, wet_list.shape[1], remap_at.shape[0] + places.shape[0]),
        "setup",
        near_by(lined(wet_list[0], wet_owner[0]), remap_lines, mix_rows)
        + fetched(diffusivity, cost_weight),
        shipped=[
            jax.ShapeDtypeStruct((sz.slot_lines, WIDTH), jnp.int32),
            (sz.facts, WIDTH),
            (CHANNELS * CHANNELS, LEVELS, WIDTH),
            row_lines,
            row_lines,
            tiles_lines,
            tiles_lines,
        ],
    )
    wider = (rows + 2, CHANNELS, LEVELS, sz.cells)
    row_surface = (sz.row_width, WIDTH)
    by_row = (rows, *native_row)

    def row_sems(kinds):
        return pltpu.SemaphoreType.DMA((kinds, rows))

    field, start_field = call(
        functools.partial(load_kernel, sz),
        "load",
        far_off(perturbation, base_state),
        kept=[sz.whole],
        shipped=[sz.whole],
        scratch=[by_row, by_row, row_sems(2)],
    )

    saved = []
    surface = None
    told = None
    for hour in range(hours):
        first, last = hour == 0, hour == hours - 1
        inputs = near_by(*edges) + fetched(diffusivity_rows, mix) + scalars(table, facts)
        scratch = [wider]
        if first:
            inputs += near_by(field) + fetched(facts)
        else:
            inputs += far_off(field) + near_by(surface, *surface_edges)
            scratch += [row_sems(2)]
        if last:
            inputs += fetched(weight_rows) + far_off(target_state)
            scratch += [by_row]
        field, drive, surface, packed, *sends = call(
            functools.partial(forward_kernel, sz, first, last),
            "step",
            inputs,
            shipped=[
                sz.whole, sz.whole, sz.surface, sz.narrow, sz.told, sz.told, sz.edge, sz.edge
            ],
            scratch=scratch,
        )
        arrived = exchange(packed, devices)
        got = swap(*sends[:2])
        arrived, *got = lax.optimization_barrier((arrived, *got))
        if first:
            told = got
        inputs = (
            near_by(arrived)
            + fetched(owner_mix, at=(0,))
            + fetched(air_temp, wind_speed, at=(hour, 0))
            + scalars(facts)
        )
        decoded = []
        if first:
            inputs += near_by(*told) + fetched(table, facts)
            decoded = [jax.ShapeDtypeStruct(sz.tables, jnp.int32), sz.weights]
        *decoded, flux, mixed_slope, flux_slope = call(
            functools.partial(owner_kernel, sz, first),
            "owners",
            inputs,
            shipped=[*decoded, sz.wide, sz.by_slot, sz.by_slot],
            scratch=[sz.narrow, (sz.slots, WIDTH)],
        )
        if first:
            tables, weights = decoded
        flux, *sends = lax.optimization_barrier((flux, *sends[2:]))
        flux = exchange(flux, devices)
        edges = swap(*sends)
        inputs = near_by(flux, *got) + fetched(surface) + scalars(tables, weights)
        near = [sz.near, sz.near]
        if last:
            surface, slope, packed, *sends = call(
                functools.partial(surface_kernel, sz, True),
                "surface",
                inputs + fetched(target_state, at=(0,)) + fetched(weight_tiles),
                shipped=[sz.surface, sz.slope, sz.wide, sz.lats, sz.lats],
                scratch=near,
            )
        else:
            surface, *sends, slope = call(
                functools.partial(surface_kernel, sz, False),
                "surface",
                inputs,
                kept=[sz.surface, row_surface, row_surface],
                shipped=[sz.slope],
                scratch=near,
            )
            surface_edges = swap(*sends)
        saved.append((drive, slope, mixed_slope, flux_slope))

    edge_sends = None
    for hour in reversed(range(hours)):
        drive, slope, mixed_slope, flux_slope = saved[hour]
        arrived = exchange(packed, devices)
        got = swap(*sends)
        arrived, *got = lax.optimization_barrier((arrived, *got))
        back = call(
            functools.partial(owner_back_kernel, sz),
            "owners_back",
            near_by(arrived)
            + fetched(owner_mix, at=(0,))
            + fetched(mixed_slope, flux_slope)
            + scalars(facts),
            shipped=[sz.narrow],
            scratch=[sz.narrow, (sz.slots, WIDTH)],
        )[0]
        if edge_sends is not None:
            back, *edge_sends = lax.optimization_barrier((back, *edge_sends))
            edges = swap(*edge_sends)
        back = exchange(back, devices)
        surface, *row_sends = call(
            functools.partial(merge_kernel, sz),
            "merge",
            near_by(back, *got)
            + fetched(surface, slope)
            + scalars(table, facts)
            + fetched(diffusivity_tiles),
            kept=[sz.surface, row_surface, row_surface],
        )
        surface_edges = swap(*row_sends)
        inputs = (
            near_by(surface, *edges, *surface_edges)
            + fetched(diffusivity_rows, mix)
            + far_off(field, drive)
        )
        if hour > 0:
            field, surface, packed, *sends = call(
                functools.partial(backward_kernel, sz, False),
                "step_back",
                inputs + scalars(tables, weights) + fetched(saved[hour - 1][1]),
                shipped=[sz.whole, sz.surface, sz.wide, sz.lats, sz.lats, sz.edge, sz.edge],
                scratch=[sz.whole, sz.whole, wider, row_sems(2), sz.near, sz.near],
            )
            sends, edge_sends = sends[:2], sends[2:]
        else:
            gradient, sums = call(
                functools.partial(backward_kernel, sz, True),
                "step_back_sums",
                inputs + far_off(start_field),
                shipped=[sz.whole, (devices, WIDTH)],
                scratch=[sz.whole, sz.whole, wider, row_sems(3), sz.whole],
            )

    everyones = lax.all_to_all(sums, "horiz", split_axis=0, concat_axis=0, tiled=True)
    block = perturbation.shape
    return call(
        functools.partial(final_kernel, perturbation.size * devices),
        "finish",
        near_by(everyones, perturbation, gradient.transpose(2, 0, 1, 3)),
        shipped=[block],
    )[0]


def solution(mesh):
    placed = (
        P("member", "horiz", None, None),
        P(None, "horiz", None, None),
        P(None, "horiz", None, None),
        P("horiz", None),
        P("horiz", None),
        P(),
        P(),
        P("horiz", None, None),
        P(None, "horiz", None, None),
        P(None, "horiz", None, None),
        P("horiz", None),
        P("horiz", None),
        P("horiz"),
        P("horiz"),
        P("horiz"),
    )
    return jax.shard_map(
        body,
        mesh=mesh,
        in_specs=placed,
        out_specs=P("member", "horiz", None, None),
        check_vma=False,
    )
```

profile of v0, /device:TPU:0, one launch (start us, length us, event | category | flops | bytes accessed | tf_op | source)
XLA Modules:
  0.0 195.9 jit_solution(3726354646877954818)
XLA Ops:
  0.0 1.7 edges.1
  1.8 2.4 %collective-permute-start = (f32[4,8,1920]{2,1,0:T(8,128)S(1)}, f32[4,8,1920]{2,1,0:T(8,128)S(1)}, u32[]{:S(2)}, u32[]{:S(2)}) collective-permute-start(f32[4,8,1920]{2,1,0:T(8,128)S(1)} %get-tuple-element.85), channel_id=1, source_target_pairs={{0,1},{1,2},{2,3},{3,4},{4,5},{5,6},{6,7},{7,8},{8,9},{9,10},{10,1... | collective-permute-start | bytes 737288 | tf_op jit(solution)/shard_map/ppermute | solution.py:871
  4.1 1.3 collective-permute-start.1
  5.5 0.1 reshape.82
  5.7 3.0 %load.1 = (f32[5,4,8,1920]{3,2,1,0:T(8,128)S(1)}, f32[5,4,8,1920]{3,2,1,0:T(8,128)}) custom-call(f32[8,5,4,1920]{3,2,1,0:T(4,128)} %refs_1_.13, f32[8,5,4,1920]{3,2,1,0:T(4,128)} %refs_1_.8), custom_call_target="tpu_custom_call" | custom-call | tf_op jit(solution)/shard_map/load/pallas_call | solution.py:851
  8.8 1.9 setup.1
  10.7 3.6 %step.2 = (f32[5,4,8,1920]{3,2,1,0:T(8,128)}, f32[5,4,8,1920]{3,2,1,0:T(8,128)}, f32[304,128]{1,0:T(8,128)}, f32[320,128]{1,0:T(8,128)}, f32[40,128]{1,0:T(8,128...) custom-call(f32[4,8,1920]{2,1,0:T(8,128)S(1)} %collective-permute-done.refs_0_, ...), custom_call_target="tpu_custom_call" | custom-call | tf_op jit(solution)/shard_map/step/pallas_call | solution.py:851
  14.3 9.4 %all-to-all-start = ((f32[16,5,4,128]{3,2,1,0:T(4,128)}), f32[16,5,4,128]{3,2,1,0:T(4,128)S(1)}, u32[]{:S(2)}, u32[]{:S(2)}) async-start(f32[16,5,4,128]{3,2,1,0:T(4,128)} %bitcast.50), calls=%async_computation | async-start | bytes 327680 | tf_op jit(solution)/shard_map/all_to_all | solution.py:877
  23.8 2.3 %collective-permute-start.2 = (f32[40,128]{1,0:T(8,128)}, f32[40,128]{1,0:T(8,128)S(1)}, u32[]{:S(2)}, u32[]{:S(2)}) collective-permute-start(f32[40,128]{1,0:T(8,128)} %get-tuple-element.93), channel_id=1, source_target_pairs={{0,1},{1,2},{2,3},{3,4},{4,5},{5,6},{6,7},{7,8},{8,9},{9,10},{10,1... | collective-permute-start | bytes 61448 | tf_op jit(solution)/shard_map/ppermute | solution.py:871
  26.1 1.3 collective-permute-start.3
  27.4 3.1 %collective-permute-done.3.refs_6_.refs_2_ = f32[40,128]{1,0:T(8,128)S(1)} collective-permute-done((f32[40,128]{1,0:T(8,128)}, f32[40,128]{1,0:T(8,128)S(1)}, u32[]{:S(2)}, u32[]{:S(2)}) %collective-permute-start.3) | collective-permute-done | bytes 20512 | tf_op jit(solution)/shard_map/ppermute | solution.py:871
  30.5 1.7 all-to-all-done
  32.2 2.2 %owners.2 = (s32[3,128]{1,0:T(4,128)}, f32[24,128]{1,0:T(8,128)}, f32[512,128]{1,0:T(8,128)}, f32[4,80,128]{2,1,0:T(8,128)}, f32[4,80,128]{2,1,0:T(8,128)}) custom-call(f32[320,128]{1,0:T(8,128)S(1)} %bitcast.37, f32[1,80,80]{2,1,0:T(8,128)} %refs_1_.12, f32[2,1,80,128]{3,2,1,0:T(8,128)} %refs_2_.5, f32[2,1,80,128]{3,2,1,0:T(8,128)} %refs_3_.7, ...), custom_call_target="tpu_custom_call" | custom-call | tf_op jit(solution)/shard_map/owners/pallas_call | solution.py:851
  34.4 6.0 %all-to-all-start.1 = ((f32[16,8,4,128]{3,2,1,0:T(4,128)}), f32[16,8,4,128]{3,2,1,0:T(4,128)S(1)}, u32[]{:S(2)}, u32[]{:S(2)}) async-start(f32[16,8,4,128]{3,2,1,0:T(4,128)} %bitcast.47), calls=%async_computation.1 | async-start | bytes 524288 | tf_op jit(solution)/shard_map/all_to_all | solution.py:877
  40.4 2.3 %collective-permute-start.4 = (f32[4,8,1920]{2,1,0:T(8,128)S(1)}, f32[4,8,1920]{2,1,0:T(8,128)S(1)}, u32[]{:S(2)}, u32[]{:S(2)}) collective-permute-start(f32[4,8,1920]{2,1,0:T(8,128)S(1)} %copy-done.10), channel_id=1, source_target_pairs={{0,1},{1,2},{2,3},{3,4},{4,5},{5,6},{6,7},{7,8},{8,9},{9,10},{10,1... | collective-permute-start | bytes 737288 | tf_op jit(solution)/shard_map/ppermute | solution.py:871
  42.7 1.3 collective-permute-start.5
  44.0 6.4 %all-to-all-done.1 = f32[16,8,4,128]{3,2,1,0:T(4,128)S(1)} async-done(((f32[16,8,4,128]{3,2,1,0:T(4,128)}), f32[16,8,4,128]{3,2,1,0:T(4,128)S(1)}, u32[]{:S(2)}, u32[]{:S(2)}) %all-to-all-start.1) | async-done | bytes 262176 | tf_op jit(solution)/shard_map/all_to_all | solution.py:877
  50.4 1.9 surface.2
  52.3 1.7 collective-permute-start.6
  54.1 1.3 collective-permute-start.7
  55.4 1.8 collective-permute-done.7.refs_9_
  57.2 4.9 %step.3 = (f32[5,4,8,1920]{3,2,1,0:T(8,128)}, f32[5,4,8,1920]{3,2,1,0:T(8,128)}, f32[304,128]{1,0:T(8,128)}, f32[320,128]{1,0:T(8,128)}, f32[40,128]{1,0:T(8,128...) custom-call(f32[4,8,1920]{2,1,0:T(8,128)S(1)} %collective-permute-done.4.refs_0_, ...), custom_call_target="tpu_custom_call" | custom-call | tf_op jit(solution)/shard_map/step/pallas_call | solution.py:851
  62.1 7.1 %all-to-all-start.2 = ((f32[16,5,4,128]{3,2,1,0:T(4,128)}), f32[16,5,4,128]{3,2,1,0:T(4,128)S(1)}, u32[]{:S(2)}, u32[]{:S(2)}) async-start(f32[16,5,4,128]{3,2,1,0:T(4,128)} %bitcast.49), calls=%async_computation.2 | async-start | bytes 327680 | tf_op jit(solution)/shard_map/all_to_all | solution.py:877
  69.2 2.3 %collective-permute-start.8 = (f32[40,128]{1,0:T(8,128)}, f32[40,128]{1,0:T(8,128)S(1)}, u32[]{:S(2)}, u32[]{:S(2)}) collective-permute-start(f32[40,128]{1,0:T(8,128)} %get-tuple-element.113), channel_id=1, source_target_pairs={{0,1},{1,2},{2,3},{3,4},{4,5},{5,6},{6,7},{7,8},{8,9},{9,10},{10,1... | collective-permute-start | bytes 61448 | tf_op jit(solution)/shard_map/ppermute | solution.py:871
  71.5 1.3 collective-permute-start.9
  72.8 3.1 %collective-permute-done.9.refs_2_ = f32[40,128]{1,0:T(8,128)S(1)} collective-permute-done((f32[40,128]{1,0:T(8,128)}, f32[40,128]{1,0:T(8,128)S(1)}, u32[]{:S(2)}, u32[]{:S(2)}) %collective-permute-start.9) | collective-permute-done | bytes 20512 | tf_op jit(solution)/shard_map/ppermute | solution.py:871
  75.9 1.7 all-to-all-done.2
  77.7 2.1 %owners.3 = (f32[512,128]{1,0:T(8,128)}, f32[4,80,128]{2,1,0:T(8,128)}, f32[4,80,128]{2,1,0:T(8,128)}) custom-call(f32[320,128]{1,0:T(8,128)S(1)} %bitcast.40, f32[1,80,80]{2,1,0:T(8,128)} %refs_1_.12, f32[2,1,80,128]{3,2,1,0:T(8,128)} %refs_2_.5, f32[2,1,80,128]{3,2,1,0:T(8,128)} %refs_3_.7, f32[8,128]{1,0:T(8,128)} %get-tuple-element.90.refs_5_.refs_7_.refs_4_.refs_8_.refs_6_), custom_call_target="tpu_custom_call" | custom-call | tf_op jit(solution)/shard_map/owners/pallas_call | solution.py:851
  79.8 16.0 %all_to_all.51 = f32[16,8,4,128]{3,2,1,0:T(4,128)S(1)} all-to-all(f32[16,8,4,128]{3,2,1,0:T(4,128)} %bitcast.48), channel_id=1, replica_groups=mesh['member'=2,'horiz'=16] {'horiz'}, dimensions={0} | all-to-all | bytes 524288 | tf_op jit(solution)/shard_map/all_to_all | solution.py:877
  95.8 2.3 %surface.3 = (f32[304,128]{1,0:T(8,128)}, f32[64,128]{1,0:T(8,128)}, f32[512,128]{1,0:T(8,128)}, f32[32,128]{1,0:T(8,128)}, f32[32,128]{1,0:T(8,128)}) custom-call(f32[512,128]{1,0:T(8,128)S(1)} %bitcast.36, f32[40,128]{1,0:T(8,128)S(1)} %collective-permute-done.8.refs_1_, f32[40,128]{1,0:T(8,128)S(1)} %collective-permute-done.9.refs_2_, ...), custom_call_target="tpu_custom_call" | custom-call | tf_op jit(solution)/shard_map/surface/pallas_call | solution.py:851
  98.2 3.7 %all-to-all-start.4 = ((f32[16,8,4,128]{3,2,1,0:T(4,128)}), f32[16,8,4,128]{3,2,1,0:T(4,128)S(1)}, u32[]{:S(2)}, u32[]{:S(2)}) async-start(f32[16,8,4,128]{3,2,1,0:T(4,128)} %bitcast.46), calls=%async_computation.4 | async-start | bytes 524288 | tf_op jit(solution)/shard_map/all_to_all | solution.py:877
  101.9 2.2 %collective-permute-start.10 = (f32[32,128]{1,0:T(8,128)}, f32[32,128]{1,0:T(8,128)S(1)}, u32[]{:S(2)}, u32[]{:S(2)}) collective-permute-start(f32[32,128]{1,0:T(8,128)} %get-tuple-element.125), channel_id=1, source_target_pairs={{0,1},{1,2},{2,3},{3,4},{4,5},{5,6},{6,7},{7,8},{8,9},{9,10},{10,1... | collective-permute-start | bytes 49160 | tf_op jit(solution)/shard_map/ppermute | solution.py:871
  104.0 1.3 collective-permute-start.11
  105.4 3.1 %collective-permute-done.11.refs_2_ = f32[32,128]{1,0:T(8,128)S(1)} collective-permute-done((f32[32,128]{1,0:T(8,128)}, f32[32,128]{1,0:T(8,128)S(1)}, u32[]{:S(2)}, u32[]{:S(2)}) %collective-permute-start.11) | collective-permute-done | bytes 16416 | tf_op jit(solution)/shard_map/ppermute | solution.py:871
  108.5 3.4 %all-to-all-done.4 = f32[16,8,4,128]{3,2,1,0:T(4,128)S(1)} async-done(((f32[16,8,4,128]{3,2,1,0:T(4,128)}), f32[16,8,4,128]{3,2,1,0:T(4,128)S(1)}, u32[]{:S(2)}, u32[]{:S(2)}) %all-to-all-start.4) | async-done | bytes 262176 | tf_op jit(solution)/shard_map/all_to_all | solution.py:877
  111.9 2.1 %owners_back.2 = f32[320,128]{1,0:T(8,128)} custom-call(f32[512,128]{1,0:T(8,128)S(1)} %bitcast.33, f32[1,80,80]{2,1,0:T(8,128)} %refs_1_.12, f32[4,80,128]{2,1,0:T(8,128)} %get-tuple-element.128.refs_2_, f32[4,80,128]{2,1,0:T(8,128)} %get-tuple-element.129.refs_3_, f32[8,128]{1,0:T(8,128)} %get-tuple-element.90.refs_5_.refs_7_.refs_4_.refs_8_.refs_6_), custom_call_target="tpu_custom_call" | custom-call | tf_op jit(solution)/shard_map/owners_back/pallas_call | solution.py:851
  114.0 4.3 %all-to-all-start.5 = ((f32[16,5,4,128]{3,2,1,0:T(4,128)}), f32[16,5,4,128]{3,2,1,0:T(4,128)S(1)}, u32[]{:S(2)}, u32[]{:S(2)}) async-start(f32[16,5,4,128]{3,2,1,0:T(4,128)} %bitcast.43), calls=%async_computation.5 | async-start | bytes 327680 | tf_op jit(solution)/shard_map/all_to_all | solution.py:877
  118.3 2.3 %collective-permute-start.12 = (f32[4,8,1920]{2,1,0:T(8,128)S(1)}, f32[4,8,1920]{2,1,0:T(8,128)S(1)}, u32[]{:S(2)}, u32[]{:S(2)}) collective-permute-start(f32[4,8,1920]{2,1,0:T(8,128)S(1)} %copy-done.6), channel_id=1, source_target_pairs={{0,1},{1,2},{2,3},{3,4},{4,5},{5,6},{6,7},{7,8},{8,9},{9,10},{10,1... | collective-permute-start | bytes 737288 | tf_op jit(solution)/shard_map/ppermute | solution.py:871
  120.6 1.3 collective-permute-start.13
  121.9 4.8 %all-to-all-done.5 = f32[16,5,4,128]{3,2,1,0:T(4,128)S(1)} async-done(((f32[16,5,4,128]{3,2,1,0:T(4,128)}), f32[16,5,4,128]{3,2,1,0:T(4,128)S(1)}, u32[]{:S(2)}, u32[]{:S(2)}) %all-to-all-start.5) | async-done | bytes 163872 | tf_op jit(solution)/shard_map/all_to_all | solution.py:877
  126.7 1.2 merge.2
  127.9 1.3 collective-permute-start.14
  129.2 1.3 collective-permute-start.15
  130.5 1.8 collective-permute-done.15.refs_4_
  132.3 4.5 %step_back.1 = (f32[5,4,8,1920]{3,2,1,0:T(8,128)}, f32[304,128]{1,0:T(8,128)}, f32[512,128]{1,0:T(8,128)}, f32[32,128]{1,0:T(8,128)}, f32[32,128]{1,0:T(8,128)},...) custom-call(f32[304,128]{1,0:T(8,128)S(1)} %get-tuple-element.135.refs_0_, ...), custom_call_target="tpu_custom_call" | custom-call | tf_op jit(solution)/shard_map/step_back/pallas_call | solution.py:851
  136.8 8.1 %all-to-all-start.6 = ((f32[16,8,4,128]{3,2,1,0:T(4,128)}), f32[16,8,4,128]{3,2,1,0:T(4,128)S(1)}, u32[]{:S(2)}, u32[]{:S(2)}) async-start(f32[16,8,4,128]{3,2,1,0:T(4,128)} %bitcast.45), calls=%async_computation.6 | async-start | bytes 524288 | tf_op jit(solution)/shard_map/all_to_all | solution.py:877
  145.0 2.3 %collective-permute-start.16 = (f32[32,128]{1,0:T(8,128)}, f32[32,128]{1,0:T(8,128)S(1)}, u32[]{:S(2)}, u32[]{:S(2)}) collective-permute-start(f32[32,128]{1,0:T(8,128)} %get-tuple-element.144), channel_id=1, source_target_pairs={{0,1},{1,2},{2,3},{3,4},{4,5},{5,6},{6,7},{7,8},{8,9},{9,10},{10,1... | collective-permute-start | bytes 49160 | tf_op jit(solution)/shard_map/ppermute | solution.py:871
  147.3 1.3 collective-permute-start.17
  148.6 3.1 %collective-permute-done.17.refs_2_ = f32[32,128]{1,0:T(8,128)S(1)} collective-permute-done((f32[32,128]{1,0:T(8,128)}, f32[32,128]{1,0:T(8,128)S(1)}, u32[]{:S(2)}, u32[]{:S(2)}) %collective-permute-start.17) | collective-permute-done | bytes 16416 | tf_op jit(solution)/shard_map/ppermute | solution.py:871
  151.7 3.3 %all-to-all-done.6 = f32[16,8,4,128]{3,2,1,0:T(4,128)S(1)} async-done(((f32[16,8,4,128]{3,2,1,0:T(4,128)}), f32[16,8,4,128]{3,2,1,0:T(4,128)S(1)}, u32[]{:S(2)}, u32[]{:S(2)}) %all-to-all-start.6) | async-done | bytes 262176 | tf_op jit(solution)/shard_map/all_to_all | solution.py:877
  155.0 2.1 %owners_back.3 = f32[320,128]{1,0:T(8,128)} custom-call(f32[512,128]{1,0:T(8,128)S(1)} %bitcast.34, f32[1,80,80]{2,1,0:T(8,128)} %refs_1_.12, f32[4,80,128]{2,1,0:T(8,128)} %get-tuple-element.147.refs_2_, f32[4,80,128]{2,1,0:T(8,128)} %get-tuple-element.148.refs_3_, f32[8,128]{1,0:T(8,128)} %get-tuple-element.90.refs_5_.refs_7_.refs_4_.refs_8_.refs_6_), custom_call_target="tpu_custom_call" | custom-call | tf_op jit(solution)/shard_map/owners_back/pallas_call | solution.py:851
  157.1 4.3 %all-to-all-start.7 = ((f32[16,5,4,128]{3,2,1,0:T(4,128)}), f32[16,5,4,128]{3,2,1,0:T(4,128)S(1)}, u32[]{:S(2)}, u32[]{:S(2)}) async-start(f32[16,5,4,128]{3,2,1,0:T(4,128)} %bitcast.44), calls=%async_computation.7 | async-start | bytes 327680 | tf_op jit(solution)/shard_map/all_to_all | solution.py:877
  161.4 2.3 %collective-permute-start.18 = (f32[4,8,1920]{2,1,0:T(8,128)S(1)}, f32[4,8,1920]{2,1,0:T(8,128)S(1)}, u32[]{:S(2)}, u32[]{:S(2)}) collective-permute-start(f32[4,8,1920]{2,1,0:T(8,128)S(1)} %copy-done.8), channel_id=1, source_target_pairs={{0,1},{1,2},{2,3},{3,4},{4,5},{5,6},{6,7},{7,8},{8,9},{9,10},{10,1... | collective-permute-start | bytes 737288 | tf_op jit(solution)/shard_map/ppermute | solution.py:871
  163.8 1.3 collective-permute-start.19
  165.1 4.8 %all-to-all-done.7 = f32[16,5,4,128]{3,2,1,0:T(4,128)S(1)} async-done(((f32[16,5,4,128]{3,2,1,0:T(4,128)}), f32[16,5,4,128]{3,2,1,0:T(4,128)S(1)}, u32[]{:S(2)}, u32[]{:S(2)}) %all-to-all-start.7) | async-done | bytes 163872 | tf_op jit(solution)/shard_map/all_to_all | solution.py:877
  169.9 1.2 merge.3
  171.1 1.3 collective-permute-start.20
  172.4 1.3 collective-permute-start.21
  173.7 1.8 collective-permute-done.21.refs_4_
  175.5 4.8 %step_back_sums.1 = (f32[5,4,8,1920]{3,2,1,0:T(8,128)}, f32[16,128]{1,0:T(8,128)}) custom-call(f32[304,128]{1,0:T(8,128)S(1)} %get-tuple-element.155.refs_0_, f32[4,8,1920]{2,1,0:T(8,128)S(1)} %collective-permute-done.18.refs_1_, f32[4,8,1920]{2,1,0:T(8,128)S(1)} %collective-permute-done.19.refs_2_, f32[60,128]{1,0:T(8,128)S(1)} %collective-permute-done.20.refs_3_, ...), custom_call_target="tpu_custom_call" | custom-call | tf_op jit(solution)/shard_map/step_back_sums/pallas_call | solution.py:851
  180.2 8.0 %all-to-all-start.8 = ((f32[16,1,128]{2,1,0:T(1,128)}), f32[16,1,128]{2,1,0:T(1,128)S(1)}, u32[]{:S(2)}, u32[]{:S(2)}) async-start(f32[16,1,128]{2,1,0:T(1,128)} %bitcast.51), calls=%async_computation.8 | async-start | bytes 16384 | tf_op jit(solution)/shard_map/all_to_all | solution.py:1084
  188.3 1.7 copy.20
  190.0 4.7 %all-to-all-done.8 = f32[16,1,128]{2,1,0:T(1,128)S(1)} async-done(((f32[16,1,128]{2,1,0:T(1,128)}), f32[16,1,128]{2,1,0:T(1,128)S(1)}, u32[]{:S(2)}, u32[]{:S(2)}) %all-to-all-start.8) | async-done | bytes 8224 | tf_op jit(solution)/shard_map/all_to_all | solution.py:1084
  194.7 1.2 finish.1
  (50 shorter events, 0.3 us)
Async XLA Ops:
  0.0 5.5 %copy-start.2 = (f32[4,4]{1,0:T(4,128)S(1)}, f32[4,4]{1,0:T(4,128)}, u32[]{:S(2)}) copy-start(f32[4,4]{1,0:T(4,128)} %param.21) | copy-start | bytes 196
  0.0 5.6 %copy-start.4 = (s32[15]{0:T(128)S(1)}, s32[15]{0:T(128)}, u32[]{:S(2)}) copy-start(s32[15]{0:T(128)} %param.28) | copy-start | bytes 184
  0.0 5.6 %copy-start.3 = (s32[15]{0:T(128)S(1)}, s32[15]{0:T(128)}, u32[]{:S(2)}) copy-start(s32[15]{0:T(128)} %param.27) | copy-start | bytes 184
  0.0 5.6 %copy-start.11 = (f32[15]{0:T(128)S(1)}, f32[15]{0:T(128)}, u32[]{:S(2)}) copy-start(f32[15]{0:T(128)} %param.29) | copy-start | bytes 184
  1.8 8.9 %collective-permute-start = (f32[4,8,1920]{2,1,0:T(8,128)S(1)}, f32[4,8,1920]{2,1,0:T(8,128)S(1)}, u32[]{:S(2)}, u32[]{:S(2)}) collective-permute-start(f32[4,8,1920]{2,1,0:T(8,128)S(1)} %get-tuple-element.85), channel_id=1, source_target_pairs={{0,1},{1,2},{2,3},{3,4},{4,5},{5,6},{6,7},{7,8},{8,9},{9,10},{10,1... | collective-permute-start | bytes 737288 | tf_op jit(solution)/shard_map/ppermute | solution.py:871
  4.1 6.5 %collective-permute-start.1 = (f32[4,8,1920]{2,1,0:T(8,128)S(1)}, f32[4,8,1920]{2,1,0:T(8,128)S(1)}, u32[]{:S(2)}, u32[]{:S(2)}) collective-permute-start(f32[4,8,1920]{2,1,0:T(8,128)S(1)} %get-tuple-element.86), channel_id=1, source_target_pairs={{1,0},{2,1},{3,2},{4,3},{5,4},{6,5},{7,6},{8,7},{9,8},{10,9},{11,1... | collective-permute-start | bytes 737288 | tf_op jit(solution)/shard_map/ppermute | solution.py:871
  5.7 3.0 %copy-start.12 = (s32[1,75]{1,0:T(1,128)S(1)}, s32[1,75]{1,0:T(1,128)}, u32[]{:S(2)}) copy-start(s32[1,75]{1,0:T(1,128)} %param.25) | copy-start | bytes 904
  5.7 3.0 %copy-start.13 = (s32[1,75]{1,0:T(1,128)S(1)}, s32[1,75]{1,0:T(1,128)}, u32[]{:S(2)}) copy-start(s32[1,75]{1,0:T(1,128)} %param.26) | copy-start | bytes 904
  5.7 3.1 %copy-start.1 = (f32[8,4,4]{0,2,1:T(4,128)S(1)}, f32[8,4,4]{0,2,1:T(4,128)}, u32[]{:S(2)}) copy-start(f32[8,4,4]{0,2,1:T(4,128)} %param.20) | copy-start | bytes 1540
  14.3 26.1 %copy-start.10 = (f32[4,8,1920]{2,1,0:T(8,128)S(1)}, f32[4,8,1920]{2,1,0:T(8,128)}, u32[]{:S(2)}) copy-start(f32[4,8,1920]{2,1,0:T(8,128)} %get-tuple-element.101) | copy-start | bytes 737284
  14.3 28.4 %copy-start.9 = (f32[4,8,1920]{2,1,0:T(8,128)S(1)}, f32[4,8,1920]{2,1,0:T(8,128)}, u32[]{:S(2)}) copy-start(f32[4,8,1920]{2,1,0:T(8,128)} %get-tuple-element.102) | copy-start | bytes 737284
  14.3 17.9 %all-to-all-start = ((f32[16,5,4,128]{3,2,1,0:T(4,128)}), f32[16,5,4,128]{3,2,1,0:T(4,128)S(1)}, u32[]{:S(2)}, u32[]{:S(2)}) async-start(f32[16,5,4,128]{3,2,1,0:T(4,128)} %bitcast.50), calls=%async_computation | async-start | bytes 327680 | tf_op jit(solution)/shard_map/all_to_all | solution.py:877
  23.8 3.6 %collective-permute-start.2 = (f32[40,128]{1,0:T(8,128)}, f32[40,128]{1,0:T(8,128)S(1)}, u32[]{:S(2)}, u32[]{:S(2)}) collective-permute-start(f32[40,128]{1,0:T(8,128)} %get-tuple-element.93), channel_id=1, source_target_pairs={{0,1},{1,2},{2,3},{3,4},{4,5},{5,6},{6,7},{7,8},{8,9},{9,10},{10,1... | collective-permute-start | bytes 61448 | tf_op jit(solution)/shard_map/ppermute | solution.py:871
  26.1 4.4 %collective-permute-start.3 = (f32[40,128]{1,0:T(8,128)}, f32[40,128]{1,0:T(8,128)S(1)}, u32[]{:S(2)}, u32[]{:S(2)}) collective-permute-start(f32[40,128]{1,0:T(8,128)} %get-tuple-element.94), channel_id=1, source_target_pairs={{1,0},{2,1},{3,2},{4,3},{5,4},{6,5},{7,6},{8,7},{9,8},{10,9},{11,1... | collective-permute-start | bytes 61448 | tf_op jit(solution)/shard_map/ppermute | solution.py:871
  34.4 16.0 %all-to-all-start.1 = ((f32[16,8,4,128]{3,2,1,0:T(4,128)}), f32[16,8,4,128]{3,2,1,0:T(4,128)S(1)}, u32[]{:S(2)}, u32[]{:S(2)}) async-start(f32[16,8,4,128]{3,2,1,0:T(4,128)} %bitcast.47), calls=%async_computation.1 | async-start | bytes 524288 | tf_op jit(solution)/shard_map/all_to_all | solution.py:877
  40.4 15.0 %collective-permute-start.4 = (f32[4,8,1920]{2,1,0:T(8,128)S(1)}, f32[4,8,1920]{2,1,0:T(8,128)S(1)}, u32[]{:S(2)}, u32[]{:S(2)}) collective-permute-start(f32[4,8,1920]{2,1,0:T(8,128)S(1)} %copy-done.10), channel_id=1, source_target_pairs={{0,1},{1,2},{2,3},{3,4},{4,5},{5,6},{6,7},{7,8},{8,9},{9,10},{10,1... | collective-permute-start | bytes 737288 | tf_op jit(solution)/shard_map/ppermute | solution.py:871
  42.7 12.7 %collective-permute-start.5 = (f32[4,8,1920]{2,1,0:T(8,128)S(1)}, f32[4,8,1920]{2,1,0:T(8,128)S(1)}, u32[]{:S(2)}, u32[]{:S(2)}) collective-permute-start(f32[4,8,1920]{2,1,0:T(8,128)S(1)} %copy-done.9), channel_id=1, source_target_pairs={{1,0},{2,1},{3,2},{4,3},{5,4},{6,5},{7,6},{8,7},{9,8},{10,9},{11,1... | collective-permute-start | bytes 737288 | tf_op jit(solution)/shard_map/ppermute | solution.py:871
  52.3 3.1 %collective-permute-start.6 = (f32[60,128]{1,0:T(8,128)S(1)}, f32[60,128]{1,0:T(8,128)S(1)}, u32[]{:S(2)}, u32[]{:S(2)}) collective-permute-start(f32[60,128]{1,0:T(8,128)S(1)} %get-tuple-element.109), channel_id=1, source_target_pairs={{0,1},{1,2},{2,3},{3,4},{4,5},{5,6},{6,7},{7,8},{8,9},{9,10},{10,1... | collective-permute-start | bytes 92168 | tf_op jit(solution)/shard_map/ppermute | solution.py:871
  54.1 3.1 %collective-permute-start.7 = (f32[60,128]{1,0:T(8,128)S(1)}, f32[60,128]{1,0:T(8,128)S(1)}, u32[]{:S(2)}, u32[]{:S(2)}) collective-permute-start(f32[60,128]{1,0:T(8,128)S(1)} %get-tuple-element.110), channel_id=1, source_target_pairs={{1,0},{2,1},{3,2},{4,3},{5,4},{6,5},{7,6},{8,7},{9,8},{10,9},{11,1... | collective-permute-start | bytes 92168 | tf_op jit(solution)/shard_map/ppermute | solution.py:871
  62.1 15.6 %all-to-all-start.2 = ((f32[16,5,4,128]{3,2,1,0:T(4,128)}), f32[16,5,4,128]{3,2,1,0:T(4,128)S(1)}, u32[]{:S(2)}, u32[]{:S(2)}) async-start(f32[16,5,4,128]{3,2,1,0:T(4,128)} %bitcast.49), calls=%async_computation.2 | async-start | bytes 327680 | tf_op jit(solution)/shard_map/all_to_all | solution.py:877
  69.2 3.6 %collective-permute-start.8 = (f32[40,128]{1,0:T(8,128)}, f32[40,128]{1,0:T(8,128)S(1)}, u32[]{:S(2)}, u32[]{:S(2)}) collective-permute-start(f32[40,128]{1,0:T(8,128)} %get-tuple-element.113), channel_id=1, source_target_pairs={{0,1},{1,2},{2,3},{3,4},{4,5},{5,6},{6,7},{7,8},{8,9},{9,10},{10,1... | collective-permute-start | bytes 61448 | tf_op jit(solution)/shard_map/ppermute | solution.py:871
  71.5 4.4 %collective-permute-start.9 = (f32[40,128]{1,0:T(8,128)}, f32[40,128]{1,0:T(8,128)S(1)}, u32[]{:S(2)}, u32[]{:S(2)}) collective-permute-start(f32[40,128]{1,0:T(8,128)} %get-tuple-element.114), channel_id=1, source_target_pairs={{1,0},{2,1},{3,2},{4,3},{5,4},{6,5},{7,6},{8,7},{9,8},{10,9},{11,1... | collective-permute-start | bytes 61448 | tf_op jit(solution)/shard_map/ppermute | solution.py:871
  98.2 20.1 %copy-start.6 = (f32[4,8,1920]{2,1,0:T(8,128)S(1)}, f32[4,8,1920]{2,1,0:T(8,128)}, u32[]{:S(2)}) copy-start(f32[4,8,1920]{2,1,0:T(8,128)} %get-tuple-element.136) | copy-start | bytes 737284
  98.2 22.5 %copy-start.5 = (f32[4,8,1920]{2,1,0:T(8,128)S(1)}, f32[4,8,1920]{2,1,0:T(8,128)}, u32[]{:S(2)}) copy-start(f32[4,8,1920]{2,1,0:T(8,128)} %get-tuple-element.137) | copy-start | bytes 737284
  98.2 13.7 %all-to-all-start.4 = ((f32[16,8,4,128]{3,2,1,0:T(4,128)}), f32[16,8,4,128]{3,2,1,0:T(4,128)S(1)}, u32[]{:S(2)}, u32[]{:S(2)}) async-start(f32[16,8,4,128]{3,2,1,0:T(4,128)} %bitcast.46), calls=%async_computation.4 | async-start | bytes 524288 | tf_op jit(solution)/shard_map/all_to_all | solution.py:877
  101.9 3.5 %collective-permute-start.10 = (f32[32,128]{1,0:T(8,128)}, f32[32,128]{1,0:T(8,128)S(1)}, u32[]{:S(2)}, u32[]{:S(2)}) collective-permute-start(f32[32,128]{1,0:T(8,128)} %get-tuple-element.125), channel_id=1, source_target_pairs={{0,1},{1,2},{2,3},{3,4},{4,5},{5,6},{6,7},{7,8},{8,9},{9,10},{10,1... | collective-permute-start | bytes 49160 | tf_op jit(solution)/shard_map/ppermute | solution.py:871
  104.0 4.4 %collective-permute-start.11 = (f32[32,128]{1,0:T(8,128)}, f32[32,128]{1,0:T(8,128)S(1)}, u32[]{:S(2)}, u32[]{:S(2)}) collective-permute-start(f32[32,128]{1,0:T(8,128)} %get-tuple-element.126), channel_id=1, source_target_pairs={{1,0},{2,1},{3,2},{4,3},{5,4},{6,5},{7,6},{8,7},{9,8},{10,9},{11,1... | collective-permute-start | bytes 49160 | tf_op jit(solution)/shard_map/ppermute | solution.py:871
  114.0 12.8 %all-to-all-start.5 = ((f32[16,5,4,128]{3,2,1,0:T(4,128)}), f32[16,5,4,128]{3,2,1,0:T(4,128)S(1)}, u32[]{:S(2)}, u32[]{:S(2)}) async-start(f32[16,5,4,128]{3,2,1,0:T(4,128)} %bitcast.43), calls=%async_computation.5 | async-start | bytes 327680 | tf_op jit(solution)/shard_map/all_to_all | solution.py:877
  118.3 12.2 %collective-permute-start.12 = (f32[4,8,1920]{2,1,0:T(8,128)S(1)}, f32[4,8,1920]{2,1,0:T(8,128)S(1)}, u32[]{:S(2)}, u32[]{:S(2)}) collective-permute-start(f32[4,8,1920]{2,1,0:T(8,128)S(1)} %copy-done.6), channel_id=1, source_target_pairs={{0,1},{1,2},{2,3},{3,4},{4,5},{5,6},{6,7},{7,8},{8,9},{9,10},{10,1... | collective-permute-start | bytes 737288 | tf_op jit(solution)/shard_map/ppermute | solution.py:871
  120.6 9.9 %collective-permute-start.13 = (f32[4,8,1920]{2,1,0:T(8,128)S(1)}, f32[4,8,1920]{2,1,0:T(8,128)S(1)}, u32[]{:S(2)}, u32[]{:S(2)}) collective-permute-start(f32[4,8,1920]{2,1,0:T(8,128)S(1)} %copy-done.5), channel_id=1, source_target_pairs={{1,0},{2,1},{3,2},{4,3},{5,4},{6,5},{7,6},{8,7},{9,8},{10,9},{11,1... | collective-permute-start | bytes 737288 | tf_op jit(solution)/shard_map/ppermute | solution.py:871
  127.9 2.6 %collective-permute-start.14 = (f32[60,128]{1,0:T(8,128)S(1)}, f32[60,128]{1,0:T(8,128)S(1)}, u32[]{:S(2)}, u32[]{:S(2)}) collective-permute-start(f32[60,128]{1,0:T(8,128)S(1)} %get-tuple-element.138), channel_id=1, source_target_pairs={{0,1},{1,2},{2,3},{3,4},{4,5},{5,6},{6,7},{7,8},{8,9},{9,10},{10,1... | collective-permute-start | bytes 92168 | tf_op jit(solution)/shard_map/ppermute | solution.py:871
  129.2 3.1 %collective-permute-start.15 = (f32[60,128]{1,0:T(8,128)S(1)}, f32[60,128]{1,0:T(8,128)S(1)}, u32[]{:S(2)}, u32[]{:S(2)}) collective-permute-start(f32[60,128]{1,0:T(8,128)S(1)} %get-tuple-element.139), channel_id=1, source_target_pairs={{1,0},{2,1},{3,2},{4,3},{5,4},{6,5},{7,6},{8,7},{9,8},{10,9},{11,1... | collective-permute-start | bytes 92168 | tf_op jit(solution)/shard_map/ppermute | solution.py:871
  136.8 24.6 %copy-start.8 = (f32[4,8,1920]{2,1,0:T(8,128)S(1)}, f32[4,8,1920]{2,1,0:T(8,128)}, u32[]{:S(2)}) copy-start(f32[4,8,1920]{2,1,0:T(8,128)} %get-tuple-element.156) | copy-start | bytes 737284
  136.8 27.0 %copy-start.7 = (f32[4,8,1920]{2,1,0:T(8,128)S(1)}, f32[4,8,1920]{2,1,0:T(8,128)}, u32[]{:S(2)}) copy-start(f32[4,8,1920]{2,1,0:T(8,128)} %get-tuple-element.157) | copy-start | bytes 737284
  136.8 18.2 %all-to-all-start.6 = ((f32[16,8,4,128]{3,2,1,0:T(4,128)}), f32[16,8,4,128]{3,2,1,0:T(4,128)S(1)}, u32[]{:S(2)}, u32[]{:S(2)}) async-start(f32[16,8,4,128]{3,2,1,0:T(4,128)} %bitcast.45), calls=%async_computation.6 | async-start | bytes 524288 | tf_op jit(solution)/shard_map/all_to_all | solution.py:877
  145.0 3.6 %collective-permute-start.16 = (f32[32,128]{1,0:T(8,128)}, f32[32,128]{1,0:T(8,128)S(1)}, u32[]{:S(2)}, u32[]{:S(2)}) collective-permute-start(f32[32,128]{1,0:T(8,128)} %get-tuple-element.144), channel_id=1, source_target_pairs={{0,1},{1,2},{2,3},{3,4},{4,5},{5,6},{6,7},{7,8},{8,9},{9,10},{10,1... | collective-permute-start | bytes 49160 | tf_op jit(solution)/shard_map/ppermute | solution.py:871
  147.3 4.4 %collective-permute-start.17 = (f32[32,128]{1,0:T(8,128)}, f32[32,128]{1,0:T(8,128)S(1)}, u32[]{:S(2)}, u32[]{:S(2)}) collective-permute-start(f32[32,128]{1,0:T(8,128)} %get-tuple-element.145), channel_id=1, source_target_pairs={{1,0},{2,1},{3,2},{4,3},{5,4},{6,5},{7,6},{8,7},{9,8},{10,9},{11,1... | collective-permute-start | bytes 49160 | tf_op jit(solution)/shard_map/ppermute | solution.py:871
  157.1 12.8 %all-to-all-start.7 = ((f32[16,5,4,128]{3,2,1,0:T(4,128)}), f32[16,5,4,128]{3,2,1,0:T(4,128)S(1)}, u32[]{:S(2)}, u32[]{:S(2)}) async-start(f32[16,5,4,128]{3,2,1,0:T(4,128)} %bitcast.44), calls=%async_computation.7 | async-start | bytes 327680 | tf_op jit(solution)/shard_map/all_to_all | solution.py:877
  161.4 12.2 %collective-permute-start.18 = (f32[4,8,1920]{2,1,0:T(8,128)S(1)}, f32[4,8,1920]{2,1,0:T(8,128)S(1)}, u32[]{:S(2)}, u32[]{:S(2)}) collective-permute-start(f32[4,8,1920]{2,1,0:T(8,128)S(1)} %copy-done.8), channel_id=1, source_target_pairs={{0,1},{1,2},{2,3},{3,4},{4,5},{5,6},{6,7},{7,8},{8,9},{9,10},{10,1... | collective-permute-start | bytes 737288 | tf_op jit(solution)/shard_map/ppermute | solution.py:871
  163.8 9.9 %collective-permute-start.19 = (f32[4,8,1920]{2,1,0:T(8,128)S(1)}, f32[4,8,1920]{2,1,0:T(8,128)S(1)}, u32[]{:S(2)}, u32[]{:S(2)}) collective-permute-start(f32[4,8,1920]{2,1,0:T(8,128)S(1)} %copy-done.7), channel_id=1, source_target_pairs={{1,0},{2,1},{3,2},{4,3},{5,4},{6,5},{7,6},{8,7},{9,8},{10,9},{11,1... | collective-permute-start | bytes 737288 | tf_op jit(solution)/shard_map/ppermute | solution.py:871
  171.1 2.6 %collective-permute-start.20 = (f32[60,128]{1,0:T(8,128)S(1)}, f32[60,128]{1,0:T(8,128)S(1)}, u32[]{:S(2)}, u32[]{:S(2)}) collective-permute-start(f32[60,128]{1,0:T(8,128)S(1)} %get-tuple-element.158), channel_id=1, source_target_pairs={{0,1},{1,2},{2,3},{3,4},{4,5},{5,6},{6,7},{7,8},{8,9},{9,10},{10,1... | collective-permute-start | bytes 92168 | tf_op jit(solution)/shard_map/ppermute | solution.py:871
  172.4 3.1 %collective-permute-start.21 = (f32[60,128]{1,0:T(8,128)S(1)}, f32[60,128]{1,0:T(8,128)S(1)}, u32[]{:S(2)}, u32[]{:S(2)}) collective-permute-start(f32[60,128]{1,0:T(8,128)S(1)} %get-tuple-element.159), channel_id=1, source_target_pairs={{1,0},{2,1},{3,2},{4,3},{5,4},{6,5},{7,6},{8,7},{9,8},{10,9},{11,1... | collective-permute-start | bytes 92168 | tf_op jit(solution)/shard_map/ppermute | solution.py:871
  180.2 14.4 %all-to-all-start.8 = ((f32[16,1,128]{2,1,0:T(1,128)}), f32[16,1,128]{2,1,0:T(1,128)S(1)}, u32[]{:S(2)}, u32[]{:S(2)}) async-start(f32[16,1,128]{2,1,0:T(1,128)} %bitcast.51), calls=%async_computation.8 | async-start | bytes 16384 | tf_op jit(solution)/shard_map/all_to_all | solution.py:1084
  188.3 6.4 %copy-start = (f32[8,5,4,1920]{3,2,1,0:T(4,128)S(1)}, f32[8,5,4,1920]{3,2,1,0:T(4,128)}, u32[]{:S(2)}) copy-start(f32[8,5,4,1920]{3,2,1,0:T(4,128)} %refs_1_.13) | copy-start | bytes 3686404
where the time goes:
time: 198 us; the launch traced here: 196 us
  starting transfers between devices  87.9 us (44%)
  waiting for transfers between devices  48.7 us (25%)
  Pallas kernels  40.6 us (21%)
  blocking collectives  16 us (8%)
    all_to_all x7, starting transfers between devices, exchange(): lax.all_to_all(split, 'horiz', split_axis=0, concat_axis=0, tiled=True)  42.9 us
    pallas_call x16, Pallas kernels, call(): pl.pallas_call(run, name=name, in_specs=[pl.BlockSpec(memory_space=item.s...  40.6 us
    all_to_all x7, waiting for transfers between devices, exchange(): lax.all_to_all(split, 'horiz', split_axis=0, concat_axis=0, tiled=True)  26.2 us
    ppermute x11, starting transfers between devices, swap(): lax.ppermute(high, 'horiz', upward)  22.8 us
    ppermute x11, waiting for transfers between devices, swap(): lax.ppermute(low, 'horiz', downward)  17.8 us
    all_to_all x1, blocking collectives, exchange(): lax.all_to_all(split, 'horiz', split_axis=0, concat_axis=0, tiled=True)  16 us
    ppermute x11, starting transfers between devices, swap(): lax.ppermute(low, 'horiz', downward)  14.2 us
    all_to_all x1, starting transfers between devices, body(): lax.all_to_all(sums, 'horiz', split_axis=0, concat_axis=0, tiled=True)  8 us
  transfers between devices with their start and end apart: 30, of which 15 were waited for; matrix products, arithmetic and copies ran while one was open for 1% of the time, Pallas kernels for 5%

commit v1 on v0

--- a/solution.py
+++ b/solution.py
@@ -115,6 +115,19 @@
 
 def near_row(sz, ref, row):
     return ref[row * sz.row_tiles : (row + 1) * sz.row_tiles, :]
+
+
+def high_first():
+    return 1 - lax.rem(lax.axis_index("horiz").astype(jnp.int32), 2)
+
+
+def pick(flag, one, other):
+    return jnp.where(jnp.full(one.shape, flag, jnp.int32) == 1, one, other)
+
+
+def sided(first, second):
+    flag = high_first()
+    return pick(flag, second, first), pick(flag, first, second)
 
 
 def load_surface_row(sz, target, row, source, base):
@@ -182,14 +195,17 @@
     return total
 
 
-def edges_kernel(sz, arrive, low_start, high_start, low_base, high_base, low, high):
+def edges_kernel(sz, arrive, low_start, high_start, low_base, high_base, send_first, send_second):
     arrive_all(arrive)
-    for start, base, edge in ((low_start, low_base, low), (high_start, high_base, high)):
-        for channel in range(CHANNELS):
-            for tile in range(sz.row_tiles):
-                edge[channel, :, cols(tile)] = gather_levels(
-                    start, (), channel, tile
-                ) + gather_levels(base, (), channel, tile)
+    flag = high_first()
+    for channel in range(CHANNELS):
+        for tile in range(sz.row_tiles):
+            low = gather_levels(low_start, (), channel, tile)
+            low = low + gather_levels(low_base, (), channel, tile)
+            high = gather_levels(high_start, (), channel, tile)
+            high = high + gather_levels(high_base, (), channel, tile)
+            send_first[channel, :, cols(tile)] = pick(flag, high, low)
+            send_second[channel, :, cols(tile)] = pick(flag, low, high)
 
 
 def load_kernel(sz, arrive, perturbation, base, field, start, start_block, base_block, in_sems):
@@ -257,22 +273,45 @@
     ]
 
 
-def send_sums(sz, sums, send_low, send_high):
-    for lat in range(NEAR_LAT):
-        send = send_low if lat < LAT_DEV else send_high
-        at = (lat % LAT_DEV) * sz.pitch
-        send[at : at + sz.row_tiles, :] = sums[lat]
+def send_sums(sz, sums, tell_first, tell_second):
+    flag = high_first()
+    for index in range(LAT_DEV):
+        low, high = sums[index], sums[LAT_DEV + index]
+        at = index * sz.pitch
+        tell_first[at : at + sz.row_tiles, :] = pick(flag, high, low)
+        tell_second[at : at + sz.row_tiles, :] = pick(flag, low, high)
 
 
 def lat_rows(sz, ref, lat):
     return ref[lat * sz.pitch : lat * sz.pitch + sz.row_tiles, :]
 
 
-def told_sums(sz, from_low, from_high):
-    return [
-        lat_rows(sz, from_low if lat < LAT_DEV else from_high, lat % LAT_DEV)
-        for lat in range(NEAR_LAT)
-    ]
+def told_sums(sz, from_first, from_second):
+    lows, highs = [], []
+    for index in range(LAT_DEV):
+        low, high = sided(lat_rows(sz, from_first, index), lat_rows(sz, from_second, index))
+        lows.append(low)
+        highs.append(high)
+    return lows + highs
+
+
+def place_edges(sz, padded, first, second, first_surface=None, second_surface=None):
+    side = high_first() * (sz.rows + 1)
+    for at, edge, surface in ((side, first, first_surface), (sz.rows + 1 - side, second, second_surface)):
+        padded[at] = edge[...]
+        if surface is not None:
+            load_surface_row(sz, padded, at, surface, 0)
+
+
+def store_rows(sz, surface, send_first, send_second, factor=None):
+    row = high_first() * (sz.rows - 1)
+    for at, send in ((row, send_first), (sz.rows - 1 - row, send_second)):
+        for tile in range(sz.row_tiles):
+            start = pl.multiple_of((at * sz.row_tiles + tile) * CHANNELS, CHANNELS)
+            value = surface[pl.ds(start, CHANNELS), :]
+            if factor is not None:
+                value = factor[pl.ds(start, CHANNELS), :] * value
+            send[tile * CHANNELS : (tile + 1) * CHANNELS, :] = value
 
 
 def forward_kernel(sz, first, last, arrive, *refs):
@@ -283,12 +322,12 @@
         told_facts = refs[0]
         refs = refs[1:]
     else:
-        surface, low_surface, high_surface = refs[:3]
+        surface, first_surface, second_surface = refs[:3]
         refs = refs[3:]
     if last:
         weight, target = refs[:2]
         refs = refs[2:]
-    out, drive, new_surface, packed, tell_low, tell_high, edge_low, edge_high, padded = refs[:9]
+    out, drive, new_surface, packed, tell_first, tell_second, edge_first, edge_second, padded = refs[:9]
     remap = Remap(sz, facts)
     if not first:
         in_sems = refs[9]
@@ -306,11 +345,10 @@
             for arrival in arrivals(row):
                 arrival.start()
     arrive_all(arrive)
-    padded[0] = low[...]
-    padded[sz.rows + 1] = high[...]
-    if not first:
-        load_surface_row(sz, padded, 0, low_surface, 0)
-        load_surface_row(sz, padded, sz.rows + 1, high_surface, 0)
+    if first:
+        place_edges(sz, padded, low, high)
+    else:
+        place_edges(sz, padded, low, high, first_surface, second_surface)
 
     def ready(row):
         if first:
@@ -371,12 +409,12 @@
     pack_slots(sz, tables, new_surface, packed)
     packed.start()
     own = [row_tiles_of(sz, new_surface.block, row) for row in range(sz.rows)]
-    send_sums(sz, own_sums(sz, remap, own, 1.0), tell_low, tell_high)
+    send_sums(sz, own_sums(sz, remap, own, 1.0), tell_first, tell_second)
     blank = told_facts[...] if first else jnp.zeros((sz.facts, WIDTH), jnp.float32)
-    for tell in (tell_low, tell_high):
+    for tell in (tell_first, tell_second):
         tell[sz.lat_lines :, :] = blank
         tell.start()
-    store_edges(sz, out, diffusivity if last else None, edge_low, edge_high)
+    store_edges(sz, out, diffusivity if last else None, edge_first, edge_second)
 
 
 def pack_slots(sz, tables, surface, packed):
@@ -385,8 +423,9 @@
         packed[slot * CHANNELS : (slot + 1) * CHANNELS, :] = surface[pl.ds(at, CHANNELS), :]
 
 
-def store_edges(sz, field, diffusivity, send_low, send_high):
-    for row, send in ((0, send_low), (sz.rows - 1, send_high)):
+def store_edges(sz, field, diffusivity, send_first, send_second):
+    outer = high_first() * (sz.rows - 1)
+    for row, send in ((outer, send_first), (sz.rows - 1 - outer, send_second)):
         for channel in range(CHANNELS):
             for tile in range(sz.row_tiles):
                 value = field[row, channel, :, cols(tile)]
@@ -401,7 +440,7 @@
 def owner_kernel(sz, decode, arrive, arrived, mixing, air, wind, facts, *refs):
     slots = sz.slots
     if decode:
-        told_low, told_high, own_table, own_facts, tables, weights = refs[:6]
+        told_first, told_second, own_table, own_facts, tables, weights = refs[:6]
         refs = refs[6:]
     flux, mixed_slope, flux_slope, flat, first = refs
     arrive_all(arrive)
@@ -409,11 +448,12 @@
         lines = sz.slot_lines
         tables[0:lines, :] = own_table[...]
         weights[0 : sz.facts, :] = own_facts[...]
-        for which, told in ((1, told_low), (2, told_high)):
-            got = told[sz.lat_lines : sz.lat_lines + lines, :]
-            tables[which * lines : (which + 1) * lines, :] = sz.tiles - got.astype(jnp.int32)
+        both = sided(told_first[sz.lat_lines :, :], told_second[sz.lat_lines :, :])
+        for which, told in ((1, both[0]), (2, both[1])):
+            got = told[0:lines, :].astype(jnp.int32)
+            tables[which * lines : (which + 1) * lines, :] = sz.tiles - got
             at = which * sz.facts
-            weights[at : at + sz.facts, :] = told[sz.lat_lines :, :]
+            weights[at : at + sz.facts, :] = told
         tables.start()
         weights.start()
 
@@ -502,14 +542,14 @@
         back.block[pl.ds(k, slots, stride=CHANNELS), :] = through[:, cols(k)] + sign * direct[k]
 
 
-def spread_back(sz, surface, slope, remap, tables, packed, near_low, near_high, tell_low, tell_high):
+def spread_back(sz, surface, slope, remap, tables, packed, near_low, near_high, tell_first, tell_second):
     rows, count, cap = sz.rows, sz.row_tiles, sz.capacity
     block = surface.block
     own = [row_tiles_of(sz, block, row) for row in range(rows)]
     sums = own_sums(sz, remap, own, FEEDBACK)
-    send_sums(sz, sums, tell_low, tell_high)
-    tell_low.start()
-    tell_high.start()
+    send_sums(sz, sums, tell_first, tell_second)
+    tell_first.start()
+    tell_second.start()
     lats = [lat_rows(sz, slope, lat) * sums[lat] for lat in range(NEAR_LAT)]
     every = range(NEAR_LAT)
     for row in range(rows):
@@ -542,14 +582,14 @@
 
 def surface_kernel(sz, last, arrive, *refs):
     refs = list(refs)
-    flux, from_low, from_high, before, tables, weights = refs[:6]
+    flux, from_first, from_second, before, tables, weights = refs[:6]
     refs = refs[6:]
     if last:
         target, weight = refs[:2]
-        surface, slope, packed, tell_low, tell_high, near_low, near_high = refs[2:]
+        surface, slope, packed, tell_first, tell_second, near_low, near_high = refs[2:]
         block = surface.block
     else:
-        surface, send_low, send_high, slope, near_low, near_high = refs
+        surface, send_first, send_second, slope, near_low, near_high = refs
         block = surface
     remap = Remap(sz, weights)
     arrive_all(arrive)
@@ -571,7 +611,7 @@
     block[CHANNELS * sz.tiles :, :] = jnp.zeros((CHANNELS, WIDTH), jnp.float32)
     own = [row_tiles_of(sz, block, row) for row in range(rows)]
     sums = own_sums(sz, remap, own, 1.0)
-    told = told_sums(sz, from_low, from_high)
+    told = told_sums(sz, from_first, from_second)
     air = []
     for lat in range(NEAR_LAT):
         if lat < LAT_DEV:
@@ -594,17 +634,16 @@
                 off = block[at : at + CHANNELS, :] - target[row, :, cols(tile)]
                 block[at : at + CHANNELS, :] = scale * scale * off
         spread_back(
-            sz, surface, slope, remap, tables, packed, near_low, near_high, tell_low, tell_high
+            sz, surface, slope, remap, tables, packed, near_low, near_high, tell_first, tell_second
         )
     else:
-        send_low[...] = surface[0 : sz.row_width, :]
-        send_high[...] = surface[(rows - 1) * sz.row_width : rows * sz.row_width, :]
+        store_rows(sz, surface, send_first, send_second)
 
 
 def merge_kernel(
-    sz, arrive, back, from_low, from_high, before, slope, tables, facts, diffusivity, surface, send_low, send_high
+    sz, arrive, back, from_first, from_second, before, slope, tables, facts, diffusivity, surface, send_first, send_second
 ):
-    rows, width = sz.rows, sz.row_width
+    rows = sz.rows
     remap = Remap(sz, facts)
     arrive_all(arrive)
     surface[...] = before[...]
@@ -614,20 +653,18 @@
             before[pl.ds(tile, CHANNELS), :] + back[slot * CHANNELS : (slot + 1) * CHANNELS, :]
         )
     surface[CHANNELS * sz.tiles :, :] = jnp.zeros((CHANNELS, WIDTH), jnp.float32)
-    told = told_sums(sz, from_low, from_high)
+    told = told_sums(sz, from_first, from_second)
     lats = [lat_rows(sz, slope, lat) * told[lat] for lat in range(NEAR_LAT)]
     for row in range(rows):
         own = row_tiles_of(sz, surface, row)
         weights = [remap.own(lat, row) for lat in range(NEAR_LAT)]
         put_row_tiles(sz, surface, row, own + sum_of(weights, lats))
-    send_low[...] = diffusivity[0:width, :] * surface[0:width, :]
-    end = rows * width
-    send_high[...] = diffusivity[end - width : end, :] * surface[end - width : end, :]
+    store_rows(sz, surface, send_first, send_second, diffusivity)
 
 
 def backward_kernel(sz, last, arrive, *refs):
     refs = list(refs)
-    surface, low, high, low_surface, high_surface, diffusivity, mix = refs[:7]
+    surface, low, high, first_surface, second_surface, diffusivity, mix = refs[:7]
     field, drive = refs[7:9]
     refs = refs[9:]
     if last:
@@ -635,7 +672,7 @@
         local, bent_all, padded, in_sems, start_all = refs[3:]
     else:
         tables, weights, slope = refs[:3]
-        out, new_surface, packed, tell_low, tell_high, edge_low, edge_high = refs[3:10]
+        out, new_surface, packed, tell_first, tell_second, edge_first, edge_second = refs[3:10]
         local, bent_all, padded, in_sems, near_low, near_high = refs[10:]
         remap = Remap(sz, weights)
     count = sz.row_tiles
@@ -665,10 +702,7 @@
             for c in range(CHANNELS):
                 padded[row + 1, c, :, cols(t)] = coeff * local[row, c, :, cols(t)]
 
-    padded[0] = low[...]
-    padded[sz.rows + 1] = high[...]
-    load_surface_row(sz, padded, 0, low_surface, 0)
-    load_surface_row(sz, padded, sz.rows + 1, high_surface, 0)
+    place_edges(sz, padded, low, high, first_surface, second_surface)
     ready(0)
     lane = lax.broadcasted_iota(jnp.int32, (LEVELS, WIDTH), 1)
     sub = lax.broadcasted_iota(jnp.int32, (LEVELS, WIDTH), 0)
@@ -729,10 +763,10 @@
     else:
         new_surface[CHANNELS * sz.tiles :, :] = jnp.zeros((CHANNELS, WIDTH), jnp.float32)
         spread_back(
-            sz, new_surface, slope, remap, tables, packed, near_low, near_high, tell_low, tell_high
+            sz, new_surface, slope, remap, tables, packed, near_low, near_high, tell_first, tell_second
         )
         packed.start()
-        store_edges(sz, out, diffusivity, edge_low, edge_high)
+        store_edges(sz, out, diffusivity, edge_first, edge_second)
 
 
 def final_kernel(cell_total, arrive, everyones, perturbation, gradient, out):
@@ -864,11 +898,12 @@
         wait()
 
 
-def swap(low, high):
+def swap(first, second):
     count = lax.axis_size("horiz")
-    upward = [(i, i + 1) for i in range(count - 1)]
-    downward = [(target, source) for source, target in upward]
-    return lax.ppermute(high, "horiz", upward), lax.ppermute(low, "horiz", downward)
+    inner = [(i, i ^ 1) for i in range(count)]
+    outer = [(i, i + 1) for i in range(1, count - 1, 2)]
+    outer = outer + [(target, source) for source, target in outer]
+    return lax.ppermute(first, "horiz", inner), lax.ppermute(second, "horiz", outer)
 
 
 def exchange(array, devices):

time: 198 us -> 179 us (0.904)
  starting transfers between devices: 87.9 us -> 58 us
  waiting for transfers between devices: 48.7 us -> 62.4 us
  blocking collectives: 16 us -> 13.5 us
    all_to_all x7, waiting for transfers between devices: 26.2 us -> 54.5 us  [exchange(): lax.all_to_all(split, 'horiz', split_axis=0, concat_axis=0, tiled=True)]
    ppermute x22, starting transfers between devices: 37 us -> 10.9 us  [the longest x11 7.25 us: swap(): lax.ppermute(second, 'horiz', outer)]
    ppermute x22, waiting for transfers between devices: 17.8 us -> 3.24 us  [the longest x11 3.21 us: swap(): lax.ppermute(first, 'horiz', inner)]
    all_to_all x7, starting transfers between devices: 42.9 us -> 39.9 us  [exchange(): lax.all_to_all(split, 'horiz', split_axis=0, concat_axis=0, tiled=True)]
    all_to_all x1, blocking collectives: 16 us -> 13.5 us  [exchange(): lax.all_to_all(split, 'horiz', split_axis=0, concat_axis=0, tiled=True)]
where the time goes in v1:
time: 179 us; the launch traced here: 177 us
  waiting for transfers between devices  62.4 us (35%)
  starting transfers between devices  58 us (32%)
  Pallas kernels  40.6 us (23%)
  blocking collectives  13.5 us (8%)
  local copies, waits for them, and re-layouts  1.84 us (1%)
    all_to_all x7, waiting for transfers between devices, exchange(): lax.all_to_all(split, 'horiz', split_axis=0, concat_axis=0, tiled=True)  54.5 us
    pallas_call x16, Pallas kernels, call(): pl.pallas_call(run, name=name, in_specs=[pl.BlockSpec(memory_space=item.s...  40.6 us
    all_to_all x7, starting transfers between devices, exchange(): lax.all_to_all(split, 'horiz', split_axis=0, concat_axis=0, tiled=True)  39.9 us
    all_to_all x1, blocking collectives, exchange(): lax.all_to_all(split, 'horiz', split_axis=0, concat_axis=0, tiled=True)  13.5 us
    ppermute x11, starting transfers between devices, swap(): lax.ppermute(second, 'horiz', outer)  7.25 us
    all_to_all x1, starting transfers between devices, body(): lax.all_to_all(sums, 'horiz', split_axis=0, concat_axis=0, tiled=True)  7.24 us
    all_to_all x1, waiting for transfers between devices, body(): lax.all_to_all(sums, 'horiz', split_axis=0, concat_axis=0, tiled=True)  4.68 us
    ppermute x11, starting transfers between devices, swap(): lax.ppermute(first, 'horiz', inner)  3.7 us
  transfers between devices with their start and end apart: 30, of which 15 were waited for; matrix products, arithmetic and copies ran while one was open for 1% of the time, Pallas kernels for 5%

profile of v1, /device:TPU:0, one launch (start us, length us, event | category | flops | bytes accessed | tf_op | source)
XLA Modules:
  0.0 177.2 jit_solution(12526789916115721880)
XLA Ops:
  0.0 1.7 edges.1
  1.8 0.5 collective-permute-start
  2.3 0.7 collective-permute-start.1
  3.0 0.1 reshape.82
  3.1 0.1 maximum_bitcast_fusion
  3.2 3.0 %load.1 = (f32[5,4,8,1920]{3,2,1,0:T(8,128)S(1)}, f32[5,4,8,1920]{3,2,1,0:T(8,128)}) custom-call(f32[8,5,4,1920]{3,2,1,0:T(4,128)} %refs_1_.13, f32[8,5,4,1920]{3,2,1,0:T(4,128)} %refs_1_.8), custom_call_target="tpu_custom_call" | custom-call | tf_op jit(solution)/shard_map/load/pallas_call | solution.py:885
  6.2 0.1 add_convert_fusion
  6.3 1.9 %setup.1 = (s32[1,128]{1,0:T(1,128)}, f32[8,128]{1,0:T(8,128)}, f32[16,8,128]{2,1,0:T(8,128)}, f32[5,1,1920]{2,1,0:T(1,128)}, f32[5,1,1920]{2,1,0:T(1,128)}, /*index=5*/f32[300,128]{1,0:T(8,128)}, f32[300,128]{1,0:T(8,128)}) custom-call(f32[2,128]{1,0:T(2,128)S(1)} %get-tuple-element.166.refs_0_, f32[2,128]{1,0:T(2,128)S(1)} %get-tuple-element.165.refs_1_, ...), custom_call_target="tpu_custom_call" | custom-call | tf_op jit(solution)/shard_map/setup/pallas_call | solution.py:885
  8.2 3.7 %step.2 = (f32[5,4,8,1920]{3,2,1,0:T(8,128)}, f32[5,4,8,1920]{3,2,1,0:T(8,128)}, f32[304,128]{1,0:T(8,128)}, f32[320,128]{1,0:T(8,128)}, f32[40,128]{1,0:T(8,128...) custom-call(f32[4,8,1920]{2,1,0:T(8,128)S(1)} %collective-permute-done.refs_0_, ...), custom_call_target="tpu_custom_call" | custom-call | tf_op jit(solution)/shard_map/step/pallas_call | solution.py:885
  11.9 10.5 %all-to-all-start = ((f32[16,5,4,128]{3,2,1,0:T(4,128)}), f32[16,5,4,128]{3,2,1,0:T(4,128)S(1)}, u32[]{:S(2)}, u32[]{:S(2)}) async-start(f32[16,5,4,128]{3,2,1,0:T(4,128)} %bitcast.50), calls=%async_computation | async-start | bytes 327680 | tf_op jit(solution)/shard_map/all_to_all | solution.py:912
  22.3 0.4 collective-permute-start.2
  22.7 0.7 collective-permute-start.3
  23.4 0.4 collective-permute-done.2.refs_5_.refs_1_
  23.8 7.0 %all-to-all-done = f32[16,5,4,128]{3,2,1,0:T(4,128)S(1)} async-done(((f32[16,5,4,128]{3,2,1,0:T(4,128)}), f32[16,5,4,128]{3,2,1,0:T(4,128)S(1)}, u32[]{:S(2)}, u32[]{:S(2)}) %all-to-all-start) | async-done | bytes 163872 | tf_op jit(solution)/shard_map/all_to_all | solution.py:912
  30.8 2.2 %owners.2 = (s32[3,128]{1,0:T(4,128)}, f32[24,128]{1,0:T(8,128)}, f32[512,128]{1,0:T(8,128)}, f32[4,80,128]{2,1,0:T(8,128)}, f32[4,80,128]{2,1,0:T(8,128)}) custom-call(f32[320,128]{1,0:T(8,128)S(1)} %bitcast.37, f32[1,80,80]{2,1,0:T(8,128)} %refs_1_.12, f32[2,1,80,128]{3,2,1,0:T(8,128)} %refs_2_.5, f32[2,1,80,128]{3,2,1,0:T(8,128)} %refs_3_.7, ...), custom_call_target="tpu_custom_call" | custom-call | tf_op jit(solution)/shard_map/owners/pallas_call | solution.py:885
  33.0 3.5 %all-to-all-start.1 = ((f32[16,8,4,128]{3,2,1,0:T(4,128)}), f32[16,8,4,128]{3,2,1,0:T(4,128)S(1)}, u32[]{:S(2)}, u32[]{:S(2)}) async-start(f32[16,8,4,128]{3,2,1,0:T(4,128)} %bitcast.47), calls=%async_computation.1 | async-start | bytes 524288 | tf_op jit(solution)/shard_map/all_to_all | solution.py:912
  36.5 0.4 collective-permute-start.4
  36.9 0.7 collective-permute-start.5
  37.6 9.0 %all-to-all-done.1 = f32[16,8,4,128]{3,2,1,0:T(4,128)S(1)} async-done(((f32[16,8,4,128]{3,2,1,0:T(4,128)}), f32[16,8,4,128]{3,2,1,0:T(4,128)S(1)}, u32[]{:S(2)}, u32[]{:S(2)}) %all-to-all-start.1) | async-done | bytes 262176 | tf_op jit(solution)/shard_map/all_to_all | solution.py:912
  46.5 1.9 %surface.2 = (f32[304,128]{1,0:T(8,128)S(1)}, f32[60,128]{1,0:T(8,128)S(1)}, f32[60,128]{1,0:T(8,128)S(1)}, f32[64,128]{1,0:T(8,128)}) custom-call(f32[512,128]{1,0:T(8,128)S(1)} %bitcast.35, f32[40,128]{1,0:T(8,128)S(1)} %collective-permute-done.2.refs_5_.refs_1_, f32[40,128]{1,0:T(8,128)S(1)} %collective-permute-done.3.refs_6_.refs_2_, ...), custom_call_target="tpu_custom_call" | custom-call | tf_op jit(solution)/shard_map/surface/pallas_call | solution.py:885
  48.5 0.7 collective-permute-start.7
  49.2 0.5 collective-permute-done.6.refs_8_
  49.7 4.9 %step.3 = (f32[5,4,8,1920]{3,2,1,0:T(8,128)}, f32[5,4,8,1920]{3,2,1,0:T(8,128)}, f32[304,128]{1,0:T(8,128)}, f32[320,128]{1,0:T(8,128)}, f32[40,128]{1,0:T(8,128...) custom-call(f32[4,8,1920]{2,1,0:T(8,128)S(1)} %collective-permute-done.4.refs_0_, ...), custom_call_target="tpu_custom_call" | custom-call | tf_op jit(solution)/shard_map/step/pallas_call | solution.py:885
  54.6 7.7 %all-to-all-start.2 = ((f32[16,5,4,128]{3,2,1,0:T(4,128)}), f32[16,5,4,128]{3,2,1,0:T(4,128)S(1)}, u32[]{:S(2)}, u32[]{:S(2)}) async-start(f32[16,5,4,128]{3,2,1,0:T(4,128)} %bitcast.49), calls=%async_computation.2 | async-start | bytes 327680 | tf_op jit(solution)/shard_map/all_to_all | solution.py:912
  62.4 0.4 collective-permute-start.8
  62.8 0.7 collective-permute-start.9
  63.4 0.4 collective-permute-done.8.refs_1_
  63.8 7.0 %all-to-all-done.2 = f32[16,5,4,128]{3,2,1,0:T(4,128)S(1)} async-done(((f32[16,5,4,128]{3,2,1,0:T(4,128)}), f32[16,5,4,128]{3,2,1,0:T(4,128)S(1)}, u32[]{:S(2)}, u32[]{:S(2)}) %all-to-all-start.2) | async-done | bytes 163872 | tf_op jit(solution)/shard_map/all_to_all | solution.py:912
  70.8 2.1 %owners.3 = (f32[512,128]{1,0:T(8,128)}, f32[4,80,128]{2,1,0:T(8,128)}, f32[4,80,128]{2,1,0:T(8,128)}) custom-call(f32[320,128]{1,0:T(8,128)S(1)} %bitcast.40, f32[1,80,80]{2,1,0:T(8,128)} %refs_1_.12, f32[2,1,80,128]{3,2,1,0:T(8,128)} %refs_2_.5, f32[2,1,80,128]{3,2,1,0:T(8,128)} %refs_3_.7, f32[8,128]{1,0:T(8,128)} %get-tuple-element.90.refs_5_.refs_7_.refs_4_.refs_8_.refs_6_), custom_call_target="tpu_custom_call" | custom-call | tf_op jit(solution)/shard_map/owners/pallas_call | solution.py:885
  73.0 13.5 %all_to_all.51 = f32[16,8,4,128]{3,2,1,0:T(4,128)S(1)} all-to-all(f32[16,8,4,128]{3,2,1,0:T(4,128)} %bitcast.48), channel_id=1, replica_groups=mesh['member'=2,'horiz'=16] {'horiz'}, dimensions={0} | all-to-all | bytes 524288 | tf_op jit(solution)/shard_map/all_to_all | solution.py:912
  86.5 2.3 %surface.3 = (f32[304,128]{1,0:T(8,128)}, f32[64,128]{1,0:T(8,128)}, f32[512,128]{1,0:T(8,128)}, f32[32,128]{1,0:T(8,128)}, f32[32,128]{1,0:T(8,128)}) custom-call(f32[512,128]{1,0:T(8,128)S(1)} %bitcast.36, f32[40,128]{1,0:T(8,128)S(1)} %collective-permute-done.8.refs_1_, f32[40,128]{1,0:T(8,128)S(1)} %collective-permute-done.9.refs_2_, ...), custom_call_target="tpu_custom_call" | custom-call | tf_op jit(solution)/shard_map/surface/pallas_call | solution.py:885
  88.9 3.7 %all-to-all-start.4 = ((f32[16,8,4,128]{3,2,1,0:T(4,128)}), f32[16,8,4,128]{3,2,1,0:T(4,128)S(1)}, u32[]{:S(2)}, u32[]{:S(2)}) async-start(f32[16,8,4,128]{3,2,1,0:T(4,128)} %bitcast.46), calls=%async_computation.4 | async-start | bytes 524288 | tf_op jit(solution)/shard_map/all_to_all | solution.py:912
  92.5 0.3 collective-permute-start.10
  92.8 0.7 collective-permute-start.11
  93.5 0.5 collective-permute-done.10.refs_1_
  94.0 8.5 %all-to-all-done.4 = f32[16,8,4,128]{3,2,1,0:T(4,128)S(1)} async-done(((f32[16,8,4,128]{3,2,1,0:T(4,128)}), f32[16,8,4,128]{3,2,1,0:T(4,128)S(1)}, u32[]{:S(2)}, u32[]{:S(2)}) %all-to-all-start.4) | async-done | bytes 262176 | tf_op jit(solution)/shard_map/all_to_all | solution.py:912
  102.5 2.1 %owners_back.2 = f32[320,128]{1,0:T(8,128)} custom-call(f32[512,128]{1,0:T(8,128)S(1)} %bitcast.33, f32[1,80,80]{2,1,0:T(8,128)} %refs_1_.12, f32[4,80,128]{2,1,0:T(8,128)} %get-tuple-element.128.refs_2_, f32[4,80,128]{2,1,0:T(8,128)} %get-tuple-element.129.refs_3_, f32[8,128]{1,0:T(8,128)} %get-tuple-element.90.refs_5_.refs_7_.refs_4_.refs_8_.refs_6_), custom_call_target="tpu_custom_call" | custom-call | tf_op jit(solution)/shard_map/owners_back/pallas_call | solution.py:885
  104.6 3.5 %all-to-all-start.5 = ((f32[16,5,4,128]{3,2,1,0:T(4,128)}), f32[16,5,4,128]{3,2,1,0:T(4,128)S(1)}, u32[]{:S(2)}, u32[]{:S(2)}) async-start(f32[16,5,4,128]{3,2,1,0:T(4,128)} %bitcast.43), calls=%async_computation.5 | async-start | bytes 327680 | tf_op jit(solution)/shard_map/all_to_all | solution.py:912
  108.2 0.4 collective-permute-start.12
  108.5 0.7 collective-permute-start.13
  109.2 7.4 %all-to-all-done.5 = f32[16,5,4,128]{3,2,1,0:T(4,128)S(1)} async-done(((f32[16,5,4,128]{3,2,1,0:T(4,128)}), f32[16,5,4,128]{3,2,1,0:T(4,128)S(1)}, u32[]{:S(2)}, u32[]{:S(2)}) %all-to-all-start.5) | async-done | bytes 163872 | tf_op jit(solution)/shard_map/all_to_all | solution.py:912
  116.6 1.2 merge.2
  117.9 0.7 collective-permute-start.15
  118.6 0.5 collective-permute-done.14.refs_3_
  119.1 4.5 %step_back.1 = (f32[5,4,8,1920]{3,2,1,0:T(8,128)}, f32[304,128]{1,0:T(8,128)}, f32[512,128]{1,0:T(8,128)}, f32[32,128]{1,0:T(8,128)}, f32[32,128]{1,0:T(8,128)},...) custom-call(f32[304,128]{1,0:T(8,128)S(1)} %get-tuple-element.135.refs_0_, ...), custom_call_target="tpu_custom_call" | custom-call | tf_op jit(solution)/shard_map/step_back/pallas_call | solution.py:885
  123.6 7.4 %all-to-all-start.6 = ((f32[16,8,4,128]{3,2,1,0:T(4,128)}), f32[16,8,4,128]{3,2,1,0:T(4,128)S(1)}, u32[]{:S(2)}, u32[]{:S(2)}) async-start(f32[16,8,4,128]{3,2,1,0:T(4,128)} %bitcast.45), calls=%async_computation.6 | async-start | bytes 524288 | tf_op jit(solution)/shard_map/all_to_all | solution.py:912
  131.0 0.8 collective-permute-start.16
  131.7 0.7 collective-permute-start.17
  132.4 0.4 collective-permute-done.16.refs_1_
  132.8 8.2 %all-to-all-done.6 = f32[16,8,4,128]{3,2,1,0:T(4,128)S(1)} async-done(((f32[16,8,4,128]{3,2,1,0:T(4,128)}), f32[16,8,4,128]{3,2,1,0:T(4,128)S(1)}, u32[]{:S(2)}, u32[]{:S(2)}) %all-to-all-start.6) | async-done | bytes 262176 | tf_op jit(solution)/shard_map/all_to_all | solution.py:912
  141.0 2.1 %owners_back.3 = f32[320,128]{1,0:T(8,128)} custom-call(f32[512,128]{1,0:T(8,128)S(1)} %bitcast.34, f32[1,80,80]{2,1,0:T(8,128)} %refs_1_.12, f32[4,80,128]{2,1,0:T(8,128)} %get-tuple-element.147.refs_2_, f32[4,80,128]{2,1,0:T(8,128)} %get-tuple-element.148.refs_3_, f32[8,128]{1,0:T(8,128)} %get-tuple-element.90.refs_5_.refs_7_.refs_4_.refs_8_.refs_6_), custom_call_target="tpu_custom_call" | custom-call | tf_op jit(solution)/shard_map/owners_back/pallas_call | solution.py:885
  143.1 3.5 %all-to-all-start.7 = ((f32[16,5,4,128]{3,2,1,0:T(4,128)}), f32[16,5,4,128]{3,2,1,0:T(4,128)S(1)}, u32[]{:S(2)}, u32[]{:S(2)}) async-start(f32[16,5,4,128]{3,2,1,0:T(4,128)} %bitcast.44), calls=%async_computation.7 | async-start | bytes 327680 | tf_op jit(solution)/shard_map/all_to_all | solution.py:912
  146.6 0.4 collective-permute-start.18
  147.0 0.7 collective-permute-start.19
  147.7 7.4 %all-to-all-done.7 = f32[16,5,4,128]{3,2,1,0:T(4,128)S(1)} async-done(((f32[16,5,4,128]{3,2,1,0:T(4,128)}), f32[16,5,4,128]{3,2,1,0:T(4,128)S(1)}, u32[]{:S(2)}, u32[]{:S(2)}) %all-to-all-start.7) | async-done | bytes 163872 | tf_op jit(solution)/shard_map/all_to_all | solution.py:912
  155.1 1.2 merge.3
  156.2 0.1 collective-permute-start.20
  156.3 0.7 collective-permute-start.21
  157.0 0.5 collective-permute-done.20.refs_3_
  157.5 4.8 %step_back_sums.1 = (f32[5,4,8,1920]{3,2,1,0:T(8,128)}, f32[16,128]{1,0:T(8,128)}) custom-call(f32[304,128]{1,0:T(8,128)S(1)} %get-tuple-element.155.refs_0_, f32[4,8,1920]{2,1,0:T(8,128)S(1)} %collective-permute-done.18.refs_1_, f32[4,8,1920]{2,1,0:T(8,128)S(1)} %collective-permute-done.19.refs_2_, f32[60,128]{1,0:T(8,128)S(1)} %collective-permute-done.20.refs_3_, ...), custom_call_target="tpu_custom_call" | custom-call | tf_op jit(solution)/shard_map/step_back_sums/pallas_call | solution.py:885
  162.3 7.2 %all-to-all-start.8 = ((f32[16,1,128]{2,1,0:T(1,128)}), f32[16,1,128]{2,1,0:T(1,128)S(1)}, u32[]{:S(2)}, u32[]{:S(2)}) async-start(f32[16,1,128]{2,1,0:T(1,128)} %bitcast.51), calls=%async_computation.8 | async-start | bytes 16384 | tf_op jit(solution)/shard_map/all_to_all | solution.py:1119
  169.6 1.7 copy.20
  171.3 4.7 %all-to-all-done.8 = f32[16,1,128]{2,1,0:T(1,128)S(1)} async-done(((f32[16,1,128]{2,1,0:T(1,128)}), f32[16,1,128]{2,1,0:T(1,128)S(1)}, u32[]{:S(2)}, u32[]{:S(2)}) %all-to-all-start.8) | async-done | bytes 8224 | tf_op jit(solution)/shard_map/all_to_all | solution.py:1119
  175.9 1.2 finish.1
  (50 shorter events, 0.3 us)
Async XLA Ops:
  0.0 3.0 %copy-start.2 = (f32[4,4]{1,0:T(4,128)S(1)}, f32[4,4]{1,0:T(4,128)}, u32[]{:S(2)}) copy-start(f32[4,4]{1,0:T(4,128)} %param.21) | copy-start | bytes 196
  0.0 3.1 %copy-start.4 = (s32[15]{0:T(128)S(1)}, s32[15]{0:T(128)}, u32[]{:S(2)}) copy-start(s32[15]{0:T(128)} %param.28) | copy-start | bytes 184
  0.0 3.1 %copy-start.3 = (s32[15]{0:T(128)S(1)}, s32[15]{0:T(128)}, u32[]{:S(2)}) copy-start(s32[15]{0:T(128)} %param.27) | copy-start | bytes 184
  0.0 3.1 %copy-start.11 = (f32[15]{0:T(128)S(1)}, f32[15]{0:T(128)}, u32[]{:S(2)}) copy-start(f32[15]{0:T(128)} %param.29) | copy-start | bytes 184
  1.8 6.4 %collective-permute-start = (f32[4,8,1920]{2,1,0:T(8,128)S(1)}, f32[4,8,1920]{2,1,0:T(8,128)S(1)}, u32[]{:S(2)}, u32[]{:S(2)}) collective-permute-start(f32[4,8,1920]{2,1,0:T(8,128)S(1)} %get-tuple-element.85), channel_id=1, source_target_pairs={{0,1},{1,0},{2,3},{3,2},{4,5},{5,4},{6,7},{7,6},{8,9},{9,8},{10,11... | collective-permute-start | bytes 737288 | tf_op jit(solution)/shard_map/ppermute | solution.py:906
  2.3 5.9 %collective-permute-start.1 = (f32[4,8,1920]{2,1,0:T(8,128)S(1)}, f32[4,8,1920]{2,1,0:T(8,128)S(1)}, u32[]{:S(2)}, u32[]{:S(2)}) collective-permute-start(f32[4,8,1920]{2,1,0:T(8,128)S(1)} %get-tuple-element.86), channel_id=1, source_target_pairs={{1,2},{3,4},{5,6},{7,8},{9,10},{11,12},{13,14},{2,1},{4,3},{6,5},{... | collective-permute-start | bytes 737288 | tf_op jit(solution)/shard_map/ppermute | solution.py:906
  3.2 3.0 %copy-start.12 = (s32[1,75]{1,0:T(1,128)S(1)}, s32[1,75]{1,0:T(1,128)}, u32[]{:S(2)}) copy-start(s32[1,75]{1,0:T(1,128)} %param.25) | copy-start | bytes 904
  3.2 3.0 %copy-start.13 = (s32[1,75]{1,0:T(1,128)S(1)}, s32[1,75]{1,0:T(1,128)}, u32[]{:S(2)}) copy-start(s32[1,75]{1,0:T(1,128)} %param.26) | copy-start | bytes 904
  3.2 3.1 %copy-start.1 = (f32[8,4,4]{0,2,1:T(4,128)S(1)}, f32[8,4,4]{0,2,1:T(4,128)}, u32[]{:S(2)}) copy-start(f32[8,4,4]{0,2,1:T(4,128)} %param.20) | copy-start | bytes 1540
  11.8 24.7 %copy-start.10 = (f32[4,8,1920]{2,1,0:T(8,128)S(1)}, f32[4,8,1920]{2,1,0:T(8,128)}, u32[]{:S(2)}) copy-start(f32[4,8,1920]{2,1,0:T(8,128)} %get-tuple-element.101) | copy-start | bytes 737284
  11.8 25.0 %copy-start.9 = (f32[4,8,1920]{2,1,0:T(8,128)S(1)}, f32[4,8,1920]{2,1,0:T(8,128)}, u32[]{:S(2)}) copy-start(f32[4,8,1920]{2,1,0:T(8,128)} %get-tuple-element.102) | copy-start | bytes 737284
  11.9 18.9 %all-to-all-start = ((f32[16,5,4,128]{3,2,1,0:T(4,128)}), f32[16,5,4,128]{3,2,1,0:T(4,128)S(1)}, u32[]{:S(2)}, u32[]{:S(2)}) async-start(f32[16,5,4,128]{3,2,1,0:T(4,128)} %bitcast.50), calls=%async_computation | async-start | bytes 327680 | tf_op jit(solution)/shard_map/all_to_all | solution.py:912
  22.3 1.5 collective-permute-start.2
  22.7 1.1 collective-permute-start.3
  33.0 13.6 %all-to-all-start.1 = ((f32[16,8,4,128]{3,2,1,0:T(4,128)}), f32[16,8,4,128]{3,2,1,0:T(4,128)S(1)}, u32[]{:S(2)}, u32[]{:S(2)}) async-start(f32[16,8,4,128]{3,2,1,0:T(4,128)} %bitcast.47), calls=%async_computation.1 | async-start | bytes 524288 | tf_op jit(solution)/shard_map/all_to_all | solution.py:912
  36.5 12.6 %collective-permute-start.4 = (f32[4,8,1920]{2,1,0:T(8,128)S(1)}, f32[4,8,1920]{2,1,0:T(8,128)S(1)}, u32[]{:S(2)}, u32[]{:S(2)}) collective-permute-start(f32[4,8,1920]{2,1,0:T(8,128)S(1)} %copy-done.10), channel_id=1, source_target_pairs={{0,1},{1,0},{2,3},{3,2},{4,5},{5,4},{6,7},{7,6},{8,9},{9,8},{10,11... | collective-permute-start | bytes 737288 | tf_op jit(solution)/shard_map/ppermute | solution.py:906
  36.9 12.3 %collective-permute-start.5 = (f32[4,8,1920]{2,1,0:T(8,128)S(1)}, f32[4,8,1920]{2,1,0:T(8,128)S(1)}, u32[]{:S(2)}, u32[]{:S(2)}) collective-permute-start(f32[4,8,1920]{2,1,0:T(8,128)S(1)} %copy-done.9), channel_id=1, source_target_pairs={{1,2},{3,4},{5,6},{7,8},{9,10},{11,12},{13,14},{2,1},{4,3},{6,5},{... | collective-permute-start | bytes 737288 | tf_op jit(solution)/shard_map/ppermute | solution.py:906
  48.4 1.3 collective-permute-start.6
  48.5 1.2 collective-permute-start.7
  54.6 16.2 %all-to-all-start.2 = ((f32[16,5,4,128]{3,2,1,0:T(4,128)}), f32[16,5,4,128]{3,2,1,0:T(4,128)S(1)}, u32[]{:S(2)}, u32[]{:S(2)}) async-start(f32[16,5,4,128]{3,2,1,0:T(4,128)} %bitcast.49), calls=%async_computation.2 | async-start | bytes 327680 | tf_op jit(solution)/shard_map/all_to_all | solution.py:912
  62.4 1.5 collective-permute-start.8
  62.8 1.1 collective-permute-start.9
  88.8 19.3 %copy-start.6 = (f32[4,8,1920]{2,1,0:T(8,128)S(1)}, f32[4,8,1920]{2,1,0:T(8,128)}, u32[]{:S(2)}) copy-start(f32[4,8,1920]{2,1,0:T(8,128)} %get-tuple-element.136) | copy-start | bytes 737284
  88.8 19.7 %copy-start.5 = (f32[4,8,1920]{2,1,0:T(8,128)S(1)}, f32[4,8,1920]{2,1,0:T(8,128)}, u32[]{:S(2)}) copy-start(f32[4,8,1920]{2,1,0:T(8,128)} %get-tuple-element.137) | copy-start | bytes 737284
  88.9 13.7 %all-to-all-start.4 = ((f32[16,8,4,128]{3,2,1,0:T(4,128)}), f32[16,8,4,128]{3,2,1,0:T(4,128)S(1)}, u32[]{:S(2)}, u32[]{:S(2)}) async-start(f32[16,8,4,128]{3,2,1,0:T(4,128)} %bitcast.46), calls=%async_computation.4 | async-start | bytes 524288 | tf_op jit(solution)/shard_map/all_to_all | solution.py:912
  92.5 1.5 collective-permute-start.10
  92.8 1.2 collective-permute-start.11
  104.6 12.0 %all-to-all-start.5 = ((f32[16,5,4,128]{3,2,1,0:T(4,128)}), f32[16,5,4,128]{3,2,1,0:T(4,128)S(1)}, u32[]{:S(2)}, u32[]{:S(2)}) async-start(f32[16,5,4,128]{3,2,1,0:T(4,128)} %bitcast.43), calls=%async_computation.5 | async-start | bytes 327680 | tf_op jit(solution)/shard_map/all_to_all | solution.py:912
  108.2 10.4 %collective-permute-start.12 = (f32[4,8,1920]{2,1,0:T(8,128)S(1)}, f32[4,8,1920]{2,1,0:T(8,128)S(1)}, u32[]{:S(2)}, u32[]{:S(2)}) collective-permute-start(f32[4,8,1920]{2,1,0:T(8,128)S(1)} %copy-done.6), channel_id=1, source_target_pairs={{0,1},{1,0},{2,3},{3,2},{4,5},{5,4},{6,7},{7,6},{8,9},{9,8},{10,11... | collective-permute-start | bytes 737288 | tf_op jit(solution)/shard_map/ppermute | solution.py:906
  108.5 10.0 %collective-permute-start.13 = (f32[4,8,1920]{2,1,0:T(8,128)S(1)}, f32[4,8,1920]{2,1,0:T(8,128)S(1)}, u32[]{:S(2)}, u32[]{:S(2)}) collective-permute-start(f32[4,8,1920]{2,1,0:T(8,128)S(1)} %copy-done.5), channel_id=1, source_target_pairs={{1,2},{3,4},{5,6},{7,8},{9,10},{11,12},{13,14},{2,1},{4,3},{6,5},{... | collective-permute-start | bytes 737288 | tf_op jit(solution)/shard_map/ppermute | solution.py:906
  117.8 1.3 collective-permute-start.14
  117.9 1.2 collective-permute-start.15
  123.6 23.1 %copy-start.8 = (f32[4,8,1920]{2,1,0:T(8,128)S(1)}, f32[4,8,1920]{2,1,0:T(8,128)}, u32[]{:S(2)}) copy-start(f32[4,8,1920]{2,1,0:T(8,128)} %get-tuple-element.156) | copy-start | bytes 737284
  123.6 23.4 %copy-start.7 = (f32[4,8,1920]{2,1,0:T(8,128)S(1)}, f32[4,8,1920]{2,1,0:T(8,128)}, u32[]{:S(2)}) copy-start(f32[4,8,1920]{2,1,0:T(8,128)} %get-tuple-element.157) | copy-start | bytes 737284
  123.6 17.4 %all-to-all-start.6 = ((f32[16,8,4,128]{3,2,1,0:T(4,128)}), f32[16,8,4,128]{3,2,1,0:T(4,128)S(1)}, u32[]{:S(2)}, u32[]{:S(2)}) async-start(f32[16,8,4,128]{3,2,1,0:T(4,128)} %bitcast.45), calls=%async_computation.6 | async-start | bytes 524288 | tf_op jit(solution)/shard_map/all_to_all | solution.py:912
  131.0 1.8 %collective-permute-start.16 = (f32[32,128]{1,0:T(8,128)}, f32[32,128]{1,0:T(8,128)S(1)}, u32[]{:S(2)}, u32[]{:S(2)}) collective-permute-start(f32[32,128]{1,0:T(8,128)} %get-tuple-element.144), channel_id=1, source_target_pairs={{0,1},{1,0},{2,3},{3,2},{4,5},{5,4},{6,7},{7,6},{8,9},{9,8},{10,11... | collective-permute-start | bytes 49160 | tf_op jit(solution)/shard_map/ppermute | solution.py:906
  131.7 1.1 collective-permute-start.17
  143.1 12.0 %all-to-all-start.7 = ((f32[16,5,4,128]{3,2,1,0:T(4,128)}), f32[16,5,4,128]{3,2,1,0:T(4,128)S(1)}, u32[]{:S(2)}, u32[]{:S(2)}) async-start(f32[16,5,4,128]{3,2,1,0:T(4,128)} %bitcast.44), calls=%async_computation.7 | async-start | bytes 327680 | tf_op jit(solution)/shard_map/all_to_all | solution.py:912
  146.6 10.4 %collective-permute-start.18 = (f32[4,8,1920]{2,1,0:T(8,128)S(1)}, f32[4,8,1920]{2,1,0:T(8,128)S(1)}, u32[]{:S(2)}, u32[]{:S(2)}) collective-permute-start(f32[4,8,1920]{2,1,0:T(8,128)S(1)} %copy-done.8), channel_id=1, source_target_pairs={{0,1},{1,0},{2,3},{3,2},{4,5},{5,4},{6,7},{7,6},{8,9},{9,8},{10,11... | collective-permute-start | bytes 737288 | tf_op jit(solution)/shard_map/ppermute | solution.py:906
  147.0 10.0 %collective-permute-start.19 = (f32[4,8,1920]{2,1,0:T(8,128)S(1)}, f32[4,8,1920]{2,1,0:T(8,128)S(1)}, u32[]{:S(2)}, u32[]{:S(2)}) collective-permute-start(f32[4,8,1920]{2,1,0:T(8,128)S(1)} %copy-done.7), channel_id=1, source_target_pairs={{1,2},{3,4},{5,6},{7,8},{9,10},{11,12},{13,14},{2,1},{4,3},{6,5},{... | collective-permute-start | bytes 737288 | tf_op jit(solution)/shard_map/ppermute | solution.py:906
  156.2 1.3 collective-permute-start.20
  156.3 1.2 collective-permute-start.21
  162.3 13.6 %all-to-all-start.8 = ((f32[16,1,128]{2,1,0:T(1,128)}), f32[16,1,128]{2,1,0:T(1,128)S(1)}, u32[]{:S(2)}, u32[]{:S(2)}) async-start(f32[16,1,128]{2,1,0:T(1,128)} %bitcast.51), calls=%async_computation.8 | async-start | bytes 16384 | tf_op jit(solution)/shard_map/all_to_all | solution.py:1119
  169.5 6.4 %copy-start = (f32[8,5,4,1920]{3,2,1,0:T(4,128)S(1)}, f32[8,5,4,1920]{3,2,1,0:T(4,128)}, u32[]{:S(2)}) copy-start(f32[8,5,4,1920]{3,2,1,0:T(4,128)} %refs_1_.13) | copy-start | bytes 3686404

commit v2 on v1

--- a/solution.py
+++ b/solution.py
@@ -40,14 +40,15 @@
         self.slot_lines = -(-self.slots // WIDTH)
         self.facts = -(-(self.slot_lines + 1) // SUBLANES) * SUBLANES
         self.lat_lines = LAT_DEV * self.pitch
+        self.edge_lines = CHANNELS * self.row_tiles * LEVELS
         self.whole = (rows, CHANNELS, LEVELS, cells)
-        self.edge = (CHANNELS, LEVELS, cells)
+        self.edge = (self.edge_lines, WIDTH)
+        self.edge_and_lats = (self.edge_lines + self.lat_lines, WIDTH)
         self.surface = (CHANNELS * (self.tiles + 1), WIDTH)
         self.narrow = (CHANNELS * self.slots, WIDTH)
         self.wide = (devices * self.chunk, WIDTH)
         self.slope = (NEAR_LAT * self.pitch, WIDTH)
         self.lats = (self.lat_lines, WIDTH)
-        self.told = (self.lat_lines + self.facts, WIDTH)
         self.bulk_at = NEAR_LAT * rows
         self.tables = (3 * self.slot_lines, WIDTH)
         self.weights = (3 * self.facts, WIDTH)
@@ -144,7 +145,8 @@
 
 
 def setup_kernel(sz, entries, remap_entries, arrive, wet, remap, mix_rows, diffusivity, weight, *outs):
-    table, facts, mix, diffusivity_rows, weight_rows, diffusivity_tiles, weight_tiles = outs
+    first_mix, first_rows, table, facts, mix = outs[:5]
+    diffusivity_rows, weight_rows, diffusivity_tiles, weight_tiles = outs[5:]
     arrive_all(arrive)
     for source, by_row, by_tile in (
         (diffusivity, diffusivity_rows, diffusivity_tiles),
@@ -158,10 +160,12 @@
                 by_tile[at : at + CHANNELS, :] = jnp.broadcast_to(line, (CHANNELS, WIDTH))
         by_row.start()
         by_tile.start()
+    first_rows[...] = diffusivity_rows[...]
     for index in range(CHANNELS * CHANNELS):
         column = as_column(mix_rows[index : index + 1, :], LEVELS)
         mix[index] = jnp.broadcast_to(column, (LEVELS, WIDTH))
     mix.start()
+    first_mix[...] = mix[...]
     tiles, owners = wet[0:1, :], wet[1:2, :]
     size = -(-entries // SUBLANES) * SUBLANES
     shape = (size, wet.shape[1])
@@ -204,8 +208,9 @@
             low = low + gather_levels(low_base, (), channel, tile)
             high = gather_levels(high_start, (), channel, tile)
             high = high + gather_levels(high_base, (), channel, tile)
-            send_first[channel, :, cols(tile)] = pick(flag, high, low)
-            send_second[channel, :, cols(tile)] = pick(flag, low, high)
+            at = (channel * sz.row_tiles + tile) * LEVELS
+            send_first[at : at + LEVELS, :] = pick(flag, high, low)
+            send_second[at : at + LEVELS, :] = pick(flag, low, high)
 
 
 def load_kernel(sz, arrive, perturbation, base, field, start, start_block, base_block, in_sems):
@@ -273,23 +278,26 @@
     ]
 
 
-def send_sums(sz, sums, tell_first, tell_second):
+def send_sums(sz, sums, tell_first, tell_second, base):
     flag = high_first()
     for index in range(LAT_DEV):
         low, high = sums[index], sums[LAT_DEV + index]
-        at = index * sz.pitch
+        at = base + index * sz.pitch
         tell_first[at : at + sz.row_tiles, :] = pick(flag, high, low)
         tell_second[at : at + sz.row_tiles, :] = pick(flag, low, high)
 
 
-def lat_rows(sz, ref, lat):
-    return ref[lat * sz.pitch : lat * sz.pitch + sz.row_tiles, :]
-
-
-def told_sums(sz, from_first, from_second):
+def lat_rows(sz, ref, lat, base=0):
+    at = base + lat * sz.pitch
+    return ref[at : at + sz.row_tiles, :]
+
+
+def told_sums(sz, from_first, from_second, base):
     lows, highs = [], []
     for index in range(LAT_DEV):
-        low, high = sided(lat_rows(sz, from_first, index), lat_rows(sz, from_second, index))
+        low, high = sided(
+            lat_rows(sz, from_first, index, base), lat_rows(sz, from_second, index, base)
+        )
         lows.append(low)
         highs.append(high)
     return lows + highs
@@ -298,7 +306,10 @@
 def place_edges(sz, padded, first, second, first_surface=None, second_surface=None):
     side = high_first() * (sz.rows + 1)
     for at, edge, surface in ((side, first, first_surface), (sz.rows + 1 - side, second, second_surface)):
-        padded[at] = edge[...]
+        for channel in range(CHANNELS):
+            for tile in range(sz.row_tiles):
+                line = (channel * sz.row_tiles + tile) * LEVELS
+                padded[at, channel, :, cols(tile)] = edge[line : line + LEVELS, :]
         if surface is not None:
             load_surface_row(sz, padded, at, surface, 0)
 
@@ -314,49 +325,68 @@
             send[tile * CHANNELS : (tile + 1) * CHANNELS, :] = value
 
 
+def forward_load_kernel(sz, last, arrive, mix, diffusivity, *refs):
+    refs = list(refs)
+    if last:
+        weight = refs.pop(0)
+    field, surface = refs[:2]
+    refs = refs[2:]
+    if last:
+        target = refs.pop(0)
+    mix_out, rows_out, field_out = refs[:3]
+    refs = refs[3:]
+    if last:
+        weight_out, target_out = refs[:2]
+        refs = refs[2:]
+    in_sems = refs[0]
+
+    def arrivals(row):
+        copies = [pltpu.make_async_copy(field.at[row], field_out.at[row], in_sems.at[0, row])]
+        if last:
+            copies.append(
+                pltpu.make_async_copy(target.at[:, row], refs[1].at[row], in_sems.at[1, row])
+            )
+        return copies
+
+    for row in range(sz.rows):
+        for arrival in arrivals(row):
+            arrival.start()
+    arrive_all(arrive)
+    mix_out[...] = mix[...]
+    rows_out[...] = diffusivity[...]
+    if last:
+        weight_out[...] = weight[...]
+
+    def one_row(row, carry):
+        for arrival in arrivals(row):
+            arrival.wait()
+        load_surface_row(sz, field_out, row, surface, row * sz.row_width)
+        if last:
+            for c in range(CHANNELS):
+                for t in range(sz.row_tiles):
+                    target_out[row, c, :, cols(t)] = gather_levels(refs[1].at[row], (), c, t)
+        return carry
+
+    lax.fori_loop(0, sz.rows, one_row, 0)
+
+
 def forward_kernel(sz, first, last, arrive, *refs):
     refs = list(refs)
-    low, high, diffusivity, mix, tables, facts, field = refs[:7]
+    tables, facts, low, high, diffusivity, mix, field = refs[:7]
     refs = refs[7:]
-    if first:
-        told_facts = refs[0]
-        refs = refs[1:]
-    else:
-        surface, first_surface, second_surface = refs[:3]
-        refs = refs[3:]
+    surfaces = ()
+    if not first:
+        surfaces = refs[:2]
+        refs = refs[2:]
     if last:
         weight, target = refs[:2]
         refs = refs[2:]
-    out, drive, new_surface, packed, tell_first, tell_second, edge_first, edge_second, padded = refs[:9]
+    out, drive, new_surface, packed, tell_first, tell_second, padded = refs
     remap = Remap(sz, facts)
-    if not first:
-        in_sems = refs[9]
-
-    def arrivals(row):
-        copies = [pltpu.make_async_copy(field.at[row], padded.at[row + 1], in_sems.at[0, row])]
-        if last:
-            copies.append(
-                pltpu.make_async_copy(target.at[:, row], refs[10].at[row], in_sems.at[1, row])
-            )
-        return copies
-
-    if not first:
-        for row in range(sz.rows):
-            for arrival in arrivals(row):
-                arrival.start()
-    arrive_all(arrive)
-    if first:
-        place_edges(sz, padded, low, high)
-    else:
-        place_edges(sz, padded, low, high, first_surface, second_surface)
+    place_edges(sz, padded, low, high, *surfaces)
 
     def ready(row):
-        if first:
-            padded[row + 1] = field[row]
-        else:
-            for arrival in arrivals(row):
-                arrival.wait()
-            load_surface_row(sz, padded, row + 1, surface, row * sz.row_width)
+        padded[row + 1] = field[row]
 
     ready(0)
     lane = lax.broadcasted_iota(jnp.int32, (LEVELS, WIDTH), 1)
@@ -397,7 +427,7 @@
                 )
                 new_surface[pl.ds((row * count + t) * CHANNELS + c, 1), :] = stepped[0:1, :]
                 if last:
-                    stepped = scale * (stepped - gather_levels(refs[10].at[row], (), c, t))
+                    stepped = scale * (stepped - target[row, c, :, cols(t)])
                 out[row, c, :, cols(t)] = stepped
         drive.row(row).start()
         out.row(row).start()
@@ -406,15 +436,12 @@
     lax.fori_loop(0, sz.rows, one_row, 0)
     new_surface[CHANNELS * sz.tiles :, :] = jnp.zeros((CHANNELS, WIDTH), jnp.float32)
     new_surface.start()
+    arrive_all(arrive)
     pack_slots(sz, tables, new_surface, packed)
     packed.start()
     own = [row_tiles_of(sz, new_surface.block, row) for row in range(sz.rows)]
-    send_sums(sz, own_sums(sz, remap, own, 1.0), tell_first, tell_second)
-    blank = told_facts[...] if first else jnp.zeros((sz.facts, WIDTH), jnp.float32)
-    for tell in (tell_first, tell_second):
-        tell[sz.lat_lines :, :] = blank
-        tell.start()
-    store_edges(sz, out, diffusivity if last else None, edge_first, edge_second)
+    send_sums(sz, own_sums(sz, remap, own, 1.0), tell_first, tell_second, sz.edge_lines)
+    store_edges(sz, out, diffusivity if last else None, tell_first, tell_second)
 
 
 def pack_slots(sz, tables, surface, packed):
@@ -433,7 +460,8 @@
                     value = value * jnp.broadcast_to(
                         diffusivity[row, 0:1, cols(tile)], (LEVELS, WIDTH)
                     )
-                send[channel, :, cols(tile)] = value
+                at = (channel * sz.row_tiles + tile) * LEVELS
+                send[at : at + LEVELS, :] = value
         send.start()
 
 
@@ -448,7 +476,7 @@
         lines = sz.slot_lines
         tables[0:lines, :] = own_table[...]
         weights[0 : sz.facts, :] = own_facts[...]
-        both = sided(told_first[sz.lat_lines :, :], told_second[sz.lat_lines :, :])
+        both = sided(told_first[...], told_second[...])
         for which, told in ((1, both[0]), (2, both[1])):
             got = told[0:lines, :].astype(jnp.int32)
             tables[which * lines : (which + 1) * lines, :] = sz.tiles - got
@@ -542,14 +570,12 @@
         back.block[pl.ds(k, slots, stride=CHANNELS), :] = through[:, cols(k)] + sign * direct[k]
 
 
-def spread_back(sz, surface, slope, remap, tables, packed, near_low, near_high, tell_first, tell_second):
+def spread_back(sz, surface, slope, remap, tables, packed, near_low, near_high, tell_first, tell_second, base):
     rows, count, cap = sz.rows, sz.row_tiles, sz.capacity
     block = surface.block
     own = [row_tiles_of(sz, block, row) for row in range(rows)]
     sums = own_sums(sz, remap, own, FEEDBACK)
-    send_sums(sz, sums, tell_first, tell_second)
-    tell_first.start()
-    tell_second.start()
+    send_sums(sz, sums, tell_first, tell_second, base)
     lats = [lat_rows(sz, slope, lat) * sums[lat] for lat in range(NEAR_LAT)]
     every = range(NEAR_LAT)
     for row in range(rows):
@@ -611,7 +637,7 @@
     block[CHANNELS * sz.tiles :, :] = jnp.zeros((CHANNELS, WIDTH), jnp.float32)
     own = [row_tiles_of(sz, block, row) for row in range(rows)]
     sums = own_sums(sz, remap, own, 1.0)
-    told = told_sums(sz, from_first, from_second)
+    told = told_sums(sz, from_first, from_second, sz.edge_lines)
     air = []
     for lat in range(NEAR_LAT):
         if lat < LAT_DEV:
@@ -634,14 +660,14 @@
                 off = block[at : at + CHANNELS, :] - target[row, :, cols(tile)]
                 block[at : at + CHANNELS, :] = scale * scale * off
         spread_back(
-            sz, surface, slope, remap, tables, packed, near_low, near_high, tell_first, tell_second
+            sz, surface, slope, remap, tables, packed, near_low, near_high, tell_first, tell_second, 0
         )
     else:
         store_rows(sz, surface, send_first, send_second)
 
 
 def merge_kernel(
-    sz, arrive, back, from_first, from_second, before, slope, tables, facts, diffusivity, surface, send_first, send_second
+    sz, base, arrive, back, from_first, from_second, before, slope, tables, facts, diffusivity, surface, send_first, send_second
 ):
     rows = sz.rows
     remap = Remap(sz, facts)
@@ -653,7 +679,7 @@
             before[pl.ds(tile, CHANNELS), :] + back[slot * CHANNELS : (slot + 1) * CHANNELS, :]
         )
     surface[CHANNELS * sz.tiles :, :] = jnp.zeros((CHANNELS, WIDTH), jnp.float32)
-    told = told_sums(sz, from_first, from_second)
+    told = told_sums(sz, from_first, from_second, base)
     lats = [lat_rows(sz, slope, lat) * told[lat] for lat in range(NEAR_LAT)]
     for row in range(rows):
         own = row_tiles_of(sz, surface, row)
@@ -662,20 +688,15 @@
     store_rows(sz, surface, send_first, send_second, diffusivity)
 
 
-def backward_kernel(sz, last, arrive, *refs):
+def backward_load_kernel(sz, last, arrive, mix, diffusivity, field, drive, surface, *refs):
     refs = list(refs)
-    surface, low, high, first_surface, second_surface, diffusivity, mix = refs[:7]
-    field, drive = refs[7:9]
-    refs = refs[9:]
     if last:
-        perturbation, out, sums = refs[:3]
-        local, bent_all, padded, in_sems, start_all = refs[3:]
-    else:
-        tables, weights, slope = refs[:3]
-        out, new_surface, packed, tell_first, tell_second, edge_first, edge_second = refs[3:10]
-        local, bent_all, padded, in_sems, near_low, near_high = refs[10:]
-        remap = Remap(sz, weights)
-    count = sz.row_tiles
+        perturbation = refs.pop(0)
+    mix_out, rows_out, local, bent_all, scaled = refs[:5]
+    refs = refs[5:]
+    if last:
+        start_all = refs.pop(0)
+    in_sems = refs[0]
 
     def arrivals(row):
         copies = [
@@ -692,17 +713,41 @@
         for arrival in arrivals(row):
             arrival.start()
     arrive_all(arrive)
-
-    def ready(row):
+    mix_out[...] = mix[...]
+    rows_out[...] = diffusivity[...]
+
+    def one_row(row, carry):
         for arrival in arrivals(row):
             arrival.wait()
         load_surface_row(sz, local, row, surface, row * sz.row_width)
-        for t in range(count):
+        for t in range(sz.row_tiles):
             coeff = jnp.broadcast_to(diffusivity[row, 0:1, cols(t)], (LEVELS, WIDTH))
             for c in range(CHANNELS):
-                padded[row + 1, c, :, cols(t)] = coeff * local[row, c, :, cols(t)]
-
+                scaled[row, c, :, cols(t)] = coeff * local[row, c, :, cols(t)]
+        return carry
+
+    lax.fori_loop(0, sz.rows, one_row, 0)
+
+
+def backward_kernel(sz, last, arrive, *refs):
+    refs = list(refs)
+    if not last:
+        tables, weights, slope = refs[:3]
+        refs = refs[3:]
+    low, high, first_surface, second_surface, diffusivity, mix = refs[:6]
+    local, bent_all, scaled_all = refs[6:9]
+    refs = refs[9:]
+    if last:
+        start_all, out, sums, padded = refs
+    else:
+        out, new_surface, packed, tell_first, tell_second, padded, near_low, near_high = refs
+        remap = Remap(sz, weights)
+    count = sz.row_tiles
     place_edges(sz, padded, low, high, first_surface, second_surface)
+
+    def ready(row):
+        padded[row + 1] = scaled_all[row]
+
     ready(0)
     lane = lax.broadcasted_iota(jnp.int32, (LEVELS, WIDTH), 1)
     sub = lax.broadcasted_iota(jnp.int32, (LEVELS, WIDTH), 0)
@@ -762,11 +807,22 @@
         sums[...] = held
     else:
         new_surface[CHANNELS * sz.tiles :, :] = jnp.zeros((CHANNELS, WIDTH), jnp.float32)
+        arrive_all(arrive)
         spread_back(
-            sz, new_surface, slope, remap, tables, packed, near_low, near_high, tell_first, tell_second
+            sz,
+            new_surface,
+            slope,
+            remap,
+            tables,
+            packed,
+            near_low,
+            near_high,
+            tell_first,
+            tell_second,
+            sz.edge_lines,
         )
         packed.start()
-        store_edges(sz, out, diffusivity, edge_first, edge_second)
+        store_edges(sz, out, diffusivity, tell_first, tell_second)
 
 
 def final_kernel(cell_total, arrive, everyones, perturbation, gradient, out):
@@ -959,11 +1015,12 @@
     mix_rows = chan_mix.transpose(1, 2, 0).reshape(CHANNELS * CHANNELS, LEVELS)
     row_lines = (rows, 1, sz.cells)
     tiles_lines = (CHANNELS * sz.tiles, WIDTH)
-    table, facts, mix, diffusivity_rows, weight_rows, diffusivity_tiles, weight_tiles = call(
+    first_mix, first_rows, table, facts, mix, *lines = call(
         functools.partial(setup_kernel, sz, wet_list.shape[1], remap_at.shape[0] + places.shape[0]),
         "setup",
         near_by(lined(wet_list[0], wet_owner[0]), remap_lines, mix_rows)
         + fetched(diffusivity, cost_weight),
+        kept=[(CHANNELS * CHANNELS, LEVELS, WIDTH), row_lines],
         shipped=[
             jax.ShapeDtypeStruct((sz.slot_lines, WIDTH), jnp.int32),
             (sz.facts, WIDTH),
@@ -974,6 +1031,7 @@
             tiles_lines,
         ],
     )
+    diffusivity_rows, weight_rows, diffusivity_tiles, weight_tiles = lines
     wider = (rows + 2, CHANNELS, LEVELS, sz.cells)
     row_surface = (sz.row_width, WIDTH)
     by_row = (rows, *native_row)
@@ -991,42 +1049,45 @@
     )
 
     saved = []
-    surface = None
-    told = None
+    near = [sz.near, sz.near]
+    mix_shape = (CHANNELS * CHANNELS, LEVELS, WIDTH)
+    by_slot = (sz.slots, WIDTH)
     for hour in range(hours):
         first, last = hour == 0, hour == hours - 1
-        inputs = near_by(*edges) + fetched(diffusivity_rows, mix) + scalars(table, facts)
-        scratch = [wider]
+        inputs = scalars(table, facts)
         if first:
-            inputs += near_by(field) + fetched(facts)
+            inputs += near_by(*edges, first_rows, first_mix, field)
+            assert not last
         else:
-            inputs += far_off(field) + near_by(surface, *surface_edges)
-            scratch += [row_sems(2)]
-        if last:
-            inputs += fetched(weight_rows) + far_off(target_state)
-            scratch += [by_row]
+            loads = fetched(mix, diffusivity_rows, *([weight_rows] if last else []))
+            loads += far_off(field) + near_by(surface) + (far_off(target_state) if last else [])
+            mix_here, rows_here, field, *more = call(
+                functools.partial(forward_load_kernel, sz, last),
+                "step_load",
+                loads,
+                kept=[mix_shape, row_lines, sz.whole] + ([row_lines, sz.whole] if last else []),
+                scratch=[row_sems(2)] + ([by_row] if last else []),
+            )
+            inputs += near_by(*edges, rows_here, mix_here, field, *surface_edges, *more)
         field, drive, surface, packed, *sends = call(
             functools.partial(forward_kernel, sz, first, last),
             "step",
             inputs,
             shipped=[
-                sz.whole, sz.whole, sz.surface, sz.narrow, sz.told, sz.told, sz.edge, sz.edge
+                sz.whole, sz.whole, sz.surface, sz.narrow, sz.edge_and_lats, sz.edge_and_lats
             ],
-            scratch=scratch,
-        )
+            scratch=[wider],
+        )
+        if first:
+            packed, tell = lax.optimization_barrier((packed, facts))
         arrived = exchange(packed, devices)
-        got = swap(*sends[:2])
-        arrived, *got = lax.optimization_barrier((arrived, *got))
-        if first:
-            told = got
         inputs = (
-            near_by(arrived)
-            + fetched(owner_mix, at=(0,))
-            + fetched(air_temp, wind_speed, at=(hour, 0))
+            near_by(arrived, owner_mix[0], air_temp[hour, 0], wind_speed[hour, 0])
             + scalars(facts)
         )
         decoded = []
         if first:
+            told = swap(tell, tell)
             inputs += near_by(*told) + fetched(table, facts)
             decoded = [jax.ShapeDtypeStruct(sz.tables, jnp.int32), sz.weights]
         *decoded, flux, mixed_slope, flux_slope = call(
@@ -1034,15 +1095,14 @@
             "owners",
             inputs,
             shipped=[*decoded, sz.wide, sz.by_slot, sz.by_slot],
-            scratch=[sz.narrow, (sz.slots, WIDTH)],
+            scratch=[sz.narrow, by_slot],
         )
         if first:
             tables, weights = decoded
-        flux, *sends = lax.optimization_barrier((flux, *sends[2:]))
+        flux, *sends = lax.optimization_barrier((flux, *sends))
         flux = exchange(flux, devices)
         edges = swap(*sends)
-        inputs = near_by(flux, *got) + fetched(surface) + scalars(tables, weights)
-        near = [sz.near, sz.near]
+        inputs = near_by(flux, *edges) + fetched(surface) + scalars(tables, weights)
         if last:
             surface, slope, packed, *sends = call(
                 functools.partial(surface_kernel, sz, True),
@@ -1063,28 +1123,23 @@
             surface_edges = swap(*sends)
         saved.append((drive, slope, mixed_slope, flux_slope))
 
-    edge_sends = None
     for hour in reversed(range(hours)):
         drive, slope, mixed_slope, flux_slope = saved[hour]
         arrived = exchange(packed, devices)
-        got = swap(*sends)
-        arrived, *got = lax.optimization_barrier((arrived, *got))
         back = call(
             functools.partial(owner_back_kernel, sz),
             "owners_back",
-            near_by(arrived)
-            + fetched(owner_mix, at=(0,))
-            + fetched(mixed_slope, flux_slope)
-            + scalars(facts),
+            near_by(arrived, owner_mix[0]) + fetched(mixed_slope, flux_slope) + scalars(facts),
             shipped=[sz.narrow],
-            scratch=[sz.narrow, (sz.slots, WIDTH)],
+            scratch=[sz.narrow, by_slot],
         )[0]
-        if edge_sends is not None:
-            back, *edge_sends = lax.optimization_barrier((back, *edge_sends))
-            edges = swap(*edge_sends)
+        back, *sends = lax.optimization_barrier((back, *sends))
+        got = swap(*sends)
         back = exchange(back, devices)
+        if hour < hours - 1:
+            edges = got
         surface, *row_sends = call(
-            functools.partial(merge_kernel, sz),
+            functools.partial(merge_kernel, sz, sz.edge_lines if hour < hours - 1 else 0),
             "merge",
             near_by(back, *got)
             + fetched(surface, slope)
@@ -1093,27 +1148,33 @@
             kept=[sz.surface, row_surface, row_surface],
         )
         surface_edges = swap(*row_sends)
-        inputs = (
-            near_by(surface, *edges, *surface_edges)
-            + fetched(diffusivity_rows, mix)
+        last = hour == 0
+        mix_here, rows_here, *loaded = call(
+            functools.partial(backward_load_kernel, sz, last),
+            "step_back_load",
+            fetched(mix, diffusivity_rows)
             + far_off(field, drive)
-        )
-        if hour > 0:
+            + near_by(surface)
+            + (far_off(start_field) if last else []),
+            kept=[mix_shape, row_lines] + [sz.whole] * (4 if last else 3),
+            scratch=[row_sems(3)],
+        )
+        inputs = near_by(*edges, *surface_edges, rows_here, mix_here, *loaded)
+        if last:
+            gradient, sums = call(
+                functools.partial(backward_kernel, sz, True),
+                "step_back_sums",
+                inputs,
+                shipped=[sz.whole, (devices, WIDTH)],
+                scratch=[wider],
+            )
+        else:
             field, surface, packed, *sends = call(
                 functools.partial(backward_kernel, sz, False),
                 "step_back",
-                inputs + scalars(tables, weights) + fetched(saved[hour - 1][1]),
-                shipped=[sz.whole, sz.surface, sz.wide, sz.lats, sz.lats, sz.edge, sz.edge],
-                scratch=[sz.whole, sz.whole, wider, row_sems(2), sz.near, sz.near],
-            )
-            sends, edge_sends = sends[:2], sends[2:]
-        else:
-            gradient, sums = call(
-                functools.partial(backward_kernel, sz, True),
-                "step_back_sums",
-                inputs + far_off(start_field),
-                shipped=[sz.whole, (devices, WIDTH)],
-                scratch=[sz.whole, sz.whole, wider, row_sems(3), sz.whole],
+                scalars(tables, weights) + fetched(saved[hour - 1][1]) + inputs,
+                shipped=[sz.whole, sz.surface, sz.wide, sz.edge_and_lats, sz.edge_and_lats],
+                scratch=[wider, *near],
             )
 
     everyones = lax.all_to_all(sums, "horiz", split_axis=0, concat_axis=0, tiled=True)

time: 179 us -> 184 us (1.028)
  blocking collectives: 13.5 us -> 50.5 us
  waiting for transfers between devices: 62.4 us -> 41.9 us
  starting transfers between devices: 58 us -> 48 us
    all_to_all x1 -> x3, blocking collectives: 13.5 us -> 50.5 us  [exchange(): lax.all_to_all(split, 'horiz', split_axis=0, concat_axis=0, tiled=True)]
    all_to_all x7 -> x5, waiting for transfers between devices: 54.5 us -> 34.2 us  [exchange(): lax.all_to_all(split, 'horiz', split_axis=0, concat_axis=0, tiled=True)]
    all_to_all x7 -> x5, starting transfers between devices: 39.9 us -> 24.6 us  [exchange(): lax.all_to_all(split, 'horiz', split_axis=0, concat_axis=0, tiled=True)]
    ppermute x11 -> x9, starting transfers between devices: 3.7 us -> 8.7 us  [swap(): lax.ppermute(first, 'horiz', inner)]
    ppermute x11 -> x9, starting transfers between devices: 7.25 us -> 5.94 us  [swap(): lax.ppermute(second, 'horiz', outer)]
    pallas_call x16 -> x19, Pallas kernels: 40.6 us -> 39.8 us  [call(): pl.pallas_call(run, name=name, in_specs=[pl.BlockSpec(memory_space=item.s...]
  transfers between devices with their start and end apart: 30 -> 24, of which waited for: 15 -> 11; matrix products, arithmetic and copies ran while one was open for 1% -> 1% of each run, Pallas kernels for 5% -> 6%
where the time goes in v2:
time: 184 us; the launch traced here: 183 us
  blocking collectives  50.5 us (27%)
  starting transfers between devices  48 us (26%)
  waiting for transfers between devices  41.9 us (23%)
  Pallas kernels  39.8 us (22%)
  local copies, waits for them, and re-layouts  1.88 us (1%)
    all_to_all x3, blocking collectives, exchange(): lax.all_to_all(split, 'horiz', split_axis=0, concat_axis=0, tiled=True)  50.5 us
    pallas_call x19, Pallas kernels, call(): pl.pallas_call(run, name=name, in_specs=[pl.BlockSpec(memory_space=item.s...  39.8 us
    all_to_all x5, waiting for transfers between devices, exchange(): lax.all_to_all(split, 'horiz', split_axis=0, concat_axis=0, tiled=True)  34.2 us
    all_to_all x5, starting transfers between devices, exchange(): lax.all_to_all(split, 'horiz', split_axis=0, concat_axis=0, tiled=True)  24.6 us
    all_to_all x1, starting transfers between devices, body(): lax.all_to_all(sums, 'horiz', split_axis=0, concat_axis=0, tiled=True)  8.74 us
    ppermute x9, starting transfers between devices, swap(): lax.ppermute(first, 'horiz', inner)  8.7 us
    ppermute x9, starting transfers between devices, swap(): lax.ppermute(second, 'horiz', outer)  5.94 us
    all_to_all x1, waiting for transfers between devices, body(): lax.all_to_all(sums, 'horiz', split_axis=0, concat_axis=0, tiled=True)  4.68 us
  transfers between devices with their start and end apart: 24, of which 11 were waited for; matrix products, arithmetic and copies ran while one was open for 1% of the time, Pallas kernels for 6%

profile of v2, /device:TPU:0, one launch (start us, length us, event | category | flops | bytes accessed | tf_op | source)
XLA Modules:
  0.0 182.8 jit_solution(8636922425759280185)
XLA Ops:
  0.0 1.7 edges.1
  1.8 0.5 collective-permute-start
  2.3 0.7 collective-permute-start.1
  3.0 0.1 reshape.82
  3.1 0.1 maximum_bitcast_fusion
  3.2 3.0 %load.1 = (f32[5,4,8,1920]{3,2,1,0:T(8,128)S(1)}, f32[5,4,8,1920]{3,2,1,0:T(8,128)}) custom-call(f32[8,5,4,1920]{3,2,1,0:T(4,128)} %refs_1_.5, f32[8,5,4,1920]{3,2,1,0:T(4,128)} %refs_1_.4), custom_call_target="tpu_custom_call" | custom-call | tf_op jit(solution)/shard_map/load/pallas_call | solution.py:941
  6.1 0.0 copy-start.4
  6.2 0.0 copy-start.5
  6.2 0.1 add_convert_fusion
  6.3 1.9 %setup.1 = (f32[16,8,128]{2,1,0:T(8,128)S(1)}, f32[5,1,1920]{2,1,0:T(1,128)S(1)}, s32[1,128]{1,0:T(1,128)}, f32[8,128]{1,0:T(8,128)}, f32[16,8,128]{2,1,0:T(8,12...) custom-call(f32[2,128]{1,0:T(2,128)S(1)} %get-tuple-element.180.refs_0_, ...), custom_call_target="tpu_custom_call" | custom-call | tf_op jit(solution)/shard_map/setup/pallas_call | solution.py:941
  8.2 0.0 copy-start.1
  8.2 2.7 %step.2 = (f32[5,4,8,1920]{3,2,1,0:T(8,128)}, f32[5,4,8,1920]{3,2,1,0:T(8,128)}, f32[304,128]{1,0:T(8,128)}, f32[320,128]{1,0:T(8,128)}, f32[512,128]{1,0:T(8,128)}, /*index=5*/f32[512,128]{1,0:T(8,128)}) custom-call(s32[1,128]{1,0:T(1,128)} %get-tuple-element.90.refs_0_.refs_7_.refs_5_, f32[8,128]{1,0:T(8,128)} %get-tuple-element.99.refs_1_.refs_4_.refs_8_.refs_6_, ...), custom_call_target="tpu_custom_call" | custom-call | tf_op jit(solution)/shard_map/step/pallas_call | solution.py:941
  10.9 10.4 %all-to-all-start = ((f32[16,5,4,128]{3,2,1,0:T(4,128)}), f32[16,5,4,128]{3,2,1,0:T(4,128)S(1)}, u32[]{:S(2)}, u32[]{:S(2)}) async-start(f32[16,5,4,128]{3,2,1,0:T(4,128)} %bitcast.62), calls=%async_computation | async-start | bytes 327680 | tf_op jit(solution)/shard_map/all_to_all | solution.py:968
  21.4 0.7 collective-permute-start.3
  22.0 3.3 %collective-permute-start.2 = (f32[8,128]{1,0:T(8,128)S(1)}, f32[8,128]{1,0:T(8,128)S(1)}, u32[]{:S(2)}, u32[]{:S(2)}) collective-permute-start(f32[8,128]{1,0:T(8,128)S(1)} %copy-done.3), channel_id=1, source_target_pairs={{0,1},{1,0},{2,3},{3,2},{4,5},{5,4},{6,7},{7,6},{8,9},{9,8},{10,11... | collective-permute-start | bytes 12296 | tf_op jit(solution)/shard_map/ppermute | solution.py:962
  25.4 0.8 collective-permute-done.2.refs_5_
  26.2 3.6 %all-to-all-done = f32[16,5,4,128]{3,2,1,0:T(4,128)S(1)} async-done(((f32[16,5,4,128]{3,2,1,0:T(4,128)}), f32[16,5,4,128]{3,2,1,0:T(4,128)S(1)}, u32[]{:S(2)}, u32[]{:S(2)}) %all-to-all-start) | async-done | bytes 163872 | tf_op jit(solution)/shard_map/all_to_all | solution.py:968
  29.8 2.0 %owners.2 = (s32[3,128]{1,0:T(4,128)}, f32[24,128]{1,0:T(8,128)}, f32[512,128]{1,0:T(8,128)}, f32[4,80,128]{2,1,0:T(8,128)}, f32[4,80,128]{2,1,0:T(8,128)}) custom-call(f32[320,128]{1,0:T(8,128)S(1)} %bitcast.52, f32[80,80]{1,0:T(8,128)S(1)} %bitcast.46, f32[80,128]{1,0:T(8,128)S(1)} %get-tuple-element.181.refs_2_, ...), custom_call_target="tpu_custom_call" | custom-call | tf_op jit(solution)/shard_map/owners/pallas_call | solution.py:941
  31.8 3.5 %all-to-all-start.1 = ((f32[16,8,4,128]{3,2,1,0:T(4,128)}), f32[16,8,4,128]{3,2,1,0:T(4,128)S(1)}, u32[]{:S(2)}, u32[]{:S(2)}) async-start(f32[16,8,4,128]{3,2,1,0:T(4,128)} %bitcast.58), calls=%async_computation.1 | async-start | bytes 524288 | tf_op jit(solution)/shard_map/all_to_all | solution.py:968
  35.4 0.4 collective-permute-start.4
  35.7 0.7 collective-permute-start.5
  36.4 0.6 collective-permute-done.4.refs_1_.refs_2_
  37.0 8.4 %all-to-all-done.1 = f32[16,8,4,128]{3,2,1,0:T(4,128)S(1)} async-done(((f32[16,8,4,128]{3,2,1,0:T(4,128)}), f32[16,8,4,128]{3,2,1,0:T(4,128)S(1)}, u32[]{:S(2)}, u32[]{:S(2)}) %all-to-all-start.1) | async-done | bytes 262176 | tf_op jit(solution)/shard_map/all_to_all | solution.py:968
  45.4 1.9 %surface.2 = (f32[304,128]{1,0:T(8,128)S(1)}, f32[60,128]{1,0:T(8,128)S(1)}, f32[60,128]{1,0:T(8,128)S(1)}, f32[64,128]{1,0:T(8,128)}) custom-call(f32[512,128]{1,0:T(8,128)S(1)} %bitcast.44, f32[512,128]{1,0:T(8,128)S(1)} %collective-permute-done.4.refs_1_.refs_2_, f32[512,128]{1,0:T(8,128)S(1)} %collective-permute-done.5.refs_2_.refs_3_, ...), custom_call_target="tpu_custom_call" | custom-call | tf_op jit(solution)/shard_map/surface/pallas_call | solution.py:941
  47.2 1.2 collective-permute-start.6
  48.4 0.7 collective-permute-start.7
  49.1 2.3 %step_load.1 = (f32[16,8,128]{2,1,0:T(8,128)S(1)}, f32[5,1,1920]{2,1,0:T(1,128)S(1)}, f32[5,4,8,1920]{3,2,1,0:T(8,128)S(1)}, f32[5,1,1920]{2,1,0:T(1,128)S(1)}, f32[5,4,8,1920]{3,2,1,0:T(8,128)S(1)}) custom-call(f32[16,8,128]{2,1,0:T(8,128)} %get-tuple-element.110.refs_0_, f32[5,1,1920]{2,1,0:T(1,128)} %get-tuple-element.111.refs_1_, ...), custom_call_target="tpu_custom_call" | custom-call | tf_op jit(solution)/shard_map/step_load/pallas_call | solution.py:941
  51.5 2.9 %step.3 = (f32[5,4,8,1920]{3,2,1,0:T(8,128)}, f32[5,4,8,1920]{3,2,1,0:T(8,128)}, f32[304,128]{1,0:T(8,128)}, f32[320,128]{1,0:T(8,128)}, f32[512,128]{1,0:T(8,128)}, /*index=5*/f32[512,128]{1,0:T(8,128)}) custom-call(s32[1,128]{1,0:T(1,128)} %get-tuple-element.90.refs_0_.refs_7_.refs_5_, f32[8,128]{1,0:T(8,128)} %get-tuple-element.99.refs_1_.refs_4_.refs_8_.refs_6_, ...), custom_call_target="tpu_custom_call" | custom-call | tf_op jit(solution)/shard_map/step/pallas_call | solution.py:941
  54.3 17.2 %all_to_all.51 = f32[16,5,4,128]{3,2,1,0:T(4,128)S(1)} all-to-all(f32[16,5,4,128]{3,2,1,0:T(4,128)} %bitcast.63), channel_id=1, replica_groups=mesh['member'=2,'horiz'=16] {'horiz'}, dimensions={0} | all-to-all | bytes 327680 | tf_op jit(solution)/shard_map/all_to_all | solution.py:968
  71.5 2.0 %owners.3 = (f32[512,128]{1,0:T(8,128)}, f32[4,80,128]{2,1,0:T(8,128)}, f32[4,80,128]{2,1,0:T(8,128)}) custom-call(f32[320,128]{1,0:T(8,128)S(1)} %bitcast.53, f32[80,80]{1,0:T(8,128)S(1)} %bitcast.47, f32[80,128]{1,0:T(8,128)S(1)} %get-tuple-element.182.refs_2_, f32[80,128]{1,0:T(8,128)S(1)} %get-tuple-element.175.refs_3_, ...), custom_call_target="tpu_custom_call" | custom-call | tf_op jit(solution)/shard_map/owners/pallas_call | solution.py:941
  73.5 3.5 %all-to-all-start.3 = ((f32[16,8,4,128]{3,2,1,0:T(4,128)}), f32[16,8,4,128]{3,2,1,0:T(4,128)S(1)}, u32[]{:S(2)}, u32[]{:S(2)}) async-start(f32[16,8,4,128]{3,2,1,0:T(4,128)} %bitcast.59), calls=%async_computation.3 | async-start | bytes 524288 | tf_op jit(solution)/shard_map/all_to_all | solution.py:968
  77.0 0.3 collective-permute-start.8
  77.3 0.7 collective-permute-start.9
  78.0 0.8 collective-permute-done.8.refs_1_.refs_3_
  78.9 8.2 %all-to-all-done.3 = f32[16,8,4,128]{3,2,1,0:T(4,128)S(1)} async-done(((f32[16,8,4,128]{3,2,1,0:T(4,128)}), f32[16,8,4,128]{3,2,1,0:T(4,128)S(1)}, u32[]{:S(2)}, u32[]{:S(2)}) %all-to-all-start.3) | async-done | bytes 262176 | tf_op jit(solution)/shard_map/all_to_all | solution.py:968
  87.0 2.3 %surface.3 = (f32[304,128]{1,0:T(8,128)}, f32[64,128]{1,0:T(8,128)}, f32[512,128]{1,0:T(8,128)}, f32[32,128]{1,0:T(8,128)}, f32[32,128]{1,0:T(8,128)}) custom-call(f32[512,128]{1,0:T(8,128)S(1)} %bitcast.45, f32[512,128]{1,0:T(8,128)S(1)} %collective-permute-done.8.refs_1_.refs_3_, f32[512,128]{1,0:T(8,128)S(1)} %collective-permute-done.9.refs_2_.refs_4_, ...), custom_call_target="tpu_custom_call" | custom-call | tf_op jit(solution)/shard_map/surface/pallas_call | solution.py:941
  89.4 16.7 %all_to_all.52 = f32[16,8,4,128]{3,2,1,0:T(4,128)S(1)} all-to-all(f32[16,8,4,128]{3,2,1,0:T(4,128)} %bitcast.61), channel_id=1, replica_groups=mesh['member'=2,'horiz'=16] {'horiz'}, dimensions={0} | all-to-all | bytes 524288 | tf_op jit(solution)/shard_map/all_to_all | solution.py:968
  106.1 2.0 %owners_back.2 = f32[320,128]{1,0:T(8,128)} custom-call(f32[512,128]{1,0:T(8,128)S(1)} %bitcast.42, f32[80,80]{1,0:T(8,128)S(1)} %bitcast.48, f32[4,80,128]{2,1,0:T(8,128)} %get-tuple-element.132.refs_2_, f32[4,80,128]{2,1,0:T(8,128)} %get-tuple-element.133.refs_3_, f32[8,128]{1,0:T(8,128)} %get-tuple-element.99.refs_1_.refs_4_.refs_8_.refs_6_), custom_call_target="tpu_custom_call" | custom-call | tf_op jit(solution)/shard_map/owners_back/pallas_call | solution.py:941
  108.2 3.5 %all-to-all-start.5 = ((f32[16,5,4,128]{3,2,1,0:T(4,128)}), f32[16,5,4,128]{3,2,1,0:T(4,128)S(1)}, u32[]{:S(2)}, u32[]{:S(2)}) async-start(f32[16,5,4,128]{3,2,1,0:T(4,128)} %bitcast.56), calls=%async_computation.5 | async-start | bytes 327680 | tf_op jit(solution)/shard_map/all_to_all | solution.py:968
  111.7 0.4 collective-permute-start.10
  112.1 0.7 collective-permute-start.11
  112.7 0.2 collective-permute-done.10.refs_1_
  113.0 7.2 %all-to-all-done.5 = f32[16,5,4,128]{3,2,1,0:T(4,128)S(1)} async-done(((f32[16,5,4,128]{3,2,1,0:T(4,128)}), f32[16,5,4,128]{3,2,1,0:T(4,128)S(1)}, u32[]{:S(2)}, u32[]{:S(2)}) %all-to-all-start.5) | async-done | bytes 163872 | tf_op jit(solution)/shard_map/all_to_all | solution.py:968
  120.1 1.2 merge.2
  121.3 0.1 collective-permute-start.12
  121.4 0.7 collective-permute-start.13
  122.1 2.0 %step_back_load.2 = (f32[16,8,128]{2,1,0:T(8,128)S(1)}, f32[5,1,1920]{2,1,0:T(1,128)S(1)}, f32[5,4,8,1920]{3,2,1,0:T(8,128)S(1)}, f32[5,4,8,1920]{3,2,1,0:T(8,128)S(1)}, f32[5,4,8,1920]{3,2,1,0:T(8,128)S(1)}) custom-call(f32[16,8,128]{2,1,0:T(8,128)} %get-tuple-element.110.refs_0_, f32[5,1,1920]{2,1,0:T(1,128)} %get-tuple-element.111.refs_1_, ...), custom_call_target="tpu_custom_call" | custom-call | tf_op jit(solution)/shard_map/step_back_load/pallas_call | solution.py:941
  124.1 2.8 %step_back.1 = (f32[5,4,8,1920]{3,2,1,0:T(8,128)}, f32[304,128]{1,0:T(8,128)}, f32[512,128]{1,0:T(8,128)}, f32[512,128]{1,0:T(8,128)}, f32[512,128]{1,0:T(8,128)}) custom-call(s32[3,128]{1,0:T(4,128)} %get-tuple-element.100.refs_4_.refs_0_, f32[24,128]{1,0:T(8,128)} %get-tuple-element.101.refs_5_.refs_1_, f32[64,128]{1,0:T(8,128)} %get-tuple-element.109.refs_2_.refs_4_, ...), custom_call_target="tpu_custom_call" | custom-call | tf_op jit(solution)/shard_map/step_back/pallas_call | solution.py:941
  126.8 16.6 %all_to_all.53 = f32[16,8,4,128]{3,2,1,0:T(4,128)S(1)} all-to-all(f32[16,8,4,128]{3,2,1,0:T(4,128)} %bitcast.60), channel_id=1, replica_groups=mesh['member'=2,'horiz'=16] {'horiz'}, dimensions={0} | all-to-all | bytes 524288 | tf_op jit(solution)/shard_map/all_to_all | solution.py:968
  143.4 2.0 %owners_back.3 = f32[320,128]{1,0:T(8,128)} custom-call(f32[512,128]{1,0:T(8,128)S(1)} %bitcast.43, f32[80,80]{1,0:T(8,128)S(1)} %bitcast.49, f32[4,80,128]{2,1,0:T(8,128)} %get-tuple-element.153.refs_2_, f32[4,80,128]{2,1,0:T(8,128)} %get-tuple-element.154.refs_3_, f32[8,128]{1,0:T(8,128)} %get-tuple-element.99.refs_1_.refs_4_.refs_8_.refs_6_), custom_call_target="tpu_custom_call" | custom-call | tf_op jit(solution)/shard_map/owners_back/pallas_call | solution.py:941
  145.5 3.5 %all-to-all-start.7 = ((f32[16,5,4,128]{3,2,1,0:T(4,128)}), f32[16,5,4,128]{3,2,1,0:T(4,128)S(1)}, u32[]{:S(2)}, u32[]{:S(2)}) async-start(f32[16,5,4,128]{3,2,1,0:T(4,128)} %bitcast.57), calls=%async_computation.7 | async-start | bytes 327680 | tf_op jit(solution)/shard_map/all_to_all | solution.py:968
  149.0 0.4 collective-permute-start.14
  149.4 0.7 collective-permute-start.15
  150.0 0.6 collective-permute-done.14.refs_1_.refs_0_
  150.6 6.8 %all-to-all-done.7 = f32[16,5,4,128]{3,2,1,0:T(4,128)S(1)} async-done(((f32[16,5,4,128]{3,2,1,0:T(4,128)}), f32[16,5,4,128]{3,2,1,0:T(4,128)S(1)}, u32[]{:S(2)}, u32[]{:S(2)}) %all-to-all-start.7) | async-done | bytes 163872 | tf_op jit(solution)/shard_map/all_to_all | solution.py:968
  157.4 1.2 merge.3
  158.6 2.2 %collective-permute-start.16 = (f32[60,128]{1,0:T(8,128)S(1)}, f32[60,128]{1,0:T(8,128)S(1)}, u32[]{:S(2)}, u32[]{:S(2)}) collective-permute-start(f32[60,128]{1,0:T(8,128)S(1)} %get-tuple-element.161), channel_id=1, source_target_pairs={{0,1},{1,0},{2,3},{3,2},{4,5},{5,4},{6,7},{7,6},{8,9},{9,8},{10,11... | collective-permute-start | bytes 92168 | tf_op jit(solution)/shard_map/ppermute | solution.py:962
  160.9 0.7 collective-permute-start.17
  161.5 2.4 %step_back_load.3 = (f32[16,8,128]{2,1,0:T(8,128)S(1)}, f32[5,1,1920]{2,1,0:T(1,128)S(1)}, f32[5,4,8,1920]{3,2,1,0:T(8,128)S(1)}, f32[5,4,8,1920]{3,2,1,0:T(8,12...) custom-call(f32[16,8,128]{2,1,0:T(8,128)} %get-tuple-element.110.refs_0_, ...), custom_call_target="tpu_custom_call" | custom-call | tf_op jit(solution)/shard_map/step_back_load/pallas_call | solution.py:941
  163.9 2.5 %step_back_sums.1 = (f32[5,4,8,1920]{3,2,1,0:T(8,128)}, f32[16,128]{1,0:T(8,128)}) custom-call(f32[512,128]{1,0:T(8,128)S(1)} %collective-permute-done.14.refs_1_.refs_0_, f32[512,128]{1,0:T(8,128)S(1)} %collective-permute-done.15.refs_2_.refs_1_, f32[60,128]{1,0:T(8,128)S(1)} %collective-permute-done.16.refs_2_, ...), custom_call_target="tpu_custom_call" | custom-call | tf_op jit(solution)/shard_map/step_back_sums/pallas_call | solution.py:941
  166.4 8.7 %all-to-all-start.8 = ((f32[16,1,128]{2,1,0:T(1,128)}), f32[16,1,128]{2,1,0:T(1,128)S(1)}, u32[]{:S(2)}, u32[]{:S(2)}) async-start(f32[16,1,128]{2,1,0:T(1,128)} %bitcast.64), calls=%async_computation.8 | async-start | bytes 16384 | tf_op jit(solution)/shard_map/all_to_all | solution.py:1180
  175.2 1.7 copy.20
  176.9 4.7 %all-to-all-done.8 = f32[16,1,128]{2,1,0:T(1,128)S(1)} async-done(((f32[16,1,128]{2,1,0:T(1,128)}), f32[16,1,128]{2,1,0:T(1,128)S(1)}, u32[]{:S(2)}, u32[]{:S(2)}) %all-to-all-start.8) | async-done | bytes 8224 | tf_op jit(solution)/shard_map/all_to_all | solution.py:1180
  181.6 1.2 finish.1
  (52 shorter events, 0.1 us)
Async XLA Ops:
  0.0 3.0 %copy-start.6 = (f32[4,4]{1,0:T(4,128)S(1)}, f32[4,4]{1,0:T(4,128)}, u32[]{:S(2)}) copy-start(f32[4,4]{1,0:T(4,128)} %param.21) | copy-start | bytes 196
  0.0 3.1 %copy-start.8 = (s32[15]{0:T(128)S(1)}, s32[15]{0:T(128)}, u32[]{:S(2)}) copy-start(s32[15]{0:T(128)} %param.28) | copy-start | bytes 184
  0.0 3.1 %copy-start.7 = (s32[15]{0:T(128)S(1)}, s32[15]{0:T(128)}, u32[]{:S(2)}) copy-start(s32[15]{0:T(128)} %param.27) | copy-start | bytes 184
  0.0 3.1 %copy-start.15 = (f32[15]{0:T(128)S(1)}, f32[15]{0:T(128)}, u32[]{:S(2)}) copy-start(f32[15]{0:T(128)} %param.29) | copy-start | bytes 184
  1.8 6.4 %collective-permute-start = (f32[480,128]{1,0:T(8,128)S(1)}, f32[480,128]{1,0:T(8,128)S(1)}, u32[]{:S(2)}, u32[]{:S(2)}) collective-permute-start(f32[480,128]{1,0:T(8,128)S(1)} %get-tuple-element.92), channel_id=1, source_target_pairs={{0,1},{1,0},{2,3},{3,2},{4,5},{5,4},{6,7},{7,6},{8,9},{9,8},{10,11... | collective-permute-start | bytes 737288 | tf_op jit(solution)/shard_map/ppermute | solution.py:962
  2.3 5.9 %collective-permute-start.1 = (f32[480,128]{1,0:T(8,128)S(1)}, f32[480,128]{1,0:T(8,128)S(1)}, u32[]{:S(2)}, u32[]{:S(2)}) collective-permute-start(f32[480,128]{1,0:T(8,128)S(1)} %get-tuple-element.93), channel_id=1, source_target_pairs={{1,2},{3,4},{5,6},{7,8},{9,10},{11,12},{13,14},{2,1},{4,3},{6,5},{... | collective-permute-start | bytes 737288 | tf_op jit(solution)/shard_map/ppermute | solution.py:962
  3.2 3.0 %copy-start.16 = (s32[1,75]{1,0:T(1,128)S(1)}, s32[1,75]{1,0:T(1,128)}, u32[]{:S(2)}) copy-start(s32[1,75]{1,0:T(1,128)} %param.25) | copy-start | bytes 904
  3.2 3.0 %copy-start.17 = (s32[1,75]{1,0:T(1,128)S(1)}, s32[1,75]{1,0:T(1,128)}, u32[]{:S(2)}) copy-start(s32[1,75]{1,0:T(1,128)} %param.26) | copy-start | bytes 904
  3.2 3.1 %copy-start.2 = (f32[8,4,4]{0,2,1:T(4,128)S(1)}, f32[8,4,4]{0,2,1:T(4,128)}, u32[]{:S(2)}) copy-start(f32[8,4,4]{0,2,1:T(4,128)} %param.20) | copy-start | bytes 1540
  6.1 19.2 %copy-start.4 = (f32[2,1,80,128]{3,2,1,0:T(8,128)S(1)}, f32[2,1,80,128]{3,2,1,0:T(8,128)}, u32[]{:S(2)}) copy-start(f32[2,1,80,128]{3,2,1,0:T(8,128)} %param.24) | copy-start | bytes 245764
  6.2 19.2 %copy-start.5 = (f32[2,1,80,128]{3,2,1,0:T(8,128)S(1)}, f32[2,1,80,128]{3,2,1,0:T(8,128)}, u32[]{:S(2)}) copy-start(f32[2,1,80,128]{3,2,1,0:T(8,128)} %param.23) | copy-start | bytes 245764
  8.2 13.2 %copy-start.3 = (f32[8,128]{1,0:T(8,128)S(1)}, f32[8,128]{1,0:T(8,128)}, u32[]{:S(2)}) copy-start(f32[8,128]{1,0:T(8,128)} %get-tuple-element.99.refs_1_.refs_4_.refs_8_.refs_6_) | copy-start | bytes 12292
  8.2 21.6 %copy-start.1 = (f32[1,80,80]{2,1,0:T(8,128)S(1)}, f32[1,80,80]{2,1,0:T(8,128)}, u32[]{:S(2)}) copy-start(f32[1,80,80]{2,1,0:T(8,128)} %param.22) | copy-start | bytes 76804
  10.9 24.5 %copy-start.10 = (f32[512,128]{1,0:T(8,128)S(1)}, f32[512,128]{1,0:T(8,128)}, u32[]{:S(2)}) copy-start(f32[512,128]{1,0:T(8,128)} %get-tuple-element.106) | copy-start | bytes 786436
  10.9 24.8 %copy-start.9 = (f32[512,128]{1,0:T(8,128)S(1)}, f32[512,128]{1,0:T(8,128)}, u32[]{:S(2)}) copy-start(f32[512,128]{1,0:T(8,128)} %get-tuple-element.107) | copy-start | bytes 786436
  10.9 18.9 %all-to-all-start = ((f32[16,5,4,128]{3,2,1,0:T(4,128)}), f32[16,5,4,128]{3,2,1,0:T(4,128)S(1)}, u32[]{:S(2)}, u32[]{:S(2)}) async-start(f32[16,5,4,128]{3,2,1,0:T(4,128)} %bitcast.62), calls=%async_computation | async-start | bytes 327680 | tf_op jit(solution)/shard_map/all_to_all | solution.py:968
  21.4 4.0 %collective-permute-start.3 = (f32[8,128]{1,0:T(8,128)S(1)}, f32[8,128]{1,0:T(8,128)S(1)}, u32[]{:S(2)}, u32[]{:S(2)}) collective-permute-start(f32[8,128]{1,0:T(8,128)S(1)} %copy-done.3), channel_id=1, source_target_pairs={{1,2},{3,4},{5,6},{7,8},{9,10},{11,12},{13,14},{2,1},{4,3},{6,5},{... | collective-permute-start | bytes 12296 | tf_op jit(solution)/shard_map/ppermute | solution.py:962
  22.0 4.2 %collective-permute-start.2 = (f32[8,128]{1,0:T(8,128)S(1)}, f32[8,128]{1,0:T(8,128)S(1)}, u32[]{:S(2)}, u32[]{:S(2)}) collective-permute-start(f32[8,128]{1,0:T(8,128)S(1)} %copy-done.3), channel_id=1, source_target_pairs={{0,1},{1,0},{2,3},{3,2},{4,5},{5,4},{6,7},{7,6},{8,9},{9,8},{10,11... | collective-permute-start | bytes 12296 | tf_op jit(solution)/shard_map/ppermute | solution.py:962
  31.8 13.6 %all-to-all-start.1 = ((f32[16,8,4,128]{3,2,1,0:T(4,128)}), f32[16,8,4,128]{3,2,1,0:T(4,128)S(1)}, u32[]{:S(2)}, u32[]{:S(2)}) async-start(f32[16,8,4,128]{3,2,1,0:T(4,128)} %bitcast.58), calls=%async_computation.1 | async-start | bytes 524288 | tf_op jit(solution)/shard_map/all_to_all | solution.py:968
  35.4 1.6 collective-permute-start.4
  35.7 1.2 collective-permute-start.5
  47.2 4.2 %collective-permute-start.6 = (f32[60,128]{1,0:T(8,128)S(1)}, f32[60,128]{1,0:T(8,128)S(1)}, u32[]{:S(2)}, u32[]{:S(2)}) collective-permute-start(f32[60,128]{1,0:T(8,128)S(1)} %get-tuple-element.118), channel_id=1, source_target_pairs={{0,1},{1,0},{2,3},{3,2},{4,5},{5,4},{6,7},{7,6},{8,9},{9,8},{10,11... | collective-permute-start | bytes 92168 | tf_op jit(solution)/shard_map/ppermute | solution.py:962
  48.4 3.0 %collective-permute-start.7 = (f32[60,128]{1,0:T(8,128)S(1)}, f32[60,128]{1,0:T(8,128)S(1)}, u32[]{:S(2)}, u32[]{:S(2)}) collective-permute-start(f32[60,128]{1,0:T(8,128)S(1)} %get-tuple-element.119), channel_id=1, source_target_pairs={{1,2},{3,4},{5,6},{7,8},{9,10},{11,12},{13,14},{2,1},{4,3},{6,5},{... | collective-permute-start | bytes 92168 | tf_op jit(solution)/shard_map/ppermute | solution.py:962
  73.5 13.6 %all-to-all-start.3 = ((f32[16,8,4,128]{3,2,1,0:T(4,128)}), f32[16,8,4,128]{3,2,1,0:T(4,128)S(1)}, u32[]{:S(2)}, u32[]{:S(2)}) async-start(f32[16,8,4,128]{3,2,1,0:T(4,128)} %bitcast.59), calls=%async_computation.3 | async-start | bytes 524288 | tf_op jit(solution)/shard_map/all_to_all | solution.py:968
  77.0 1.8 collective-permute-start.8
  77.3 1.5 collective-permute-start.9
  89.4 22.3 %copy-start.14 = (f32[32,128]{1,0:T(8,128)S(1)}, f32[32,128]{1,0:T(8,128)}, u32[]{:S(2)}) copy-start(f32[32,128]{1,0:T(8,128)} %get-tuple-element.137) | copy-start | bytes 49156
  89.4 22.7 %copy-start.13 = (f32[32,128]{1,0:T(8,128)S(1)}, f32[32,128]{1,0:T(8,128)}, u32[]{:S(2)}) copy-start(f32[32,128]{1,0:T(8,128)} %get-tuple-element.138) | copy-start | bytes 49156
  108.2 12.0 %all-to-all-start.5 = ((f32[16,5,4,128]{3,2,1,0:T(4,128)}), f32[16,5,4,128]{3,2,1,0:T(4,128)S(1)}, u32[]{:S(2)}, u32[]{:S(2)}) async-start(f32[16,5,4,128]{3,2,1,0:T(4,128)} %bitcast.56), calls=%async_computation.5 | async-start | bytes 327680 | tf_op jit(solution)/shard_map/all_to_all | solution.py:968
  111.7 1.2 collective-permute-start.10
  112.1 0.9 collective-permute-start.11
  121.3 2.7 %collective-permute-start.12 = (f32[60,128]{1,0:T(8,128)S(1)}, f32[60,128]{1,0:T(8,128)S(1)}, u32[]{:S(2)}, u32[]{:S(2)}) collective-permute-start(f32[60,128]{1,0:T(8,128)S(1)} %get-tuple-element.142), channel_id=1, source_target_pairs={{0,1},{1,0},{2,3},{3,2},{4,5},{5,4},{6,7},{7,6},{8,9},{9,8},{10,11... | collective-permute-start | bytes 92168 | tf_op jit(solution)/shard_map/ppermute | solution.py:962
  121.4 2.7 %collective-permute-start.13 = (f32[60,128]{1,0:T(8,128)S(1)}, f32[60,128]{1,0:T(8,128)S(1)}, u32[]{:S(2)}, u32[]{:S(2)}) collective-permute-start(f32[60,128]{1,0:T(8,128)S(1)} %get-tuple-element.143), channel_id=1, source_target_pairs={{1,2},{3,4},{5,6},{7,8},{9,10},{11,12},{13,14},{2,1},{4,3},{6,5},{... | collective-permute-start | bytes 92168 | tf_op jit(solution)/shard_map/ppermute | solution.py:962
  126.8 22.2 %copy-start.12 = (f32[512,128]{1,0:T(8,128)S(1)}, f32[512,128]{1,0:T(8,128)}, u32[]{:S(2)}) copy-start(f32[512,128]{1,0:T(8,128)} %get-tuple-element.157) | copy-start | bytes 786436
  126.8 22.5 %copy-start.11 = (f32[512,128]{1,0:T(8,128)S(1)}, f32[512,128]{1,0:T(8,128)}, u32[]{:S(2)}) copy-start(f32[512,128]{1,0:T(8,128)} %get-tuple-element.158) | copy-start | bytes 786436
  145.5 12.0 %all-to-all-start.7 = ((f32[16,5,4,128]{3,2,1,0:T(4,128)}), f32[16,5,4,128]{3,2,1,0:T(4,128)S(1)}, u32[]{:S(2)}, u32[]{:S(2)}) async-start(f32[16,5,4,128]{3,2,1,0:T(4,128)} %bitcast.57), calls=%async_computation.7 | async-start | bytes 327680 | tf_op jit(solution)/shard_map/all_to_all | solution.py:968
  149.0 1.6 collective-permute-start.14
  149.4 1.2 collective-permute-start.15
  158.6 5.2 %collective-permute-start.16 = (f32[60,128]{1,0:T(8,128)S(1)}, f32[60,128]{1,0:T(8,128)S(1)}, u32[]{:S(2)}, u32[]{:S(2)}) collective-permute-start(f32[60,128]{1,0:T(8,128)S(1)} %get-tuple-element.161), channel_id=1, source_target_pairs={{0,1},{1,0},{2,3},{3,2},{4,5},{5,4},{6,7},{7,6},{8,9},{9,8},{10,11... | collective-permute-start | bytes 92168 | tf_op jit(solution)/shard_map/ppermute | solution.py:962
  160.9 3.0 %collective-permute-start.17 = (f32[60,128]{1,0:T(8,128)S(1)}, f32[60,128]{1,0:T(8,128)S(1)}, u32[]{:S(2)}, u32[]{:S(2)}) collective-permute-start(f32[60,128]{1,0:T(8,128)S(1)} %get-tuple-element.162), channel_id=1, source_target_pairs={{1,2},{3,4},{5,6},{7,8},{9,10},{11,12},{13,14},{2,1},{4,3},{6,5},{... | collective-permute-start | bytes 92168 | tf_op jit(solution)/shard_map/ppermute | solution.py:962
  166.4 15.1 %all-to-all-start.8 = ((f32[16,1,128]{2,1,0:T(1,128)}), f32[16,1,128]{2,1,0:T(1,128)S(1)}, u32[]{:S(2)}, u32[]{:S(2)}) async-start(f32[16,1,128]{2,1,0:T(1,128)} %bitcast.64), calls=%async_computation.8 | async-start | bytes 16384 | tf_op jit(solution)/shard_map/all_to_all | solution.py:1180
  175.2 6.4 %copy-start = (f32[8,5,4,1920]{3,2,1,0:T(4,128)S(1)}, f32[8,5,4,1920]{3,2,1,0:T(4,128)}, u32[]{:S(2)}) copy-start(f32[8,5,4,1920]{3,2,1,0:T(4,128)} %refs_1_.5) | copy-start | bytes 3686404

commit v3 on v2

--- a/solution.py
+++ b/solution.py
@@ -43,7 +43,7 @@
         self.edge_lines = CHANNELS * self.row_tiles * LEVELS
         self.whole = (rows, CHANNELS, LEVELS, cells)
         self.edge = (self.edge_lines, WIDTH)
-        self.edge_and_lats = (self.edge_lines + self.lat_lines, WIDTH)
+        self.told = (self.lat_lines + self.facts, WIDTH)
         self.surface = (CHANNELS * (self.tiles + 1), WIDTH)
         self.narrow = (CHANNELS * self.slots, WIDTH)
         self.wide = (devices * self.chunk, WIDTH)
@@ -144,23 +144,11 @@
     return jnp.sum(jnp.where(diagonal, row, 0.0), axis=1, keepdims=True)
 
 
-def setup_kernel(sz, entries, remap_entries, arrive, wet, remap, mix_rows, diffusivity, weight, *outs):
-    first_mix, first_rows, table, facts, mix = outs[:5]
-    diffusivity_rows, weight_rows, diffusivity_tiles, weight_tiles = outs[5:]
+def setup_kernel(sz, entries, remap_entries, arrive, wet, remap, mix_rows, diffusivity, *outs):
+    first_mix, first_rows, table, facts, mix = outs
     arrive_all(arrive)
-    for source, by_row, by_tile in (
-        (diffusivity, diffusivity_rows, diffusivity_tiles),
-        (weight, weight_rows, weight_tiles),
-    ):
-        for row in range(sz.rows):
-            for tile in range(sz.row_tiles):
-                line = source[row : row + 1, cols(tile)]
-                by_row[row, 0:1, cols(tile)] = line
-                at = (row * sz.row_tiles + tile) * CHANNELS
-                by_tile[at : at + CHANNELS, :] = jnp.broadcast_to(line, (CHANNELS, WIDTH))
-        by_row.start()
-        by_tile.start()
-    first_rows[...] = diffusivity_rows[...]
+    for row in range(sz.rows):
+        first_rows[row] = diffusivity[row : row + 1, :]
     for index in range(CHANNELS * CHANNELS):
         column = as_column(mix_rows[index : index + 1, :], LEVELS)
         mix[index] = jnp.broadcast_to(column, (LEVELS, WIDTH))
@@ -189,11 +177,26 @@
     )
 
 
-def gather_levels(block, rows_at, channel, tile):
+def columns_kernel(sz, arrive, diffusivity, weight, *outs):
+    diffusivity_rows, weight_rows, diffusivity_tiles, weight_tiles = outs
+    arrive_all(arrive)
+    for source, by_row, by_tile in (
+        (diffusivity, diffusivity_rows, diffusivity_tiles),
+        (weight, weight_rows, weight_tiles),
+    ):
+        for row in range(sz.rows):
+            by_row[row] = source[row : row + 1, :]
+            for tile in range(sz.row_tiles):
+                line = source[row : row + 1, cols(tile)]
+                at = (row * sz.row_tiles + tile) * CHANNELS
+                by_tile[at : at + CHANNELS, :] = jnp.broadcast_to(line, (CHANNELS, WIDTH))
+
+
+def gather_levels(block, channel, tile):
     sub = lax.broadcasted_iota(jnp.int32, (LEVELS, WIDTH), 0)
     total = None
     for level in range(LEVELS):
-        line = block[(level, *rows_at, slice(channel, channel + 1), cols(tile))]
+        line = block[level, channel : channel + 1, cols(tile)]
         line = jnp.broadcast_to(line, (LEVELS, WIDTH))
         total = line if total is None else jnp.where(sub == level, line, total)
     return total
@@ -201,19 +204,19 @@
 
 def edges_kernel(sz, arrive, low_start, high_start, low_base, high_base, send_first, send_second):
     arrive_all(arrive)
+    low_start[...] = low_start[...] + low_base[...]
+    high_start[...] = high_start[...] + high_base[...]
     flag = high_first()
     for channel in range(CHANNELS):
         for tile in range(sz.row_tiles):
-            low = gather_levels(low_start, (), channel, tile)
-            low = low + gather_levels(low_base, (), channel, tile)
-            high = gather_levels(high_start, (), channel, tile)
-            high = high + gather_levels(high_base, (), channel, tile)
+            low = gather_levels(low_start, channel, tile)
+            high = gather_levels(high_start, channel, tile)
             at = (channel * sz.row_tiles + tile) * LEVELS
             send_first[at : at + LEVELS, :] = pick(flag, high, low)
             send_second[at : at + LEVELS, :] = pick(flag, low, high)
 
 
-def load_kernel(sz, arrive, perturbation, base, field, start, start_block, base_block, in_sems):
+def load_kernel(sz, arrive, perturbation, base, field, start_block, base_block, in_sems):
     def arrivals(row):
         return [
             pltpu.make_async_copy(source.at[:, row], block.at[row], in_sems.at[index, row])
@@ -229,14 +232,30 @@
     def one_row(row, carry):
         for arrival in arrivals(row):
             arrival.wait()
+        start_block[row] = start_block[row] + base_block[row]
         for channel in range(CHANNELS):
             for tile in range(sz.row_tiles):
-                here = gather_levels(start_block.at[row], (), channel, tile)
-                start[row, channel, :, cols(tile)] = here
-                field[row, channel, :, cols(tile)] = here + gather_levels(
-                    base_block.at[row], (), channel, tile
+                field[row, channel, :, cols(tile)] = gather_levels(
+                    start_block.at[row], channel, tile
                 )
-        start.row(row).start()
+        return carry
+
+    lax.fori_loop(0, sz.rows, one_row, 0)
+
+
+def relayout_kernel(sz, arrive, source, out, block, in_sems):
+    def arrival(row):
+        return pltpu.make_async_copy(source.at[:, row], block.at[row], in_sems.at[0, row])
+
+    for row in range(sz.rows):
+        arrival(row).start()
+
+    def one_row(row, carry):
+        arrival(row).wait()
+        for channel in range(CHANNELS):
+            for tile in range(sz.row_tiles):
+                out[row, channel, :, cols(tile)] = gather_levels(block.at[row], channel, tile)
+        out.row(row).start()
         return carry
 
     lax.fori_loop(0, sz.rows, one_row, 0)
@@ -278,26 +297,24 @@
     ]
 
 
-def send_sums(sz, sums, tell_first, tell_second, base):
+def send_sums(sz, sums, tell_first, tell_second):
     flag = high_first()
     for index in range(LAT_DEV):
         low, high = sums[index], sums[LAT_DEV + index]
-        at = base + index * sz.pitch
+        at = index * sz.pitch
         tell_first[at : at + sz.row_tiles, :] = pick(flag, high, low)
         tell_second[at : at + sz.row_tiles, :] = pick(flag, low, high)
 
 
-def lat_rows(sz, ref, lat, base=0):
-    at = base + lat * sz.pitch
+def lat_rows(sz, ref, lat):
+    at = lat * sz.pitch
     return ref[at : at + sz.row_tiles, :]
 
 
-def told_sums(sz, from_first, from_second, base):
+def told_sums(sz, from_first, from_second):
     lows, highs = [], []
     for index in range(LAT_DEV):
-        low, high = sided(
-            lat_rows(sz, from_first, index, base), lat_rows(sz, from_second, index, base)
-        )
+        low, high = sided(lat_rows(sz, from_first, index), lat_rows(sz, from_second, index))
         lows.append(low)
         highs.append(high)
     return lows + highs
@@ -364,7 +381,7 @@
         if last:
             for c in range(CHANNELS):
                 for t in range(sz.row_tiles):
-                    target_out[row, c, :, cols(t)] = gather_levels(refs[1].at[row], (), c, t)
+                    target_out[row, c, :, cols(t)] = gather_levels(refs[1].at[row], c, t)
         return carry
 
     lax.fori_loop(0, sz.rows, one_row, 0)
@@ -374,6 +391,8 @@
     refs = list(refs)
     tables, facts, low, high, diffusivity, mix, field = refs[:7]
     refs = refs[7:]
+    if first:
+        facts_block = refs.pop(0)
     surfaces = ()
     if not first:
         surfaces = refs[:2]
@@ -381,7 +400,7 @@
     if last:
         weight, target = refs[:2]
         refs = refs[2:]
-    out, drive, new_surface, packed, tell_first, tell_second, padded = refs
+    out, drive, new_surface, packed, tell_first, tell_second, edge_first, edge_second, padded = refs
     remap = Remap(sz, facts)
     place_edges(sz, padded, low, high, *surfaces)
 
@@ -401,6 +420,7 @@
         here = [[padded[row + 1, c, :, cols(t)] for t in range(count)] for c in range(CHANNELS)]
         for t in range(count):
             coeff = jnp.broadcast_to(diffusivity[row, 0:1, cols(t)], (LEVELS, WIDTH))
+            center = (1.0 - 2.0 * KAPPA_V) - 4.0 * coeff
             if last:
                 scale = weight[row, 0:1, cols(t)]
                 scale = jnp.broadcast_to(scale * scale, (LEVELS, WIDTH))
@@ -420,9 +440,9 @@
                 )
                 around = around + (padded[row, c, :, cols(t)] + padded[row + 2, c, :, cols(t)])
                 stepped = (
-                    field_here
-                    + coeff * (around - 4.0 * field_here)
-                    + KAPPA_V * (levels_sum(field_here, sub) - 2.0 * field_here)
+                    center * field_here
+                    + coeff * around
+                    + KAPPA_V * levels_sum(field_here, sub)
                     + TIME_STEP * bent
                 )
                 new_surface[pl.ds((row * count + t) * CHANNELS + c, 1), :] = stepped[0:1, :]
@@ -440,8 +460,12 @@
     pack_slots(sz, tables, new_surface, packed)
     packed.start()
     own = [row_tiles_of(sz, new_surface.block, row) for row in range(sz.rows)]
-    send_sums(sz, own_sums(sz, remap, own, 1.0), tell_first, tell_second, sz.edge_lines)
-    store_edges(sz, out, diffusivity if last else None, tell_first, tell_second)
+    send_sums(sz, own_sums(sz, remap, own, 1.0), tell_first, tell_second)
+    for tell in (tell_first, tell_second):
+        if first:
+            tell[sz.lat_lines :, :] = facts_block[...]
+        tell.start()
+    store_edges(sz, out, diffusivity if last else None, edge_first, edge_second)
 
 
 def pack_slots(sz, tables, surface, packed):
@@ -476,7 +500,7 @@
         lines = sz.slot_lines
         tables[0:lines, :] = own_table[...]
         weights[0 : sz.facts, :] = own_facts[...]
-        both = sided(told_first[...], told_second[...])
+        both = sided(told_first[sz.lat_lines :, :], told_second[sz.lat_lines :, :])
         for which, told in ((1, both[0]), (2, both[1])):
             got = told[0:lines, :].astype(jnp.int32)
             tables[which * lines : (which + 1) * lines, :] = sz.tiles - got
@@ -570,12 +594,14 @@
         back.block[pl.ds(k, slots, stride=CHANNELS), :] = through[:, cols(k)] + sign * direct[k]
 
 
-def spread_back(sz, surface, slope, remap, tables, packed, near_low, near_high, tell_first, tell_second, base):
+def spread_back(sz, surface, slope, remap, tables, packed, near_low, near_high, tell_first, tell_second):
     rows, count, cap = sz.rows, sz.row_tiles, sz.capacity
     block = surface.block
     own = [row_tiles_of(sz, block, row) for row in range(rows)]
     sums = own_sums(sz, remap, own, FEEDBACK)
-    send_sums(sz, sums, tell_first, tell_second, base)
+    send_sums(sz, sums, tell_first, tell_second)
+    tell_first.start()
+    tell_second.start()
     lats = [lat_rows(sz, slope, lat) * sums[lat] for lat in range(NEAR_LAT)]
     every = range(NEAR_LAT)
     for row in range(rows):
@@ -637,7 +663,7 @@
     block[CHANNELS * sz.tiles :, :] = jnp.zeros((CHANNELS, WIDTH), jnp.float32)
     own = [row_tiles_of(sz, block, row) for row in range(rows)]
     sums = own_sums(sz, remap, own, 1.0)
-    told = told_sums(sz, from_first, from_second, sz.edge_lines)
+    told = told_sums(sz, from_first, from_second)
     air = []
     for lat in range(NEAR_LAT):
         if lat < LAT_DEV:
@@ -660,14 +686,14 @@
                 off = block[at : at + CHANNELS, :] - target[row, :, cols(tile)]
                 block[at : at + CHANNELS, :] = scale * scale * off
         spread_back(
-            sz, surface, slope, remap, tables, packed, near_low, near_high, tell_first, tell_second, 0
+            sz, surface, slope, remap, tables, packed, near_low, near_high, tell_first, tell_second
         )
     else:
         store_rows(sz, surface, send_first, send_second)
 
 
 def merge_kernel(
-    sz, base, arrive, back, from_first, from_second, before, slope, tables, facts, diffusivity, surface, send_first, send_second
+    sz, arrive, back, from_first, from_second, before, slope, tables, facts, diffusivity, surface, send_first, send_second
 ):
     rows = sz.rows
     remap = Remap(sz, facts)
@@ -679,7 +705,7 @@
             before[pl.ds(tile, CHANNELS), :] + back[slot * CHANNELS : (slot + 1) * CHANNELS, :]
         )
     surface[CHANNELS * sz.tiles :, :] = jnp.zeros((CHANNELS, WIDTH), jnp.float32)
-    told = told_sums(sz, from_first, from_second, base)
+    told = told_sums(sz, from_first, from_second)
     lats = [lat_rows(sz, slope, lat) * told[lat] for lat in range(NEAR_LAT)]
     for row in range(rows):
         own = row_tiles_of(sz, surface, row)
@@ -740,7 +766,8 @@
     if last:
         start_all, out, sums, padded = refs
     else:
-        out, new_surface, packed, tell_first, tell_second, padded, near_low, near_high = refs
+        out, new_surface, packed, tell_first, tell_second, edge_first, edge_second = refs[:7]
+        padded, near_low, near_high = refs[7:]
         remap = Remap(sz, weights)
     count = sz.row_tiles
     place_edges(sz, padded, low, high, first_surface, second_surface)
@@ -778,9 +805,9 @@
                 )
                 around = around + (padded[row, c, :, cols(t)] + padded[row + 2, c, :, cols(t)])
                 stepped = (
-                    here[c]
-                    + (around - 4.0 * scaled[c][t])
-                    + KAPPA_V * (levels_sum(here[c], sub) - 2.0 * here[c])
+                    ((1.0 - 2.0 * KAPPA_V) * here[c] - 4.0 * scaled[c][t])
+                    + around
+                    + KAPPA_V * levels_sum(here[c], sub)
                     + TIME_STEP * mixed
                 )
                 out[row, c, :, cols(t)] = stepped
@@ -819,10 +846,9 @@
             near_high,
             tell_first,
             tell_second,
-            sz.edge_lines,
         )
         packed.start()
-        store_edges(sz, out, diffusivity, tell_first, tell_second)
+        store_edges(sz, out, diffusivity, edge_first, edge_second)
 
 
 def final_kernel(cell_total, arrive, everyones, perturbation, gradient, out):
@@ -1015,23 +1041,18 @@
     mix_rows = chan_mix.transpose(1, 2, 0).reshape(CHANNELS * CHANNELS, LEVELS)
     row_lines = (rows, 1, sz.cells)
     tiles_lines = (CHANNELS * sz.tiles, WIDTH)
-    first_mix, first_rows, table, facts, mix, *lines = call(
+    first_mix, first_rows, table, facts, mix = call(
         functools.partial(setup_kernel, sz, wet_list.shape[1], remap_at.shape[0] + places.shape[0]),
         "setup",
         near_by(lined(wet_list[0], wet_owner[0]), remap_lines, mix_rows)
-        + fetched(diffusivity, cost_weight),
+        + fetched(diffusivity),
         kept=[(CHANNELS * CHANNELS, LEVELS, WIDTH), row_lines],
         shipped=[
             jax.ShapeDtypeStruct((sz.slot_lines, WIDTH), jnp.int32),
             (sz.facts, WIDTH),
             (CHANNELS * CHANNELS, LEVELS, WIDTH),
-            row_lines,
-            row_lines,
-            tiles_lines,
-            tiles_lines,
         ],
     )
-    diffusivity_rows, weight_rows, diffusivity_tiles, weight_tiles = lines
     wider = (rows + 2, CHANNELS, LEVELS, sz.cells)
     row_surface = (sz.row_width, WIDTH)
     by_row = (rows, *native_row)
@@ -1039,12 +1060,11 @@
     def row_sems(kinds):
         return pltpu.SemaphoreType.DMA((kinds, rows))
 
-    field, start_field = call(
+    (field,) = call(
         functools.partial(load_kernel, sz),
         "load",
         far_off(perturbation, base_state),
         kept=[sz.whole],
-        shipped=[sz.whole],
         scratch=[by_row, by_row, row_sems(2)],
     )
 
@@ -1056,7 +1076,7 @@
         first, last = hour == 0, hour == hours - 1
         inputs = scalars(table, facts)
         if first:
-            inputs += near_by(*edges, first_rows, first_mix, field)
+            inputs += near_by(*edges, first_rows, first_mix, field) + fetched(facts)
             assert not last
         else:
             loads = fetched(mix, diffusivity_rows, *([weight_rows] if last else []))
@@ -1073,22 +1093,21 @@
             functools.partial(forward_kernel, sz, first, last),
             "step",
             inputs,
-            shipped=[
-                sz.whole, sz.whole, sz.surface, sz.narrow, sz.edge_and_lats, sz.edge_and_lats
-            ],
+            shipped=[sz.whole, sz.whole, sz.surface, sz.narrow]
+            + [sz.told if first else sz.lats] * 2
+            + [sz.edge] * 2,
             scratch=[wider],
         )
-        if first:
-            packed, tell = lax.optimization_barrier((packed, facts))
         arrived = exchange(packed, devices)
+        got = swap(*sends[:2])
+        arrived, *got = lax.optimization_barrier((arrived, *got))
         inputs = (
             near_by(arrived, owner_mix[0], air_temp[hour, 0], wind_speed[hour, 0])
             + scalars(facts)
         )
         decoded = []
         if first:
-            told = swap(tell, tell)
-            inputs += near_by(*told) + fetched(table, facts)
+            inputs += near_by(*got) + fetched(table, facts)
             decoded = [jax.ShapeDtypeStruct(sz.tables, jnp.int32), sz.weights]
         *decoded, flux, mixed_slope, flux_slope = call(
             functools.partial(owner_kernel, sz, first),
@@ -1099,10 +1118,18 @@
         )
         if first:
             tables, weights = decoded
-        flux, *sends = lax.optimization_barrier((flux, *sends))
+        flux, *sends = lax.optimization_barrier((flux, *sends[2:]))
+        if first:
+            flux, diffusivity = lax.optimization_barrier((flux, diffusivity))
+            diffusivity_rows, weight_rows, diffusivity_tiles, weight_tiles = call(
+                functools.partial(columns_kernel, sz),
+                "columns",
+                fetched(diffusivity, cost_weight),
+                shipped=[row_lines, row_lines, tiles_lines, tiles_lines],
+            )
         flux = exchange(flux, devices)
         edges = swap(*sends)
-        inputs = near_by(flux, *edges) + fetched(surface) + scalars(tables, weights)
+        inputs = near_by(flux, *got) + fetched(surface) + scalars(tables, weights)
         if last:
             surface, slope, packed, *sends = call(
                 functools.partial(surface_kernel, sz, True),
@@ -1123,9 +1150,12 @@
             surface_edges = swap(*sends)
         saved.append((drive, slope, mixed_slope, flux_slope))
 
+    edge_sends = None
     for hour in reversed(range(hours)):
         drive, slope, mixed_slope, flux_slope = saved[hour]
         arrived = exchange(packed, devices)
+        got = swap(*sends)
+        arrived, *got = lax.optimization_barrier((arrived, *got))
         back = call(
             functools.partial(owner_back_kernel, sz),
             "owners_back",
@@ -1133,13 +1163,21 @@
             shipped=[sz.narrow],
             scratch=[sz.narrow, by_slot],
         )[0]
-        back, *sends = lax.optimization_barrier((back, *sends))
-        got = swap(*sends)
+        if edge_sends is not None:
+            back, *edge_sends = lax.optimization_barrier((back, *edge_sends))
+            edges = swap(*edge_sends)
+        else:
+            back, perturbation = lax.optimization_barrier((back, perturbation))
+            start_field = call(
+                functools.partial(relayout_kernel, sz),
+                "relayout",
+                far_off(perturbation),
+                shipped=[sz.whole],
+                scratch=[by_row, row_sems(1)],
+            )[0]
         back = exchange(back, devices)
-        if hour < hours - 1:
-            edges = got
         surface, *row_sends = call(
-            functools.partial(merge_kernel, sz, sz.edge_lines if hour < hours - 1 else 0),
+            functools.partial(merge_kernel, sz),
             "merge",
             near_by(back, *got)
             + fetched(surface, slope)
@@ -1169,13 +1207,14 @@
                 scratch=[wider],
             )
         else:
-            field, surface, packed, *sends = call(
+            field, surface, packed, *outs = call(
                 functools.partial(backward_kernel, sz, False),
                 "step_back",
                 scalars(tables, weights) + fetched(saved[hour - 1][1]) + inputs,
-                shipped=[sz.whole, sz.surface, sz.wide, sz.edge_and_lats, sz.edge_and_lats],
+                shipped=[sz.whole, sz.surface, sz.wide, sz.lats, sz.lats, sz.edge, sz.edge],
                 scratch=[wider, *near],
             )
+            sends, edge_sends = outs[:2], outs[2:]
 
     everyones = lax.all_to_all(sums, "horiz", split_axis=0, concat_axis=0, tiled=True)
     block = perturbation.shape

time: 184 us -> 174 us (0.946)
  blocking collectives: 50.5 us -> 13.5 us
  waiting for transfers between devices: 41.9 us -> 60.9 us
  starting transfers between devices: 48 us -> 53.1 us
  Pallas kernels: 39.8 us -> 42.3 us
    all_to_all x3 -> x1, blocking collectives: 50.5 us -> 13.5 us  [exchange(): lax.all_to_all(split, 'horiz', split_axis=0, concat_axis=0, tiled=True)]
    all_to_all x5 -> x7, waiting for transfers between devices: 34.2 us -> 54.5 us  [exchange(): lax.all_to_all(split, 'horiz', split_axis=0, concat_axis=0, tiled=True)]
    all_to_all x5 -> x7, starting transfers between devices: 24.6 us -> 37.2 us  [exchange(): lax.all_to_all(split, 'horiz', split_axis=0, concat_axis=0, tiled=True)]
    ppermute x9 -> x11, starting transfers between devices: 8.7 us -> 3.69 us  [swap(): lax.ppermute(first, 'horiz', inner)]
    all_to_all x1, starting transfers between devices: 8.74 us -> 4.94 us  [body(): lax.all_to_all(sums, 'horiz', split_axis=0, concat_axis=0, tiled=True)]
    pallas_call x19 -> x21, Pallas kernels: 39.8 us -> 42.3 us  [call(): pl.pallas_call(run, name=name, in_specs=[pl.BlockSpec(memory_space=item.s...]
    ppermute x9 -> x11, starting transfers between devices: 5.94 us -> 7.25 us  [swap(): lax.ppermute(second, 'horiz', outer)]
  transfers between devices with their start and end apart: 24 -> 30, of which waited for: 11 -> 12; matrix products, arithmetic and copies ran while one was open for 1% -> 1% of each run, Pallas kernels for 6% -> 11%
where the time goes in v3:
time: 174 us; the launch traced here: 173 us
  waiting for transfers between devices  60.9 us (35%)
  starting transfers between devices  53.1 us (31%)
  Pallas kernels  42.3 us (24%)
  blocking collectives  13.5 us (8%)
  local copies, waits for them, and re-layouts  1.88 us (1%)
    all_to_all x7, waiting for transfers between devices, exchange(): lax.all_to_all(split, 'horiz', split_axis=0, concat_axis=0, tiled=True)  54.5 us
    pallas_call x21, Pallas kernels, call(): pl.pallas_call(run, name=name, in_specs=[pl.BlockSpec(memory_space=item.s...  42.3 us
    all_to_all x7, starting transfers between devices, exchange(): lax.all_to_all(split, 'horiz', split_axis=0, concat_axis=0, tiled=True)  37.2 us
    all_to_all x1, blocking collectives, exchange(): lax.all_to_all(split, 'horiz', split_axis=0, concat_axis=0, tiled=True)  13.5 us
    ppermute x11, starting transfers between devices, swap(): lax.ppermute(second, 'horiz', outer)  7.25 us
    all_to_all x1, starting transfers between devices, body(): lax.all_to_all(sums, 'horiz', split_axis=0, concat_axis=0, tiled=True)  4.94 us
    all_to_all x1, waiting for transfers between devices, body(): lax.all_to_all(sums, 'horiz', split_axis=0, concat_axis=0, tiled=True)  4.68 us
    ppermute x11, starting transfers between devices, swap(): lax.ppermute(first, 'horiz', inner)  3.69 us
  transfers between devices with their start and end apart: 30, of which 12 were waited for; matrix products, arithmetic and copies ran while one was open for 1% of the time, Pallas kernels for 11%

profile of v3, /device:TPU:0, one launch (start us, length us, event | category | flops | bytes accessed | tf_op | source)
XLA Modules:
  0.0 172.5 jit_solution(4215886904435867732)
XLA Ops:
  0.0 1.6 edges.1
  1.6 0.5 collective-permute-start
  2.2 0.7 collective-permute-start.1
  2.9 0.1 reshape.82
  3.0 2.0 %load.1.refs_6_ = f32[5,4,8,1920]{3,2,1,0:T(8,128)S(1)} custom-call(f32[8,5,4,1920]{3,2,1,0:T(4,128)} %refs_1_.6, f32[8,5,4,1920]{3,2,1,0:T(4,128)} %refs_1_.4), custom_call_target="tpu_custom_call" | custom-call | tf_op jit(solution)/shard_map/load/pallas_call | solution.py:967
  5.1 0.1 add_convert_fusion
  5.2 1.7 setup.1
  6.9 2.7 %step.2 = (f32[5,4,8,1920]{3,2,1,0:T(8,128)}, f32[5,4,8,1920]{3,2,1,0:T(8,128)}, f32[304,128]{1,0:T(8,128)}, f32[320,128]{1,0:T(8,128)}, f32[40,128]{1,0:T(8,128...) custom-call(s32[1,128]{1,0:T(1,128)} %get-tuple-element.105.refs_0_.refs_7_.refs_5_, ...), custom_call_target="tpu_custom_call" | custom-call | tf_op jit(solution)/shard_map/step/pallas_call | solution.py:967
  9.6 11.6 %all-to-all-start = ((f32[16,5,4,128]{3,2,1,0:T(4,128)}), f32[16,5,4,128]{3,2,1,0:T(4,128)S(1)}, u32[]{:S(2)}, u32[]{:S(2)}) async-start(f32[16,5,4,128]{3,2,1,0:T(4,128)} %bitcast.62), calls=%async_computation | async-start | bytes 327680 | tf_op jit(solution)/shard_map/all_to_all | solution.py:994
  21.2 0.4 collective-permute-start.2
  21.6 0.7 collective-permute-start.3
  22.3 0.4 collective-permute-done.2.refs_5_.refs_1_
  22.7 7.0 %all-to-all-done = f32[16,5,4,128]{3,2,1,0:T(4,128)S(1)} async-done(((f32[16,5,4,128]{3,2,1,0:T(4,128)}), f32[16,5,4,128]{3,2,1,0:T(4,128)S(1)}, u32[]{:S(2)}, u32[]{:S(2)}) %all-to-all-start) | async-done | bytes 163872 | tf_op jit(solution)/shard_map/all_to_all | solution.py:994
  29.7 2.0 %owners.2 = (s32[3,128]{1,0:T(4,128)}, f32[24,128]{1,0:T(8,128)}, f32[512,128]{1,0:T(8,128)}, f32[4,80,128]{2,1,0:T(8,128)}, f32[4,80,128]{2,1,0:T(8,128)}) custom-call(f32[320,128]{1,0:T(8,128)S(1)} %bitcast.52, f32[80,80]{1,0:T(8,128)S(1)} %bitcast.46, f32[80,128]{1,0:T(8,128)S(1)} %get-tuple-element.211.refs_2_, ...), custom_call_target="tpu_custom_call" | custom-call | tf_op jit(solution)/shard_map/owners/pallas_call | solution.py:967
  31.7 3.5 %all-to-all-start.1 = ((f32[16,8,4,128]{3,2,1,0:T(4,128)}), f32[16,8,4,128]{3,2,1,0:T(4,128)S(1)}, u32[]{:S(2)}, u32[]{:S(2)}) async-start(f32[16,8,4,128]{3,2,1,0:T(4,128)} %bitcast.60), calls=%async_computation.1 | async-start | bytes 524288 | tf_op jit(solution)/shard_map/all_to_all | solution.py:994
  35.2 0.4 collective-permute-start.4
  35.6 0.7 collective-permute-start.5
  36.3 9.0 %all-to-all-done.1 = f32[16,8,4,128]{3,2,1,0:T(4,128)S(1)} async-done(((f32[16,8,4,128]{3,2,1,0:T(4,128)}), f32[16,8,4,128]{3,2,1,0:T(4,128)S(1)}, u32[]{:S(2)}, u32[]{:S(2)}) %all-to-all-start.1) | async-done | bytes 262176 | tf_op jit(solution)/shard_map/all_to_all | solution.py:994
  45.2 1.9 %surface.2 = (f32[304,128]{1,0:T(8,128)S(1)}, f32[60,128]{1,0:T(8,128)S(1)}, f32[60,128]{1,0:T(8,128)S(1)}, f32[64,128]{1,0:T(8,128)}) custom-call(f32[512,128]{1,0:T(8,128)S(1)} %bitcast.44, f32[40,128]{1,0:T(8,128)S(1)} %collective-permute-done.2.refs_5_.refs_1_, f32[40,128]{1,0:T(8,128)S(1)} %collective-permute-done.3.refs_6_.refs_2_, ...), custom_call_target="tpu_custom_call" | custom-call | tf_op jit(solution)/shard_map/surface/pallas_call | solution.py:967
  47.2 0.7 collective-permute-start.7
  47.9 1.7 %columns.1 = (f32[5,1,1920]{2,1,0:T(1,128)}, f32[5,1,1920]{2,1,0:T(1,128)}, f32[300,128]{1,0:T(8,128)}, f32[300,128]{1,0:T(8,128)}) custom-call(f32[5,1920]{1,0:T(8,128)} %refs_0_.4, f32[5,1920]{1,0:T(8,128)} %refs_1_.5), custom_call_target="tpu_custom_call" | custom-call | tf_op jit(solution)/shard_map/columns/pallas_call | solution.py:967
  49.6 2.3 %step_load.1 = (f32[16,8,128]{2,1,0:T(8,128)S(1)}, f32[5,1,1920]{2,1,0:T(1,128)S(1)}, f32[5,4,8,1920]{3,2,1,0:T(8,128)S(1)}, f32[5,1,1920]{2,1,0:T(1,128)S(1)}, f32[5,4,8,1920]{3,2,1,0:T(8,128)S(1)}) custom-call(f32[16,8,128]{2,1,0:T(8,128)} %get-tuple-element.128.refs_0_, f32[5,1,1920]{2,1,0:T(1,128)} %get-tuple-element.130.refs_1_, ...), custom_call_target="tpu_custom_call" | custom-call | tf_op jit(solution)/shard_map/step_load/pallas_call | solution.py:967
  52.0 2.7 %step.3 = (f32[5,4,8,1920]{3,2,1,0:T(8,128)}, f32[5,4,8,1920]{3,2,1,0:T(8,128)}, f32[304,128]{1,0:T(8,128)}, f32[320,128]{1,0:T(8,128)}, f32[32,128]{1,0:T(8,128...) custom-call(s32[1,128]{1,0:T(1,128)} %get-tuple-element.105.refs_0_.refs_7_.refs_5_, ...), custom_call_target="tpu_custom_call" | custom-call | tf_op jit(solution)/shard_map/step/pallas_call | solution.py:967
  54.7 5.5 %all-to-all-start.2 = ((f32[16,5,4,128]{3,2,1,0:T(4,128)}), f32[16,5,4,128]{3,2,1,0:T(4,128)S(1)}, u32[]{:S(2)}, u32[]{:S(2)}) async-start(f32[16,5,4,128]{3,2,1,0:T(4,128)} %bitcast.63), calls=%async_computation.2 | async-start | bytes 327680 | tf_op jit(solution)/shard_map/all_to_all | solution.py:994
  60.2 0.4 collective-permute-start.8
  60.6 0.7 collective-permute-start.9
  61.3 0.4 collective-permute-done.8.refs_1_
  61.7 7.0 %all-to-all-done.2 = f32[16,5,4,128]{3,2,1,0:T(4,128)S(1)} async-done(((f32[16,5,4,128]{3,2,1,0:T(4,128)}), f32[16,5,4,128]{3,2,1,0:T(4,128)S(1)}, u32[]{:S(2)}, u32[]{:S(2)}) %all-to-all-start.2) | async-done | bytes 163872 | tf_op jit(solution)/shard_map/all_to_all | solution.py:994
  68.7 2.0 %owners.3 = (f32[512,128]{1,0:T(8,128)}, f32[4,80,128]{2,1,0:T(8,128)}, f32[4,80,128]{2,1,0:T(8,128)}) custom-call(f32[320,128]{1,0:T(8,128)S(1)} %bitcast.53, f32[80,80]{1,0:T(8,128)S(1)} %bitcast.47, f32[80,128]{1,0:T(8,128)S(1)} %get-tuple-element.212.refs_2_, f32[80,128]{1,0:T(8,128)S(1)} %get-tuple-element.205.refs_3_, ...), custom_call_target="tpu_custom_call" | custom-call | tf_op jit(solution)/shard_map/owners/pallas_call | solution.py:967
  70.6 13.5 %all_to_all.51 = f32[16,8,4,128]{3,2,1,0:T(4,128)S(1)} all-to-all(f32[16,8,4,128]{3,2,1,0:T(4,128)} %bitcast.61), channel_id=1, replica_groups=mesh['member'=2,'horiz'=16] {'horiz'}, dimensions={0} | all-to-all | bytes 524288 | tf_op jit(solution)/shard_map/all_to_all | solution.py:994
  84.2 2.3 %surface.3 = (f32[304,128]{1,0:T(8,128)}, f32[64,128]{1,0:T(8,128)}, f32[512,128]{1,0:T(8,128)}, f32[32,128]{1,0:T(8,128)}, f32[32,128]{1,0:T(8,128)}) custom-call(f32[512,128]{1,0:T(8,128)S(1)} %bitcast.45, f32[32,128]{1,0:T(8,128)S(1)} %collective-permute-done.8.refs_1_, f32[32,128]{1,0:T(8,128)S(1)} %collective-permute-done.9.refs_2_, ...), custom_call_target="tpu_custom_call" | custom-call | tf_op jit(solution)/shard_map/surface/pallas_call | solution.py:967
  86.5 3.7 %all-to-all-start.4 = ((f32[16,8,4,128]{3,2,1,0:T(4,128)}), f32[16,8,4,128]{3,2,1,0:T(4,128)S(1)}, u32[]{:S(2)}, u32[]{:S(2)}) async-start(f32[16,8,4,128]{3,2,1,0:T(4,128)} %bitcast.59), calls=%async_computation.4 | async-start | bytes 524288 | tf_op jit(solution)/shard_map/all_to_all | solution.py:994
  90.2 0.3 collective-permute-start.12
  90.5 0.7 collective-permute-start.13
  91.2 0.5 collective-permute-done.12.refs_1_
  91.7 8.5 %all-to-all-done.4 = f32[16,8,4,128]{3,2,1,0:T(4,128)S(1)} async-done(((f32[16,8,4,128]{3,2,1,0:T(4,128)}), f32[16,8,4,128]{3,2,1,0:T(4,128)S(1)}, u32[]{:S(2)}, u32[]{:S(2)}) %all-to-all-start.4) | async-done | bytes 262176 | tf_op jit(solution)/shard_map/all_to_all | solution.py:994
  100.2 2.0 %owners_back.2 = f32[320,128]{1,0:T(8,128)} custom-call(f32[512,128]{1,0:T(8,128)S(1)} %bitcast.42, f32[80,80]{1,0:T(8,128)S(1)} %bitcast.48, f32[4,80,128]{2,1,0:T(8,128)} %get-tuple-element.159.refs_2_, f32[4,80,128]{2,1,0:T(8,128)} %get-tuple-element.160.refs_3_, f32[8,128]{1,0:T(8,128)} %get-tuple-element.106.refs_1_.refs_7_.refs_4_.refs_8_.refs_6_), custom_call_target="tpu_custom_call" | custom-call | tf_op jit(solution)/shard_map/owners_back/pallas_call | solution.py:967
  102.3 3.5 %all-to-all-start.5 = ((f32[16,5,4,128]{3,2,1,0:T(4,128)}), f32[16,5,4,128]{3,2,1,0:T(4,128)S(1)}, u32[]{:S(2)}, u32[]{:S(2)}) async-start(f32[16,5,4,128]{3,2,1,0:T(4,128)} %bitcast.56), calls=%async_computation.5 | async-start | bytes 327680 | tf_op jit(solution)/shard_map/all_to_all | solution.py:994
  105.8 0.4 collective-permute-start.10
  106.2 0.7 collective-permute-start.11
  106.8 7.4 %all-to-all-done.5 = f32[16,5,4,128]{3,2,1,0:T(4,128)S(1)} async-done(((f32[16,5,4,128]{3,2,1,0:T(4,128)}), f32[16,5,4,128]{3,2,1,0:T(4,128)S(1)}, u32[]{:S(2)}, u32[]{:S(2)}) %all-to-all-start.5) | async-done | bytes 163872 | tf_op jit(solution)/shard_map/all_to_all | solution.py:994
  114.2 1.2 merge.2
  115.5 0.7 collective-permute-start.15
  116.2 2.0 %step_back_load.2 = (f32[16,8,128]{2,1,0:T(8,128)S(1)}, f32[5,1,1920]{2,1,0:T(1,128)S(1)}, f32[5,4,8,1920]{3,2,1,0:T(8,128)S(1)}, f32[5,4,8,1920]{3,2,1,0:T(8,128)S(1)}, f32[5,4,8,1920]{3,2,1,0:T(8,128)S(1)}) custom-call(f32[16,8,128]{2,1,0:T(8,128)} %get-tuple-element.128.refs_0_, f32[5,1,1920]{2,1,0:T(1,128)} %get-tuple-element.130.refs_1_, ...), custom_call_target="tpu_custom_call" | custom-call | tf_op jit(solution)/shard_map/step_back_load/pallas_call | solution.py:967
  118.2 2.7 %step_back.1 = (f32[5,4,8,1920]{3,2,1,0:T(8,128)}, f32[304,128]{1,0:T(8,128)}, f32[512,128]{1,0:T(8,128)}, f32[32,128]{1,0:T(8,128)}, f32[32,128]{1,0:T(8,128)}, /*index=5*/f32[480,128]{1,0:T(8,128)}, f32[480,128]{1,0:T(8,128)}) custom-call(s32[3,128]{1,0:T(4,128)} %get-tuple-element.117.refs_4_.refs_0_, f32[24,128]{1,0:T(8,128)} %get-tuple-element.118.refs_5_.refs_1_, ...), custom_call_target="tpu_custom_call" | custom-call | tf_op jit(solution)/shard_map/step_back/pallas_call | solution.py:967
  120.9 5.9 %all-to-all-start.6 = ((f32[16,8,4,128]{3,2,1,0:T(4,128)}), f32[16,8,4,128]{3,2,1,0:T(4,128)S(1)}, u32[]{:S(2)}, u32[]{:S(2)}) async-start(f32[16,8,4,128]{3,2,1,0:T(4,128)} %bitcast.58), calls=%async_computation.6 | async-start | bytes 524288 | tf_op jit(solution)/shard_map/all_to_all | solution.py:994
  126.8 0.8 collective-permute-start.16
  127.6 0.7 collective-permute-start.17
  128.2 0.4 collective-permute-done.16.refs_1_
  128.6 8.2 %all-to-all-done.6 = f32[16,8,4,128]{3,2,1,0:T(4,128)S(1)} async-done(((f32[16,8,4,128]{3,2,1,0:T(4,128)}), f32[16,8,4,128]{3,2,1,0:T(4,128)S(1)}, u32[]{:S(2)}, u32[]{:S(2)}) %all-to-all-start.6) | async-done | bytes 262176 | tf_op jit(solution)/shard_map/all_to_all | solution.py:994
  136.8 2.0 %owners_back.3 = f32[320,128]{1,0:T(8,128)} custom-call(f32[512,128]{1,0:T(8,128)S(1)} %bitcast.43, f32[80,80]{1,0:T(8,128)S(1)} %bitcast.49, f32[4,80,128]{2,1,0:T(8,128)} %get-tuple-element.181.refs_2_, f32[4,80,128]{2,1,0:T(8,128)} %get-tuple-element.182.refs_3_, f32[8,128]{1,0:T(8,128)} %get-tuple-element.106.refs_1_.refs_7_.refs_4_.refs_8_.refs_6_), custom_call_target="tpu_custom_call" | custom-call | tf_op jit(solution)/shard_map/owners_back/pallas_call | solution.py:967
  138.9 3.5 %all-to-all-start.7 = ((f32[16,5,4,128]{3,2,1,0:T(4,128)}), f32[16,5,4,128]{3,2,1,0:T(4,128)S(1)}, u32[]{:S(2)}, u32[]{:S(2)}) async-start(f32[16,5,4,128]{3,2,1,0:T(4,128)} %bitcast.57), calls=%async_computation.7 | async-start | bytes 327680 | tf_op jit(solution)/shard_map/all_to_all | solution.py:994
  142.4 0.4 collective-permute-start.18
  142.8 0.7 collective-permute-start.19
  143.5 7.4 %all-to-all-done.7 = f32[16,5,4,128]{3,2,1,0:T(4,128)S(1)} async-done(((f32[16,5,4,128]{3,2,1,0:T(4,128)}), f32[16,5,4,128]{3,2,1,0:T(4,128)S(1)}, u32[]{:S(2)}, u32[]{:S(2)}) %all-to-all-start.7) | async-done | bytes 163872 | tf_op jit(solution)/shard_map/all_to_all | solution.py:994
  150.9 1.2 merge.3
  152.1 0.7 collective-permute-start.21
  152.8 2.3 %relayout.1.refs_5_ = f32[5,4,8,1920]{3,2,1,0:T(8,128)} custom-call(f32[8,5,4,1920]{3,2,1,0:T(4,128)} %refs_1_.6), custom_call_target="tpu_custom_call" | custom-call | tf_op jit(solution)/shard_map/relayout/pallas_call | solution.py:967
  155.1 2.4 %step_back_load.3 = (f32[16,8,128]{2,1,0:T(8,128)S(1)}, f32[5,1,1920]{2,1,0:T(1,128)S(1)}, f32[5,4,8,1920]{3,2,1,0:T(8,128)S(1)}, f32[5,4,8,1920]{3,2,1,0:T(8,12...) custom-call(f32[16,8,128]{2,1,0:T(8,128)} %get-tuple-element.128.refs_0_, ...), custom_call_target="tpu_custom_call" | custom-call | tf_op jit(solution)/shard_map/step_back_load/pallas_call | solution.py:967
  157.5 2.5 %step_back_sums.1 = (f32[5,4,8,1920]{3,2,1,0:T(8,128)}, f32[16,128]{1,0:T(8,128)}) custom-call(f32[480,128]{1,0:T(8,128)S(1)} %collective-permute-done.18.refs_0_, f32[480,128]{1,0:T(8,128)S(1)} %collective-permute-done.19.refs_1_, f32[60,128]{1,0:T(8,128)S(1)} %collective-permute-done.20.refs_2_, f32[60,128]{1,0:T(8,128)S(1)} %collective-permute-done.21.refs_3_, ...), custom_call_target="tpu_custom_call" | custom-call | tf_op jit(solution)/shard_map/step_back_sums/pallas_call | solution.py:967
  160.0 4.9 %all-to-all-start.8 = ((f32[16,1,128]{2,1,0:T(1,128)}), f32[16,1,128]{2,1,0:T(1,128)S(1)}, u32[]{:S(2)}, u32[]{:S(2)}) async-start(f32[16,1,128]{2,1,0:T(1,128)} %bitcast.64), calls=%async_computation.8 | async-start | bytes 16384 | tf_op jit(solution)/shard_map/all_to_all | solution.py:1219
  164.9 1.7 copy.20
  166.6 4.7 %all-to-all-done.8 = f32[16,1,128]{2,1,0:T(1,128)S(1)} async-done(((f32[16,1,128]{2,1,0:T(1,128)}), f32[16,1,128]{2,1,0:T(1,128)S(1)}, u32[]{:S(2)}, u32[]{:S(2)}) %all-to-all-start.8) | async-done | bytes 8224 | tf_op jit(solution)/shard_map/all_to_all | solution.py:1219
  171.3 1.2 finish.1
  (62 shorter events, 0.5 us)
Async XLA Ops:
  0.0 2.8 %copy-start.5 = (f32[4,4]{1,0:T(4,128)S(1)}, f32[4,4]{1,0:T(4,128)}, u32[]{:S(2)}) copy-start(f32[4,4]{1,0:T(4,128)} %param.21) | copy-start | bytes 196
  0.0 2.9 %copy-start.6 = (s32[15]{0:T(128)S(1)}, s32[15]{0:T(128)}, u32[]{:S(2)}) copy-start(s32[15]{0:T(128)} %param.27) | copy-start | bytes 184
  0.0 2.9 %copy-start.7 = (s32[15]{0:T(128)S(1)}, s32[15]{0:T(128)}, u32[]{:S(2)}) copy-start(s32[15]{0:T(128)} %param.28) | copy-start | bytes 184
  0.0 3.0 %copy-start.14 = (f32[15]{0:T(128)S(1)}, f32[15]{0:T(128)}, u32[]{:S(2)}) copy-start(f32[15]{0:T(128)} %param.29) | copy-start | bytes 184
  1.6 5.3 %collective-permute-start = (f32[480,128]{1,0:T(8,128)S(1)}, f32[480,128]{1,0:T(8,128)S(1)}, u32[]{:S(2)}, u32[]{:S(2)}) collective-permute-start(f32[480,128]{1,0:T(8,128)S(1)} %get-tuple-element.107), channel_id=1, source_target_pairs={{0,1},{1,0},{2,3},{3,2},{4,5},{5,4},{6,7},{7,6},{8,9},{9,8},{10,11... | collective-permute-start | bytes 737288 | tf_op jit(solution)/shard_map/ppermute | solution.py:988
  2.2 4.8 %collective-permute-start.1 = (f32[480,128]{1,0:T(8,128)S(1)}, f32[480,128]{1,0:T(8,128)S(1)}, u32[]{:S(2)}, u32[]{:S(2)}) collective-permute-start(f32[480,128]{1,0:T(8,128)S(1)} %get-tuple-element.108), channel_id=1, source_target_pairs={{1,2},{3,4},{5,6},{7,8},{9,10},{11,12},{13,14},{2,1},{4,3},{6,5},{... | collective-permute-start | bytes 737288 | tf_op jit(solution)/shard_map/ppermute | solution.py:988
  3.0 2.0 %copy-start.15 = (s32[1,75]{1,0:T(1,128)S(1)}, s32[1,75]{1,0:T(1,128)}, u32[]{:S(2)}) copy-start(s32[1,75]{1,0:T(1,128)} %param.26) | copy-start | bytes 904
  3.0 2.1 %copy-start.16 = (s32[1,75]{1,0:T(1,128)S(1)}, s32[1,75]{1,0:T(1,128)}, u32[]{:S(2)}) copy-start(s32[1,75]{1,0:T(1,128)} %param.25) | copy-start | bytes 904
  3.0 2.2 %copy-start.2 = (f32[8,4,4]{0,2,1:T(4,128)S(1)}, f32[8,4,4]{0,2,1:T(4,128)}, u32[]{:S(2)}) copy-start(f32[8,4,4]{0,2,1:T(4,128)} %param.20) | copy-start | bytes 1540
  5.1 17.2 %copy-start.3 = (f32[2,1,80,128]{3,2,1,0:T(8,128)S(1)}, f32[2,1,80,128]{3,2,1,0:T(8,128)}, u32[]{:S(2)}) copy-start(f32[2,1,80,128]{3,2,1,0:T(8,128)} %param.24) | copy-start | bytes 245764
  5.1 17.2 %copy-start.4 = (f32[2,1,80,128]{3,2,1,0:T(8,128)S(1)}, f32[2,1,80,128]{3,2,1,0:T(8,128)}, u32[]{:S(2)}) copy-start(f32[2,1,80,128]{3,2,1,0:T(8,128)} %param.23) | copy-start | bytes 245764
  6.9 22.8 %copy-start.1 = (f32[1,80,80]{2,1,0:T(8,128)S(1)}, f32[1,80,80]{2,1,0:T(8,128)}, u32[]{:S(2)}) copy-start(f32[1,80,80]{2,1,0:T(8,128)} %param.22) | copy-start | bytes 76804
  9.6 25.6 %copy-start.12 = (f32[480,128]{1,0:T(8,128)S(1)}, f32[480,128]{1,0:T(8,128)}, u32[]{:S(2)}) copy-start(f32[480,128]{1,0:T(8,128)} %get-tuple-element.126) | copy-start | bytes 737284
  9.6 26.0 %copy-start.10 = (f32[480,128]{1,0:T(8,128)S(1)}, f32[480,128]{1,0:T(8,128)}, u32[]{:S(2)}) copy-start(f32[480,128]{1,0:T(8,128)} %get-tuple-element.127) | copy-start | bytes 737284
  9.6 20.1 %all-to-all-start = ((f32[16,5,4,128]{3,2,1,0:T(4,128)}), f32[16,5,4,128]{3,2,1,0:T(4,128)S(1)}, u32[]{:S(2)}, u32[]{:S(2)}) async-start(f32[16,5,4,128]{3,2,1,0:T(4,128)} %bitcast.62), calls=%async_computation | async-start | bytes 327680 | tf_op jit(solution)/shard_map/all_to_all | solution.py:994
  21.2 1.5 collective-permute-start.2
  21.6 1.1 collective-permute-start.3
  31.7 13.6 %all-to-all-start.1 = ((f32[16,8,4,128]{3,2,1,0:T(4,128)}), f32[16,8,4,128]{3,2,1,0:T(4,128)S(1)}, u32[]{:S(2)}, u32[]{:S(2)}) async-start(f32[16,8,4,128]{3,2,1,0:T(4,128)} %bitcast.60), calls=%async_computation.1 | async-start | bytes 524288 | tf_op jit(solution)/shard_map/all_to_all | solution.py:994
  35.2 16.7 %collective-permute-start.4 = (f32[480,128]{1,0:T(8,128)S(1)}, f32[480,128]{1,0:T(8,128)S(1)}, u32[]{:S(2)}, u32[]{:S(2)}) collective-permute-start(f32[480,128]{1,0:T(8,128)S(1)} %copy-done.12), channel_id=1, source_target_pairs={{0,1},{1,0},{2,3},{3,2},{4,5},{5,4},{6,7},{7,6},{8,9},{9,8},{10,11... | collective-permute-start | bytes 737288 | tf_op jit(solution)/shard_map/ppermute | solution.py:988
  35.6 16.4 %collective-permute-start.5 = (f32[480,128]{1,0:T(8,128)S(1)}, f32[480,128]{1,0:T(8,128)S(1)}, u32[]{:S(2)}, u32[]{:S(2)}) collective-permute-start(f32[480,128]{1,0:T(8,128)S(1)} %copy-done.10), channel_id=1, source_target_pairs={{1,2},{3,4},{5,6},{7,8},{9,10},{11,12},{13,14},{2,1},{4,3},{6,5},{... | collective-permute-start | bytes 737288 | tf_op jit(solution)/shard_map/ppermute | solution.py:988
  47.1 4.9 %collective-permute-start.6 = (f32[60,128]{1,0:T(8,128)S(1)}, f32[60,128]{1,0:T(8,128)S(1)}, u32[]{:S(2)}, u32[]{:S(2)}) collective-permute-start(f32[60,128]{1,0:T(8,128)S(1)} %get-tuple-element.137), channel_id=1, source_target_pairs={{0,1},{1,0},{2,3},{3,2},{4,5},{5,4},{6,7},{7,6},{8,9},{9,8},{10,11... | collective-permute-start | bytes 92168 | tf_op jit(solution)/shard_map/ppermute | solution.py:988
  47.2 4.8 %collective-permute-start.7 = (f32[60,128]{1,0:T(8,128)S(1)}, f32[60,128]{1,0:T(8,128)S(1)}, u32[]{:S(2)}, u32[]{:S(2)}) collective-permute-start(f32[60,128]{1,0:T(8,128)S(1)} %get-tuple-element.138), channel_id=1, source_target_pairs={{1,2},{3,4},{5,6},{7,8},{9,10},{11,12},{13,14},{2,1},{4,3},{6,5},{... | collective-permute-start | bytes 92168 | tf_op jit(solution)/shard_map/ppermute | solution.py:988
  54.7 14.0 %all-to-all-start.2 = ((f32[16,5,4,128]{3,2,1,0:T(4,128)}), f32[16,5,4,128]{3,2,1,0:T(4,128)S(1)}, u32[]{:S(2)}, u32[]{:S(2)}) async-start(f32[16,5,4,128]{3,2,1,0:T(4,128)} %bitcast.63), calls=%async_computation.2 | async-start | bytes 327680 | tf_op jit(solution)/shard_map/all_to_all | solution.py:994
  60.2 1.5 collective-permute-start.8
  60.6 1.1 collective-permute-start.9
  86.5 19.3 %copy-start.9 = (f32[480,128]{1,0:T(8,128)S(1)}, f32[480,128]{1,0:T(8,128)}, u32[]{:S(2)}) copy-start(f32[480,128]{1,0:T(8,128)} %get-tuple-element.148) | copy-start | bytes 737284
  86.5 19.6 %copy-start.8 = (f32[480,128]{1,0:T(8,128)S(1)}, f32[480,128]{1,0:T(8,128)}, u32[]{:S(2)}) copy-start(f32[480,128]{1,0:T(8,128)} %get-tuple-element.149) | copy-start | bytes 737284
  86.5 13.7 %all-to-all-start.4 = ((f32[16,8,4,128]{3,2,1,0:T(4,128)}), f32[16,8,4,128]{3,2,1,0:T(4,128)S(1)}, u32[]{:S(2)}, u32[]{:S(2)}) async-start(f32[16,8,4,128]{3,2,1,0:T(4,128)} %bitcast.59), calls=%async_computation.4 | async-start | bytes 524288 | tf_op jit(solution)/shard_map/all_to_all | solution.py:994
  90.2 1.5 collective-permute-start.12
  90.5 1.2 collective-permute-start.13
  102.3 12.0 %all-to-all-start.5 = ((f32[16,5,4,128]{3,2,1,0:T(4,128)}), f32[16,5,4,128]{3,2,1,0:T(4,128)S(1)}, u32[]{:S(2)}, u32[]{:S(2)}) async-start(f32[16,5,4,128]{3,2,1,0:T(4,128)} %bitcast.56), calls=%async_computation.5 | async-start | bytes 327680 | tf_op jit(solution)/shard_map/all_to_all | solution.py:994
  105.8 12.4 %collective-permute-start.10 = (f32[480,128]{1,0:T(8,128)S(1)}, f32[480,128]{1,0:T(8,128)S(1)}, u32[]{:S(2)}, u32[]{:S(2)}) collective-permute-start(f32[480,128]{1,0:T(8,128)S(1)} %copy-done.9), channel_id=1, source_target_pairs={{0,1},{1,0},{2,3},{3,2},{4,5},{5,4},{6,7},{7,6},{8,9},{9,8},{10,11... | collective-permute-start | bytes 737288 | tf_op jit(solution)/shard_map/ppermute | solution.py:988
  106.2 12.0 %collective-permute-start.11 = (f32[480,128]{1,0:T(8,128)S(1)}, f32[480,128]{1,0:T(8,128)S(1)}, u32[]{:S(2)}, u32[]{:S(2)}) collective-permute-start(f32[480,128]{1,0:T(8,128)S(1)} %copy-done.8), channel_id=1, source_target_pairs={{1,2},{3,4},{5,6},{7,8},{9,10},{11,12},{13,14},{2,1},{4,3},{6,5},{... | collective-permute-start | bytes 737288 | tf_op jit(solution)/shard_map/ppermute | solution.py:988
  115.4 2.8 %collective-permute-start.14 = (f32[60,128]{1,0:T(8,128)S(1)}, f32[60,128]{1,0:T(8,128)S(1)}, u32[]{:S(2)}, u32[]{:S(2)}) collective-permute-start(f32[60,128]{1,0:T(8,128)S(1)} %get-tuple-element.167), channel_id=1, source_target_pairs={{0,1},{1,0},{2,3},{3,2},{4,5},{5,4},{6,7},{7,6},{8,9},{9,8},{10,11... | collective-permute-start | bytes 92168 | tf_op jit(solution)/shard_map/ppermute | solution.py:988
  115.5 2.7 %collective-permute-start.15 = (f32[60,128]{1,0:T(8,128)S(1)}, f32[60,128]{1,0:T(8,128)S(1)}, u32[]{:S(2)}, u32[]{:S(2)}) collective-permute-start(f32[60,128]{1,0:T(8,128)S(1)} %get-tuple-element.168), channel_id=1, source_target_pairs={{1,2},{3,4},{5,6},{7,8},{9,10},{11,12},{13,14},{2,1},{4,3},{6,5},{... | collective-permute-start | bytes 92168 | tf_op jit(solution)/shard_map/ppermute | solution.py:988
  120.9 21.5 %copy-start.13 = (f32[480,128]{1,0:T(8,128)S(1)}, f32[480,128]{1,0:T(8,128)}, u32[]{:S(2)}) copy-start(f32[480,128]{1,0:T(8,128)} %get-tuple-element.185) | copy-start | bytes 737284
  120.9 21.9 %copy-start.11 = (f32[480,128]{1,0:T(8,128)S(1)}, f32[480,128]{1,0:T(8,128)}, u32[]{:S(2)}) copy-start(f32[480,128]{1,0:T(8,128)} %get-tuple-element.186) | copy-start | bytes 737284
  120.9 15.9 %all-to-all-start.6 = ((f32[16,8,4,128]{3,2,1,0:T(4,128)}), f32[16,8,4,128]{3,2,1,0:T(4,128)S(1)}, u32[]{:S(2)}, u32[]{:S(2)}) async-start(f32[16,8,4,128]{3,2,1,0:T(4,128)} %bitcast.58), calls=%async_computation.6 | async-start | bytes 524288 | tf_op jit(solution)/shard_map/all_to_all | solution.py:994
  126.8 1.8 %collective-permute-start.16 = (f32[32,128]{1,0:T(8,128)}, f32[32,128]{1,0:T(8,128)S(1)}, u32[]{:S(2)}, u32[]{:S(2)}) collective-permute-start(f32[32,128]{1,0:T(8,128)} %get-tuple-element.178), channel_id=1, source_target_pairs={{0,1},{1,0},{2,3},{3,2},{4,5},{5,4},{6,7},{7,6},{8,9},{9,8},{10,11... | collective-permute-start | bytes 49160 | tf_op jit(solution)/shard_map/ppermute | solution.py:988
  127.6 1.1 collective-permute-start.17
  138.9 12.0 %all-to-all-start.7 = ((f32[16,5,4,128]{3,2,1,0:T(4,128)}), f32[16,5,4,128]{3,2,1,0:T(4,128)S(1)}, u32[]{:S(2)}, u32[]{:S(2)}) async-start(f32[16,5,4,128]{3,2,1,0:T(4,128)} %bitcast.57), calls=%async_computation.7 | async-start | bytes 327680 | tf_op jit(solution)/shard_map/all_to_all | solution.py:994
  142.4 15.0 %collective-permute-start.18 = (f32[480,128]{1,0:T(8,128)S(1)}, f32[480,128]{1,0:T(8,128)S(1)}, u32[]{:S(2)}, u32[]{:S(2)}) collective-permute-start(f32[480,128]{1,0:T(8,128)S(1)} %copy-done.13), channel_id=1, source_target_pairs={{0,1},{1,0},{2,3},{3,2},{4,5},{5,4},{6,7},{7,6},{8,9},{9,8},{10,11... | collective-permute-start | bytes 737288 | tf_op jit(solution)/shard_map/ppermute | solution.py:988
  142.8 14.7 %collective-permute-start.19 = (f32[480,128]{1,0:T(8,128)S(1)}, f32[480,128]{1,0:T(8,128)S(1)}, u32[]{:S(2)}, u32[]{:S(2)}) collective-permute-start(f32[480,128]{1,0:T(8,128)S(1)} %copy-done.11), channel_id=1, source_target_pairs={{1,2},{3,4},{5,6},{7,8},{9,10},{11,12},{13,14},{2,1},{4,3},{6,5},{... | collective-permute-start | bytes 737288 | tf_op jit(solution)/shard_map/ppermute | solution.py:988
  152.1 5.4 %collective-permute-start.20 = (f32[60,128]{1,0:T(8,128)S(1)}, f32[60,128]{1,0:T(8,128)S(1)}, u32[]{:S(2)}, u32[]{:S(2)}) collective-permute-start(f32[60,128]{1,0:T(8,128)S(1)} %get-tuple-element.191), channel_id=1, source_target_pairs={{0,1},{1,0},{2,3},{3,2},{4,5},{5,4},{6,7},{7,6},{8,9},{9,8},{10,11... | collective-permute-start | bytes 92168 | tf_op jit(solution)/shard_map/ppermute | solution.py:988
  152.1 5.4 %collective-permute-start.21 = (f32[60,128]{1,0:T(8,128)S(1)}, f32[60,128]{1,0:T(8,128)S(1)}, u32[]{:S(2)}, u32[]{:S(2)}) collective-permute-start(f32[60,128]{1,0:T(8,128)S(1)} %get-tuple-element.192), channel_id=1, source_target_pairs={{1,2},{3,4},{5,6},{7,8},{9,10},{11,12},{13,14},{2,1},{4,3},{6,5},{... | collective-permute-start | bytes 92168 | tf_op jit(solution)/shard_map/ppermute | solution.py:988
  160.0 11.3 %all-to-all-start.8 = ((f32[16,1,128]{2,1,0:T(1,128)}), f32[16,1,128]{2,1,0:T(1,128)S(1)}, u32[]{:S(2)}, u32[]{:S(2)}) async-start(f32[16,1,128]{2,1,0:T(1,128)} %bitcast.64), calls=%async_computation.8 | async-start | bytes 16384 | tf_op jit(solution)/shard_map/all_to_all | solution.py:1219
  164.9 6.4 %copy-start = (f32[8,5,4,1920]{3,2,1,0:T(4,128)S(1)}, f32[8,5,4,1920]{3,2,1,0:T(4,128)}, u32[]{:S(2)}) copy-start(f32[8,5,4,1920]{3,2,1,0:T(4,128)} %refs_1_.6) | copy-start | bytes 3686404

commit v4 on v3

--- a/solution.py
+++ b/solution.py
@@ -361,7 +361,7 @@
         copies = [pltpu.make_async_copy(field.at[row], field_out.at[row], in_sems.at[0, row])]
         if last:
             copies.append(
-                pltpu.make_async_copy(target.at[:, row], refs[1].at[row], in_sems.at[1, row])
+                pltpu.make_async_copy(target.at[row], target_out.at[row], in_sems.at[1, row])
             )
         return copies
 
@@ -378,10 +378,6 @@
         for arrival in arrivals(row):
             arrival.wait()
         load_surface_row(sz, field_out, row, surface, row * sz.row_width)
-        if last:
-            for c in range(CHANNELS):
-                for t in range(sz.row_tiles):
-                    target_out[row, c, :, cols(t)] = gather_levels(refs[1].at[row], c, t)
         return carry
 
     lax.fori_loop(0, sz.rows, one_row, 0)
@@ -495,8 +491,8 @@
         told_first, told_second, own_table, own_facts, tables, weights = refs[:6]
         refs = refs[6:]
     flux, mixed_slope, flux_slope, flat, first = refs
-    arrive_all(arrive)
     if decode:
+        arrive_all(arrive)
         lines = sz.slot_lines
         tables[0:lines, :] = own_table[...]
         weights[0 : sz.facts, :] = own_facts[...]
@@ -527,6 +523,8 @@
         mixed_slope[c] = 1.0 - mixed_here * mixed_here
         contrast.append((air[...] - values[0] if c == 0 else values[c]) + mixed_here)
     mixed_slope.start()
+    if not decode:
+        arrive_all(arrive)
     rate = FLUX_RATE * wind[...]
     for c in range(CHANNELS):
         forcing = bulk(c, 0) * contrast[0]
@@ -1068,6 +1066,15 @@
         scratch=[by_row, by_row, row_sems(2)],
     )
 
+    def relayout(array):
+        return call(
+            functools.partial(relayout_kernel, sz),
+            "relayout",
+            far_off(array),
+            shipped=[sz.whole],
+            scratch=[by_row, row_sems(1)],
+        )
+
     saved = []
     near = [sz.near, sz.near]
     mix_shape = (CHANNELS * CHANNELS, LEVELS, WIDTH)
@@ -1080,13 +1087,13 @@
             assert not last
         else:
             loads = fetched(mix, diffusivity_rows, *([weight_rows] if last else []))
-            loads += far_off(field) + near_by(surface) + (far_off(target_state) if last else [])
+            loads += far_off(field) + near_by(surface) + (far_off(target) if last else [])
             mix_here, rows_here, field, *more = call(
                 functools.partial(forward_load_kernel, sz, last),
                 "step_load",
                 loads,
                 kept=[mix_shape, row_lines, sz.whole] + ([row_lines, sz.whole] if last else []),
-                scratch=[row_sems(2)] + ([by_row] if last else []),
+                scratch=[row_sems(2)],
             )
             inputs += near_by(*edges, rows_here, mix_here, field, *surface_edges, *more)
         field, drive, surface, packed, *sends = call(
@@ -1120,14 +1127,24 @@
             tables, weights = decoded
         flux, *sends = lax.optimization_barrier((flux, *sends[2:]))
         if first:
-            flux, diffusivity = lax.optimization_barrier((flux, diffusivity))
-            diffusivity_rows, weight_rows, diffusivity_tiles, weight_tiles = call(
+            flux, diffusivity, target_state = lax.optimization_barrier(
+                (flux, diffusivity, target_state)
+            )
+            beside = call(
                 functools.partial(columns_kernel, sz),
                 "columns",
                 fetched(diffusivity, cost_weight),
                 shipped=[row_lines, row_lines, tiles_lines, tiles_lines],
-            )
+            ) + relayout(target_state)
+        else:
+            flux, perturbation = lax.optimization_barrier((flux, perturbation))
+            beside = relayout(perturbation)
         flux = exchange(flux, devices)
+        flux, *beside = lax.optimization_barrier((flux, *beside))
+        if first:
+            diffusivity_rows, weight_rows, diffusivity_tiles, weight_tiles, target = beside
+        else:
+            start_field = beside[0]
         edges = swap(*sends)
         inputs = near_by(flux, *got) + fetched(surface) + scalars(tables, weights)
         if last:
@@ -1166,15 +1183,6 @@
         if edge_sends is not None:
             back, *edge_sends = lax.optimization_barrier((back, *edge_sends))
             edges = swap(*edge_sends)
-        else:
-            back, perturbation = lax.optimization_barrier((back, perturbation))
-            start_field = call(
-                functools.partial(relayout_kernel, sz),
-                "relayout",
-                far_off(perturbation),
-                shipped=[sz.whole],
-                scratch=[by_row, row_sems(1)],
-            )[0]
         back = exchange(back, devices)
         surface, *row_sends = call(
             functools.partial(merge_kernel, sz),

time: 174 us -> 171 us (0.983)
  blocking collectives: 13.5 us -> 0 us
  starting transfers between devices: 53.1 us -> 57.8 us
  waiting for transfers between devices: 60.9 us -> 64.5 us
    all_to_all x1 -> x0, blocking collectives: 13.5 us -> none  [exchange(): lax.all_to_all(split, 'horiz', split_axis=0, concat_axis=0, tiled=True)]
    all_to_all x7 -> x8, starting transfers between devices: 37.2 us -> 41.5 us  [exchange(): lax.all_to_all(split, 'horiz', split_axis=0, concat_axis=0, tiled=True)]
    all_to_all x7 -> x8, waiting for transfers between devices: 54.5 us -> 58.2 us  [exchange(): lax.all_to_all(split, 'horiz', split_axis=0, concat_axis=0, tiled=True)]
    pallas_call x21 -> x22, Pallas kernels: 42.3 us -> 43.9 us  [call(): pl.pallas_call(run, name=name, in_specs=[pl.BlockSpec(memory_space=item.s...]
  transfers between devices with their start and end apart: 30 -> 31, of which waited for: 12 -> 13; matrix products, arithmetic and copies ran while one was open for 1% -> 1% of each run, Pallas kernels for 11% -> 12%
where the time goes in v4:
time: 171 us; the launch traced here: 169 us
  waiting for transfers between devices  64.5 us (38%)
  starting transfers between devices  57.8 us (34%)
  Pallas kernels  43.9 us (26%)
  local copies, waits for them, and re-layouts  1.88 us (1%)
    all_to_all x8, waiting for transfers between devices, exchange(): lax.all_to_all(split, 'horiz', split_axis=0, concat_axis=0, tiled=True)  58.2 us
    pallas_call x22, Pallas kernels, call(): pl.pallas_call(run, name=name, in_specs=[pl.BlockSpec(memory_space=item.s...  43.9 us
    all_to_all x8, starting transfers between devices, exchange(): lax.all_to_all(split, 'horiz', split_axis=0, concat_axis=0, tiled=True)  41.5 us
    ppermute x11, starting transfers between devices, swap(): lax.ppermute(second, 'horiz', outer)  7.25 us
    all_to_all x1, starting transfers between devices, body(): lax.all_to_all(sums, 'horiz', split_axis=0, concat_axis=0, tiled=True)  5.36 us
    all_to_all x1, waiting for transfers between devices, body(): lax.all_to_all(sums, 'horiz', split_axis=0, concat_axis=0, tiled=True)  4.68 us
    ppermute x11, starting transfers between devices, swap(): lax.ppermute(first, 'horiz', inner)  3.7 us
  transfers between devices with their start and end apart: 31, of which 13 were waited for; matrix products, arithmetic and copies ran while one was open for 1% of the time, Pallas kernels for 12%

profile of v4, /device:TPU:0, one launch (start us, length us, event | category | flops | bytes accessed | tf_op | source)
XLA Modules:
  0.0 169.1 jit_solution(12198495465069477105)
XLA Ops:
  0.0 1.6 edges.1
  1.6 0.5 collective-permute-start
  2.2 0.7 collective-permute-start.1
  3.1 2.0 %load.1.refs_6_ = f32[5,4,8,1920]{3,2,1,0:T(8,128)S(1)} custom-call(f32[8,5,4,1920]{3,2,1,0:T(4,128)} %refs_1_.6, f32[8,5,4,1920]{3,2,1,0:T(4,128)} %refs_1_.4), custom_call_target="tpu_custom_call" | custom-call | tf_op jit(solution)/shard_map/load/pallas_call | solution.py:965
  5.2 1.7 setup.1
  6.9 2.6 %step.2 = (f32[5,4,8,1920]{3,2,1,0:T(8,128)}, f32[5,4,8,1920]{3,2,1,0:T(8,128)}, f32[304,128]{1,0:T(8,128)}, f32[320,128]{1,0:T(8,128)}, f32[40,128]{1,0:T(8,128...) custom-call(s32[1,128]{1,0:T(1,128)} %get-tuple-element.114.refs_0_.refs_7_.refs_5_, ...), custom_call_target="tpu_custom_call" | custom-call | tf_op jit(solution)/shard_map/step/pallas_call | solution.py:965
  9.6 11.6 %all-to-all-start = ((f32[16,5,4,128]{3,2,1,0:T(4,128)}), f32[16,5,4,128]{3,2,1,0:T(4,128)S(1)}, u32[]{:S(2)}, u32[]{:S(2)}) async-start(f32[16,5,4,128]{3,2,1,0:T(4,128)} %bitcast.62), calls=%async_computation | async-start | bytes 327680 | tf_op jit(solution)/shard_map/all_to_all | solution.py:992
  21.2 0.4 collective-permute-start.2
  21.6 0.7 collective-permute-start.3
  22.3 0.4 collective-permute-done.2.refs_5_.refs_1_
  22.7 7.0 %all-to-all-done = f32[16,5,4,128]{3,2,1,0:T(4,128)S(1)} async-done(((f32[16,5,4,128]{3,2,1,0:T(4,128)}), f32[16,5,4,128]{3,2,1,0:T(4,128)S(1)}, u32[]{:S(2)}, u32[]{:S(2)}) %all-to-all-start) | async-done | bytes 163872 | tf_op jit(solution)/shard_map/all_to_all | solution.py:992
  29.7 2.0 %owners.2 = (s32[3,128]{1,0:T(4,128)}, f32[24,128]{1,0:T(8,128)}, f32[512,128]{1,0:T(8,128)}, f32[4,80,128]{2,1,0:T(8,128)}, f32[4,80,128]{2,1,0:T(8,128)}) custom-call(f32[320,128]{1,0:T(8,128)S(1)} %bitcast.52, f32[80,80]{1,0:T(8,128)S(1)} %bitcast.46, f32[80,128]{1,0:T(8,128)S(1)} %get-tuple-element.229.refs_2_, ...), custom_call_target="tpu_custom_call" | custom-call | tf_op jit(solution)/shard_map/owners/pallas_call | solution.py:965
  31.7 3.5 %all-to-all-start.1 = ((f32[16,8,4,128]{3,2,1,0:T(4,128)}), f32[16,8,4,128]{3,2,1,0:T(4,128)S(1)}, u32[]{:S(2)}, u32[]{:S(2)}) async-start(f32[16,8,4,128]{3,2,1,0:T(4,128)} %bitcast.60), calls=%async_computation.1 | async-start | bytes 524288 | tf_op jit(solution)/shard_map/all_to_all | solution.py:992
  35.2 0.4 collective-permute-start.4
  35.6 0.7 collective-permute-start.5
  36.3 2.3 %relayout.2.refs_5_ = f32[5,4,8,1920]{3,2,1,0:T(8,128)} custom-call(f32[8,5,4,1920]{3,2,1,0:T(4,128)} %refs_6_), custom_call_target="tpu_custom_call" | custom-call | tf_op jit(solution)/shard_map/relayout/pallas_call | solution.py:965
  38.6 1.7 %columns.1 = (f32[5,1,1920]{2,1,0:T(1,128)}, f32[5,1,1920]{2,1,0:T(1,128)}, f32[300,128]{1,0:T(8,128)}, f32[300,128]{1,0:T(8,128)}) custom-call(f32[5,1920]{1,0:T(8,128)} %refs_0_.4, f32[5,1920]{1,0:T(8,128)} %refs_1_.5), custom_call_target="tpu_custom_call" | custom-call | tf_op jit(solution)/shard_map/columns/pallas_call | solution.py:965
  40.3 4.9 %all-to-all-done.1 = f32[16,8,4,128]{3,2,1,0:T(4,128)S(1)} async-done(((f32[16,8,4,128]{3,2,1,0:T(4,128)}), f32[16,8,4,128]{3,2,1,0:T(4,128)S(1)}, u32[]{:S(2)}, u32[]{:S(2)}) %all-to-all-start.1) | async-done | bytes 262176 | tf_op jit(solution)/shard_map/all_to_all | solution.py:992
  45.2 1.9 %surface.2 = (f32[304,128]{1,0:T(8,128)S(1)}, f32[60,128]{1,0:T(8,128)S(1)}, f32[60,128]{1,0:T(8,128)S(1)}, f32[64,128]{1,0:T(8,128)}) custom-call(f32[512,128]{1,0:T(8,128)S(1)} %bitcast.44, f32[40,128]{1,0:T(8,128)S(1)} %collective-permute-done.2.refs_5_.refs_1_, f32[40,128]{1,0:T(8,128)S(1)} %collective-permute-done.3.refs_6_.refs_2_, ...), custom_call_target="tpu_custom_call" | custom-call | tf_op jit(solution)/shard_map/surface/pallas_call | solution.py:965
  47.2 0.7 collective-permute-start.7
  47.9 1.9 %step_load.1 = (f32[16,8,128]{2,1,0:T(8,128)S(1)}, f32[5,1,1920]{2,1,0:T(1,128)S(1)}, f32[5,4,8,1920]{3,2,1,0:T(8,128)S(1)}, f32[5,1,1920]{2,1,0:T(1,128)S(1)}, f32[5,4,8,1920]{3,2,1,0:T(8,128)S(1)}) custom-call(f32[16,8,128]{2,1,0:T(8,128)} %get-tuple-element.144.refs_0_, f32[5,1,1920]{2,1,0:T(1,128)} %get-tuple-element.145.refs_1_, ...), custom_call_target="tpu_custom_call" | custom-call | tf_op jit(solution)/shard_map/step_load/pallas_call | solution.py:965
  49.8 2.8 %step.3 = (f32[5,4,8,1920]{3,2,1,0:T(8,128)}, f32[5,4,8,1920]{3,2,1,0:T(8,128)}, f32[304,128]{1,0:T(8,128)}, f32[320,128]{1,0:T(8,128)}, f32[32,128]{1,0:T(8,128...) custom-call(s32[1,128]{1,0:T(1,128)} %get-tuple-element.114.refs_0_.refs_7_.refs_5_, ...), custom_call_target="tpu_custom_call" | custom-call | tf_op jit(solution)/shard_map/step/pallas_call | solution.py:965
  52.6 6.3 %all-to-all-start.2 = ((f32[16,5,4,128]{3,2,1,0:T(4,128)}), f32[16,5,4,128]{3,2,1,0:T(4,128)S(1)}, u32[]{:S(2)}, u32[]{:S(2)}) async-start(f32[16,5,4,128]{3,2,1,0:T(4,128)} %bitcast.63), calls=%async_computation.2 | async-start | bytes 327680 | tf_op jit(solution)/shard_map/all_to_all | solution.py:992
  58.9 0.4 collective-permute-start.8
  59.3 0.7 collective-permute-start.9
  60.0 0.4 collective-permute-done.8.refs_1_
  60.4 7.0 %all-to-all-done.2 = f32[16,5,4,128]{3,2,1,0:T(4,128)S(1)} async-done(((f32[16,5,4,128]{3,2,1,0:T(4,128)}), f32[16,5,4,128]{3,2,1,0:T(4,128)S(1)}, u32[]{:S(2)}, u32[]{:S(2)}) %all-to-all-start.2) | async-done | bytes 163872 | tf_op jit(solution)/shard_map/all_to_all | solution.py:992
  67.4 1.7 owners.3
  69.0 3.5 %all-to-all-start.3 = ((f32[16,8,4,128]{3,2,1,0:T(4,128)}), f32[16,8,4,128]{3,2,1,0:T(4,128)S(1)}, u32[]{:S(2)}, u32[]{:S(2)}) async-start(f32[16,8,4,128]{3,2,1,0:T(4,128)} %bitcast.61), calls=%async_computation.3 | async-start | bytes 524288 | tf_op jit(solution)/shard_map/all_to_all | solution.py:992
  72.6 2.3 %relayout.3.refs_5_ = f32[5,4,8,1920]{3,2,1,0:T(8,128)} custom-call(f32[8,5,4,1920]{3,2,1,0:T(4,128)} %refs_1_.6), custom_call_target="tpu_custom_call" | custom-call | tf_op jit(solution)/shard_map/relayout/pallas_call | solution.py:965
  74.9 7.7 %all-to-all-done.3 = f32[16,8,4,128]{3,2,1,0:T(4,128)S(1)} async-done(((f32[16,8,4,128]{3,2,1,0:T(4,128)}), f32[16,8,4,128]{3,2,1,0:T(4,128)S(1)}, u32[]{:S(2)}, u32[]{:S(2)}) %all-to-all-start.3) | async-done | bytes 262176 | tf_op jit(solution)/shard_map/all_to_all | solution.py:992
  82.6 2.3 %surface.3 = (f32[304,128]{1,0:T(8,128)}, f32[64,128]{1,0:T(8,128)}, f32[512,128]{1,0:T(8,128)}, f32[32,128]{1,0:T(8,128)}, f32[32,128]{1,0:T(8,128)}) custom-call(f32[512,128]{1,0:T(8,128)S(1)} %bitcast.45, f32[32,128]{1,0:T(8,128)S(1)} %collective-permute-done.8.refs_1_, f32[32,128]{1,0:T(8,128)S(1)} %collective-permute-done.9.refs_2_, ...), custom_call_target="tpu_custom_call" | custom-call | tf_op jit(solution)/shard_map/surface/pallas_call | solution.py:965
  84.9 3.7 %all-to-all-start.4 = ((f32[16,8,4,128]{3,2,1,0:T(4,128)}), f32[16,8,4,128]{3,2,1,0:T(4,128)S(1)}, u32[]{:S(2)}, u32[]{:S(2)}) async-start(f32[16,8,4,128]{3,2,1,0:T(4,128)} %bitcast.59), calls=%async_computation.4 | async-start | bytes 524288 | tf_op jit(solution)/shard_map/all_to_all | solution.py:992
  88.6 0.3 collective-permute-start.12
  88.9 0.7 collective-permute-start.13
  89.6 0.5 collective-permute-done.12.refs_1_
  90.1 8.5 %all-to-all-done.4 = f32[16,8,4,128]{3,2,1,0:T(4,128)S(1)} async-done(((f32[16,8,4,128]{3,2,1,0:T(4,128)}), f32[16,8,4,128]{3,2,1,0:T(4,128)S(1)}, u32[]{:S(2)}, u32[]{:S(2)}) %all-to-all-start.4) | async-done | bytes 262176 | tf_op jit(solution)/shard_map/all_to_all | solution.py:992
  98.6 2.1 %owners_back.2 = f32[320,128]{1,0:T(8,128)} custom-call(f32[512,128]{1,0:T(8,128)S(1)} %bitcast.42, f32[80,80]{1,0:T(8,128)S(1)} %bitcast.48, f32[4,80,128]{2,1,0:T(8,128)} %get-tuple-element.178.refs_2_, f32[4,80,128]{2,1,0:T(8,128)} %get-tuple-element.179.refs_3_, f32[8,128]{1,0:T(8,128)} %get-tuple-element.115.refs_1_.refs_7_.refs_4_.refs_8_.refs_6_), custom_call_target="tpu_custom_call" | custom-call | tf_op jit(solution)/shard_map/owners_back/pallas_call | solution.py:965
  100.7 3.5 %all-to-all-start.5 = ((f32[16,5,4,128]{3,2,1,0:T(4,128)}), f32[16,5,4,128]{3,2,1,0:T(4,128)S(1)}, u32[]{:S(2)}, u32[]{:S(2)}) async-start(f32[16,5,4,128]{3,2,1,0:T(4,128)} %bitcast.56), calls=%async_computation.5 | async-start | bytes 327680 | tf_op jit(solution)/shard_map/all_to_all | solution.py:992
  104.2 0.4 collective-permute-start.10
  104.6 0.7 collective-permute-start.11
  105.3 7.4 %all-to-all-done.5 = f32[16,5,4,128]{3,2,1,0:T(4,128)S(1)} async-done(((f32[16,5,4,128]{3,2,1,0:T(4,128)}), f32[16,5,4,128]{3,2,1,0:T(4,128)S(1)}, u32[]{:S(2)}, u32[]{:S(2)}) %all-to-all-start.5) | async-done | bytes 163872 | tf_op jit(solution)/shard_map/all_to_all | solution.py:992
  112.7 1.2 merge.2
  113.9 0.7 collective-permute-start.15
  114.6 2.0 %step_back_load.2 = (f32[16,8,128]{2,1,0:T(8,128)S(1)}, f32[5,1,1920]{2,1,0:T(1,128)S(1)}, f32[5,4,8,1920]{3,2,1,0:T(8,128)S(1)}, f32[5,4,8,1920]{3,2,1,0:T(8,128)S(1)}, f32[5,4,8,1920]{3,2,1,0:T(8,128)S(1)}) custom-call(f32[16,8,128]{2,1,0:T(8,128)} %get-tuple-element.144.refs_0_, f32[5,1,1920]{2,1,0:T(1,128)} %get-tuple-element.145.refs_1_, ...), custom_call_target="tpu_custom_call" | custom-call | tf_op jit(solution)/shard_map/step_back_load/pallas_call | solution.py:965
  116.6 2.7 %step_back.1 = (f32[5,4,8,1920]{3,2,1,0:T(8,128)}, f32[304,128]{1,0:T(8,128)}, f32[512,128]{1,0:T(8,128)}, f32[32,128]{1,0:T(8,128)}, f32[32,128]{1,0:T(8,128)}, /*index=5*/f32[480,128]{1,0:T(8,128)}, f32[480,128]{1,0:T(8,128)}) custom-call(s32[3,128]{1,0:T(4,128)} %get-tuple-element.126.refs_4_.refs_0_, f32[24,128]{1,0:T(8,128)} %get-tuple-element.127.refs_5_.refs_1_, ...), custom_call_target="tpu_custom_call" | custom-call | tf_op jit(solution)/shard_map/step_back/pallas_call | solution.py:965
  119.3 5.9 %all-to-all-start.6 = ((f32[16,8,4,128]{3,2,1,0:T(4,128)}), f32[16,8,4,128]{3,2,1,0:T(4,128)S(1)}, u32[]{:S(2)}, u32[]{:S(2)}) async-start(f32[16,8,4,128]{3,2,1,0:T(4,128)} %bitcast.58), calls=%async_computation.6 | async-start | bytes 524288 | tf_op jit(solution)/shard_map/all_to_all | solution.py:992
  125.2 0.8 collective-permute-start.16
  126.0 0.7 collective-permute-start.17
  126.6 0.4 collective-permute-done.16.refs_1_
  127.0 8.2 %all-to-all-done.6 = f32[16,8,4,128]{3,2,1,0:T(4,128)S(1)} async-done(((f32[16,8,4,128]{3,2,1,0:T(4,128)}), f32[16,8,4,128]{3,2,1,0:T(4,128)S(1)}, u32[]{:S(2)}, u32[]{:S(2)}) %all-to-all-start.6) | async-done | bytes 262176 | tf_op jit(solution)/shard_map/all_to_all | solution.py:992
  135.2 2.0 %owners_back.3 = f32[320,128]{1,0:T(8,128)} custom-call(f32[512,128]{1,0:T(8,128)S(1)} %bitcast.43, f32[80,80]{1,0:T(8,128)S(1)} %bitcast.49, f32[4,80,128]{2,1,0:T(8,128)} %get-tuple-element.199.refs_2_, f32[4,80,128]{2,1,0:T(8,128)} %get-tuple-element.200.refs_3_, f32[8,128]{1,0:T(8,128)} %get-tuple-element.115.refs_1_.refs_7_.refs_4_.refs_8_.refs_6_), custom_call_target="tpu_custom_call" | custom-call | tf_op jit(solution)/shard_map/owners_back/pallas_call | solution.py:965
  137.3 3.5 %all-to-all-start.7 = ((f32[16,5,4,128]{3,2,1,0:T(4,128)}), f32[16,5,4,128]{3,2,1,0:T(4,128)S(1)}, u32[]{:S(2)}, u32[]{:S(2)}) async-start(f32[16,5,4,128]{3,2,1,0:T(4,128)} %bitcast.57), calls=%async_computation.7 | async-start | bytes 327680 | tf_op jit(solution)/shard_map/all_to_all | solution.py:992
  140.8 0.4 collective-permute-start.18
  141.2 0.7 collective-permute-start.19
  141.9 7.4 %all-to-all-done.7 = f32[16,5,4,128]{3,2,1,0:T(4,128)S(1)} async-done(((f32[16,5,4,128]{3,2,1,0:T(4,128)}), f32[16,5,4,128]{3,2,1,0:T(4,128)S(1)}, u32[]{:S(2)}, u32[]{:S(2)}) %all-to-all-start.7) | async-done | bytes 163872 | tf_op jit(solution)/shard_map/all_to_all | solution.py:992
  149.3 1.2 merge.3
  150.5 0.7 collective-permute-start.21
  151.2 2.4 %step_back_load.3 = (f32[16,8,128]{2,1,0:T(8,128)S(1)}, f32[5,1,1920]{2,1,0:T(1,128)S(1)}, f32[5,4,8,1920]{3,2,1,0:T(8,128)S(1)}, f32[5,4,8,1920]{3,2,1,0:T(8,12...) custom-call(f32[16,8,128]{2,1,0:T(8,128)} %get-tuple-element.144.refs_0_, ...), custom_call_target="tpu_custom_call" | custom-call | tf_op jit(solution)/shard_map/step_back_load/pallas_call | solution.py:965
  153.6 2.5 %step_back_sums.1 = (f32[5,4,8,1920]{3,2,1,0:T(8,128)}, f32[16,128]{1,0:T(8,128)}) custom-call(f32[480,128]{1,0:T(8,128)S(1)} %collective-permute-done.18.refs_0_, f32[480,128]{1,0:T(8,128)S(1)} %collective-permute-done.19.refs_1_, f32[60,128]{1,0:T(8,128)S(1)} %collective-permute-done.20.refs_2_, f32[60,128]{1,0:T(8,128)S(1)} %collective-permute-done.21.refs_3_, ...), custom_call_target="tpu_custom_call" | custom-call | tf_op jit(solution)/shard_map/step_back_sums/pallas_call | solution.py:965
  156.1 5.4 %all-to-all-start.8 = ((f32[16,1,128]{2,1,0:T(1,128)}), f32[16,1,128]{2,1,0:T(1,128)S(1)}, u32[]{:S(2)}, u32[]{:S(2)}) async-start(f32[16,1,128]{2,1,0:T(1,128)} %bitcast.64), calls=%async_computation.8 | async-start | bytes 16384 | tf_op jit(solution)/shard_map/all_to_all | solution.py:1227
  161.4 1.7 %copy.20 = f32[5,4,8,1920]{3,1,0,2:T(4,128)S(1)} copy(f32[5,4,8,1920]{3,2,1,0:T(8,128)} %get-tuple-element.222) | data formatting | bytes 2457600 | tf_op jit(solution)/shard_map/step_back_sums/pallas_call | solution.py:965
  163.1 4.7 %all-to-all-done.8 = f32[16,1,128]{2,1,0:T(1,128)S(1)} async-done(((f32[16,1,128]{2,1,0:T(1,128)}), f32[16,1,128]{2,1,0:T(1,128)S(1)}, u32[]{:S(2)}, u32[]{:S(2)}) %all-to-all-start.8) | async-done | bytes 8224 | tf_op jit(solution)/shard_map/all_to_all | solution.py:1227
  167.8 1.2 finish.1
  (64 shorter events, 0.6 us)
Async XLA Ops:
  0.0 2.9 %copy-start.5 = (f32[4,4]{1,0:T(4,128)S(1)}, f32[4,4]{1,0:T(4,128)}, u32[]{:S(2)}) copy-start(f32[4,4]{1,0:T(4,128)} %param.21) | copy-start | bytes 196
  0.0 2.9 %copy-start.7 = (s32[15]{0:T(128)S(1)}, s32[15]{0:T(128)}, u32[]{:S(2)}) copy-start(s32[15]{0:T(128)} %param.28) | copy-start | bytes 184
  0.0 2.9 %copy-start.6 = (s32[15]{0:T(128)S(1)}, s32[15]{0:T(128)}, u32[]{:S(2)}) copy-start(s32[15]{0:T(128)} %param.27) | copy-start | bytes 184
  0.0 3.0 %copy-start.14 = (f32[15]{0:T(128)S(1)}, f32[15]{0:T(128)}, u32[]{:S(2)}) copy-start(f32[15]{0:T(128)} %param.29) | copy-start | bytes 184
  1.6 5.3 %collective-permute-start = (f32[480,128]{1,0:T(8,128)S(1)}, f32[480,128]{1,0:T(8,128)S(1)}, u32[]{:S(2)}, u32[]{:S(2)}) collective-permute-start(f32[480,128]{1,0:T(8,128)S(1)} %get-tuple-element.116), channel_id=1, source_target_pairs={{0,1},{1,0},{2,3},{3,2},{4,5},{5,4},{6,7},{7,6},{8,9},{9,8},{10,11... | collective-permute-start | bytes 737288 | tf_op jit(solution)/shard_map/ppermute | solution.py:986
  2.2 4.8 %collective-permute-start.1 = (f32[480,128]{1,0:T(8,128)S(1)}, f32[480,128]{1,0:T(8,128)S(1)}, u32[]{:S(2)}, u32[]{:S(2)}) collective-permute-start(f32[480,128]{1,0:T(8,128)S(1)} %get-tuple-element.117), channel_id=1, source_target_pairs={{1,2},{3,4},{5,6},{7,8},{9,10},{11,12},{13,14},{2,1},{4,3},{6,5},{... | collective-permute-start | bytes 737288 | tf_op jit(solution)/shard_map/ppermute | solution.py:986
  3.0 2.0 %copy-start.15 = (s32[1,75]{1,0:T(1,128)S(1)}, s32[1,75]{1,0:T(1,128)}, u32[]{:S(2)}) copy-start(s32[1,75]{1,0:T(1,128)} %param.25) | copy-start | bytes 904
  3.0 2.1 %copy-start.16 = (s32[1,75]{1,0:T(1,128)S(1)}, s32[1,75]{1,0:T(1,128)}, u32[]{:S(2)}) copy-start(s32[1,75]{1,0:T(1,128)} %param.26) | copy-start | bytes 904
  3.1 2.2 %copy-start.2 = (f32[8,4,4]{0,2,1:T(4,128)S(1)}, f32[8,4,4]{0,2,1:T(4,128)}, u32[]{:S(2)}) copy-start(f32[8,4,4]{0,2,1:T(4,128)} %param.20) | copy-start | bytes 1540
  5.1 17.2 %copy-start.3 = (f32[2,1,80,128]{3,2,1,0:T(8,128)S(1)}, f32[2,1,80,128]{3,2,1,0:T(8,128)}, u32[]{:S(2)}) copy-start(f32[2,1,80,128]{3,2,1,0:T(8,128)} %param.24) | copy-start | bytes 245764
  5.1 17.2 %copy-start.4 = (f32[2,1,80,128]{3,2,1,0:T(8,128)S(1)}, f32[2,1,80,128]{3,2,1,0:T(8,128)}, u32[]{:S(2)}) copy-start(f32[2,1,80,128]{3,2,1,0:T(8,128)} %param.23) | copy-start | bytes 245764
  6.9 22.7 %copy-start.1 = (f32[1,80,80]{2,1,0:T(8,128)S(1)}, f32[1,80,80]{2,1,0:T(8,128)}, u32[]{:S(2)}) copy-start(f32[1,80,80]{2,1,0:T(8,128)} %param.22) | copy-start | bytes 76804
  9.6 25.6 %copy-start.11 = (f32[480,128]{1,0:T(8,128)S(1)}, f32[480,128]{1,0:T(8,128)}, u32[]{:S(2)}) copy-start(f32[480,128]{1,0:T(8,128)} %get-tuple-element.142) | copy-start | bytes 737284
  9.6 26.0 %copy-start.10 = (f32[480,128]{1,0:T(8,128)S(1)}, f32[480,128]{1,0:T(8,128)}, u32[]{:S(2)}) copy-start(f32[480,128]{1,0:T(8,128)} %get-tuple-element.143) | copy-start | bytes 737284
  9.6 20.1 %all-to-all-start = ((f32[16,5,4,128]{3,2,1,0:T(4,128)}), f32[16,5,4,128]{3,2,1,0:T(4,128)S(1)}, u32[]{:S(2)}, u32[]{:S(2)}) async-start(f32[16,5,4,128]{3,2,1,0:T(4,128)} %bitcast.62), calls=%async_computation | async-start | bytes 327680 | tf_op jit(solution)/shard_map/all_to_all | solution.py:992
  21.2 1.5 collective-permute-start.2
  21.6 1.1 collective-permute-start.3
  31.7 13.6 %all-to-all-start.1 = ((f32[16,8,4,128]{3,2,1,0:T(4,128)}), f32[16,8,4,128]{3,2,1,0:T(4,128)S(1)}, u32[]{:S(2)}, u32[]{:S(2)}) async-start(f32[16,8,4,128]{3,2,1,0:T(4,128)} %bitcast.60), calls=%async_computation.1 | async-start | bytes 524288 | tf_op jit(solution)/shard_map/all_to_all | solution.py:992
  35.2 14.6 %collective-permute-start.4 = (f32[480,128]{1,0:T(8,128)S(1)}, f32[480,128]{1,0:T(8,128)S(1)}, u32[]{:S(2)}, u32[]{:S(2)}) collective-permute-start(f32[480,128]{1,0:T(8,128)S(1)} %copy-done.11), channel_id=1, source_target_pairs={{0,1},{1,0},{2,3},{3,2},{4,5},{5,4},{6,7},{7,6},{8,9},{9,8},{10,11... | collective-permute-start | bytes 737288 | tf_op jit(solution)/shard_map/ppermute | solution.py:986
  35.6 14.2 %collective-permute-start.5 = (f32[480,128]{1,0:T(8,128)S(1)}, f32[480,128]{1,0:T(8,128)S(1)}, u32[]{:S(2)}, u32[]{:S(2)}) collective-permute-start(f32[480,128]{1,0:T(8,128)S(1)} %copy-done.10), channel_id=1, source_target_pairs={{1,2},{3,4},{5,6},{7,8},{9,10},{11,12},{13,14},{2,1},{4,3},{6,5},{... | collective-permute-start | bytes 737288 | tf_op jit(solution)/shard_map/ppermute | solution.py:986
  47.1 2.7 %collective-permute-start.6 = (f32[60,128]{1,0:T(8,128)S(1)}, f32[60,128]{1,0:T(8,128)S(1)}, u32[]{:S(2)}, u32[]{:S(2)}) collective-permute-start(f32[60,128]{1,0:T(8,128)S(1)} %get-tuple-element.153), channel_id=1, source_target_pairs={{0,1},{1,0},{2,3},{3,2},{4,5},{5,4},{6,7},{7,6},{8,9},{9,8},{10,11... | collective-permute-start | bytes 92168 | tf_op jit(solution)/shard_map/ppermute | solution.py:986
  47.2 2.6 %collective-permute-start.7 = (f32[60,128]{1,0:T(8,128)S(1)}, f32[60,128]{1,0:T(8,128)S(1)}, u32[]{:S(2)}, u32[]{:S(2)}) collective-permute-start(f32[60,128]{1,0:T(8,128)S(1)} %get-tuple-element.154), channel_id=1, source_target_pairs={{1,2},{3,4},{5,6},{7,8},{9,10},{11,12},{13,14},{2,1},{4,3},{6,5},{... | collective-permute-start | bytes 92168 | tf_op jit(solution)/shard_map/ppermute | solution.py:986
  52.6 14.7 %all-to-all-start.2 = ((f32[16,5,4,128]{3,2,1,0:T(4,128)}), f32[16,5,4,128]{3,2,1,0:T(4,128)S(1)}, u32[]{:S(2)}, u32[]{:S(2)}) async-start(f32[16,5,4,128]{3,2,1,0:T(4,128)} %bitcast.63), calls=%async_computation.2 | async-start | bytes 327680 | tf_op jit(solution)/shard_map/all_to_all | solution.py:992
  58.9 1.5 collective-permute-start.8
  59.3 1.1 collective-permute-start.9
  69.0 13.6 %all-to-all-start.3 = ((f32[16,8,4,128]{3,2,1,0:T(4,128)}), f32[16,8,4,128]{3,2,1,0:T(4,128)S(1)}, u32[]{:S(2)}, u32[]{:S(2)}) async-start(f32[16,8,4,128]{3,2,1,0:T(4,128)} %bitcast.61), calls=%async_computation.3 | async-start | bytes 524288 | tf_op jit(solution)/shard_map/all_to_all | solution.py:992
  84.9 19.3 %copy-start.9 = (f32[480,128]{1,0:T(8,128)S(1)}, f32[480,128]{1,0:T(8,128)}, u32[]{:S(2)}) copy-start(f32[480,128]{1,0:T(8,128)} %get-tuple-element.164) | copy-start | bytes 737284
  84.9 19.7 %copy-start.8 = (f32[480,128]{1,0:T(8,128)S(1)}, f32[480,128]{1,0:T(8,128)}, u32[]{:S(2)}) copy-start(f32[480,128]{1,0:T(8,128)} %get-tuple-element.165) | copy-start | bytes 737284
  84.9 13.7 %all-to-all-start.4 = ((f32[16,8,4,128]{3,2,1,0:T(4,128)}), f32[16,8,4,128]{3,2,1,0:T(4,128)S(1)}, u32[]{:S(2)}, u32[]{:S(2)}) async-start(f32[16,8,4,128]{3,2,1,0:T(4,128)} %bitcast.59), calls=%async_computation.4 | async-start | bytes 524288 | tf_op jit(solution)/shard_map/all_to_all | solution.py:992
  88.6 1.5 collective-permute-start.12
  88.9 1.2 collective-permute-start.13
  100.7 12.0 %all-to-all-start.5 = ((f32[16,5,4,128]{3,2,1,0:T(4,128)}), f32[16,5,4,128]{3,2,1,0:T(4,128)S(1)}, u32[]{:S(2)}, u32[]{:S(2)}) async-start(f32[16,5,4,128]{3,2,1,0:T(4,128)} %bitcast.56), calls=%async_computation.5 | async-start | bytes 327680 | tf_op jit(solution)/shard_map/all_to_all | solution.py:992
  104.2 12.4 %collective-permute-start.10 = (f32[480,128]{1,0:T(8,128)S(1)}, f32[480,128]{1,0:T(8,128)S(1)}, u32[]{:S(2)}, u32[]{:S(2)}) collective-permute-start(f32[480,128]{1,0:T(8,128)S(1)} %copy-done.9), channel_id=1, source_target_pairs={{0,1},{1,0},{2,3},{3,2},{4,5},{5,4},{6,7},{7,6},{8,9},{9,8},{10,11... | collective-permute-start | bytes 737288 | tf_op jit(solution)/shard_map/ppermute | solution.py:986
  104.6 12.0 %collective-permute-start.11 = (f32[480,128]{1,0:T(8,128)S(1)}, f32[480,128]{1,0:T(8,128)S(1)}, u32[]{:S(2)}, u32[]{:S(2)}) collective-permute-start(f32[480,128]{1,0:T(8,128)S(1)} %copy-done.8), channel_id=1, source_target_pairs={{1,2},{3,4},{5,6},{7,8},{9,10},{11,12},{13,14},{2,1},{4,3},{6,5},{... | collective-permute-start | bytes 737288 | tf_op jit(solution)/shard_map/ppermute | solution.py:986
  113.9 2.8 %collective-permute-start.14 = (f32[60,128]{1,0:T(8,128)S(1)}, f32[60,128]{1,0:T(8,128)S(1)}, u32[]{:S(2)}, u32[]{:S(2)}) collective-permute-start(f32[60,128]{1,0:T(8,128)S(1)} %get-tuple-element.185), channel_id=1, source_target_pairs={{0,1},{1,0},{2,3},{3,2},{4,5},{5,4},{6,7},{7,6},{8,9},{9,8},{10,11... | collective-permute-start | bytes 92168 | tf_op jit(solution)/shard_map/ppermute | solution.py:986
  113.9 2.7 %collective-permute-start.15 = (f32[60,128]{1,0:T(8,128)S(1)}, f32[60,128]{1,0:T(8,128)S(1)}, u32[]{:S(2)}, u32[]{:S(2)}) collective-permute-start(f32[60,128]{1,0:T(8,128)S(1)} %get-tuple-element.186), channel_id=1, source_target_pairs={{1,2},{3,4},{5,6},{7,8},{9,10},{11,12},{13,14},{2,1},{4,3},{6,5},{... | collective-permute-start | bytes 92168 | tf_op jit(solution)/shard_map/ppermute | solution.py:986
  119.3 21.5 %copy-start.13 = (f32[480,128]{1,0:T(8,128)S(1)}, f32[480,128]{1,0:T(8,128)}, u32[]{:S(2)}) copy-start(f32[480,128]{1,0:T(8,128)} %get-tuple-element.203) | copy-start | bytes 737284
  119.3 21.9 %copy-start.12 = (f32[480,128]{1,0:T(8,128)S(1)}, f32[480,128]{1,0:T(8,128)}, u32[]{:S(2)}) copy-start(f32[480,128]{1,0:T(8,128)} %get-tuple-element.204) | copy-start | bytes 737284
  119.3 15.9 %all-to-all-start.6 = ((f32[16,8,4,128]{3,2,1,0:T(4,128)}), f32[16,8,4,128]{3,2,1,0:T(4,128)S(1)}, u32[]{:S(2)}, u32[]{:S(2)}) async-start(f32[16,8,4,128]{3,2,1,0:T(4,128)} %bitcast.58), calls=%async_computation.6 | async-start | bytes 524288 | tf_op jit(solution)/shard_map/all_to_all | solution.py:992
  125.2 1.8 %collective-permute-start.16 = (f32[32,128]{1,0:T(8,128)}, f32[32,128]{1,0:T(8,128)S(1)}, u32[]{:S(2)}, u32[]{:S(2)}) collective-permute-start(f32[32,128]{1,0:T(8,128)} %get-tuple-element.196), channel_id=1, source_target_pairs={{0,1},{1,0},{2,3},{3,2},{4,5},{5,4},{6,7},{7,6},{8,9},{9,8},{10,11... | collective-permute-start | bytes 49160 | tf_op jit(solution)/shard_map/ppermute | solution.py:986
  126.0 1.1 collective-permute-start.17
  137.3 12.0 %all-to-all-start.7 = ((f32[16,5,4,128]{3,2,1,0:T(4,128)}), f32[16,5,4,128]{3,2,1,0:T(4,128)S(1)}, u32[]{:S(2)}, u32[]{:S(2)}) async-start(f32[16,5,4,128]{3,2,1,0:T(4,128)} %bitcast.57), calls=%async_computation.7 | async-start | bytes 327680 | tf_op jit(solution)/shard_map/all_to_all | solution.py:992
  140.8 12.7 %collective-permute-start.18 = (f32[480,128]{1,0:T(8,128)S(1)}, f32[480,128]{1,0:T(8,128)S(1)}, u32[]{:S(2)}, u32[]{:S(2)}) collective-permute-start(f32[480,128]{1,0:T(8,128)S(1)} %copy-done.13), channel_id=1, source_target_pairs={{0,1},{1,0},{2,3},{3,2},{4,5},{5,4},{6,7},{7,6},{8,9},{9,8},{10,11... | collective-permute-start | bytes 737288 | tf_op jit(solution)/shard_map/ppermute | solution.py:986
  141.2 12.4 %collective-permute-start.19 = (f32[480,128]{1,0:T(8,128)S(1)}, f32[480,128]{1,0:T(8,128)S(1)}, u32[]{:S(2)}, u32[]{:S(2)}) collective-permute-start(f32[480,128]{1,0:T(8,128)S(1)} %copy-done.12), channel_id=1, source_target_pairs={{1,2},{3,4},{5,6},{7,8},{9,10},{11,12},{13,14},{2,1},{4,3},{6,5},{... | collective-permute-start | bytes 737288 | tf_op jit(solution)/shard_map/ppermute | solution.py:986
  150.4 3.1 %collective-permute-start.20 = (f32[60,128]{1,0:T(8,128)S(1)}, f32[60,128]{1,0:T(8,128)S(1)}, u32[]{:S(2)}, u32[]{:S(2)}) collective-permute-start(f32[60,128]{1,0:T(8,128)S(1)} %get-tuple-element.209), channel_id=1, source_target_pairs={{0,1},{1,0},{2,3},{3,2},{4,5},{5,4},{6,7},{7,6},{8,9},{9,8},{10,11... | collective-permute-start | bytes 92168 | tf_op jit(solution)/shard_map/ppermute | solution.py:986
  150.5 3.1 %collective-permute-start.21 = (f32[60,128]{1,0:T(8,128)S(1)}, f32[60,128]{1,0:T(8,128)S(1)}, u32[]{:S(2)}, u32[]{:S(2)}) collective-permute-start(f32[60,128]{1,0:T(8,128)S(1)} %get-tuple-element.210), channel_id=1, source_target_pairs={{1,2},{3,4},{5,6},{7,8},{9,10},{11,12},{13,14},{2,1},{4,3},{6,5},{... | collective-permute-start | bytes 92168 | tf_op jit(solution)/shard_map/ppermute | solution.py:986
  156.1 11.8 %all-to-all-start.8 = ((f32[16,1,128]{2,1,0:T(1,128)}), f32[16,1,128]{2,1,0:T(1,128)S(1)}, u32[]{:S(2)}, u32[]{:S(2)}) async-start(f32[16,1,128]{2,1,0:T(1,128)} %bitcast.64), calls=%async_computation.8 | async-start | bytes 16384 | tf_op jit(solution)/shard_map/all_to_all | solution.py:1227
  161.4 6.4 %copy-start = (f32[8,5,4,1920]{3,2,1,0:T(4,128)S(1)}, f32[8,5,4,1920]{3,2,1,0:T(4,128)}, u32[]{:S(2)}) copy-start(f32[8,5,4,1920]{3,2,1,0:T(4,128)} %refs_1_.6) | copy-start | bytes 3686404

commit v5 on v4

--- a/solution.py
+++ b/solution.py
@@ -36,7 +36,7 @@
         self.row_width = CHANNELS * self.row_tiles
         self.pitch = -(-self.row_tiles // SUBLANES) * SUBLANES
         self.own_rows = CHANNELS * capacity
-        self.chunk = -(-(self.own_rows + 2 * capacity) // SUBLANES) * SUBLANES
+        self.chunk = self.own_rows + 2 * capacity
         self.slot_lines = -(-self.slots // WIDTH)
         self.facts = -(-(self.slot_lines + 1) // SUBLANES) * SUBLANES
         self.lat_lines = LAT_DEV * self.pitch
@@ -988,7 +988,8 @@
 
 def exchange(array, devices):
     rows = array.shape[0] // devices
-    split = array.reshape(devices, rows // CHANNELS, CHANNELS, WIDTH)
+    step = CHANNELS if rows % CHANNELS == 0 else 2
+    split = array.reshape(devices, rows // step, step, WIDTH)
     moved = lax.all_to_all(split, "horiz", split_axis=0, concat_axis=0, tiled=True)
     return moved.reshape(array.shape)
 
@@ -1140,12 +1141,14 @@
             flux, perturbation = lax.optimization_barrier((flux, perturbation))
             beside = relayout(perturbation)
         flux = exchange(flux, devices)
+        edges = swap(*sends)
+        if last:
+            flux, *edges = lax.optimization_barrier((flux, *edges))
         flux, *beside = lax.optimization_barrier((flux, *beside))
         if first:
             diffusivity_rows, weight_rows, diffusivity_tiles, weight_tiles, target = beside
         else:
             start_field = beside[0]
-        edges = swap(*sends)
         inputs = near_by(flux, *got) + fetched(surface) + scalars(tables, weights)
         if last:
             surface, slope, packed, *sends = call(

time: 171 us -> 173 us (1.012)
  blocking collectives: 0 us -> 11.9 us
  waiting for transfers between devices: 64.5 us -> 55 us
    all_to_all x0 -> x1, blocking collectives: none -> 11.9 us  [exchange(): lax.all_to_all(split, 'horiz', split_axis=0, concat_axis=0, tiled=True)]
    all_to_all x8 -> x7, waiting for transfers between devices: 58.2 us -> 48.8 us  [exchange(): lax.all_to_all(split, 'horiz', split_axis=0, concat_axis=0, tiled=True)]
    all_to_all x8 -> x7, starting transfers between devices: 41.5 us -> 41.1 us  [exchange(): lax.all_to_all(split, 'horiz', split_axis=0, concat_axis=0, tiled=True)]
  transfers between devices with their start and end apart: 31 -> 30, of which waited for: 13 -> 12; matrix products, arithmetic and copies ran while one was open for 1% -> 1% of each run, Pallas kernels for 12% -> 11%
where the time goes in v5:
time: 173 us; the launch traced here: 171 us
  starting transfers between devices  57.4 us (33%)
  waiting for transfers between devices  55 us (32%)
  Pallas kernels  44 us (25%)
  blocking collectives  11.9 us (7%)
  local copies, waits for them, and re-layouts  1.87 us (1%)
    all_to_all x7, waiting for transfers between devices, exchange(): lax.all_to_all(split, 'horiz', split_axis=0, concat_axis=0, tiled=True)  48.8 us
    pallas_call x22, Pallas kernels, call(): pl.pallas_call(run, name=name, in_specs=[pl.BlockSpec(memory_space=item.s...  44 us
    all_to_all x7, starting transfers between devices, exchange(): lax.all_to_all(split, 'horiz', split_axis=0, concat_axis=0, tiled=True)  41.1 us
    all_to_all x1, blocking collectives, exchange(): lax.all_to_all(split, 'horiz', split_axis=0, concat_axis=0, tiled=True)  11.9 us
    ppermute x11, starting transfers between devices, swap(): lax.ppermute(second, 'horiz', outer)  7.25 us
    all_to_all x1, starting transfers between devices, body(): lax.all_to_all(sums, 'horiz', split_axis=0, concat_axis=0, tiled=True)  5.36 us
    all_to_all x1, waiting for transfers between devices, body(): lax.all_to_all(sums, 'horiz', split_axis=0, concat_axis=0, tiled=True)  4.68 us
    ppermute x11, starting transfers between devices, swap(): lax.ppermute(first, 'horiz', inner)  3.73 us
  transfers between devices with their start and end apart: 30, of which 12 were waited for; matrix products, arithmetic and copies ran while one was open for 1% of the time, Pallas kernels for 11%

profile of v5, /device:TPU:0, one launch (start us, length us, event | category | flops | bytes accessed | tf_op | source)
XLA Modules:
  0.0 171.1 jit_solution(6953272435116821648)
XLA Ops:
  0.0 1.6 edges.1
  1.6 0.5 collective-permute-start
  2.2 0.7 collective-permute-start.1
  2.9 0.1 reshape.82
  3.1 2.0 %load.1.refs_6_ = f32[5,4,8,1920]{3,2,1,0:T(8,128)S(1)} custom-call(f32[8,5,4,1920]{3,2,1,0:T(4,128)} %refs_1_.6, f32[8,5,4,1920]{3,2,1,0:T(4,128)} %refs_1_.4), custom_call_target="tpu_custom_call" | custom-call | tf_op jit(solution)/shard_map/load/pallas_call | solution.py:965
  5.2 1.7 setup.1
  7.0 2.6 %step.2 = (f32[5,4,8,1920]{3,2,1,0:T(8,128)}, f32[5,4,8,1920]{3,2,1,0:T(8,128)}, f32[304,128]{1,0:T(8,128)}, f32[320,128]{1,0:T(8,128)}, f32[40,128]{1,0:T(8,128...) custom-call(s32[1,128]{1,0:T(1,128)} %get-tuple-element.117.refs_0_.refs_7_.refs_5_, ...), custom_call_target="tpu_custom_call" | custom-call | tf_op jit(solution)/shard_map/step/pallas_call | solution.py:965
  9.6 11.6 %all-to-all-start = ((f32[16,5,4,128]{3,2,1,0:T(4,128)}), f32[16,5,4,128]{3,2,1,0:T(4,128)S(1)}, u32[]{:S(2)}, u32[]{:S(2)}) async-start(f32[16,5,4,128]{3,2,1,0:T(4,128)} %bitcast.62), calls=%async_computation | async-start | bytes 327680 | tf_op jit(solution)/shard_map/all_to_all | solution.py:993
  21.2 0.4 collective-permute-start.2
  21.6 0.7 collective-permute-start.3
  22.3 0.4 collective-permute-done.2.refs_5_.refs_1_
  22.7 7.0 %all-to-all-done = f32[16,5,4,128]{3,2,1,0:T(4,128)S(1)} async-done(((f32[16,5,4,128]{3,2,1,0:T(4,128)}), f32[16,5,4,128]{3,2,1,0:T(4,128)S(1)}, u32[]{:S(2)}, u32[]{:S(2)}) %all-to-all-start) | async-done | bytes 163872 | tf_op jit(solution)/shard_map/all_to_all | solution.py:993
  29.7 2.0 %owners.2 = (s32[3,128]{1,0:T(4,128)}, f32[24,128]{1,0:T(8,128)}, f32[480,128]{1,0:T(8,128)}, f32[4,80,128]{2,1,0:T(8,128)}, f32[4,80,128]{2,1,0:T(8,128)}) custom-call(f32[320,128]{1,0:T(8,128)S(1)} %bitcast.52, f32[80,80]{1,0:T(8,128)S(1)} %bitcast.46, f32[80,128]{1,0:T(8,128)S(1)} %get-tuple-element.235.refs_2_, ...), custom_call_target="tpu_custom_call" | custom-call | tf_op jit(solution)/shard_map/owners/pallas_call | solution.py:965
  31.7 3.5 %all-to-all-start.1 = ((f32[16,15,2,128]{3,2,1,0:T(2,128)}), f32[16,15,2,128]{3,2,1,0:T(2,128)S(1)}, u32[]{:S(2)}, u32[]{:S(2)}) async-start(f32[16,15,2,128]{3,2,1,0:T(2,128)} %bitcast.61), calls=%async_computation.1 | async-start | bytes 491520 | tf_op jit(solution)/shard_map/all_to_all | solution.py:993
  35.2 0.4 collective-permute-start.4
  35.6 0.7 collective-permute-start.5
  36.3 2.3 %relayout.2.refs_5_ = f32[5,4,8,1920]{3,2,1,0:T(8,128)} custom-call(f32[8,5,4,1920]{3,2,1,0:T(4,128)} %refs_6_), custom_call_target="tpu_custom_call" | custom-call | tf_op jit(solution)/shard_map/relayout/pallas_call | solution.py:965
  38.6 1.7 %columns.1 = (f32[5,1,1920]{2,1,0:T(1,128)}, f32[5,1,1920]{2,1,0:T(1,128)}, f32[300,128]{1,0:T(8,128)}, f32[300,128]{1,0:T(8,128)}) custom-call(f32[5,1920]{1,0:T(8,128)} %refs_0_.4, f32[5,1920]{1,0:T(8,128)} %refs_1_.5), custom_call_target="tpu_custom_call" | custom-call | tf_op jit(solution)/shard_map/columns/pallas_call | solution.py:965
  40.3 4.7 %all-to-all-done.1 = f32[16,15,2,128]{3,2,1,0:T(2,128)S(1)} async-done(((f32[16,15,2,128]{3,2,1,0:T(2,128)}), f32[16,15,2,128]{3,2,1,0:T(2,128)S(1)}, u32[]{:S(2)}, u32[]{:S(2)}) %all-to-all-start.1) | async-done | bytes 245792 | tf_op jit(solution)/shard_map/all_to_all | solution.py:993
  45.0 1.9 %surface.2 = (f32[304,128]{1,0:T(8,128)S(1)}, f32[60,128]{1,0:T(8,128)S(1)}, f32[60,128]{1,0:T(8,128)S(1)}, f32[64,128]{1,0:T(8,128)}) custom-call(f32[480,128]{1,0:T(8,128)S(1)} %bitcast.42, f32[40,128]{1,0:T(8,128)S(1)} %collective-permute-done.2.refs_5_.refs_1_, f32[40,128]{1,0:T(8,128)S(1)} %collective-permute-done.3.refs_6_.refs_2_, ...), custom_call_target="tpu_custom_call" | custom-call | tf_op jit(solution)/shard_map/surface/pallas_call | solution.py:965
  46.9 0.7 collective-permute-start.7
  47.6 1.9 %step_load.1 = (f32[16,8,128]{2,1,0:T(8,128)S(1)}, f32[5,1,1920]{2,1,0:T(1,128)S(1)}, f32[5,4,8,1920]{3,2,1,0:T(8,128)S(1)}, f32[5,1,1920]{2,1,0:T(1,128)S(1)}, f32[5,4,8,1920]{3,2,1,0:T(8,128)S(1)}) custom-call(f32[16,8,128]{2,1,0:T(8,128)} %get-tuple-element.147.refs_0_, f32[5,1,1920]{2,1,0:T(1,128)} %get-tuple-element.148.refs_1_, ...), custom_call_target="tpu_custom_call" | custom-call | tf_op jit(solution)/shard_map/step_load/pallas_call | solution.py:965
  49.6 2.8 %step.3 = (f32[5,4,8,1920]{3,2,1,0:T(8,128)}, f32[5,4,8,1920]{3,2,1,0:T(8,128)}, f32[304,128]{1,0:T(8,128)}, f32[320,128]{1,0:T(8,128)}, f32[32,128]{1,0:T(8,128...) custom-call(s32[1,128]{1,0:T(1,128)} %get-tuple-element.117.refs_0_.refs_7_.refs_5_, ...), custom_call_target="tpu_custom_call" | custom-call | tf_op jit(solution)/shard_map/step/pallas_call | solution.py:965
  52.3 6.5 %all-to-all-start.2 = ((f32[16,5,4,128]{3,2,1,0:T(4,128)}), f32[16,5,4,128]{3,2,1,0:T(4,128)S(1)}, u32[]{:S(2)}, u32[]{:S(2)}) async-start(f32[16,5,4,128]{3,2,1,0:T(4,128)} %bitcast.63), calls=%async_computation.2 | async-start | bytes 327680 | tf_op jit(solution)/shard_map/all_to_all | solution.py:993
  58.9 0.4 collective-permute-start.8
  59.3 0.7 collective-permute-start.9
  60.0 0.4 collective-permute-done.8.refs_1_
  60.4 7.0 %all-to-all-done.2 = f32[16,5,4,128]{3,2,1,0:T(4,128)S(1)} async-done(((f32[16,5,4,128]{3,2,1,0:T(4,128)}), f32[16,5,4,128]{3,2,1,0:T(4,128)S(1)}, u32[]{:S(2)}, u32[]{:S(2)}) %all-to-all-start.2) | async-done | bytes 163872 | tf_op jit(solution)/shard_map/all_to_all | solution.py:993
  67.4 1.7 owners.3
  69.0 3.5 %all-to-all-start.3 = ((f32[16,15,2,128]{3,2,1,0:T(2,128)}), f32[16,15,2,128]{3,2,1,0:T(2,128)S(1)}, u32[]{:S(2)}, u32[]{:S(2)}) async-start(f32[16,15,2,128]{3,2,1,0:T(2,128)} %bitcast.60), calls=%async_computation.3 | async-start | bytes 491520 | tf_op jit(solution)/shard_map/all_to_all | solution.py:993
  72.6 0.3 collective-permute-start.10
  72.9 0.7 collective-permute-start.11
  73.5 2.3 %relayout.3.refs_5_ = f32[5,4,8,1920]{3,2,1,0:T(8,128)} custom-call(f32[8,5,4,1920]{3,2,1,0:T(4,128)} %refs_1_.6), custom_call_target="tpu_custom_call" | custom-call | tf_op jit(solution)/shard_map/relayout/pallas_call | solution.py:965
  75.9 6.5 %all-to-all-done.3 = f32[16,15,2,128]{3,2,1,0:T(2,128)S(1)} async-done(((f32[16,15,2,128]{3,2,1,0:T(2,128)}), f32[16,15,2,128]{3,2,1,0:T(2,128)S(1)}, u32[]{:S(2)}, u32[]{:S(2)}) %all-to-all-start.3) | async-done | bytes 245792 | tf_op jit(solution)/shard_map/all_to_all | solution.py:993
  82.3 2.3 %surface.3 = (f32[304,128]{1,0:T(8,128)}, f32[64,128]{1,0:T(8,128)}, f32[480,128]{1,0:T(8,128)}, f32[32,128]{1,0:T(8,128)}, f32[32,128]{1,0:T(8,128)}) custom-call(f32[480,128]{1,0:T(8,128)S(1)} %bitcast.43, f32[32,128]{1,0:T(8,128)S(1)} %collective-permute-done.8.refs_1_, f32[32,128]{1,0:T(8,128)S(1)} %collective-permute-done.9.refs_2_, ...), custom_call_target="tpu_custom_call" | custom-call | tf_op jit(solution)/shard_map/surface/pallas_call | solution.py:965
  84.7 6.5 %all-to-all-start.4 = ((f32[16,15,2,128]{3,2,1,0:T(2,128)}), f32[16,15,2,128]{3,2,1,0:T(2,128)S(1)}, u32[]{:S(2)}, u32[]{:S(2)}) async-start(f32[16,15,2,128]{3,2,1,0:T(2,128)} %bitcast.59), calls=%async_computation.4 | async-start | bytes 491520 | tf_op jit(solution)/shard_map/all_to_all | solution.py:993
  91.2 0.4 collective-permute-start.12
  91.6 0.7 collective-permute-start.13
  92.2 0.4 collective-permute-done.12.refs_1_
  92.6 8.3 %all-to-all-done.4 = f32[16,15,2,128]{3,2,1,0:T(2,128)S(1)} async-done(((f32[16,15,2,128]{3,2,1,0:T(2,128)}), f32[16,15,2,128]{3,2,1,0:T(2,128)S(1)}, u32[]{:S(2)}, u32[]{:S(2)}) %all-to-all-start.4) | async-done | bytes 245792 | tf_op jit(solution)/shard_map/all_to_all | solution.py:993
  100.9 2.1 %owners_back.2 = f32[320,128]{1,0:T(8,128)} custom-call(f32[480,128]{1,0:T(8,128)S(1)} %bitcast.44, f32[80,80]{1,0:T(8,128)S(1)} %bitcast.48, f32[4,80,128]{2,1,0:T(8,128)} %get-tuple-element.184.refs_2_, f32[4,80,128]{2,1,0:T(8,128)} %get-tuple-element.185.refs_3_, f32[8,128]{1,0:T(8,128)} %get-tuple-element.118.refs_1_.refs_7_.refs_4_.refs_8_.refs_6_), custom_call_target="tpu_custom_call" | custom-call | tf_op jit(solution)/shard_map/owners_back/pallas_call | solution.py:965
  103.0 11.9 %all_to_all.51 = f32[16,5,4,128]{3,2,1,0:T(4,128)S(1)} all-to-all(f32[16,5,4,128]{3,2,1,0:T(4,128)} %bitcast.57), channel_id=1, replica_groups=mesh['member'=2,'horiz'=16] {'horiz'}, dimensions={0} | all-to-all | bytes 327680 | tf_op jit(solution)/shard_map/all_to_all | solution.py:993
  114.9 1.2 merge.2
  116.2 0.7 collective-permute-start.15
  116.9 2.0 %step_back_load.2 = (f32[16,8,128]{2,1,0:T(8,128)S(1)}, f32[5,1,1920]{2,1,0:T(1,128)S(1)}, f32[5,4,8,1920]{3,2,1,0:T(8,128)S(1)}, f32[5,4,8,1920]{3,2,1,0:T(8,128)S(1)}, f32[5,4,8,1920]{3,2,1,0:T(8,128)S(1)}) custom-call(f32[16,8,128]{2,1,0:T(8,128)} %get-tuple-element.147.refs_0_, f32[5,1,1920]{2,1,0:T(1,128)} %get-tuple-element.148.refs_1_, ...), custom_call_target="tpu_custom_call" | custom-call | tf_op jit(solution)/shard_map/step_back_load/pallas_call | solution.py:965
  118.9 2.7 %step_back.1 = (f32[5,4,8,1920]{3,2,1,0:T(8,128)}, f32[304,128]{1,0:T(8,128)}, f32[480,128]{1,0:T(8,128)}, f32[32,128]{1,0:T(8,128)}, f32[32,128]{1,0:T(8,128)}, /*index=5*/f32[480,128]{1,0:T(8,128)}, f32[480,128]{1,0:T(8,128)}) custom-call(s32[3,128]{1,0:T(4,128)} %get-tuple-element.129.refs_4_.refs_0_, f32[24,128]{1,0:T(8,128)} %get-tuple-element.130.refs_5_.refs_1_, ...), custom_call_target="tpu_custom_call" | custom-call | tf_op jit(solution)/shard_map/step_back/pallas_call | solution.py:965
  121.6 5.9 %all-to-all-start.6 = ((f32[16,15,2,128]{3,2,1,0:T(2,128)}), f32[16,15,2,128]{3,2,1,0:T(2,128)S(1)}, u32[]{:S(2)}, u32[]{:S(2)}) async-start(f32[16,15,2,128]{3,2,1,0:T(2,128)} %bitcast.58), calls=%async_computation.6 | async-start | bytes 491520 | tf_op jit(solution)/shard_map/all_to_all | solution.py:993
  127.5 0.8 collective-permute-start.16
  128.3 0.7 collective-permute-start.17
  128.9 0.4 collective-permute-done.16.refs_1_
  129.3 8.0 %all-to-all-done.6 = f32[16,15,2,128]{3,2,1,0:T(2,128)S(1)} async-done(((f32[16,15,2,128]{3,2,1,0:T(2,128)}), f32[16,15,2,128]{3,2,1,0:T(2,128)S(1)}, u32[]{:S(2)}, u32[]{:S(2)}) %all-to-all-start.6) | async-done | bytes 245792 | tf_op jit(solution)/shard_map/all_to_all | solution.py:993
  137.3 2.0 %owners_back.3 = f32[320,128]{1,0:T(8,128)} custom-call(f32[480,128]{1,0:T(8,128)S(1)} %bitcast.45, f32[80,80]{1,0:T(8,128)S(1)} %bitcast.49, f32[4,80,128]{2,1,0:T(8,128)} %get-tuple-element.205.refs_2_, f32[4,80,128]{2,1,0:T(8,128)} %get-tuple-element.206.refs_3_, f32[8,128]{1,0:T(8,128)} %get-tuple-element.118.refs_1_.refs_7_.refs_4_.refs_8_.refs_6_), custom_call_target="tpu_custom_call" | custom-call | tf_op jit(solution)/shard_map/owners_back/pallas_call | solution.py:965
  139.3 3.5 %all-to-all-start.7 = ((f32[16,5,4,128]{3,2,1,0:T(4,128)}), f32[16,5,4,128]{3,2,1,0:T(4,128)S(1)}, u32[]{:S(2)}, u32[]{:S(2)}) async-start(f32[16,5,4,128]{3,2,1,0:T(4,128)} %bitcast.56), calls=%async_computation.7 | async-start | bytes 327680 | tf_op jit(solution)/shard_map/all_to_all | solution.py:993
  142.9 0.4 collective-permute-start.18
  143.2 0.7 collective-permute-start.19
  143.9 7.4 %all-to-all-done.7 = f32[16,5,4,128]{3,2,1,0:T(4,128)S(1)} async-done(((f32[16,5,4,128]{3,2,1,0:T(4,128)}), f32[16,5,4,128]{3,2,1,0:T(4,128)S(1)}, u32[]{:S(2)}, u32[]{:S(2)}) %all-to-all-start.7) | async-done | bytes 163872 | tf_op jit(solution)/shard_map/all_to_all | solution.py:993
  151.3 1.2 merge.3
  152.6 0.7 collective-permute-start.21
  153.2 2.4 %step_back_load.3 = (f32[16,8,128]{2,1,0:T(8,128)S(1)}, f32[5,1,1920]{2,1,0:T(1,128)S(1)}, f32[5,4,8,1920]{3,2,1,0:T(8,128)S(1)}, f32[5,4,8,1920]{3,2,1,0:T(8,12...) custom-call(f32[16,8,128]{2,1,0:T(8,128)} %get-tuple-element.147.refs_0_, ...), custom_call_target="tpu_custom_call" | custom-call | tf_op jit(solution)/shard_map/step_back_load/pallas_call | solution.py:965
  155.6 2.4 %step_back_sums.1 = (f32[5,4,8,1920]{3,2,1,0:T(8,128)}, f32[16,128]{1,0:T(8,128)}) custom-call(f32[480,128]{1,0:T(8,128)S(1)} %collective-permute-done.18.refs_0_, f32[480,128]{1,0:T(8,128)S(1)} %collective-permute-done.19.refs_1_, f32[60,128]{1,0:T(8,128)S(1)} %collective-permute-done.20.refs_2_, f32[60,128]{1,0:T(8,128)S(1)} %collective-permute-done.21.refs_3_, ...), custom_call_target="tpu_custom_call" | custom-call | tf_op jit(solution)/shard_map/step_back_sums/pallas_call | solution.py:965
  158.1 5.4 %all-to-all-start.8 = ((f32[16,1,128]{2,1,0:T(1,128)}), f32[16,1,128]{2,1,0:T(1,128)S(1)}, u32[]{:S(2)}, u32[]{:S(2)}) async-start(f32[16,1,128]{2,1,0:T(1,128)} %bitcast.64), calls=%async_computation.8 | async-start | bytes 16384 | tf_op jit(solution)/shard_map/all_to_all | solution.py:1230
  163.5 1.7 copy.20
  165.2 4.7 %all-to-all-done.8 = f32[16,1,128]{2,1,0:T(1,128)S(1)} async-done(((f32[16,1,128]{2,1,0:T(1,128)}), f32[16,1,128]{2,1,0:T(1,128)S(1)}, u32[]{:S(2)}, u32[]{:S(2)}) %all-to-all-start.8) | async-done | bytes 8224 | tf_op jit(solution)/shard_map/all_to_all | solution.py:1230
  169.8 1.2 finish.1
  (59 shorter events, 0.5 us)
Async XLA Ops:
  0.0 2.9 %copy-start.5 = (f32[4,4]{1,0:T(4,128)S(1)}, f32[4,4]{1,0:T(4,128)}, u32[]{:S(2)}) copy-start(f32[4,4]{1,0:T(4,128)} %param.21) | copy-start | bytes 196
  0.0 2.9 %copy-start.7 = (s32[15]{0:T(128)S(1)}, s32[15]{0:T(128)}, u32[]{:S(2)}) copy-start(s32[15]{0:T(128)} %param.28) | copy-start | bytes 184
  0.0 2.9 %copy-start.6 = (s32[15]{0:T(128)S(1)}, s32[15]{0:T(128)}, u32[]{:S(2)}) copy-start(s32[15]{0:T(128)} %param.27) | copy-start | bytes 184
  0.0 3.0 %copy-start.12 = (f32[15]{0:T(128)S(1)}, f32[15]{0:T(128)}, u32[]{:S(2)}) copy-start(f32[15]{0:T(128)} %param.29) | copy-start | bytes 184
  1.6 5.3 %collective-permute-start = (f32[480,128]{1,0:T(8,128)S(1)}, f32[480,128]{1,0:T(8,128)S(1)}, u32[]{:S(2)}, u32[]{:S(2)}) collective-permute-start(f32[480,128]{1,0:T(8,128)S(1)} %get-tuple-element.119), channel_id=1, source_target_pairs={{0,1},{1,0},{2,3},{3,2},{4,5},{5,4},{6,7},{7,6},{8,9},{9,8},{10,11... | collective-permute-start | bytes 737288 | tf_op jit(solution)/shard_map/ppermute | solution.py:986
  2.2 4.8 %collective-permute-start.1 = (f32[480,128]{1,0:T(8,128)S(1)}, f32[480,128]{1,0:T(8,128)S(1)}, u32[]{:S(2)}, u32[]{:S(2)}) collective-permute-start(f32[480,128]{1,0:T(8,128)S(1)} %get-tuple-element.120), channel_id=1, source_target_pairs={{1,2},{3,4},{5,6},{7,8},{9,10},{11,12},{13,14},{2,1},{4,3},{6,5},{... | collective-permute-start | bytes 737288 | tf_op jit(solution)/shard_map/ppermute | solution.py:986
  3.0 2.0 %copy-start.13 = (s32[1,75]{1,0:T(1,128)S(1)}, s32[1,75]{1,0:T(1,128)}, u32[]{:S(2)}) copy-start(s32[1,75]{1,0:T(1,128)} %param.25) | copy-start | bytes 904
  3.0 2.1 %copy-start.14 = (s32[1,75]{1,0:T(1,128)S(1)}, s32[1,75]{1,0:T(1,128)}, u32[]{:S(2)}) copy-start(s32[1,75]{1,0:T(1,128)} %param.26) | copy-start | bytes 904
  3.1 2.2 %copy-start.2 = (f32[8,4,4]{0,2,1:T(4,128)S(1)}, f32[8,4,4]{0,2,1:T(4,128)}, u32[]{:S(2)}) copy-start(f32[8,4,4]{0,2,1:T(4,128)} %param.20) | copy-start | bytes 1540
  5.1 17.2 %copy-start.3 = (f32[2,1,80,128]{3,2,1,0:T(8,128)S(1)}, f32[2,1,80,128]{3,2,1,0:T(8,128)}, u32[]{:S(2)}) copy-start(f32[2,1,80,128]{3,2,1,0:T(8,128)} %param.24) | copy-start | bytes 245764
  5.1 17.2 %copy-start.4 = (f32[2,1,80,128]{3,2,1,0:T(8,128)S(1)}, f32[2,1,80,128]{3,2,1,0:T(8,128)}, u32[]{:S(2)}) copy-start(f32[2,1,80,128]{3,2,1,0:T(8,128)} %param.23) | copy-start | bytes 245764
  6.9 22.7 %copy-start.1 = (f32[1,80,80]{2,1,0:T(8,128)S(1)}, f32[1,80,80]{2,1,0:T(8,128)}, u32[]{:S(2)}) copy-start(f32[1,80,80]{2,1,0:T(8,128)} %param.22) | copy-start | bytes 76804
  9.6 25.6 %copy-start.9 = (f32[480,128]{1,0:T(8,128)S(1)}, f32[480,128]{1,0:T(8,128)}, u32[]{:S(2)}) copy-start(f32[480,128]{1,0:T(8,128)} %get-tuple-element.145) | copy-start | bytes 737284
  9.6 26.0 %copy-start.8 = (f32[480,128]{1,0:T(8,128)S(1)}, f32[480,128]{1,0:T(8,128)}, u32[]{:S(2)}) copy-start(f32[480,128]{1,0:T(8,128)} %get-tuple-element.146) | copy-start | bytes 737284
  9.6 20.0 %all-to-all-start = ((f32[16,5,4,128]{3,2,1,0:T(4,128)}), f32[16,5,4,128]{3,2,1,0:T(4,128)S(1)}, u32[]{:S(2)}, u32[]{:S(2)}) async-start(f32[16,5,4,128]{3,2,1,0:T(4,128)} %bitcast.62), calls=%async_computation | async-start | bytes 327680 | tf_op jit(solution)/shard_map/all_to_all | solution.py:993
  21.2 1.5 collective-permute-start.2
  21.6 1.1 collective-permute-start.3
  31.7 13.3 %all-to-all-start.1 = ((f32[16,15,2,128]{3,2,1,0:T(2,128)}), f32[16,15,2,128]{3,2,1,0:T(2,128)S(1)}, u32[]{:S(2)}, u32[]{:S(2)}) async-start(f32[16,15,2,128]{3,2,1,0:T(2,128)} %bitcast.61), calls=%async_computation.1 | async-start | bytes 491520 | tf_op jit(solution)/shard_map/all_to_all | solution.py:993
  35.2 14.3 %collective-permute-start.4 = (f32[480,128]{1,0:T(8,128)S(1)}, f32[480,128]{1,0:T(8,128)S(1)}, u32[]{:S(2)}, u32[]{:S(2)}) collective-permute-start(f32[480,128]{1,0:T(8,128)S(1)} %copy-done.9), channel_id=1, source_target_pairs={{0,1},{1,0},{2,3},{3,2},{4,5},{5,4},{6,7},{7,6},{8,9},{9,8},{10,11... | collective-permute-start | bytes 737288 | tf_op jit(solution)/shard_map/ppermute | solution.py:986
  35.6 14.0 %collective-permute-start.5 = (f32[480,128]{1,0:T(8,128)S(1)}, f32[480,128]{1,0:T(8,128)S(1)}, u32[]{:S(2)}, u32[]{:S(2)}) collective-permute-start(f32[480,128]{1,0:T(8,128)S(1)} %copy-done.8), channel_id=1, source_target_pairs={{1,2},{3,4},{5,6},{7,8},{9,10},{11,12},{13,14},{2,1},{4,3},{6,5},{... | collective-permute-start | bytes 737288 | tf_op jit(solution)/shard_map/ppermute | solution.py:986
  46.8 2.7 %collective-permute-start.6 = (f32[60,128]{1,0:T(8,128)S(1)}, f32[60,128]{1,0:T(8,128)S(1)}, u32[]{:S(2)}, u32[]{:S(2)}) collective-permute-start(f32[60,128]{1,0:T(8,128)S(1)} %get-tuple-element.156), channel_id=1, source_target_pairs={{0,1},{1,0},{2,3},{3,2},{4,5},{5,4},{6,7},{7,6},{8,9},{9,8},{10,11... | collective-permute-start | bytes 92168 | tf_op jit(solution)/shard_map/ppermute | solution.py:986
  46.9 2.6 %collective-permute-start.7 = (f32[60,128]{1,0:T(8,128)S(1)}, f32[60,128]{1,0:T(8,128)S(1)}, u32[]{:S(2)}, u32[]{:S(2)}) collective-permute-start(f32[60,128]{1,0:T(8,128)S(1)} %get-tuple-element.157), channel_id=1, source_target_pairs={{1,2},{3,4},{5,6},{7,8},{9,10},{11,12},{13,14},{2,1},{4,3},{6,5},{... | collective-permute-start | bytes 92168 | tf_op jit(solution)/shard_map/ppermute | solution.py:986
  52.3 15.0 %all-to-all-start.2 = ((f32[16,5,4,128]{3,2,1,0:T(4,128)}), f32[16,5,4,128]{3,2,1,0:T(4,128)S(1)}, u32[]{:S(2)}, u32[]{:S(2)}) async-start(f32[16,5,4,128]{3,2,1,0:T(4,128)} %bitcast.63), calls=%async_computation.2 | async-start | bytes 327680 | tf_op jit(solution)/shard_map/all_to_all | solution.py:993
  58.9 1.5 collective-permute-start.8
  59.3 1.1 collective-permute-start.9
  69.0 13.3 %all-to-all-start.3 = ((f32[16,15,2,128]{3,2,1,0:T(2,128)}), f32[16,15,2,128]{3,2,1,0:T(2,128)S(1)}, u32[]{:S(2)}, u32[]{:S(2)}) async-start(f32[16,15,2,128]{3,2,1,0:T(2,128)} %bitcast.60), calls=%async_computation.3 | async-start | bytes 491520 | tf_op jit(solution)/shard_map/all_to_all | solution.py:993
  72.6 3.3 %collective-permute-start.10 = (f32[480,128]{1,0:T(8,128)}, f32[480,128]{1,0:T(8,128)S(1)}, u32[]{:S(2)}, u32[]{:S(2)}) collective-permute-start(f32[480,128]{1,0:T(8,128)} %get-tuple-element.169), channel_id=1, source_target_pairs={{0,1},{1,0},{2,3},{3,2},{4,5},{5,4},{6,7},{7,6},{8,9},{9,8},{10,11... | collective-permute-start | bytes 737288 | tf_op jit(solution)/shard_map/ppermute | solution.py:986
  72.9 3.0 %collective-permute-start.11 = (f32[480,128]{1,0:T(8,128)}, f32[480,128]{1,0:T(8,128)S(1)}, u32[]{:S(2)}, u32[]{:S(2)}) collective-permute-start(f32[480,128]{1,0:T(8,128)} %get-tuple-element.170), channel_id=1, source_target_pairs={{1,2},{3,4},{5,6},{7,8},{9,10},{11,12},{13,14},{2,1},{4,3},{6,5},{... | collective-permute-start | bytes 737288 | tf_op jit(solution)/shard_map/ppermute | solution.py:986
  84.7 16.3 %all-to-all-start.4 = ((f32[16,15,2,128]{3,2,1,0:T(2,128)}), f32[16,15,2,128]{3,2,1,0:T(2,128)S(1)}, u32[]{:S(2)}, u32[]{:S(2)}) async-start(f32[16,15,2,128]{3,2,1,0:T(2,128)} %bitcast.59), calls=%async_computation.4 | async-start | bytes 491520 | tf_op jit(solution)/shard_map/all_to_all | solution.py:993
  91.2 1.5 collective-permute-start.12
  91.6 1.1 collective-permute-start.13
  116.1 2.7 %collective-permute-start.14 = (f32[60,128]{1,0:T(8,128)S(1)}, f32[60,128]{1,0:T(8,128)S(1)}, u32[]{:S(2)}, u32[]{:S(2)}) collective-permute-start(f32[60,128]{1,0:T(8,128)S(1)} %get-tuple-element.191), channel_id=1, source_target_pairs={{0,1},{1,0},{2,3},{3,2},{4,5},{5,4},{6,7},{7,6},{8,9},{9,8},{10,11... | collective-permute-start | bytes 92168 | tf_op jit(solution)/shard_map/ppermute | solution.py:986
  116.2 2.7 %collective-permute-start.15 = (f32[60,128]{1,0:T(8,128)S(1)}, f32[60,128]{1,0:T(8,128)S(1)}, u32[]{:S(2)}, u32[]{:S(2)}) collective-permute-start(f32[60,128]{1,0:T(8,128)S(1)} %get-tuple-element.192), channel_id=1, source_target_pairs={{1,2},{3,4},{5,6},{7,8},{9,10},{11,12},{13,14},{2,1},{4,3},{6,5},{... | collective-permute-start | bytes 92168 | tf_op jit(solution)/shard_map/ppermute | solution.py:986
  121.6 21.3 %copy-start.11 = (f32[480,128]{1,0:T(8,128)S(1)}, f32[480,128]{1,0:T(8,128)}, u32[]{:S(2)}) copy-start(f32[480,128]{1,0:T(8,128)} %get-tuple-element.209) | copy-start | bytes 737284
  121.6 21.6 %copy-start.10 = (f32[480,128]{1,0:T(8,128)S(1)}, f32[480,128]{1,0:T(8,128)}, u32[]{:S(2)}) copy-start(f32[480,128]{1,0:T(8,128)} %get-tuple-element.210) | copy-start | bytes 737284
  121.6 15.7 %all-to-all-start.6 = ((f32[16,15,2,128]{3,2,1,0:T(2,128)}), f32[16,15,2,128]{3,2,1,0:T(2,128)S(1)}, u32[]{:S(2)}, u32[]{:S(2)}) async-start(f32[16,15,2,128]{3,2,1,0:T(2,128)} %bitcast.58), calls=%async_computation.6 | async-start | bytes 491520 | tf_op jit(solution)/shard_map/all_to_all | solution.py:993
  127.5 1.8 %collective-permute-start.16 = (f32[32,128]{1,0:T(8,128)}, f32[32,128]{1,0:T(8,128)S(1)}, u32[]{:S(2)}, u32[]{:S(2)}) collective-permute-start(f32[32,128]{1,0:T(8,128)} %get-tuple-element.202), channel_id=1, source_target_pairs={{0,1},{1,0},{2,3},{3,2},{4,5},{5,4},{6,7},{7,6},{8,9},{9,8},{10,11... | collective-permute-start | bytes 49160 | tf_op jit(solution)/shard_map/ppermute | solution.py:986
  128.3 1.1 collective-permute-start.17
  139.3 12.0 %all-to-all-start.7 = ((f32[16,5,4,128]{3,2,1,0:T(4,128)}), f32[16,5,4,128]{3,2,1,0:T(4,128)S(1)}, u32[]{:S(2)}, u32[]{:S(2)}) async-start(f32[16,5,4,128]{3,2,1,0:T(4,128)} %bitcast.56), calls=%async_computation.7 | async-start | bytes 327680 | tf_op jit(solution)/shard_map/all_to_all | solution.py:993
  142.9 12.7 %collective-permute-start.18 = (f32[480,128]{1,0:T(8,128)S(1)}, f32[480,128]{1,0:T(8,128)S(1)}, u32[]{:S(2)}, u32[]{:S(2)}) collective-permute-start(f32[480,128]{1,0:T(8,128)S(1)} %copy-done.11), channel_id=1, source_target_pairs={{0,1},{1,0},{2,3},{3,2},{4,5},{5,4},{6,7},{7,6},{8,9},{9,8},{10,11... | collective-permute-start | bytes 737288 | tf_op jit(solution)/shard_map/ppermute | solution.py:986
  143.2 12.4 %collective-permute-start.19 = (f32[480,128]{1,0:T(8,128)S(1)}, f32[480,128]{1,0:T(8,128)S(1)}, u32[]{:S(2)}, u32[]{:S(2)}) collective-permute-start(f32[480,128]{1,0:T(8,128)S(1)} %copy-done.10), channel_id=1, source_target_pairs={{1,2},{3,4},{5,6},{7,8},{9,10},{11,12},{13,14},{2,1},{4,3},{6,5},{... | collective-permute-start | bytes 737288 | tf_op jit(solution)/shard_map/ppermute | solution.py:986
  152.5 3.1 %collective-permute-start.20 = (f32[60,128]{1,0:T(8,128)S(1)}, f32[60,128]{1,0:T(8,128)S(1)}, u32[]{:S(2)}, u32[]{:S(2)}) collective-permute-start(f32[60,128]{1,0:T(8,128)S(1)} %get-tuple-element.215), channel_id=1, source_target_pairs={{0,1},{1,0},{2,3},{3,2},{4,5},{5,4},{6,7},{7,6},{8,9},{9,8},{10,11... | collective-permute-start | bytes 92168 | tf_op jit(solution)/shard_map/ppermute | solution.py:986
  152.6 3.1 %collective-permute-start.21 = (f32[60,128]{1,0:T(8,128)S(1)}, f32[60,128]{1,0:T(8,128)S(1)}, u32[]{:S(2)}, u32[]{:S(2)}) collective-permute-start(f32[60,128]{1,0:T(8,128)S(1)} %get-tuple-element.216), channel_id=1, source_target_pairs={{1,2},{3,4},{5,6},{7,8},{9,10},{11,12},{13,14},{2,1},{4,3},{6,5},{... | collective-permute-start | bytes 92168 | tf_op jit(solution)/shard_map/ppermute | solution.py:986
  158.1 11.8 %all-to-all-start.8 = ((f32[16,1,128]{2,1,0:T(1,128)}), f32[16,1,128]{2,1,0:T(1,128)S(1)}, u32[]{:S(2)}, u32[]{:S(2)}) async-start(f32[16,1,128]{2,1,0:T(1,128)} %bitcast.64), calls=%async_computation.8 | async-start | bytes 16384 | tf_op jit(solution)/shard_map/all_to_all | solution.py:1230
  163.4 6.4 %copy-start = (f32[8,5,4,1920]{3,2,1,0:T(4,128)S(1)}, f32[8,5,4,1920]{3,2,1,0:T(4,128)}, u32[]{:S(2)}) copy-start(f32[8,5,4,1920]{3,2,1,0:T(4,128)} %refs_1_.6) | copy-start | bytes 3686404

commit v6 on v5

--- a/solution.py
+++ b/solution.py
@@ -50,6 +50,7 @@
         self.slope = (NEAR_LAT * self.pitch, WIDTH)
         self.lats = (self.lat_lines, WIDTH)
         self.bulk_at = NEAR_LAT * rows
+        self.drive_at = self.bulk_at + CHANNELS * CHANNELS
         self.tables = (3 * self.slot_lines, WIDTH)
         self.weights = (3 * self.facts, WIDTH)
         self.near = (-(-(self.tiles + 1) // SUBLANES) * SUBLANES, WIDTH)
@@ -144,16 +145,21 @@
     return jnp.sum(jnp.where(diagonal, row, 0.0), axis=1, keepdims=True)
 
 
-def setup_kernel(sz, entries, remap_entries, arrive, wet, remap, mix_rows, diffusivity, *outs):
-    first_mix, first_rows, table, facts, mix = outs
+def setup_kernel(sz, entries, remap_entries, arrive, wet, remap, mix_rows, diffusivity, weight, *outs):
+    first_tiles, table, facts, mix, diffusivity_rows, weight_rows = outs
     arrive_all(arrive)
     for row in range(sz.rows):
-        first_rows[row] = diffusivity[row : row + 1, :]
+        diffusivity_rows[row] = diffusivity[row : row + 1, :]
+        weight_rows[row] = weight[row : row + 1, :]
+        for tile in range(sz.row_tiles):
+            at = row * sz.pitch + tile
+            first_tiles[at : at + 1, :] = diffusivity[row : row + 1, cols(tile)]
+    diffusivity_rows.start()
+    weight_rows.start()
     for index in range(CHANNELS * CHANNELS):
         column = as_column(mix_rows[index : index + 1, :], LEVELS)
         mix[index] = jnp.broadcast_to(column, (LEVELS, WIDTH))
     mix.start()
-    first_mix[...] = mix[...]
     tiles, owners = wet[0:1, :], wet[1:2, :]
     size = -(-entries // SUBLANES) * SUBLANES
     shape = (size, wet.shape[1])
@@ -177,19 +183,68 @@
     )
 
 
-def columns_kernel(sz, arrive, diffusivity, weight, *outs):
-    diffusivity_rows, weight_rows, diffusivity_tiles, weight_tiles = outs
+def columns_kernel(sz, arrive, diffusivity, weight, diffusivity_tiles, weight_tiles):
     arrive_all(arrive)
-    for source, by_row, by_tile in (
-        (diffusivity, diffusivity_rows, diffusivity_tiles),
-        (weight, weight_rows, weight_tiles),
-    ):
+    for source, by_tile in ((diffusivity, diffusivity_tiles), (weight, weight_tiles)):
         for row in range(sz.rows):
-            by_row[row] = source[row : row + 1, :]
             for tile in range(sz.row_tiles):
                 line = source[row : row + 1, cols(tile)]
                 at = (row * sz.row_tiles + tile) * CHANNELS
                 by_tile[at : at + CHANNELS, :] = jnp.broadcast_to(line, (CHANNELS, WIDTH))
+
+
+def front_load_kernel(sz, arrive, perturbation, base, level_0, level_1, send_first, send_second):
+    arrive_all(arrive)
+    for level, out in ((0, level_0), (1, level_1)):
+        for row in range(sz.rows):
+            for tile in range(sz.row_tiles):
+                at = (row * sz.row_tiles + tile) * CHANNELS
+                out[at : at + CHANNELS, :] = (
+                    perturbation[level, row, :, cols(tile)] + base[level, row, :, cols(tile)]
+                )
+        out[CHANNELS * sz.tiles :, :] = jnp.zeros((CHANNELS, WIDTH), jnp.float32)
+    store_rows(sz, level_0, send_first, send_second)
+
+
+def front_kernel(sz, arrive, tables, facts, facts_block, level_0, level_1, first, second, diffusivity, *refs):
+    new_surface, packed, tell_first, tell_second, before, after = refs
+    arrive_all(arrive)
+    count, pitch = sz.row_tiles, sz.pitch
+    lane = lax.broadcasted_iota(jnp.int32, (count, WIDTH), 1)
+
+    def part(ref, row, channel, size=count):
+        return ref[pl.ds(row * sz.row_width + channel, size, stride=CHANNELS), :]
+
+    beside = [sided(part(first, 0, c), part(second, 0, c)) for c in range(CHANNELS)]
+    for row in range(sz.rows):
+        coeff = diffusivity[row * pitch : row * pitch + count, :]
+        center = (1.0 - 2.0 * KAPPA_V) - 4.0 * coeff
+        here = [part(level_0, row, c) for c in range(CHANNELS)]
+        for c in range(CHANNELS):
+            weights = [facts[sz.slot_lines, sz.drive_at + c * CHANNELS + k] for k in range(CHANNELS)]
+            bent = jnp.tanh(sum_of(weights, here))
+            up = part(level_0, row - 1, c) if row > 0 else beside[c][0]
+            down = part(level_0, row + 1, c) if row < sz.rows - 1 else beside[c][1]
+            index = row * CHANNELS + c
+            full = part(level_0, row, c, pitch)
+            left = pltpu.roll(full, 1, 1)[0:count, :]
+            right = pltpu.roll(full, WIDTH - 1, 1)[0:count, :]
+            before[index, 1 : count + 1, :] = left
+            before[index, 0:1, :] = left[count - 1 : count, :]
+            after[index, 0:count, :] = right
+            after[index, count : count + 1, :] = right[0:1, :]
+            around = lanes_sum(
+                left, before[index, 0:count, :], right, after[index, 1 : count + 1, :], lane
+            )
+            around = around + (up + down)
+            stepped = (
+                center * here[c]
+                + coeff * around
+                + KAPPA_V * part(level_1, row, c)
+                + TIME_STEP * bent
+            )
+            new_surface.block[pl.ds(row * sz.row_width + c, count, stride=CHANNELS), :] = stepped
+    share_surface(sz, tables, facts, new_surface, packed, tell_first, tell_second, facts_block)
 
 
 def gather_levels(block, channel, tile):
@@ -361,7 +416,7 @@
         copies = [pltpu.make_async_copy(field.at[row], field_out.at[row], in_sems.at[0, row])]
         if last:
             copies.append(
-                pltpu.make_async_copy(target.at[row], target_out.at[row], in_sems.at[1, row])
+                pltpu.make_async_copy(target.at[:, row], refs[1].at[row], in_sems.at[1, row])
             )
         return copies
 
@@ -378,6 +433,10 @@
         for arrival in arrivals(row):
             arrival.wait()
         load_surface_row(sz, field_out, row, surface, row * sz.row_width)
+        if last:
+            for c in range(CHANNELS):
+                for t in range(sz.row_tiles):
+                    target_out[row, c, :, cols(t)] = gather_levels(refs[1].at[row], c, t)
         return carry
 
     lax.fori_loop(0, sz.rows, one_row, 0)
@@ -385,19 +444,25 @@
 
 def forward_kernel(sz, first, last, arrive, *refs):
     refs = list(refs)
-    tables, facts, low, high, diffusivity, mix, field = refs[:7]
-    refs = refs[7:]
-    if first:
-        facts_block = refs.pop(0)
+    if not first:
+        tables, facts = refs[:2]
+        refs = refs[2:]
+    low, high, diffusivity, mix, field = refs[:5]
+    refs = refs[5:]
     surfaces = ()
     if not first:
         surfaces = refs[:2]
         refs = refs[2:]
+    else:
+        arrive_all(arrive)
     if last:
         weight, target = refs[:2]
         refs = refs[2:]
-    out, drive, new_surface, packed, tell_first, tell_second, edge_first, edge_second, padded = refs
-    remap = Remap(sz, facts)
+    out, drive, *refs = refs
+    if not first:
+        new_surface, packed, tell_first, tell_second = refs[:4]
+        refs = refs[4:]
+    edge_first, edge_second, padded = refs
     place_edges(sz, padded, low, high, *surfaces)
 
     def ready(row):
@@ -441,7 +506,9 @@
                     + KAPPA_V * levels_sum(field_here, sub)
                     + TIME_STEP * bent
                 )
-                new_surface[pl.ds((row * count + t) * CHANNELS + c, 1), :] = stepped[0:1, :]
+                if not first:
+                    at = (row * count + t) * CHANNELS + c
+                    new_surface[pl.ds(at, 1), :] = stepped[0:1, :]
                 if last:
                     stepped = scale * (stepped - target[row, c, :, cols(t)])
                 out[row, c, :, cols(t)] = stepped
@@ -450,18 +517,24 @@
         return carry
 
     lax.fori_loop(0, sz.rows, one_row, 0)
-    new_surface[CHANNELS * sz.tiles :, :] = jnp.zeros((CHANNELS, WIDTH), jnp.float32)
-    new_surface.start()
-    arrive_all(arrive)
-    pack_slots(sz, tables, new_surface, packed)
+    if not first:
+        arrive_all(arrive)
+        share_surface(sz, tables, facts, new_surface, packed, tell_first, tell_second)
+    store_edges(sz, out, diffusivity if last else None, edge_first, edge_second)
+
+
+def share_surface(sz, tables, facts, surface, packed, tell_first, tell_second, facts_block=None):
+    remap = Remap(sz, facts)
+    surface[CHANNELS * sz.tiles :, :] = jnp.zeros((CHANNELS, WIDTH), jnp.float32)
+    surface.start()
+    pack_slots(sz, tables, surface, packed)
     packed.start()
-    own = [row_tiles_of(sz, new_surface.block, row) for row in range(sz.rows)]
+    own = [row_tiles_of(sz, surface.block, row) for row in range(sz.rows)]
     send_sums(sz, own_sums(sz, remap, own, 1.0), tell_first, tell_second)
     for tell in (tell_first, tell_second):
-        if first:
+        if facts_block is not None:
             tell[sz.lat_lines :, :] = facts_block[...]
         tell.start()
-    store_edges(sz, out, diffusivity if last else None, edge_first, edge_second)
 
 
 def pack_slots(sz, tables, surface, packed):
@@ -883,7 +956,11 @@
 
     def block(self):
         whole = self.array.shape
-        taken = [size for size, index in zip(whole, self.at) if isinstance(index, slice)]
+        taken = [
+            len(range(*index.indices(size)))
+            for size, index in zip(whole, self.at)
+            if isinstance(index, slice)
+        ]
         return self.fetch((*taken, *whole[len(self.at) :]), self.array.dtype)
 
 
@@ -1017,54 +1094,67 @@
     rows = sz.rows
     native_row = (LEVELS, CHANNELS, sz.cells)
 
+    row_surface = (sz.row_width, WIDTH)
+    level_0, level_1, *sends = call(
+        functools.partial(front_load_kernel, sz),
+        "front_load",
+        fetched(perturbation, base_state, at=(slice(0, 2),)),
+        kept=[sz.surface, sz.surface, row_surface, row_surface],
+    )
+    surface_edges = swap(*sends)
+    me = lax.axis_index("horiz").astype(jnp.int32)
+
+    def lined(first_row, second_row):
+        size = -(-first_row.shape[0] // WIDTH) * WIDTH
+        pair = jnp.stack([first_row.astype(jnp.float32), second_row.astype(jnp.float32)])
+        return jnp.pad(pair, ((0, 0), (0, size - pair.shape[1])), constant_values=-1.0)
+
+    places = jnp.arange(2 * CHANNELS * CHANNELS, dtype=jnp.int32) + sz.bulk_at
+    remap_at = (remap_tgt - (me * LAT_DEV - 1)) * rows + remap_src - me * rows
+    remap_lines = lined(
+        jnp.concatenate([remap_at, places]),
+        jnp.concatenate([remap_weight, coupler_mix.reshape(-1), chan_mix[0].reshape(-1)]),
+    )
+    mix_rows = chan_mix.transpose(1, 2, 0).reshape(CHANNELS * CHANNELS, LEVELS)
+    row_lines = (rows, 1, sz.cells)
+    tiles_lines = (CHANNELS * sz.tiles, WIDTH)
+    first_tiles, table, facts, mix, diffusivity_rows, weight_rows = call(
+        functools.partial(setup_kernel, sz, wet_list.shape[1], remap_at.shape[0] + places.shape[0]),
+        "setup",
+        near_by(lined(wet_list[0], wet_owner[0]), remap_lines, mix_rows)
+        + fetched(diffusivity, cost_weight),
+        kept=[(rows * sz.pitch, WIDTH)],
+        shipped=[
+            jax.ShapeDtypeStruct((sz.slot_lines, WIDTH), jnp.int32),
+            (sz.facts, WIDTH),
+            (CHANNELS * CHANNELS, LEVELS, WIDTH),
+            row_lines,
+            row_lines,
+        ],
+    )
+    wider = (rows + 2, CHANNELS, LEVELS, sz.cells)
+    by_row = (rows, *native_row)
+
+    def row_sems(kinds):
+        return pltpu.SemaphoreType.DMA((kinds, rows))
+
+    shifted = (rows * CHANNELS, sz.pitch + SUBLANES, WIDTH)
+    surface, packed, *sends = call(
+        functools.partial(front_kernel, sz),
+        "front",
+        scalars(table, facts)
+        + fetched(facts)
+        + near_by(level_0, level_1, *surface_edges, first_tiles),
+        shipped=[sz.surface, sz.narrow, sz.told, sz.told],
+        scratch=[shifted, shifted],
+    )
+    packed, perturbation, base_state = lax.optimization_barrier((packed, perturbation, base_state))
     edge_inputs = []
     for array in (perturbation, base_state):
         for row in (0, rows - 1):
             edge_inputs += fetched(array, at=(slice(None), row))
     edges = swap(
         *call(functools.partial(edges_kernel, sz), "edges", edge_inputs, kept=[sz.edge, sz.edge])
-    )
-    me = lax.axis_index("horiz").astype(jnp.int32)
-
-    def lined(first_row, second_row):
-        size = -(-first_row.shape[0] // WIDTH) * WIDTH
-        pair = jnp.stack([first_row.astype(jnp.float32), second_row.astype(jnp.float32)])
-        return jnp.pad(pair, ((0, 0), (0, size - pair.shape[1])), constant_values=-1.0)
-
-    places = jnp.arange(CHANNELS * CHANNELS, dtype=jnp.int32) + sz.bulk_at
-    remap_at = (remap_tgt - (me * LAT_DEV - 1)) * rows + remap_src - me * rows
-    remap_lines = lined(
-        jnp.concatenate([remap_at, places]),
-        jnp.concatenate([remap_weight, coupler_mix.reshape(-1)]),
-    )
-    mix_rows = chan_mix.transpose(1, 2, 0).reshape(CHANNELS * CHANNELS, LEVELS)
-    row_lines = (rows, 1, sz.cells)
-    tiles_lines = (CHANNELS * sz.tiles, WIDTH)
-    first_mix, first_rows, table, facts, mix = call(
-        functools.partial(setup_kernel, sz, wet_list.shape[1], remap_at.shape[0] + places.shape[0]),
-        "setup",
-        near_by(lined(wet_list[0], wet_owner[0]), remap_lines, mix_rows)
-        + fetched(diffusivity),
-        kept=[(CHANNELS * CHANNELS, LEVELS, WIDTH), row_lines],
-        shipped=[
-            jax.ShapeDtypeStruct((sz.slot_lines, WIDTH), jnp.int32),
-            (sz.facts, WIDTH),
-            (CHANNELS * CHANNELS, LEVELS, WIDTH),
-        ],
-    )
-    wider = (rows + 2, CHANNELS, LEVELS, sz.cells)
-    row_surface = (sz.row_width, WIDTH)
-    by_row = (rows, *native_row)
-
-    def row_sems(kinds):
-        return pltpu.SemaphoreType.DMA((kinds, rows))
-
-    (field,) = call(
-        functools.partial(load_kernel, sz),
-        "load",
-        far_off(perturbation, base_state),
-        kept=[sz.whole],
-        scratch=[by_row, by_row, row_sems(2)],
     )
 
     def relayout(array):
@@ -1082,30 +1172,27 @@
     by_slot = (sz.slots, WIDTH)
     for hour in range(hours):
         first, last = hour == 0, hour == hours - 1
-        inputs = scalars(table, facts)
-        if first:
-            inputs += near_by(*edges, first_rows, first_mix, field) + fetched(facts)
-            assert not last
-        else:
+        assert not (first and last)
+        if not first:
             loads = fetched(mix, diffusivity_rows, *([weight_rows] if last else []))
-            loads += far_off(field) + near_by(surface) + (far_off(target) if last else [])
+            loads += far_off(field) + near_by(surface) + (far_off(target_state) if last else [])
             mix_here, rows_here, field, *more = call(
                 functools.partial(forward_load_kernel, sz, last),
                 "step_load",
                 loads,
                 kept=[mix_shape, row_lines, sz.whole] + ([row_lines, sz.whole] if last else []),
-                scratch=[row_sems(2)],
-            )
-            inputs += near_by(*edges, rows_here, mix_here, field, *surface_edges, *more)
-        field, drive, surface, packed, *sends = call(
-            functools.partial(forward_kernel, sz, first, last),
-            "step",
-            inputs,
-            shipped=[sz.whole, sz.whole, sz.surface, sz.narrow]
-            + [sz.told if first else sz.lats] * 2
-            + [sz.edge] * 2,
-            scratch=[wider],
-        )
+                scratch=[row_sems(2)] + ([by_row] if last else []),
+            )
+            field, drive, surface, packed, *sends = call(
+                functools.partial(forward_kernel, sz, False, last),
+                "step",
+                scalars(table, facts)
+                + near_by(*edges, rows_here, mix_here, field, *surface_edges, *more),
+                shipped=[sz.whole, sz.whole, sz.surface, sz.narrow]
+                + [sz.lats] * 2
+                + [sz.edge] * 2,
+                scratch=[wider],
+            )
         arrived = exchange(packed, devices)
         got = swap(*sends[:2])
         arrived, *got = lax.optimization_barrier((arrived, *got))
@@ -1126,29 +1213,42 @@
         )
         if first:
             tables, weights = decoded
-        flux, *sends = lax.optimization_barrier((flux, *sends[2:]))
         if first:
-            flux, diffusivity, target_state = lax.optimization_barrier(
-                (flux, diffusivity, target_state)
-            )
-            beside = call(
+            flux, perturbation, base_state, *edges = lax.optimization_barrier(
+                (flux, perturbation, base_state, *edges)
+            )
+            (field,) = call(
+                functools.partial(load_kernel, sz),
+                "load",
+                far_off(perturbation, base_state),
+                kept=[sz.whole],
+                scratch=[by_row, by_row, row_sems(2)],
+            )
+            field, drive, *sends = call(
+                functools.partial(forward_kernel, sz, True, False),
+                "step",
+                fetched(*edges, diffusivity_rows, mix) + near_by(field),
+                shipped=[sz.whole, sz.whole, sz.edge, sz.edge],
+                scratch=[wider],
+            )
+            beside = [field, drive]
+        else:
+            flux, perturbation, diffusivity, *sends = lax.optimization_barrier(
+                (flux, perturbation, diffusivity, *sends[2:])
+            )
+            beside = relayout(perturbation) + call(
                 functools.partial(columns_kernel, sz),
                 "columns",
                 fetched(diffusivity, cost_weight),
-                shipped=[row_lines, row_lines, tiles_lines, tiles_lines],
-            ) + relayout(target_state)
-        else:
-            flux, perturbation = lax.optimization_barrier((flux, perturbation))
-            beside = relayout(perturbation)
+                shipped=[tiles_lines, tiles_lines],
+            )
         flux = exchange(flux, devices)
-        edges = swap(*sends)
-        if last:
-            flux, *edges = lax.optimization_barrier((flux, *edges))
         flux, *beside = lax.optimization_barrier((flux, *beside))
         if first:
-            diffusivity_rows, weight_rows, diffusivity_tiles, weight_tiles, target = beside
+            field, drive = beside
         else:
-            start_field = beside[0]
+            start_field, diffusivity_tiles, weight_tiles = beside
+        edges = swap(*sends)
         inputs = near_by(flux, *got) + fetched(surface) + scalars(tables, weights)
         if last:
             surface, slope, packed, *sends = call(

time: 173 us -> 172 us (level)
  blocking collectives: 11.9 us -> 0 us
  starting transfers between devices: 57.4 us -> 66.3 us
  Pallas kernels: 44 us -> 45.9 us
    all_to_all x1 -> x0, blocking collectives: 11.9 us -> none  [exchange(): lax.all_to_all(split, 'horiz', split_axis=0, concat_axis=0, tiled=True)]
    all_to_all x7 -> x8, starting transfers between devices: 41.1 us -> 46.1 us  [exchange(): lax.all_to_all(split, 'horiz', split_axis=0, concat_axis=0, tiled=True)]
    ppermute x11 -> x12, starting transfers between devices: 3.73 us -> 6.94 us  [swap(): lax.ppermute(first, 'horiz', inner)]
    pallas_call x22 -> x23, Pallas kernels: 44 us -> 45.9 us  [call(): pl.pallas_call(run, name=name, in_specs=[pl.BlockSpec(memory_space=item.s...]
    ppermute x11 -> x12, starting transfers between devices: 7.25 us -> 7.9 us  [swap(): lax.ppermute(second, 'horiz', outer)]
    all_to_all x7 -> x8, waiting for transfers between devices: 48.8 us -> 48.6 us  [exchange(): lax.all_to_all(split, 'horiz', split_axis=0, concat_axis=0, tiled=True)]
  transfers between devices with their start and end apart: 30 -> 33, of which waited for: 12 -> 13; matrix products, arithmetic and copies ran while one was open for 1% -> 1% of each run, Pallas kernels for 11% -> 15%
where the time goes in v6:
time: 172 us; the launch traced here: 170 us
  starting transfers between devices  66.3 us (39%)
  waiting for transfers between devices  54.8 us (32%)
  Pallas kernels  45.9 us (27%)
  local copies, waits for them, and re-layouts  2.06 us (1%)
    all_to_all x8, waiting for transfers between devices, exchange(): lax.all_to_all(split, 'horiz', split_axis=0, concat_axis=0, tiled=True)  48.6 us
    all_to_all x8, starting transfers between devices, exchange(): lax.all_to_all(split, 'horiz', split_axis=0, concat_axis=0, tiled=True)  46.1 us
    pallas_call x23, Pallas kernels, call(): pl.pallas_call(run, name=name, in_specs=[pl.BlockSpec(memory_space=item.s...  45.9 us
    ppermute x12, starting transfers between devices, swap(): lax.ppermute(second, 'horiz', outer)  7.9 us
    ppermute x12, starting transfers between devices, swap(): lax.ppermute(first, 'horiz', inner)  6.94 us
    all_to_all x1, starting transfers between devices, body(): lax.all_to_all(sums, 'horiz', split_axis=0, concat_axis=0, tiled=True)  5.36 us
    all_to_all x1, waiting for transfers between devices, body(): lax.all_to_all(sums, 'horiz', split_axis=0, concat_axis=0, tiled=True)  4.69 us
  transfers between devices with their start and end apart: 33, of which 13 were waited for; matrix products, arithmetic and copies ran while one was open for 1% of the time, Pallas kernels for 15%

profile of v6, /device:TPU:0, one launch (start us, length us, event | category | flops | bytes accessed | tf_op | source)
XLA Modules:
  0.0 170.0 jit_solution(6902838302996051192)
XLA Ops:
  0.0 1.2 front_load.1
  1.3 0.5 collective-permute-start
  1.8 0.7 collective-permute-start.1
  3.0 1.8 %setup.1 = (f32[80,128]{1,0:T(8,128)S(1)}, s32[1,128]{1,0:T(1,128)}, f32[8,128]{1,0:T(8,128)}, f32[16,8,128]{2,1,0:T(8,128)}, f32[5,1,1920]{2,1,0:T(1,128)}, /*index=5*/f32[5,1,1920]{2,1,0:T(1,128)}) custom-call(f32[2,128]{1,0:T(2,128)S(1)} %get-tuple-element.236.refs_0_, f32[2,128]{1,0:T(2,128)S(1)} %get-tuple-element.235.refs_1_, f32[16,8]{1,0:T(8,128)S(1)} %bitcast.55, ...), custom_call_target="tpu_custom_call" | custom-call | tf_op jit(solution)/shard_map/setup/pallas_call | solution.py:1042
  4.8 1.7 %front.1 = (f32[304,128]{1,0:T(8,128)}, f32[320,128]{1,0:T(8,128)}, f32[40,128]{1,0:T(8,128)}, f32[40,128]{1,0:T(8,128)}) custom-call(s32[1,128]{1,0:T(1,128)} %get-tuple-element.118.refs_0_.refs_7_.refs_5_, f32[8,128]{1,0:T(8,128)} %get-tuple-element.119.refs_1_.refs_2_.refs_4_.refs_8_.refs_6_, ...), custom_call_target="tpu_custom_call" | custom-call | tf_op jit(solution)/shard_map/front/pallas_call | solution.py:1042
  6.5 9.3 %all-to-all-start = ((f32[16,5,4,128]{3,2,1,0:T(4,128)}), f32[16,5,4,128]{3,2,1,0:T(4,128)S(1)}, u32[]{:S(2)}, u32[]{:S(2)}) async-start(f32[16,5,4,128]{3,2,1,0:T(4,128)} %bitcast.62), calls=%async_computation | async-start | bytes 327680 | tf_op jit(solution)/shard_map/all_to_all | solution.py:1070
  15.8 1.6 edges.1
  17.5 0.5 collective-permute-start.4
  18.0 0.7 collective-permute-start.5
  18.7 3.1 %collective-permute-start.2 = (f32[40,128]{1,0:T(8,128)S(1)}, f32[40,128]{1,0:T(8,128)S(1)}, u32[]{:S(2)}, u32[]{:S(2)}) collective-permute-start(f32[40,128]{1,0:T(8,128)S(1)} %copy-done.16), channel_id=1, source_target_pairs={{0,1},{1,0},{2,3},{3,2},{4,5},{5,4},{6,7},{7,6},{8,9},{9,8},{10,11... | collective-permute-start | bytes 61448 | tf_op jit(solution)/shard_map/ppermute | solution.py:1063
  21.7 0.7 collective-permute-start.3
  22.6 1.7 all-to-all-done
  24.3 2.0 %owners.2 = (s32[3,128]{1,0:T(4,128)}, f32[24,128]{1,0:T(8,128)}, f32[480,128]{1,0:T(8,128)}, f32[4,80,128]{2,1,0:T(8,128)}, f32[4,80,128]{2,1,0:T(8,128)}) custom-call(f32[320,128]{1,0:T(8,128)S(1)} %bitcast.52, f32[80,80]{1,0:T(8,128)S(1)} %bitcast.46, f32[80,128]{1,0:T(8,128)S(1)} %get-tuple-element.237.refs_2_, ...), custom_call_target="tpu_custom_call" | custom-call | tf_op jit(solution)/shard_map/owners/pallas_call | solution.py:1042
  26.3 9.1 %all-to-all-start.1 = ((f32[16,15,2,128]{3,2,1,0:T(2,128)}), f32[16,15,2,128]{3,2,1,0:T(2,128)S(1)}, u32[]{:S(2)}, u32[]{:S(2)}) async-start(f32[16,15,2,128]{3,2,1,0:T(2,128)} %bitcast.58), calls=%async_computation.1 | async-start | bytes 491520 | tf_op jit(solution)/shard_map/all_to_all | solution.py:1070
  35.5 2.0 %load.1.refs_4_ = f32[5,4,8,1920]{3,2,1,0:T(8,128)S(1)} custom-call(f32[8,5,4,1920]{3,2,1,0:T(4,128)} %refs_1_.6, f32[8,5,4,1920]{3,2,1,0:T(4,128)} %refs_1_.4), custom_call_target="tpu_custom_call" | custom-call | tf_op jit(solution)/shard_map/load/pallas_call | solution.py:1042
  37.5 3.5 %step.2 = (f32[5,4,8,1920]{3,2,1,0:T(8,128)}, f32[5,4,8,1920]{3,2,1,0:T(8,128)}, f32[480,128]{1,0:T(8,128)}, f32[480,128]{1,0:T(8,128)}) custom-call(f32[480,128]{1,0:T(8,128)} %copy-done.3, f32[480,128]{1,0:T(8,128)} %copy-done.4, f32[5,1,1920]{2,1,0:T(1,128)} %get-tuple-element.142.refs_2_.refs_1_, f32[16,8,128]{2,1,0:T(8,128)} %get-tuple-element.143.refs_3_.refs_0_, ...), custom_call_target="tpu_custom_call" | custom-call | tf_op jit(solution)/shard_map/step/pallas_call | solution.py:1042
  41.0 0.5 collective-permute-start.6
  41.4 0.7 collective-permute-start.7
  42.1 3.1 %all-to-all-done.1 = f32[16,15,2,128]{3,2,1,0:T(2,128)S(1)} async-done(((f32[16,15,2,128]{3,2,1,0:T(2,128)}), f32[16,15,2,128]{3,2,1,0:T(2,128)S(1)}, u32[]{:S(2)}, u32[]{:S(2)}) %all-to-all-start.1) | async-done | bytes 245792 | tf_op jit(solution)/shard_map/all_to_all | solution.py:1070
  45.3 1.9 %surface.2 = (f32[304,128]{1,0:T(8,128)S(1)}, f32[60,128]{1,0:T(8,128)S(1)}, f32[60,128]{1,0:T(8,128)S(1)}, f32[64,128]{1,0:T(8,128)}) custom-call(f32[480,128]{1,0:T(8,128)S(1)} %bitcast.42, f32[40,128]{1,0:T(8,128)S(1)} %collective-permute-done.2.refs_5_.refs_1_, f32[40,128]{1,0:T(8,128)S(1)} %collective-permute-done.3.refs_6_.refs_2_, ...), custom_call_target="tpu_custom_call" | custom-call | tf_op jit(solution)/shard_map/surface/pallas_call | solution.py:1042
  47.2 0.7 collective-permute-start.9
  47.9 2.3 %step_load.1 = (f32[16,8,128]{2,1,0:T(8,128)S(1)}, f32[5,1,1920]{2,1,0:T(1,128)S(1)}, f32[5,4,8,1920]{3,2,1,0:T(8,128)S(1)}, f32[5,1,1920]{2,1,0:T(1,128)S(1)}, f32[5,4,8,1920]{3,2,1,0:T(8,128)S(1)}) custom-call(f32[16,8,128]{2,1,0:T(8,128)} %get-tuple-element.143.refs_3_.refs_0_, f32[5,1,1920]{2,1,0:T(1,128)} %get-tuple-element.142.refs_2_.refs_1_, ...), custom_call_target="tpu_custom_call" | custom-call | tf_op jit(solution)/shard_map/step_load/pallas_call | solution.py:1042
  50.3 2.7 %step.3 = (f32[5,4,8,1920]{3,2,1,0:T(8,128)}, f32[5,4,8,1920]{3,2,1,0:T(8,128)}, f32[304,128]{1,0:T(8,128)}, f32[320,128]{1,0:T(8,128)}, f32[32,128]{1,0:T(8,128...) custom-call(s32[1,128]{1,0:T(1,128)} %get-tuple-element.118.refs_0_.refs_7_.refs_5_, ...), custom_call_target="tpu_custom_call" | custom-call | tf_op jit(solution)/shard_map/step/pallas_call | solution.py:1042
  53.0 7.6 %all-to-all-start.2 = ((f32[16,5,4,128]{3,2,1,0:T(4,128)}), f32[16,5,4,128]{3,2,1,0:T(4,128)S(1)}, u32[]{:S(2)}, u32[]{:S(2)}) async-start(f32[16,5,4,128]{3,2,1,0:T(4,128)} %bitcast.63), calls=%async_computation.2 | async-start | bytes 327680 | tf_op jit(solution)/shard_map/all_to_all | solution.py:1070
  60.6 0.4 collective-permute-start.10
  61.0 0.7 collective-permute-start.11
  61.7 0.4 collective-permute-done.10.refs_1_
  62.1 7.0 %all-to-all-done.2 = f32[16,5,4,128]{3,2,1,0:T(4,128)S(1)} async-done(((f32[16,5,4,128]{3,2,1,0:T(4,128)}), f32[16,5,4,128]{3,2,1,0:T(4,128)S(1)}, u32[]{:S(2)}, u32[]{:S(2)}) %all-to-all-start.2) | async-done | bytes 163872 | tf_op jit(solution)/shard_map/all_to_all | solution.py:1070
  69.1 1.7 owners.3
  70.8 3.5 %all-to-all-start.3 = ((f32[16,15,2,128]{3,2,1,0:T(2,128)}), f32[16,15,2,128]{3,2,1,0:T(2,128)S(1)}, u32[]{:S(2)}, u32[]{:S(2)}) async-start(f32[16,15,2,128]{3,2,1,0:T(2,128)} %bitcast.61), calls=%async_computation.3 | async-start | bytes 491520 | tf_op jit(solution)/shard_map/all_to_all | solution.py:1070
  74.3 1.7 columns.1
  76.0 2.3 %relayout.1.refs_5_ = f32[5,4,8,1920]{3,2,1,0:T(8,128)} custom-call(f32[8,5,4,1920]{3,2,1,0:T(4,128)} %refs_1_.6), custom_call_target="tpu_custom_call" | custom-call | tf_op jit(solution)/shard_map/relayout/pallas_call | solution.py:1042
  78.3 5.8 %all-to-all-done.3 = f32[16,15,2,128]{3,2,1,0:T(2,128)S(1)} async-done(((f32[16,15,2,128]{3,2,1,0:T(2,128)}), f32[16,15,2,128]{3,2,1,0:T(2,128)S(1)}, u32[]{:S(2)}, u32[]{:S(2)}) %all-to-all-start.3) | async-done | bytes 245792 | tf_op jit(solution)/shard_map/all_to_all | solution.py:1070
  84.1 2.3 %surface.3 = (f32[304,128]{1,0:T(8,128)}, f32[64,128]{1,0:T(8,128)}, f32[480,128]{1,0:T(8,128)}, f32[32,128]{1,0:T(8,128)}, f32[32,128]{1,0:T(8,128)}) custom-call(f32[480,128]{1,0:T(8,128)S(1)} %bitcast.45, f32[32,128]{1,0:T(8,128)S(1)} %collective-permute-done.10.refs_1_, f32[32,128]{1,0:T(8,128)S(1)} %collective-permute-done.11.refs_2_, ...), custom_call_target="tpu_custom_call" | custom-call | tf_op jit(solution)/shard_map/surface/pallas_call | solution.py:1042
  86.4 3.7 %all-to-all-start.4 = ((f32[16,15,2,128]{3,2,1,0:T(2,128)}), f32[16,15,2,128]{3,2,1,0:T(2,128)S(1)}, u32[]{:S(2)}, u32[]{:S(2)}) async-start(f32[16,15,2,128]{3,2,1,0:T(2,128)} %bitcast.60), calls=%async_computation.4 | async-start | bytes 491520 | tf_op jit(solution)/shard_map/all_to_all | solution.py:1070
  90.4 0.7 collective-permute-start.15
  91.1 0.5 collective-permute-done.14.refs_1_
  91.6 8.3 %all-to-all-done.4 = f32[16,15,2,128]{3,2,1,0:T(2,128)S(1)} async-done(((f32[16,15,2,128]{3,2,1,0:T(2,128)}), f32[16,15,2,128]{3,2,1,0:T(2,128)S(1)}, u32[]{:S(2)}, u32[]{:S(2)}) %all-to-all-start.4) | async-done | bytes 245792 | tf_op jit(solution)/shard_map/all_to_all | solution.py:1070
  99.8 2.1 %owners_back.2 = f32[320,128]{1,0:T(8,128)} custom-call(f32[480,128]{1,0:T(8,128)S(1)} %bitcast.43, f32[80,80]{1,0:T(8,128)S(1)} %bitcast.48, f32[4,80,128]{2,1,0:T(8,128)} %get-tuple-element.186.refs_2_, f32[4,80,128]{2,1,0:T(8,128)} %get-tuple-element.187.refs_3_, f32[8,128]{1,0:T(8,128)} %get-tuple-element.119.refs_1_.refs_2_.refs_4_.refs_8_.refs_6_), custom_call_target="tpu_custom_call" | custom-call | tf_op jit(solution)/shard_map/owners_back/pallas_call | solution.py:1042
  101.9 3.5 %all-to-all-start.5 = ((f32[16,5,4,128]{3,2,1,0:T(4,128)}), f32[16,5,4,128]{3,2,1,0:T(4,128)S(1)}, u32[]{:S(2)}, u32[]{:S(2)}) async-start(f32[16,5,4,128]{3,2,1,0:T(4,128)} %bitcast.56), calls=%async_computation.5 | async-start | bytes 327680 | tf_op jit(solution)/shard_map/all_to_all | solution.py:1070
  105.5 0.4 collective-permute-start.12
  105.8 0.7 collective-permute-start.13
  106.5 7.4 %all-to-all-done.5 = f32[16,5,4,128]{3,2,1,0:T(4,128)S(1)} async-done(((f32[16,5,4,128]{3,2,1,0:T(4,128)}), f32[16,5,4,128]{3,2,1,0:T(4,128)S(1)}, u32[]{:S(2)}, u32[]{:S(2)}) %all-to-all-start.5) | async-done | bytes 163872 | tf_op jit(solution)/shard_map/all_to_all | solution.py:1070
  113.9 1.2 merge.2
  115.2 0.7 collective-permute-start.17
  115.8 2.0 %step_back_load.2 = (f32[16,8,128]{2,1,0:T(8,128)S(1)}, f32[5,1,1920]{2,1,0:T(1,128)S(1)}, f32[5,4,8,1920]{3,2,1,0:T(8,128)S(1)}, f32[5,4,8,1920]{3,2,1,0:T(8,128)S(1)}, f32[5,4,8,1920]{3,2,1,0:T(8,128)S(1)}) custom-call(f32[16,8,128]{2,1,0:T(8,128)} %get-tuple-element.143.refs_3_.refs_0_, f32[5,1,1920]{2,1,0:T(1,128)} %get-tuple-element.142.refs_2_.refs_1_, ...), custom_call_target="tpu_custom_call" | custom-call | tf_op jit(solution)/shard_map/step_back_load/pallas_call | solution.py:1042
  117.9 2.7 %step_back.1 = (f32[5,4,8,1920]{3,2,1,0:T(8,128)}, f32[304,128]{1,0:T(8,128)}, f32[480,128]{1,0:T(8,128)}, f32[32,128]{1,0:T(8,128)}, f32[32,128]{1,0:T(8,128)}, /*index=5*/f32[480,128]{1,0:T(8,128)}, f32[480,128]{1,0:T(8,128)}) custom-call(s32[3,128]{1,0:T(4,128)} %get-tuple-element.132.refs_4_.refs_0_, f32[24,128]{1,0:T(8,128)} %get-tuple-element.133.refs_5_.refs_1_, ...), custom_call_target="tpu_custom_call" | custom-call | tf_op jit(solution)/shard_map/step_back/pallas_call | solution.py:1042
  120.5 5.9 %all-to-all-start.6 = ((f32[16,15,2,128]{3,2,1,0:T(2,128)}), f32[16,15,2,128]{3,2,1,0:T(2,128)S(1)}, u32[]{:S(2)}, u32[]{:S(2)}) async-start(f32[16,15,2,128]{3,2,1,0:T(2,128)} %bitcast.59), calls=%async_computation.6 | async-start | bytes 491520 | tf_op jit(solution)/shard_map/all_to_all | solution.py:1070
  126.4 0.8 collective-permute-start.18
  127.2 0.7 collective-permute-start.19
  127.8 0.4 collective-permute-done.18.refs_1_
  128.2 7.9 %all-to-all-done.6 = f32[16,15,2,128]{3,2,1,0:T(2,128)S(1)} async-done(((f32[16,15,2,128]{3,2,1,0:T(2,128)}), f32[16,15,2,128]{3,2,1,0:T(2,128)S(1)}, u32[]{:S(2)}, u32[]{:S(2)}) %all-to-all-start.6) | async-done | bytes 245792 | tf_op jit(solution)/shard_map/all_to_all | solution.py:1070
  136.2 2.0 %owners_back.3 = f32[320,128]{1,0:T(8,128)} custom-call(f32[480,128]{1,0:T(8,128)S(1)} %bitcast.44, f32[80,80]{1,0:T(8,128)S(1)} %bitcast.49, f32[4,80,128]{2,1,0:T(8,128)} %get-tuple-element.207.refs_2_, f32[4,80,128]{2,1,0:T(8,128)} %get-tuple-element.208.refs_3_, f32[8,128]{1,0:T(8,128)} %get-tuple-element.119.refs_1_.refs_2_.refs_4_.refs_8_.refs_6_), custom_call_target="tpu_custom_call" | custom-call | tf_op jit(solution)/shard_map/owners_back/pallas_call | solution.py:1042
  138.2 3.5 %all-to-all-start.7 = ((f32[16,5,4,128]{3,2,1,0:T(4,128)}), f32[16,5,4,128]{3,2,1,0:T(4,128)S(1)}, u32[]{:S(2)}, u32[]{:S(2)}) async-start(f32[16,5,4,128]{3,2,1,0:T(4,128)} %bitcast.57), calls=%async_computation.7 | async-start | bytes 327680 | tf_op jit(solution)/shard_map/all_to_all | solution.py:1070
  142.1 0.7 collective-permute-start.21
  142.8 7.4 %all-to-all-done.7 = f32[16,5,4,128]{3,2,1,0:T(4,128)S(1)} async-done(((f32[16,5,4,128]{3,2,1,0:T(4,128)}), f32[16,5,4,128]{3,2,1,0:T(4,128)S(1)}, u32[]{:S(2)}, u32[]{:S(2)}) %all-to-all-start.7) | async-done | bytes 163872 | tf_op jit(solution)/shard_map/all_to_all | solution.py:1070
  150.2 1.2 merge.3
  151.5 0.7 collective-permute-start.23
  152.1 2.4 %step_back_load.3 = (f32[16,8,128]{2,1,0:T(8,128)S(1)}, f32[5,1,1920]{2,1,0:T(1,128)S(1)}, f32[5,4,8,1920]{3,2,1,0:T(8,128)S(1)}, f32[5,4,8,1920]{3,2,1,0:T(8,12...) custom-call(f32[16,8,128]{2,1,0:T(8,128)} %get-tuple-element.143.refs_3_.refs_0_, ...), custom_call_target="tpu_custom_call" | custom-call | tf_op jit(solution)/shard_map/step_back_load/pallas_call | solution.py:1042
  154.5 2.4 %step_back_sums.1 = (f32[5,4,8,1920]{3,2,1,0:T(8,128)}, f32[16,128]{1,0:T(8,128)}) custom-call(f32[480,128]{1,0:T(8,128)S(1)} %collective-permute-done.20.refs_0_, f32[480,128]{1,0:T(8,128)S(1)} %collective-permute-done.21.refs_1_, f32[60,128]{1,0:T(8,128)S(1)} %collective-permute-done.22.refs_2_, f32[60,128]{1,0:T(8,128)S(1)} %collective-permute-done.23.refs_3_, ...), custom_call_target="tpu_custom_call" | custom-call | tf_op jit(solution)/shard_map/step_back_sums/pallas_call | solution.py:1042
  157.0 5.4 %all-to-all-start.8 = ((f32[16,1,128]{2,1,0:T(1,128)}), f32[16,1,128]{2,1,0:T(1,128)S(1)}, u32[]{:S(2)}, u32[]{:S(2)}) async-start(f32[16,1,128]{2,1,0:T(1,128)} %bitcast.64), calls=%async_computation.8 | async-start | bytes 16384 | tf_op jit(solution)/shard_map/all_to_all | solution.py:1330
  162.4 1.7 %copy.21 = f32[5,4,8,1920]{3,1,0,2:T(4,128)S(1)} copy(f32[5,4,8,1920]{3,2,1,0:T(8,128)} %get-tuple-element.230) | data formatting | bytes 2457600 | tf_op jit(solution)/shard_map/step_back_sums/pallas_call | solution.py:1042
  164.1 4.7 %all-to-all-done.8 = f32[16,1,128]{2,1,0:T(1,128)S(1)} async-done(((f32[16,1,128]{2,1,0:T(1,128)}), f32[16,1,128]{2,1,0:T(1,128)S(1)}, u32[]{:S(2)}, u32[]{:S(2)}) %all-to-all-start.8) | async-done | bytes 8224 | tf_op jit(solution)/shard_map/all_to_all | solution.py:1330
  168.8 1.2 finish.1
  (75 shorter events, 1.6 us)
Async XLA Ops:
  0.0 2.5 %copy-start.7 = (f32[4,4]{1,0:T(4,128)S(1)}, f32[4,4]{1,0:T(4,128)}, u32[]{:S(2)}) copy-start(f32[4,4]{1,0:T(4,128)} %param.21) | copy-start | bytes 196
  0.0 2.6 %copy-start.17 = (s32[1,75]{1,0:T(1,128)S(1)}, s32[1,75]{1,0:T(1,128)}, u32[]{:S(2)}) copy-start(s32[1,75]{1,0:T(1,128)} %param.25) | copy-start | bytes 904
  0.0 2.6 %copy-start.18 = (s32[1,75]{1,0:T(1,128)S(1)}, s32[1,75]{1,0:T(1,128)}, u32[]{:S(2)}) copy-start(s32[1,75]{1,0:T(1,128)} %param.26) | copy-start | bytes 904
  0.0 2.6 %copy-start.2 = (f32[8,4,4]{0,2,1:T(4,128)S(1)}, f32[8,4,4]{0,2,1:T(4,128)}, u32[]{:S(2)}) copy-start(f32[8,4,4]{0,2,1:T(4,128)} %param.20) | copy-start | bytes 1540
  0.0 2.8 %copy-start.9 = (s32[15]{0:T(128)S(1)}, s32[15]{0:T(128)}, u32[]{:S(2)}) copy-start(s32[15]{0:T(128)} %param.28) | copy-start | bytes 184
  0.0 2.8 %copy-start.8 = (s32[15]{0:T(128)S(1)}, s32[15]{0:T(128)}, u32[]{:S(2)}) copy-start(s32[15]{0:T(128)} %param.27) | copy-start | bytes 184
  0.0 2.8 %copy-start.10 = (f32[15]{0:T(128)S(1)}, f32[15]{0:T(128)}, u32[]{:S(2)}) copy-start(f32[15]{0:T(128)} %param.29) | copy-start | bytes 184
  1.3 3.5 %collective-permute-start = (f32[60,128]{1,0:T(8,128)S(1)}, f32[60,128]{1,0:T(8,128)S(1)}, u32[]{:S(2)}, u32[]{:S(2)}) collective-permute-start(f32[60,128]{1,0:T(8,128)S(1)} %get-tuple-element.122), channel_id=1, source_target_pairs={{0,1},{1,0},{2,3},{3,2},{4,5},{5,4},{6,7},{7,6},{8,9},{9,8},{10,11... | collective-permute-start | bytes 92168 | tf_op jit(solution)/shard_map/ppermute | solution.py:1063
  1.8 3.0 %collective-permute-start.1 = (f32[60,128]{1,0:T(8,128)S(1)}, f32[60,128]{1,0:T(8,128)S(1)}, u32[]{:S(2)}, u32[]{:S(2)}) collective-permute-start(f32[60,128]{1,0:T(8,128)S(1)} %get-tuple-element.123), channel_id=1, source_target_pairs={{1,2},{3,4},{5,6},{7,8},{9,10},{11,12},{13,14},{2,1},{4,3},{6,5},{... | collective-permute-start | bytes 92168 | tf_op jit(solution)/shard_map/ppermute | solution.py:1063
  6.5 17.7 %all-to-all-start = ((f32[16,5,4,128]{3,2,1,0:T(4,128)}), f32[16,5,4,128]{3,2,1,0:T(4,128)S(1)}, u32[]{:S(2)}, u32[]{:S(2)}) async-start(f32[16,5,4,128]{3,2,1,0:T(4,128)} %bitcast.62), calls=%async_computation | async-start | bytes 327680 | tf_op jit(solution)/shard_map/all_to_all | solution.py:1070
  15.8 2.9 %copy-start.16 = (f32[40,128]{1,0:T(8,128)S(1)}, f32[40,128]{1,0:T(8,128)}, u32[]{:S(2)}) copy-start(f32[40,128]{1,0:T(8,128)} %get-tuple-element.127) | copy-start | bytes 61444
  15.8 5.9 %copy-start.15 = (f32[40,128]{1,0:T(8,128)S(1)}, f32[40,128]{1,0:T(8,128)}, u32[]{:S(2)}) copy-start(f32[40,128]{1,0:T(8,128)} %get-tuple-element.128) | copy-start | bytes 61444
  15.8 6.6 %copy-start.5 = (f32[2,1,80,128]{3,2,1,0:T(8,128)S(1)}, f32[2,1,80,128]{3,2,1,0:T(8,128)}, u32[]{:S(2)}) copy-start(f32[2,1,80,128]{3,2,1,0:T(8,128)} %param.24) | copy-start | bytes 245764
  15.8 6.6 %copy-start.6 = (f32[2,1,80,128]{3,2,1,0:T(8,128)S(1)}, f32[2,1,80,128]{3,2,1,0:T(8,128)}, u32[]{:S(2)}) copy-start(f32[2,1,80,128]{3,2,1,0:T(8,128)} %param.23) | copy-start | bytes 245764
  15.8 8.4 %copy-start.1 = (f32[1,80,80]{2,1,0:T(8,128)S(1)}, f32[1,80,80]{2,1,0:T(8,128)}, u32[]{:S(2)}) copy-start(f32[1,80,80]{2,1,0:T(8,128)} %param.22) | copy-start | bytes 76804
  17.5 8.8 %collective-permute-start.4 = (f32[480,128]{1,0:T(8,128)S(1)}, f32[480,128]{1,0:T(8,128)S(1)}, u32[]{:S(2)}, u32[]{:S(2)}) collective-permute-start(f32[480,128]{1,0:T(8,128)S(1)} %get-tuple-element.137), channel_id=1, source_target_pairs={{0,1},{1,0},{2,3},{3,2},{4,5},{5,4},{6,7},{7,6},{8,9},{9,8},{10,11... | collective-permute-start | bytes 737288 | tf_op jit(solution)/shard_map/ppermute | solution.py:1063
  18.0 8.3 %collective-permute-start.5 = (f32[480,128]{1,0:T(8,128)S(1)}, f32[480,128]{1,0:T(8,128)S(1)}, u32[]{:S(2)}, u32[]{:S(2)}) collective-permute-start(f32[480,128]{1,0:T(8,128)S(1)} %get-tuple-element.138), channel_id=1, source_target_pairs={{1,2},{3,4},{5,6},{7,8},{9,10},{11,12},{13,14},{2,1},{4,3},{6,5},{... | collective-permute-start | bytes 737288 | tf_op jit(solution)/shard_map/ppermute | solution.py:1063
  18.7 3.9 %collective-permute-start.2 = (f32[40,128]{1,0:T(8,128)S(1)}, f32[40,128]{1,0:T(8,128)S(1)}, u32[]{:S(2)}, u32[]{:S(2)}) collective-permute-start(f32[40,128]{1,0:T(8,128)S(1)} %copy-done.16), channel_id=1, source_target_pairs={{0,1},{1,0},{2,3},{3,2},{4,5},{5,4},{6,7},{7,6},{8,9},{9,8},{10,11... | collective-permute-start | bytes 61448 | tf_op jit(solution)/shard_map/ppermute | solution.py:1063
  21.7 0.8 collective-permute-start.3
  26.3 11.2 %copy-start.3 = (f32[480,128]{1,0:T(8,128)}, f32[480,128]{1,0:T(8,128)S(1)}, u32[]{:S(2)}) copy-start(f32[480,128]{1,0:T(8,128)S(1)} %collective-permute-done.4.refs_0_) | copy-start | bytes 737284
  26.3 11.2 %copy-start.4 = (f32[480,128]{1,0:T(8,128)}, f32[480,128]{1,0:T(8,128)S(1)}, u32[]{:S(2)}) copy-start(f32[480,128]{1,0:T(8,128)S(1)} %collective-permute-done.5.refs_1_) | copy-start | bytes 737284
  26.3 18.9 %all-to-all-start.1 = ((f32[16,15,2,128]{3,2,1,0:T(2,128)}), f32[16,15,2,128]{3,2,1,0:T(2,128)S(1)}, u32[]{:S(2)}, u32[]{:S(2)}) async-start(f32[16,15,2,128]{3,2,1,0:T(2,128)} %bitcast.58), calls=%async_computation.1 | async-start | bytes 491520 | tf_op jit(solution)/shard_map/all_to_all | solution.py:1070
  41.0 9.3 %collective-permute-start.6 = (f32[480,128]{1,0:T(8,128)}, f32[480,128]{1,0:T(8,128)S(1)}, u32[]{:S(2)}, u32[]{:S(2)}) collective-permute-start(f32[480,128]{1,0:T(8,128)} %get-tuple-element.151), channel_id=1, source_target_pairs={{0,1},{1,0},{2,3},{3,2},{4,5},{5,4},{6,7},{7,6},{8,9},{9,8},{10,11... | collective-permute-start | bytes 737288 | tf_op jit(solution)/shard_map/ppermute | solution.py:1063
  41.4 8.8 %collective-permute-start.7 = (f32[480,128]{1,0:T(8,128)}, f32[480,128]{1,0:T(8,128)S(1)}, u32[]{:S(2)}, u32[]{:S(2)}) collective-permute-start(f32[480,128]{1,0:T(8,128)} %get-tuple-element.152), channel_id=1, source_target_pairs={{1,2},{3,4},{5,6},{7,8},{9,10},{11,12},{13,14},{2,1},{4,3},{6,5},{... | collective-permute-start | bytes 737288 | tf_op jit(solution)/shard_map/ppermute | solution.py:1063
  47.1 3.1 %collective-permute-start.8 = (f32[60,128]{1,0:T(8,128)S(1)}, f32[60,128]{1,0:T(8,128)S(1)}, u32[]{:S(2)}, u32[]{:S(2)}) collective-permute-start(f32[60,128]{1,0:T(8,128)S(1)} %get-tuple-element.159), channel_id=1, source_target_pairs={{0,1},{1,0},{2,3},{3,2},{4,5},{5,4},{6,7},{7,6},{8,9},{9,8},{10,11... | collective-permute-start | bytes 92168 | tf_op jit(solution)/shard_map/ppermute | solution.py:1063
  47.2 3.1 %collective-permute-start.9 = (f32[60,128]{1,0:T(8,128)S(1)}, f32[60,128]{1,0:T(8,128)S(1)}, u32[]{:S(2)}, u32[]{:S(2)}) collective-permute-start(f32[60,128]{1,0:T(8,128)S(1)} %get-tuple-element.160), channel_id=1, source_target_pairs={{1,2},{3,4},{5,6},{7,8},{9,10},{11,12},{13,14},{2,1},{4,3},{6,5},{... | collective-permute-start | bytes 92168 | tf_op jit(solution)/shard_map/ppermute | solution.py:1063
  53.0 16.1 %all-to-all-start.2 = ((f32[16,5,4,128]{3,2,1,0:T(4,128)}), f32[16,5,4,128]{3,2,1,0:T(4,128)S(1)}, u32[]{:S(2)}, u32[]{:S(2)}) async-start(f32[16,5,4,128]{3,2,1,0:T(4,128)} %bitcast.63), calls=%async_computation.2 | async-start | bytes 327680 | tf_op jit(solution)/shard_map/all_to_all | solution.py:1070
  60.6 1.5 collective-permute-start.10
  61.0 1.1 collective-permute-start.11
  70.8 13.3 %all-to-all-start.3 = ((f32[16,15,2,128]{3,2,1,0:T(2,128)}), f32[16,15,2,128]{3,2,1,0:T(2,128)S(1)}, u32[]{:S(2)}, u32[]{:S(2)}) async-start(f32[16,15,2,128]{3,2,1,0:T(2,128)} %bitcast.61), calls=%async_computation.3 | async-start | bytes 491520 | tf_op jit(solution)/shard_map/all_to_all | solution.py:1070
  86.4 19.0 %copy-start.12 = (f32[480,128]{1,0:T(8,128)S(1)}, f32[480,128]{1,0:T(8,128)}, u32[]{:S(2)}) copy-start(f32[480,128]{1,0:T(8,128)} %get-tuple-element.170) | copy-start | bytes 737284
  86.4 19.4 %copy-start.11 = (f32[480,128]{1,0:T(8,128)S(1)}, f32[480,128]{1,0:T(8,128)}, u32[]{:S(2)}) copy-start(f32[480,128]{1,0:T(8,128)} %get-tuple-element.171) | copy-start | bytes 737284
  86.4 13.4 %all-to-all-start.4 = ((f32[16,15,2,128]{3,2,1,0:T(2,128)}), f32[16,15,2,128]{3,2,1,0:T(2,128)S(1)}, u32[]{:S(2)}, u32[]{:S(2)}) async-start(f32[16,15,2,128]{3,2,1,0:T(2,128)} %bitcast.60), calls=%async_computation.4 | async-start | bytes 491520 | tf_op jit(solution)/shard_map/all_to_all | solution.py:1070
  90.1 1.5 collective-permute-start.14
  90.4 1.2 collective-permute-start.15
  101.9 12.0 %all-to-all-start.5 = ((f32[16,5,4,128]{3,2,1,0:T(4,128)}), f32[16,5,4,128]{3,2,1,0:T(4,128)S(1)}, u32[]{:S(2)}, u32[]{:S(2)}) async-start(f32[16,5,4,128]{3,2,1,0:T(4,128)} %bitcast.56), calls=%async_computation.5 | async-start | bytes 327680 | tf_op jit(solution)/shard_map/all_to_all | solution.py:1070
  105.5 12.4 %collective-permute-start.12 = (f32[480,128]{1,0:T(8,128)S(1)}, f32[480,128]{1,0:T(8,128)S(1)}, u32[]{:S(2)}, u32[]{:S(2)}) collective-permute-start(f32[480,128]{1,0:T(8,128)S(1)} %copy-done.12), channel_id=1, source_target_pairs={{0,1},{1,0},{2,3},{3,2},{4,5},{5,4},{6,7},{7,6},{8,9},{9,8},{10,11... | collective-permute-start | bytes 737288 | tf_op jit(solution)/shard_map/ppermute | solution.py:1063
  105.8 12.0 %collective-permute-start.13 = (f32[480,128]{1,0:T(8,128)S(1)}, f32[480,128]{1,0:T(8,128)S(1)}, u32[]{:S(2)}, u32[]{:S(2)}) collective-permute-start(f32[480,128]{1,0:T(8,128)S(1)} %copy-done.11), channel_id=1, source_target_pairs={{1,2},{3,4},{5,6},{7,8},{9,10},{11,12},{13,14},{2,1},{4,3},{6,5},{... | collective-permute-start | bytes 737288 | tf_op jit(solution)/shard_map/ppermute | solution.py:1063
  115.1 2.8 %collective-permute-start.16 = (f32[60,128]{1,0:T(8,128)S(1)}, f32[60,128]{1,0:T(8,128)S(1)}, u32[]{:S(2)}, u32[]{:S(2)}) collective-permute-start(f32[60,128]{1,0:T(8,128)S(1)} %get-tuple-element.193), channel_id=1, source_target_pairs={{0,1},{1,0},{2,3},{3,2},{4,5},{5,4},{6,7},{7,6},{8,9},{9,8},{10,11... | collective-permute-start | bytes 92168 | tf_op jit(solution)/shard_map/ppermute | solution.py:1063
  115.2 2.7 %collective-permute-start.17 = (f32[60,128]{1,0:T(8,128)S(1)}, f32[60,128]{1,0:T(8,128)S(1)}, u32[]{:S(2)}, u32[]{:S(2)}) collective-permute-start(f32[60,128]{1,0:T(8,128)S(1)} %get-tuple-element.194), channel_id=1, source_target_pairs={{1,2},{3,4},{5,6},{7,8},{9,10},{11,12},{13,14},{2,1},{4,3},{6,5},{... | collective-permute-start | bytes 92168 | tf_op jit(solution)/shard_map/ppermute | solution.py:1063
  120.5 21.3 %copy-start.14 = (f32[480,128]{1,0:T(8,128)S(1)}, f32[480,128]{1,0:T(8,128)}, u32[]{:S(2)}) copy-start(f32[480,128]{1,0:T(8,128)} %get-tuple-element.211) | copy-start | bytes 737284
  120.5 21.6 %copy-start.13 = (f32[480,128]{1,0:T(8,128)S(1)}, f32[480,128]{1,0:T(8,128)}, u32[]{:S(2)}) copy-start(f32[480,128]{1,0:T(8,128)} %get-tuple-element.212) | copy-start | bytes 737284
  120.5 15.6 %all-to-all-start.6 = ((f32[16,15,2,128]{3,2,1,0:T(2,128)}), f32[16,15,2,128]{3,2,1,0:T(2,128)S(1)}, u32[]{:S(2)}, u32[]{:S(2)}) async-start(f32[16,15,2,128]{3,2,1,0:T(2,128)} %bitcast.59), calls=%async_computation.6 | async-start | bytes 491520 | tf_op jit(solution)/shard_map/all_to_all | solution.py:1070
  126.4 1.8 %collective-permute-start.18 = (f32[32,128]{1,0:T(8,128)}, f32[32,128]{1,0:T(8,128)S(1)}, u32[]{:S(2)}, u32[]{:S(2)}) collective-permute-start(f32[32,128]{1,0:T(8,128)} %get-tuple-element.204), channel_id=1, source_target_pairs={{0,1},{1,0},{2,3},{3,2},{4,5},{5,4},{6,7},{7,6},{8,9},{9,8},{10,11... | collective-permute-start | bytes 49160 | tf_op jit(solution)/shard_map/ppermute | solution.py:1063
  127.2 1.1 collective-permute-start.19
  138.2 12.0 %all-to-all-start.7 = ((f32[16,5,4,128]{3,2,1,0:T(4,128)}), f32[16,5,4,128]{3,2,1,0:T(4,128)S(1)}, u32[]{:S(2)}, u32[]{:S(2)}) async-start(f32[16,5,4,128]{3,2,1,0:T(4,128)} %bitcast.57), calls=%async_computation.7 | async-start | bytes 327680 | tf_op jit(solution)/shard_map/all_to_all | solution.py:1070
  141.8 12.7 %collective-permute-start.20 = (f32[480,128]{1,0:T(8,128)S(1)}, f32[480,128]{1,0:T(8,128)S(1)}, u32[]{:S(2)}, u32[]{:S(2)}) collective-permute-start(f32[480,128]{1,0:T(8,128)S(1)} %copy-done.14), channel_id=1, source_target_pairs={{0,1},{1,0},{2,3},{3,2},{4,5},{5,4},{6,7},{7,6},{8,9},{9,8},{10,11... | collective-permute-start | bytes 737288 | tf_op jit(solution)/shard_map/ppermute | solution.py:1063
  142.1 12.4 %collective-permute-start.21 = (f32[480,128]{1,0:T(8,128)S(1)}, f32[480,128]{1,0:T(8,128)S(1)}, u32[]{:S(2)}, u32[]{:S(2)}) collective-permute-start(f32[480,128]{1,0:T(8,128)S(1)} %copy-done.13), channel_id=1, source_target_pairs={{1,2},{3,4},{5,6},{7,8},{9,10},{11,12},{13,14},{2,1},{4,3},{6,5},{... | collective-permute-start | bytes 737288 | tf_op jit(solution)/shard_map/ppermute | solution.py:1063
  151.4 3.1 %collective-permute-start.22 = (f32[60,128]{1,0:T(8,128)S(1)}, f32[60,128]{1,0:T(8,128)S(1)}, u32[]{:S(2)}, u32[]{:S(2)}) collective-permute-start(f32[60,128]{1,0:T(8,128)S(1)} %get-tuple-element.217), channel_id=1, source_target_pairs={{0,1},{1,0},{2,3},{3,2},{4,5},{5,4},{6,7},{7,6},{8,9},{9,8},{10,11... | collective-permute-start | bytes 92168 | tf_op jit(solution)/shard_map/ppermute | solution.py:1063
  151.5 3.1 %collective-permute-start.23 = (f32[60,128]{1,0:T(8,128)S(1)}, f32[60,128]{1,0:T(8,128)S(1)}, u32[]{:S(2)}, u32[]{:S(2)}) collective-permute-start(f32[60,128]{1,0:T(8,128)S(1)} %get-tuple-element.218), channel_id=1, source_target_pairs={{1,2},{3,4},{5,6},{7,8},{9,10},{11,12},{13,14},{2,1},{4,3},{6,5},{... | collective-permute-start | bytes 92168 | tf_op jit(solution)/shard_map/ppermute | solution.py:1063
  157.0 11.8 %all-to-all-start.8 = ((f32[16,1,128]{2,1,0:T(1,128)}), f32[16,1,128]{2,1,0:T(1,128)S(1)}, u32[]{:S(2)}, u32[]{:S(2)}) async-start(f32[16,1,128]{2,1,0:T(1,128)} %bitcast.64), calls=%async_computation.8 | async-start | bytes 16384 | tf_op jit(solution)/shard_map/all_to_all | solution.py:1330
  162.4 6.4 %copy-start = (f32[8,5,4,1920]{3,2,1,0:T(4,128)S(1)}, f32[8,5,4,1920]{3,2,1,0:T(4,128)}, u32[]{:S(2)}) copy-start(f32[8,5,4,1920]{3,2,1,0:T(4,128)} %refs_1_.6) | copy-start | bytes 3686404

commit v7 on v5

--- a/solution.py
+++ b/solution.py
@@ -100,10 +100,19 @@
     )
 
 
-def levels_sum(field, sub):
-    return jnp.where(sub == 0, 0.0, pltpu.roll(field, 1, 0)) + jnp.where(
-        sub == LEVELS - 1, 0.0, pltpu.roll(field, LEVELS - 1, 0)
-    )
+def level_masks():
+    sub = lax.broadcasted_iota(jnp.int32, (LEVELS, WIDTH), 0)
+    return jnp.where(sub == 0, 0.0, KAPPA_V), jnp.where(sub == LEVELS - 1, 0.0, KAPPA_V)
+
+
+def levels_sum(field, masks):
+    return masks[0] * pltpu.roll(field, 1, 0) + masks[1] * pltpu.roll(field, LEVELS - 1, 0)
+
+
+def rolled(tiles):
+    return [pltpu.roll(tile, 1, 1) for tile in tiles], [
+        pltpu.roll(tile, WIDTH - 1, 1) for tile in tiles
+    ]
 
 
 def row_tiles_of(sz, ref, row):
@@ -405,7 +414,7 @@
 
     ready(0)
     lane = lax.broadcasted_iota(jnp.int32, (LEVELS, WIDTH), 1)
-    sub = lax.broadcasted_iota(jnp.int32, (LEVELS, WIDTH), 0)
+    masks = level_masks()
     count = sz.row_tiles
 
     def one_row(row, carry):
@@ -414,6 +423,7 @@
             ready(row + 1)
 
         here = [[padded[row + 1, c, :, cols(t)] for t in range(count)] for c in range(CHANNELS)]
+        moved = [rolled(tiles) for tiles in here]
         for t in range(count):
             coeff = jnp.broadcast_to(diffusivity[row, 0:1, cols(t)], (LEVELS, WIDTH))
             center = (1.0 - 2.0 * KAPPA_V) - 4.0 * coeff
@@ -427,18 +437,15 @@
                 bent = jnp.tanh(mixed)
                 drive[row, c, :, cols(t)] = bent
                 field_here = here[c][t]
+                to_right, to_left = moved[c]
                 around = lanes_sum(
-                    pltpu.roll(field_here, 1, 1),
-                    pltpu.roll(here[c][(t - 1) % count], 1, 1),
-                    pltpu.roll(field_here, WIDTH - 1, 1),
-                    pltpu.roll(here[c][(t + 1) % count], WIDTH - 1, 1),
-                    lane,
+                    to_right[t], to_right[t - 1], to_left[t], to_left[(t + 1) % count], lane
                 )
                 around = around + (padded[row, c, :, cols(t)] + padded[row + 2, c, :, cols(t)])
                 stepped = (
                     center * field_here
                     + coeff * around
-                    + KAPPA_V * levels_sum(field_here, sub)
+                    + levels_sum(field_here, masks)
                     + TIME_STEP * bent
                 )
                 new_surface[pl.ds((row * count + t) * CHANNELS + c, 1), :] = stepped[0:1, :]
@@ -775,7 +782,7 @@
 
     ready(0)
     lane = lax.broadcasted_iota(jnp.int32, (LEVELS, WIDTH), 1)
-    sub = lax.broadcasted_iota(jnp.int32, (LEVELS, WIDTH), 0)
+    masks = level_masks()
 
     def one_row(row, carry):
         @pl.when(row < sz.rows - 1)
@@ -783,6 +790,7 @@
             ready(row + 1)
 
         scaled = [[padded[row + 1, c, :, cols(t)] for t in range(count)] for c in range(CHANNELS)]
+        moved = [rolled(tiles) for tiles in scaled]
         for t in range(count):
             here, bent = [], []
             for c in range(CHANNELS):
@@ -794,18 +802,15 @@
                 mixed = mix[c] * bent[0]
                 for k in range(1, CHANNELS):
                     mixed = mixed + mix[k * CHANNELS + c] * bent[k]
+                to_right, to_left = moved[c]
                 around = lanes_sum(
-                    pltpu.roll(scaled[c][t], 1, 1),
-                    pltpu.roll(scaled[c][(t - 1) % count], 1, 1),
-                    pltpu.roll(scaled[c][t], WIDTH - 1, 1),
-                    pltpu.roll(scaled[c][(t + 1) % count], WIDTH - 1, 1),
-                    lane,
+                    to_right[t], to_right[t - 1], to_left[t], to_left[(t + 1) % count], lane
                 )
                 around = around + (padded[row, c, :, cols(t)] + padded[row + 2, c, :, cols(t)])
                 stepped = (
                     ((1.0 - 2.0 * KAPPA_V) * here[c] - 4.0 * scaled[c][t])
                     + around
-                    + KAPPA_V * levels_sum(here[c], sub)
+                    + levels_sum(here[c], masks)
                     + TIME_STEP * mixed
                 )
                 out[row, c, :, cols(t)] = stepped
@@ -1141,14 +1146,12 @@
             flux, perturbation = lax.optimization_barrier((flux, perturbation))
             beside = relayout(perturbation)
         flux = exchange(flux, devices)
-        edges = swap(*sends)
-        if last:
-            flux, *edges = lax.optimization_barrier((flux, *edges))
         flux, *beside = lax.optimization_barrier((flux, *beside))
         if first:
             diffusivity_rows, weight_rows, diffusivity_tiles, weight_tiles, target = beside
         else:
             start_field = beside[0]
+        edges = swap(*sends)
         inputs = near_by(flux, *got) + fetched(surface) + scalars(tables, weights)
         if last:
             surface, slope, packed, *sends = call(

time: 173 us -> 170 us (0.983)
  blocking collectives: 11.9 us -> 0 us
  waiting for transfers between devices: 55 us -> 63.5 us
    all_to_all x1 -> x0, blocking collectives: 11.9 us -> none  [exchange(): lax.all_to_all(split, 'horiz', split_axis=0, concat_axis=0, tiled=True)]
    all_to_all x7 -> x8, waiting for transfers between devices: 48.8 us -> 57.1 us  [exchange(): lax.all_to_all(split, 'horiz', split_axis=0, concat_axis=0, tiled=True)]
    all_to_all x7 -> x8, starting transfers between devices: 41.1 us -> 41.8 us  [exchange(): lax.all_to_all(split, 'horiz', split_axis=0, concat_axis=0, tiled=True)]
  transfers between devices with their start and end apart: 30 -> 31, of which waited for: 12 -> 13; matrix products, arithmetic and copies ran while one was open for 1% -> 1% of each run, Pallas kernels for 11% -> 12%
where the time goes in v7:
time: 170 us; the launch traced here: 168 us
  waiting for transfers between devices  63.5 us (37%)
  starting transfers between devices  58.1 us (34%)
  Pallas kernels  44 us (26%)
  local copies, waits for them, and re-layouts  1.88 us (1%)
    all_to_all x8, waiting for transfers between devices, exchange(): lax.all_to_all(split, 'horiz', split_axis=0, concat_axis=0, tiled=True)  57.1 us
    pallas_call x22, Pallas kernels, call(): pl.pallas_call(run, name=name, in_specs=[pl.BlockSpec(memory_space=item.s...  44 us
    all_to_all x8, starting transfers between devices, exchange(): lax.all_to_all(split, 'horiz', split_axis=0, concat_axis=0, tiled=True)  41.8 us
    ppermute x11, starting transfers between devices, swap(): lax.ppermute(second, 'horiz', outer)  7.25 us
    all_to_all x1, starting transfers between devices, body(): lax.all_to_all(sums, 'horiz', split_axis=0, concat_axis=0, tiled=True)  5.36 us
    all_to_all x1, waiting for transfers between devices, body(): lax.all_to_all(sums, 'horiz', split_axis=0, concat_axis=0, tiled=True)  4.68 us
    ppermute x11, starting transfers between devices, swap(): lax.ppermute(first, 'horiz', inner)  3.69 us
  transfers between devices with their start and end apart: 31, of which 13 were waited for; matrix products, arithmetic and copies ran while one was open for 1% of the time, Pallas kernels for 12%

profile of v7, /device:TPU:0, one launch (start us, length us, event | category | flops | bytes accessed | tf_op | source)
XLA Modules:
  0.0 168.3 jit_solution(16174179697656446008)
XLA Ops:
  0.0 1.6 edges.1
  1.6 0.5 collective-permute-start
  2.2 0.7 collective-permute-start.1
  3.1 2.0 %load.1.refs_6_ = f32[5,4,8,1920]{3,2,1,0:T(8,128)S(1)} custom-call(f32[8,5,4,1920]{3,2,1,0:T(4,128)} %refs_1_.6, f32[8,5,4,1920]{3,2,1,0:T(4,128)} %refs_1_.4), custom_call_target="tpu_custom_call" | custom-call | tf_op jit(solution)/shard_map/load/pallas_call | solution.py:970
  5.2 1.7 %setup.1 = (f32[16,8,128]{2,1,0:T(8,128)S(1)}, f32[5,1,1920]{2,1,0:T(1,128)S(1)}, s32[1,128]{1,0:T(1,128)}, f32[8,128]{1,0:T(8,128)}, f32[16,8,128]{2,1,0:T(8,128)}) custom-call(f32[2,128]{1,0:T(2,128)S(1)} %get-tuple-element.228.refs_0_, f32[2,128]{1,0:T(2,128)S(1)} %get-tuple-element.227.refs_1_, f32[16,8]{1,0:T(8,128)S(1)} %bitcast.55, f32[5,1920]{1,0:T(8,128)} %refs_0_.4), custom_call_target="tpu_custom_call" | custom-call | tf_op jit(solution)/shard_map/setup/pallas_call | solution.py:970
  7.0 2.6 %step.2 = (f32[5,4,8,1920]{3,2,1,0:T(8,128)}, f32[5,4,8,1920]{3,2,1,0:T(8,128)}, f32[304,128]{1,0:T(8,128)}, f32[320,128]{1,0:T(8,128)}, f32[40,128]{1,0:T(8,128...) custom-call(s32[1,128]{1,0:T(1,128)} %get-tuple-element.114.refs_0_.refs_7_.refs_5_, ...), custom_call_target="tpu_custom_call" | custom-call | tf_op jit(solution)/shard_map/step/pallas_call | solution.py:970
  9.6 11.6 %all-to-all-start = ((f32[16,5,4,128]{3,2,1,0:T(4,128)}), f32[16,5,4,128]{3,2,1,0:T(4,128)S(1)}, u32[]{:S(2)}, u32[]{:S(2)}) async-start(f32[16,5,4,128]{3,2,1,0:T(4,128)} %bitcast.62), calls=%async_computation | async-start | bytes 327680 | tf_op jit(solution)/shard_map/all_to_all | solution.py:998
  21.2 0.4 collective-permute-start.2
  21.6 0.7 collective-permute-start.3
  22.3 0.4 collective-permute-done.2.refs_5_.refs_1_
  22.7 7.0 %all-to-all-done = f32[16,5,4,128]{3,2,1,0:T(4,128)S(1)} async-done(((f32[16,5,4,128]{3,2,1,0:T(4,128)}), f32[16,5,4,128]{3,2,1,0:T(4,128)S(1)}, u32[]{:S(2)}, u32[]{:S(2)}) %all-to-all-start) | async-done | bytes 163872 | tf_op jit(solution)/shard_map/all_to_all | solution.py:998
  29.6 2.0 %owners.2 = (s32[3,128]{1,0:T(4,128)}, f32[24,128]{1,0:T(8,128)}, f32[480,128]{1,0:T(8,128)}, f32[4,80,128]{2,1,0:T(8,128)}, f32[4,80,128]{2,1,0:T(8,128)}) custom-call(f32[320,128]{1,0:T(8,128)S(1)} %bitcast.52, f32[80,80]{1,0:T(8,128)S(1)} %bitcast.46, f32[80,128]{1,0:T(8,128)S(1)} %get-tuple-element.229.refs_2_, ...), custom_call_target="tpu_custom_call" | custom-call | tf_op jit(solution)/shard_map/owners/pallas_call | solution.py:970
  31.7 3.5 %all-to-all-start.1 = ((f32[16,15,2,128]{3,2,1,0:T(2,128)}), f32[16,15,2,128]{3,2,1,0:T(2,128)S(1)}, u32[]{:S(2)}, u32[]{:S(2)}) async-start(f32[16,15,2,128]{3,2,1,0:T(2,128)} %bitcast.60), calls=%async_computation.1 | async-start | bytes 491520 | tf_op jit(solution)/shard_map/all_to_all | solution.py:998
  35.2 0.4 collective-permute-start.4
  35.6 0.7 collective-permute-start.5
  36.3 2.3 %relayout.2.refs_5_ = f32[5,4,8,1920]{3,2,1,0:T(8,128)} custom-call(f32[8,5,4,1920]{3,2,1,0:T(4,128)} %refs_6_), custom_call_target="tpu_custom_call" | custom-call | tf_op jit(solution)/shard_map/relayout/pallas_call | solution.py:970
  38.6 1.7 %columns.1 = (f32[5,1,1920]{2,1,0:T(1,128)}, f32[5,1,1920]{2,1,0:T(1,128)}, f32[300,128]{1,0:T(8,128)}, f32[300,128]{1,0:T(8,128)}) custom-call(f32[5,1920]{1,0:T(8,128)} %refs_0_.4, f32[5,1920]{1,0:T(8,128)} %refs_1_.5), custom_call_target="tpu_custom_call" | custom-call | tf_op jit(solution)/shard_map/columns/pallas_call | solution.py:970
  40.3 4.7 %all-to-all-done.1 = f32[16,15,2,128]{3,2,1,0:T(2,128)S(1)} async-done(((f32[16,15,2,128]{3,2,1,0:T(2,128)}), f32[16,15,2,128]{3,2,1,0:T(2,128)S(1)}, u32[]{:S(2)}, u32[]{:S(2)}) %all-to-all-start.1) | async-done | bytes 245792 | tf_op jit(solution)/shard_map/all_to_all | solution.py:998
  45.0 1.9 %surface.2 = (f32[304,128]{1,0:T(8,128)S(1)}, f32[60,128]{1,0:T(8,128)S(1)}, f32[60,128]{1,0:T(8,128)S(1)}, f32[64,128]{1,0:T(8,128)}) custom-call(f32[480,128]{1,0:T(8,128)S(1)} %bitcast.42, f32[40,128]{1,0:T(8,128)S(1)} %collective-permute-done.2.refs_5_.refs_1_, f32[40,128]{1,0:T(8,128)S(1)} %collective-permute-done.3.refs_6_.refs_2_, ...), custom_call_target="tpu_custom_call" | custom-call | tf_op jit(solution)/shard_map/surface/pallas_call | solution.py:970
  46.9 0.7 collective-permute-start.7
  47.6 1.9 %step_load.1 = (f32[16,8,128]{2,1,0:T(8,128)S(1)}, f32[5,1,1920]{2,1,0:T(1,128)S(1)}, f32[5,4,8,1920]{3,2,1,0:T(8,128)S(1)}, f32[5,1,1920]{2,1,0:T(1,128)S(1)}, f32[5,4,8,1920]{3,2,1,0:T(8,128)S(1)}) custom-call(f32[16,8,128]{2,1,0:T(8,128)} %get-tuple-element.144.refs_0_, f32[5,1,1920]{2,1,0:T(1,128)} %get-tuple-element.145.refs_1_, ...), custom_call_target="tpu_custom_call" | custom-call | tf_op jit(solution)/shard_map/step_load/pallas_call | solution.py:970
  49.6 2.7 %step.3 = (f32[5,4,8,1920]{3,2,1,0:T(8,128)}, f32[5,4,8,1920]{3,2,1,0:T(8,128)}, f32[304,128]{1,0:T(8,128)}, f32[320,128]{1,0:T(8,128)}, f32[32,128]{1,0:T(8,128...) custom-call(s32[1,128]{1,0:T(1,128)} %get-tuple-element.114.refs_0_.refs_7_.refs_5_, ...), custom_call_target="tpu_custom_call" | custom-call | tf_op jit(solution)/shard_map/step/pallas_call | solution.py:970
  52.3 6.6 %all-to-all-start.2 = ((f32[16,5,4,128]{3,2,1,0:T(4,128)}), f32[16,5,4,128]{3,2,1,0:T(4,128)S(1)}, u32[]{:S(2)}, u32[]{:S(2)}) async-start(f32[16,5,4,128]{3,2,1,0:T(4,128)} %bitcast.63), calls=%async_computation.2 | async-start | bytes 327680 | tf_op jit(solution)/shard_map/all_to_all | solution.py:998
  58.9 0.4 collective-permute-start.8
  59.3 0.7 collective-permute-start.9
  59.9 0.4 collective-permute-done.8.refs_1_
  60.3 7.0 %all-to-all-done.2 = f32[16,5,4,128]{3,2,1,0:T(4,128)S(1)} async-done(((f32[16,5,4,128]{3,2,1,0:T(4,128)}), f32[16,5,4,128]{3,2,1,0:T(4,128)S(1)}, u32[]{:S(2)}, u32[]{:S(2)}) %all-to-all-start.2) | async-done | bytes 163872 | tf_op jit(solution)/shard_map/all_to_all | solution.py:998
  67.3 1.7 %owners.3 = (f32[480,128]{1,0:T(8,128)}, f32[4,80,128]{2,1,0:T(8,128)}, f32[4,80,128]{2,1,0:T(8,128)}) custom-call(f32[320,128]{1,0:T(8,128)S(1)} %bitcast.53, f32[80,80]{1,0:T(8,128)S(1)} %bitcast.47, f32[80,128]{1,0:T(8,128)S(1)} %get-tuple-element.230.refs_2_, f32[80,128]{1,0:T(8,128)S(1)} %get-tuple-element.223.refs_3_, ...), custom_call_target="tpu_custom_call" | custom-call | tf_op jit(solution)/shard_map/owners/pallas_call | solution.py:970
  69.0 3.5 %all-to-all-start.3 = ((f32[16,15,2,128]{3,2,1,0:T(2,128)}), f32[16,15,2,128]{3,2,1,0:T(2,128)S(1)}, u32[]{:S(2)}, u32[]{:S(2)}) async-start(f32[16,15,2,128]{3,2,1,0:T(2,128)} %bitcast.61), calls=%async_computation.3 | async-start | bytes 491520 | tf_op jit(solution)/shard_map/all_to_all | solution.py:998
  72.6 2.3 %relayout.3.refs_5_ = f32[5,4,8,1920]{3,2,1,0:T(8,128)} custom-call(f32[8,5,4,1920]{3,2,1,0:T(4,128)} %refs_1_.6), custom_call_target="tpu_custom_call" | custom-call | tf_op jit(solution)/shard_map/relayout/pallas_call | solution.py:970
  74.9 7.4 %all-to-all-done.3 = f32[16,15,2,128]{3,2,1,0:T(2,128)S(1)} async-done(((f32[16,15,2,128]{3,2,1,0:T(2,128)}), f32[16,15,2,128]{3,2,1,0:T(2,128)S(1)}, u32[]{:S(2)}, u32[]{:S(2)}) %all-to-all-start.3) | async-done | bytes 245792 | tf_op jit(solution)/shard_map/all_to_all | solution.py:998
  82.3 2.3 %surface.3 = (f32[304,128]{1,0:T(8,128)}, f32[64,128]{1,0:T(8,128)}, f32[480,128]{1,0:T(8,128)}, f32[32,128]{1,0:T(8,128)}, f32[32,128]{1,0:T(8,128)}) custom-call(f32[480,128]{1,0:T(8,128)S(1)} %bitcast.45, f32[32,128]{1,0:T(8,128)S(1)} %collective-permute-done.8.refs_1_, f32[32,128]{1,0:T(8,128)S(1)} %collective-permute-done.9.refs_2_, ...), custom_call_target="tpu_custom_call" | custom-call | tf_op jit(solution)/shard_map/surface/pallas_call | solution.py:970
  84.7 3.7 %all-to-all-start.4 = ((f32[16,15,2,128]{3,2,1,0:T(2,128)}), f32[16,15,2,128]{3,2,1,0:T(2,128)S(1)}, u32[]{:S(2)}, u32[]{:S(2)}) async-start(f32[16,15,2,128]{3,2,1,0:T(2,128)} %bitcast.59), calls=%async_computation.4 | async-start | bytes 491520 | tf_op jit(solution)/shard_map/all_to_all | solution.py:998
  88.4 0.3 collective-permute-start.12
  88.7 0.7 collective-permute-start.13
  89.3 0.5 collective-permute-done.12.refs_1_
  89.8 8.3 %all-to-all-done.4 = f32[16,15,2,128]{3,2,1,0:T(2,128)S(1)} async-done(((f32[16,15,2,128]{3,2,1,0:T(2,128)}), f32[16,15,2,128]{3,2,1,0:T(2,128)S(1)}, u32[]{:S(2)}, u32[]{:S(2)}) %all-to-all-start.4) | async-done | bytes 245792 | tf_op jit(solution)/shard_map/all_to_all | solution.py:998
  98.1 2.0 %owners_back.2 = f32[320,128]{1,0:T(8,128)} custom-call(f32[480,128]{1,0:T(8,128)S(1)} %bitcast.43, f32[80,80]{1,0:T(8,128)S(1)} %bitcast.48, f32[4,80,128]{2,1,0:T(8,128)} %get-tuple-element.178.refs_2_, f32[4,80,128]{2,1,0:T(8,128)} %get-tuple-element.179.refs_3_, f32[8,128]{1,0:T(8,128)} %get-tuple-element.115.refs_1_.refs_7_.refs_4_.refs_8_.refs_6_), custom_call_target="tpu_custom_call" | custom-call | tf_op jit(solution)/shard_map/owners_back/pallas_call | solution.py:970
  100.2 3.5 %all-to-all-start.5 = ((f32[16,5,4,128]{3,2,1,0:T(4,128)}), f32[16,5,4,128]{3,2,1,0:T(4,128)S(1)}, u32[]{:S(2)}, u32[]{:S(2)}) async-start(f32[16,5,4,128]{3,2,1,0:T(4,128)} %bitcast.56), calls=%async_computation.5 | async-start | bytes 327680 | tf_op jit(solution)/shard_map/all_to_all | solution.py:998
  103.7 0.4 collective-permute-start.10
  104.1 0.7 collective-permute-start.11
  104.8 7.4 %all-to-all-done.5 = f32[16,5,4,128]{3,2,1,0:T(4,128)S(1)} async-done(((f32[16,5,4,128]{3,2,1,0:T(4,128)}), f32[16,5,4,128]{3,2,1,0:T(4,128)S(1)}, u32[]{:S(2)}, u32[]{:S(2)}) %all-to-all-start.5) | async-done | bytes 163872 | tf_op jit(solution)/shard_map/all_to_all | solution.py:998
  112.2 1.2 merge.2
  113.4 0.7 collective-permute-start.15
  114.1 2.0 %step_back_load.2 = (f32[16,8,128]{2,1,0:T(8,128)S(1)}, f32[5,1,1920]{2,1,0:T(1,128)S(1)}, f32[5,4,8,1920]{3,2,1,0:T(8,128)S(1)}, f32[5,4,8,1920]{3,2,1,0:T(8,128)S(1)}, f32[5,4,8,1920]{3,2,1,0:T(8,128)S(1)}) custom-call(f32[16,8,128]{2,1,0:T(8,128)} %get-tuple-element.144.refs_0_, f32[5,1,1920]{2,1,0:T(1,128)} %get-tuple-element.145.refs_1_, ...), custom_call_target="tpu_custom_call" | custom-call | tf_op jit(solution)/shard_map/step_back_load/pallas_call | solution.py:970
  116.1 2.7 %step_back.1 = (f32[5,4,8,1920]{3,2,1,0:T(8,128)}, f32[304,128]{1,0:T(8,128)}, f32[480,128]{1,0:T(8,128)}, f32[32,128]{1,0:T(8,128)}, f32[32,128]{1,0:T(8,128)}, /*index=5*/f32[480,128]{1,0:T(8,128)}, f32[480,128]{1,0:T(8,128)}) custom-call(s32[3,128]{1,0:T(4,128)} %get-tuple-element.126.refs_4_.refs_0_, f32[24,128]{1,0:T(8,128)} %get-tuple-element.127.refs_5_.refs_1_, ...), custom_call_target="tpu_custom_call" | custom-call | tf_op jit(solution)/shard_map/step_back/pallas_call | solution.py:970
  118.8 5.9 %all-to-all-start.6 = ((f32[16,15,2,128]{3,2,1,0:T(2,128)}), f32[16,15,2,128]{3,2,1,0:T(2,128)S(1)}, u32[]{:S(2)}, u32[]{:S(2)}) async-start(f32[16,15,2,128]{3,2,1,0:T(2,128)} %bitcast.58), calls=%async_computation.6 | async-start | bytes 491520 | tf_op jit(solution)/shard_map/all_to_all | solution.py:998
  124.7 0.8 collective-permute-start.16
  125.5 0.7 collective-permute-start.17
  126.2 0.4 collective-permute-done.16.refs_1_
  126.6 7.9 %all-to-all-done.6 = f32[16,15,2,128]{3,2,1,0:T(2,128)S(1)} async-done(((f32[16,15,2,128]{3,2,1,0:T(2,128)}), f32[16,15,2,128]{3,2,1,0:T(2,128)S(1)}, u32[]{:S(2)}, u32[]{:S(2)}) %all-to-all-start.6) | async-done | bytes 245792 | tf_op jit(solution)/shard_map/all_to_all | solution.py:998
  134.5 2.0 %owners_back.3 = f32[320,128]{1,0:T(8,128)} custom-call(f32[480,128]{1,0:T(8,128)S(1)} %bitcast.44, f32[80,80]{1,0:T(8,128)S(1)} %bitcast.49, f32[4,80,128]{2,1,0:T(8,128)} %get-tuple-element.199.refs_2_, f32[4,80,128]{2,1,0:T(8,128)} %get-tuple-element.200.refs_3_, f32[8,128]{1,0:T(8,128)} %get-tuple-element.115.refs_1_.refs_7_.refs_4_.refs_8_.refs_6_), custom_call_target="tpu_custom_call" | custom-call | tf_op jit(solution)/shard_map/owners_back/pallas_call | solution.py:970
  136.5 3.5 %all-to-all-start.7 = ((f32[16,5,4,128]{3,2,1,0:T(4,128)}), f32[16,5,4,128]{3,2,1,0:T(4,128)S(1)}, u32[]{:S(2)}, u32[]{:S(2)}) async-start(f32[16,5,4,128]{3,2,1,0:T(4,128)} %bitcast.57), calls=%async_computation.7 | async-start | bytes 327680 | tf_op jit(solution)/shard_map/all_to_all | solution.py:998
  140.1 0.4 collective-permute-start.18
  140.4 0.7 collective-permute-start.19
  141.1 7.4 %all-to-all-done.7 = f32[16,5,4,128]{3,2,1,0:T(4,128)S(1)} async-done(((f32[16,5,4,128]{3,2,1,0:T(4,128)}), f32[16,5,4,128]{3,2,1,0:T(4,128)S(1)}, u32[]{:S(2)}, u32[]{:S(2)}) %all-to-all-start.7) | async-done | bytes 163872 | tf_op jit(solution)/shard_map/all_to_all | solution.py:998
  148.5 1.2 merge.3
  149.8 0.7 collective-permute-start.21
  150.5 2.4 %step_back_load.3 = (f32[16,8,128]{2,1,0:T(8,128)S(1)}, f32[5,1,1920]{2,1,0:T(1,128)S(1)}, f32[5,4,8,1920]{3,2,1,0:T(8,128)S(1)}, f32[5,4,8,1920]{3,2,1,0:T(8,12...) custom-call(f32[16,8,128]{2,1,0:T(8,128)} %get-tuple-element.144.refs_0_, ...), custom_call_target="tpu_custom_call" | custom-call | tf_op jit(solution)/shard_map/step_back_load/pallas_call | solution.py:970
  152.9 2.4 %step_back_sums.1 = (f32[5,4,8,1920]{3,2,1,0:T(8,128)}, f32[16,128]{1,0:T(8,128)}) custom-call(f32[480,128]{1,0:T(8,128)S(1)} %collective-permute-done.18.refs_0_, f32[480,128]{1,0:T(8,128)S(1)} %collective-permute-done.19.refs_1_, f32[60,128]{1,0:T(8,128)S(1)} %collective-permute-done.20.refs_2_, f32[60,128]{1,0:T(8,128)S(1)} %collective-permute-done.21.refs_3_, ...), custom_call_target="tpu_custom_call" | custom-call | tf_op jit(solution)/shard_map/step_back_sums/pallas_call | solution.py:970
  155.3 5.4 %all-to-all-start.8 = ((f32[16,1,128]{2,1,0:T(1,128)}), f32[16,1,128]{2,1,0:T(1,128)S(1)}, u32[]{:S(2)}, u32[]{:S(2)}) async-start(f32[16,1,128]{2,1,0:T(1,128)} %bitcast.64), calls=%async_computation.8 | async-start | bytes 16384 | tf_op jit(solution)/shard_map/all_to_all | solution.py:1233
  160.6 1.7 %copy.20 = f32[5,4,8,1920]{3,1,0,2:T(4,128)S(1)} copy(f32[5,4,8,1920]{3,2,1,0:T(8,128)} %get-tuple-element.222) | data formatting | bytes 2457600 | tf_op jit(solution)/shard_map/step_back_sums/pallas_call | solution.py:970
  162.3 4.7 %all-to-all-done.8 = f32[16,1,128]{2,1,0:T(1,128)S(1)} async-done(((f32[16,1,128]{2,1,0:T(1,128)}), f32[16,1,128]{2,1,0:T(1,128)S(1)}, u32[]{:S(2)}, u32[]{:S(2)}) %all-to-all-start.8) | async-done | bytes 8224 | tf_op jit(solution)/shard_map/all_to_all | solution.py:1233
  167.0 1.2 finish.1
  (64 shorter events, 0.6 us)
Async XLA Ops:
  0.0 2.9 %copy-start.5 = (f32[4,4]{1,0:T(4,128)S(1)}, f32[4,4]{1,0:T(4,128)}, u32[]{:S(2)}) copy-start(f32[4,4]{1,0:T(4,128)} %param.21) | copy-start | bytes 196
  0.0 2.9 %copy-start.7 = (s32[15]{0:T(128)S(1)}, s32[15]{0:T(128)}, u32[]{:S(2)}) copy-start(s32[15]{0:T(128)} %param.28) | copy-start | bytes 184
  0.0 2.9 %copy-start.6 = (s32[15]{0:T(128)S(1)}, s32[15]{0:T(128)}, u32[]{:S(2)}) copy-start(s32[15]{0:T(128)} %param.27) | copy-start | bytes 184
  0.0 3.0 %copy-start.14 = (f32[15]{0:T(128)S(1)}, f32[15]{0:T(128)}, u32[]{:S(2)}) copy-start(f32[15]{0:T(128)} %param.29) | copy-start | bytes 184
  1.6 5.3 %collective-permute-start = (f32[480,128]{1,0:T(8,128)S(1)}, f32[480,128]{1,0:T(8,128)S(1)}, u32[]{:S(2)}, u32[]{:S(2)}) collective-permute-start(f32[480,128]{1,0:T(8,128)S(1)} %get-tuple-element.116), channel_id=1, source_target_pairs={{0,1},{1,0},{2,3},{3,2},{4,5},{5,4},{6,7},{7,6},{8,9},{9,8},{10,11... | collective-permute-start | bytes 737288 | tf_op jit(solution)/shard_map/ppermute | solution.py:991
  2.2 4.8 %collective-permute-start.1 = (f32[480,128]{1,0:T(8,128)S(1)}, f32[480,128]{1,0:T(8,128)S(1)}, u32[]{:S(2)}, u32[]{:S(2)}) collective-permute-start(f32[480,128]{1,0:T(8,128)S(1)} %get-tuple-element.117), channel_id=1, source_target_pairs={{1,2},{3,4},{5,6},{7,8},{9,10},{11,12},{13,14},{2,1},{4,3},{6,5},{... | collective-permute-start | bytes 737288 | tf_op jit(solution)/shard_map/ppermute | solution.py:991
  3.0 2.0 %copy-start.15 = (s32[1,75]{1,0:T(1,128)S(1)}, s32[1,75]{1,0:T(1,128)}, u32[]{:S(2)}) copy-start(s32[1,75]{1,0:T(1,128)} %param.25) | copy-start | bytes 904
  3.0 2.1 %copy-start.16 = (s32[1,75]{1,0:T(1,128)S(1)}, s32[1,75]{1,0:T(1,128)}, u32[]{:S(2)}) copy-start(s32[1,75]{1,0:T(1,128)} %param.26) | copy-start | bytes 904
  3.1 2.2 %copy-start.2 = (f32[8,4,4]{0,2,1:T(4,128)S(1)}, f32[8,4,4]{0,2,1:T(4,128)}, u32[]{:S(2)}) copy-start(f32[8,4,4]{0,2,1:T(4,128)} %param.20) | copy-start | bytes 1540
  5.1 17.2 %copy-start.3 = (f32[2,1,80,128]{3,2,1,0:T(8,128)S(1)}, f32[2,1,80,128]{3,2,1,0:T(8,128)}, u32[]{:S(2)}) copy-start(f32[2,1,80,128]{3,2,1,0:T(8,128)} %param.24) | copy-start | bytes 245764
  5.1 17.2 %copy-start.4 = (f32[2,1,80,128]{3,2,1,0:T(8,128)S(1)}, f32[2,1,80,128]{3,2,1,0:T(8,128)}, u32[]{:S(2)}) copy-start(f32[2,1,80,128]{3,2,1,0:T(8,128)} %param.23) | copy-start | bytes 245764
  6.9 22.7 %copy-start.1 = (f32[1,80,80]{2,1,0:T(8,128)S(1)}, f32[1,80,80]{2,1,0:T(8,128)}, u32[]{:S(2)}) copy-start(f32[1,80,80]{2,1,0:T(8,128)} %param.22) | copy-start | bytes 76804
  9.6 25.6 %copy-start.11 = (f32[480,128]{1,0:T(8,128)S(1)}, f32[480,128]{1,0:T(8,128)}, u32[]{:S(2)}) copy-start(f32[480,128]{1,0:T(8,128)} %get-tuple-element.142) | copy-start | bytes 737284
  9.6 26.0 %copy-start.10 = (f32[480,128]{1,0:T(8,128)S(1)}, f32[480,128]{1,0:T(8,128)}, u32[]{:S(2)}) copy-start(f32[480,128]{1,0:T(8,128)} %get-tuple-element.143) | copy-start | bytes 737284
  9.6 20.0 %all-to-all-start = ((f32[16,5,4,128]{3,2,1,0:T(4,128)}), f32[16,5,4,128]{3,2,1,0:T(4,128)S(1)}, u32[]{:S(2)}, u32[]{:S(2)}) async-start(f32[16,5,4,128]{3,2,1,0:T(4,128)} %bitcast.62), calls=%async_computation | async-start | bytes 327680 | tf_op jit(solution)/shard_map/all_to_all | solution.py:998
  21.2 1.5 collective-permute-start.2
  21.6 1.1 collective-permute-start.3
  31.7 13.3 %all-to-all-start.1 = ((f32[16,15,2,128]{3,2,1,0:T(2,128)}), f32[16,15,2,128]{3,2,1,0:T(2,128)S(1)}, u32[]{:S(2)}, u32[]{:S(2)}) async-start(f32[16,15,2,128]{3,2,1,0:T(2,128)} %bitcast.60), calls=%async_computation.1 | async-start | bytes 491520 | tf_op jit(solution)/shard_map/all_to_all | solution.py:998
  35.2 14.3 %collective-permute-start.4 = (f32[480,128]{1,0:T(8,128)S(1)}, f32[480,128]{1,0:T(8,128)S(1)}, u32[]{:S(2)}, u32[]{:S(2)}) collective-permute-start(f32[480,128]{1,0:T(8,128)S(1)} %copy-done.11), channel_id=1, source_target_pairs={{0,1},{1,0},{2,3},{3,2},{4,5},{5,4},{6,7},{7,6},{8,9},{9,8},{10,11... | collective-permute-start | bytes 737288 | tf_op jit(solution)/shard_map/ppermute | solution.py:991
  35.6 14.0 %collective-permute-start.5 = (f32[480,128]{1,0:T(8,128)S(1)}, f32[480,128]{1,0:T(8,128)S(1)}, u32[]{:S(2)}, u32[]{:S(2)}) collective-permute-start(f32[480,128]{1,0:T(8,128)S(1)} %copy-done.10), channel_id=1, source_target_pairs={{1,2},{3,4},{5,6},{7,8},{9,10},{11,12},{13,14},{2,1},{4,3},{6,5},{... | collective-permute-start | bytes 737288 | tf_op jit(solution)/shard_map/ppermute | solution.py:991
  46.8 2.7 %collective-permute-start.6 = (f32[60,128]{1,0:T(8,128)S(1)}, f32[60,128]{1,0:T(8,128)S(1)}, u32[]{:S(2)}, u32[]{:S(2)}) collective-permute-start(f32[60,128]{1,0:T(8,128)S(1)} %get-tuple-element.153), channel_id=1, source_target_pairs={{0,1},{1,0},{2,3},{3,2},{4,5},{5,4},{6,7},{7,6},{8,9},{9,8},{10,11... | collective-permute-start | bytes 92168 | tf_op jit(solution)/shard_map/ppermute | solution.py:991
  46.9 2.6 %collective-permute-start.7 = (f32[60,128]{1,0:T(8,128)S(1)}, f32[60,128]{1,0:T(8,128)S(1)}, u32[]{:S(2)}, u32[]{:S(2)}) collective-permute-start(f32[60,128]{1,0:T(8,128)S(1)} %get-tuple-element.154), channel_id=1, source_target_pairs={{1,2},{3,4},{5,6},{7,8},{9,10},{11,12},{13,14},{2,1},{4,3},{6,5},{... | collective-permute-start | bytes 92168 | tf_op jit(solution)/shard_map/ppermute | solution.py:991
  52.3 15.0 %all-to-all-start.2 = ((f32[16,5,4,128]{3,2,1,0:T(4,128)}), f32[16,5,4,128]{3,2,1,0:T(4,128)S(1)}, u32[]{:S(2)}, u32[]{:S(2)}) async-start(f32[16,5,4,128]{3,2,1,0:T(4,128)} %bitcast.63), calls=%async_computation.2 | async-start | bytes 327680 | tf_op jit(solution)/shard_map/all_to_all | solution.py:998
  58.9 1.5 collective-permute-start.8
  59.3 1.1 collective-permute-start.9
  69.0 13.3 %all-to-all-start.3 = ((f32[16,15,2,128]{3,2,1,0:T(2,128)}), f32[16,15,2,128]{3,2,1,0:T(2,128)S(1)}, u32[]{:S(2)}, u32[]{:S(2)}) async-start(f32[16,15,2,128]{3,2,1,0:T(2,128)} %bitcast.61), calls=%async_computation.3 | async-start | bytes 491520 | tf_op jit(solution)/shard_map/all_to_all | solution.py:998
  84.7 19.0 %copy-start.9 = (f32[480,128]{1,0:T(8,128)S(1)}, f32[480,128]{1,0:T(8,128)}, u32[]{:S(2)}) copy-start(f32[480,128]{1,0:T(8,128)} %get-tuple-element.164) | copy-start | bytes 737284
  84.7 19.4 %copy-start.8 = (f32[480,128]{1,0:T(8,128)S(1)}, f32[480,128]{1,0:T(8,128)}, u32[]{:S(2)}) copy-start(f32[480,128]{1,0:T(8,128)} %get-tuple-element.165) | copy-start | bytes 737284
  84.7 13.4 %all-to-all-start.4 = ((f32[16,15,2,128]{3,2,1,0:T(2,128)}), f32[16,15,2,128]{3,2,1,0:T(2,128)S(1)}, u32[]{:S(2)}, u32[]{:S(2)}) async-start(f32[16,15,2,128]{3,2,1,0:T(2,128)} %bitcast.59), calls=%async_computation.4 | async-start | bytes 491520 | tf_op jit(solution)/shard_map/all_to_all | solution.py:998
  88.4 1.5 collective-permute-start.12
  88.7 1.2 collective-permute-start.13
  100.2 12.0 %all-to-all-start.5 = ((f32[16,5,4,128]{3,2,1,0:T(4,128)}), f32[16,5,4,128]{3,2,1,0:T(4,128)S(1)}, u32[]{:S(2)}, u32[]{:S(2)}) async-start(f32[16,5,4,128]{3,2,1,0:T(4,128)} %bitcast.56), calls=%async_computation.5 | async-start | bytes 327680 | tf_op jit(solution)/shard_map/all_to_all | solution.py:998
  103.7 12.4 %collective-permute-start.10 = (f32[480,128]{1,0:T(8,128)S(1)}, f32[480,128]{1,0:T(8,128)S(1)}, u32[]{:S(2)}, u32[]{:S(2)}) collective-permute-start(f32[480,128]{1,0:T(8,128)S(1)} %copy-done.9), channel_id=1, source_target_pairs={{0,1},{1,0},{2,3},{3,2},{4,5},{5,4},{6,7},{7,6},{8,9},{9,8},{10,11... | collective-permute-start | bytes 737288 | tf_op jit(solution)/shard_map/ppermute | solution.py:991
  104.1 12.0 %collective-permute-start.11 = (f32[480,128]{1,0:T(8,128)S(1)}, f32[480,128]{1,0:T(8,128)S(1)}, u32[]{:S(2)}, u32[]{:S(2)}) collective-permute-start(f32[480,128]{1,0:T(8,128)S(1)} %copy-done.8), channel_id=1, source_target_pairs={{1,2},{3,4},{5,6},{7,8},{9,10},{11,12},{13,14},{2,1},{4,3},{6,5},{... | collective-permute-start | bytes 737288 | tf_op jit(solution)/shard_map/ppermute | solution.py:991
  113.3 2.8 %collective-permute-start.14 = (f32[60,128]{1,0:T(8,128)S(1)}, f32[60,128]{1,0:T(8,128)S(1)}, u32[]{:S(2)}, u32[]{:S(2)}) collective-permute-start(f32[60,128]{1,0:T(8,128)S(1)} %get-tuple-element.185), channel_id=1, source_target_pairs={{0,1},{1,0},{2,3},{3,2},{4,5},{5,4},{6,7},{7,6},{8,9},{9,8},{10,11... | collective-permute-start | bytes 92168 | tf_op jit(solution)/shard_map/ppermute | solution.py:991
  113.4 2.7 %collective-permute-start.15 = (f32[60,128]{1,0:T(8,128)S(1)}, f32[60,128]{1,0:T(8,128)S(1)}, u32[]{:S(2)}, u32[]{:S(2)}) collective-permute-start(f32[60,128]{1,0:T(8,128)S(1)} %get-tuple-element.186), channel_id=1, source_target_pairs={{1,2},{3,4},{5,6},{7,8},{9,10},{11,12},{13,14},{2,1},{4,3},{6,5},{... | collective-permute-start | bytes 92168 | tf_op jit(solution)/shard_map/ppermute | solution.py:991
  118.8 21.3 %copy-start.13 = (f32[480,128]{1,0:T(8,128)S(1)}, f32[480,128]{1,0:T(8,128)}, u32[]{:S(2)}) copy-start(f32[480,128]{1,0:T(8,128)} %get-tuple-element.203) | copy-start | bytes 737284
  118.8 21.6 %copy-start.12 = (f32[480,128]{1,0:T(8,128)S(1)}, f32[480,128]{1,0:T(8,128)}, u32[]{:S(2)}) copy-start(f32[480,128]{1,0:T(8,128)} %get-tuple-element.204) | copy-start | bytes 737284
  118.8 15.6 %all-to-all-start.6 = ((f32[16,15,2,128]{3,2,1,0:T(2,128)}), f32[16,15,2,128]{3,2,1,0:T(2,128)S(1)}, u32[]{:S(2)}, u32[]{:S(2)}) async-start(f32[16,15,2,128]{3,2,1,0:T(2,128)} %bitcast.58), calls=%async_computation.6 | async-start | bytes 491520 | tf_op jit(solution)/shard_map/all_to_all | solution.py:998
  124.7 1.8 %collective-permute-start.16 = (f32[32,128]{1,0:T(8,128)}, f32[32,128]{1,0:T(8,128)S(1)}, u32[]{:S(2)}, u32[]{:S(2)}) collective-permute-start(f32[32,128]{1,0:T(8,128)} %get-tuple-element.196), channel_id=1, source_target_pairs={{0,1},{1,0},{2,3},{3,2},{4,5},{5,4},{6,7},{7,6},{8,9},{9,8},{10,11... | collective-permute-start | bytes 49160 | tf_op jit(solution)/shard_map/ppermute | solution.py:991
  125.5 1.1 collective-permute-start.17
  136.5 12.0 %all-to-all-start.7 = ((f32[16,5,4,128]{3,2,1,0:T(4,128)}), f32[16,5,4,128]{3,2,1,0:T(4,128)S(1)}, u32[]{:S(2)}, u32[]{:S(2)}) async-start(f32[16,5,4,128]{3,2,1,0:T(4,128)} %bitcast.57), calls=%async_computation.7 | async-start | bytes 327680 | tf_op jit(solution)/shard_map/all_to_all | solution.py:998
  140.1 12.7 %collective-permute-start.18 = (f32[480,128]{1,0:T(8,128)S(1)}, f32[480,128]{1,0:T(8,128)S(1)}, u32[]{:S(2)}, u32[]{:S(2)}) collective-permute-start(f32[480,128]{1,0:T(8,128)S(1)} %copy-done.13), channel_id=1, source_target_pairs={{0,1},{1,0},{2,3},{3,2},{4,5},{5,4},{6,7},{7,6},{8,9},{9,8},{10,11... | collective-permute-start | bytes 737288 | tf_op jit(solution)/shard_map/ppermute | solution.py:991
  140.4 12.4 %collective-permute-start.19 = (f32[480,128]{1,0:T(8,128)S(1)}, f32[480,128]{1,0:T(8,128)S(1)}, u32[]{:S(2)}, u32[]{:S(2)}) collective-permute-start(f32[480,128]{1,0:T(8,128)S(1)} %copy-done.12), channel_id=1, source_target_pairs={{1,2},{3,4},{5,6},{7,8},{9,10},{11,12},{13,14},{2,1},{4,3},{6,5},{... | collective-permute-start | bytes 737288 | tf_op jit(solution)/shard_map/ppermute | solution.py:991
  149.7 3.1 %collective-permute-start.20 = (f32[60,128]{1,0:T(8,128)S(1)}, f32[60,128]{1,0:T(8,128)S(1)}, u32[]{:S(2)}, u32[]{:S(2)}) collective-permute-start(f32[60,128]{1,0:T(8,128)S(1)} %get-tuple-element.209), channel_id=1, source_target_pairs={{0,1},{1,0},{2,3},{3,2},{4,5},{5,4},{6,7},{7,6},{8,9},{9,8},{10,11... | collective-permute-start | bytes 92168 | tf_op jit(solution)/shard_map/ppermute | solution.py:991
  149.8 3.1 %collective-permute-start.21 = (f32[60,128]{1,0:T(8,128)S(1)}, f32[60,128]{1,0:T(8,128)S(1)}, u32[]{:S(2)}, u32[]{:S(2)}) collective-permute-start(f32[60,128]{1,0:T(8,128)S(1)} %get-tuple-element.210), channel_id=1, source_target_pairs={{1,2},{3,4},{5,6},{7,8},{9,10},{11,12},{13,14},{2,1},{4,3},{6,5},{... | collective-permute-start | bytes 92168 | tf_op jit(solution)/shard_map/ppermute | solution.py:991
  155.3 11.8 %all-to-all-start.8 = ((f32[16,1,128]{2,1,0:T(1,128)}), f32[16,1,128]{2,1,0:T(1,128)S(1)}, u32[]{:S(2)}, u32[]{:S(2)}) async-start(f32[16,1,128]{2,1,0:T(1,128)} %bitcast.64), calls=%async_computation.8 | async-start | bytes 16384 | tf_op jit(solution)/shard_map/all_to_all | solution.py:1233
  160.6 6.4 %copy-start = (f32[8,5,4,1920]{3,2,1,0:T(4,128)S(1)}, f32[8,5,4,1920]{3,2,1,0:T(4,128)}, u32[]{:S(2)}) copy-start(f32[8,5,4,1920]{3,2,1,0:T(4,128)} %refs_1_.6) | copy-start | bytes 3686404

commit v8 on v7

--- a/solution.py
+++ b/solution.py
@@ -109,10 +109,28 @@
     return masks[0] * pltpu.roll(field, 1, 0) + masks[1] * pltpu.roll(field, LEVELS - 1, 0)
 
 
-def rolled(tiles):
-    return [pltpu.roll(tile, 1, 1) for tile in tiles], [
-        pltpu.roll(tile, WIDTH - 1, 1) for tile in tiles
-    ]
+class RowTiles:
+    def __init__(self, count, load):
+        self.count, self.load, self.held = count, load, {}
+
+    def make(self, channel, tile):
+        value = self.load(channel, tile)
+        return value, pltpu.roll(value, 1, 1), pltpu.roll(value, WIDTH - 1, 1)
+
+    def get(self, channel, tile):
+        if (channel, tile) not in self.held:
+            self.held[channel, tile] = self.make(channel, tile)
+        return self.held[channel, tile]
+
+    def here(self, channel, tile):
+        return self.get(channel, tile)[0]
+
+    def around(self, channel, tile, lane):
+        last = self.count - 1
+        before = self.get(channel, tile - 1) if tile > 0 else self.make(channel, last)
+        after = self.get(channel, tile + 1) if tile < last else self.make(channel, 0)
+        _, to_right, to_left = self.get(channel, tile)
+        return lanes_sum(to_right, before[1], to_left, after[2], lane)
 
 
 def row_tiles_of(sz, ref, row):
@@ -422,8 +440,7 @@
         def _():
             ready(row + 1)
 
-        here = [[padded[row + 1, c, :, cols(t)] for t in range(count)] for c in range(CHANNELS)]
-        moved = [rolled(tiles) for tiles in here]
+        tiles = RowTiles(count, lambda c, t: padded[row + 1, c, :, cols(t)])
         for t in range(count):
             coeff = jnp.broadcast_to(diffusivity[row, 0:1, cols(t)], (LEVELS, WIDTH))
             center = (1.0 - 2.0 * KAPPA_V) - 4.0 * coeff
@@ -431,16 +448,13 @@
                 scale = weight[row, 0:1, cols(t)]
                 scale = jnp.broadcast_to(scale * scale, (LEVELS, WIDTH))
             for c in range(CHANNELS):
-                mixed = mix[c * CHANNELS] * here[0][t]
+                mixed = mix[c * CHANNELS] * tiles.here(0, t)
                 for k in range(1, CHANNELS):
-                    mixed = mixed + mix[c * CHANNELS + k] * here[k][t]
+                    mixed = mixed + mix[c * CHANNELS + k] * tiles.here(k, t)
                 bent = jnp.tanh(mixed)
                 drive[row, c, :, cols(t)] = bent
-                field_here = here[c][t]
-                to_right, to_left = moved[c]
-                around = lanes_sum(
-                    to_right[t], to_right[t - 1], to_left[t], to_left[(t + 1) % count], lane
-                )
+                field_here = tiles.here(c, t)
+                around = tiles.around(c, t, lane)
                 around = around + (padded[row, c, :, cols(t)] + padded[row + 2, c, :, cols(t)])
                 stepped = (
                     center * field_here
@@ -498,8 +512,26 @@
         told_first, told_second, own_table, own_facts, tables, weights = refs[:6]
         refs = refs[6:]
     flux, mixed_slope, flux_slope, flat, first = refs
+    def bulk(row, column):
+        return facts[sz.slot_lines, sz.bulk_at + row * CHANNELS + column]
+
+    values = [arrived[pl.ds(c, slots, stride=CHANNELS), :] for c in range(CHANNELS)]
+    mixed = jnp.tanh(
+        jnp.dot(
+            mixing[...],
+            jnp.concatenate(values, axis=1),
+            precision=HIGHEST,
+            preferred_element_type=jnp.float32,
+        )
+    )
+    contrast = []
+    for c in range(CHANNELS):
+        mixed_here = mixed[:, cols(c)]
+        mixed_slope[c] = 1.0 - mixed_here * mixed_here
+        contrast.append((air[...] - values[0] if c == 0 else values[c]) + mixed_here)
+    mixed_slope.start()
+    arrive_all(arrive)
     if decode:
-        arrive_all(arrive)
         lines = sz.slot_lines
         tables[0:lines, :] = own_table[...]
         weights[0 : sz.facts, :] = own_facts[...]
@@ -512,26 +544,6 @@
         tables.start()
         weights.start()
 
-    def bulk(row, column):
-        return facts[sz.slot_lines, sz.bulk_at + row * CHANNELS + column]
-
-    values = [arrived[pl.ds(c, slots, stride=CHANNELS), :] for c in range(CHANNELS)]
-    mixed = jnp.tanh(
-        jnp.dot(
-            mixing[...],
-            jnp.concatenate(values, axis=1),
-            precision=HIGHEST,
-            preferred_element_type=jnp.float32,
-        )
-    )
-    contrast = []
-    for c in range(CHANNELS):
-        mixed_here = mixed[:, cols(c)]
-        mixed_slope[c] = 1.0 - mixed_here * mixed_here
-        contrast.append((air[...] - values[0] if c == 0 else values[c]) + mixed_here)
-    mixed_slope.start()
-    if not decode:
-        arrive_all(arrive)
     rate = FLUX_RATE * wind[...]
     for c in range(CHANNELS):
         forcing = bulk(c, 0) * contrast[0]
@@ -789,8 +801,7 @@
         def _():
             ready(row + 1)
 
-        scaled = [[padded[row + 1, c, :, cols(t)] for t in range(count)] for c in range(CHANNELS)]
-        moved = [rolled(tiles) for tiles in scaled]
+        tiles = RowTiles(count, lambda c, t: padded[row + 1, c, :, cols(t)])
         for t in range(count):
             here, bent = [], []
             for c in range(CHANNELS):
@@ -802,13 +813,10 @@
                 mixed = mix[c] * bent[0]
                 for k in range(1, CHANNELS):
                     mixed = mixed + mix[k * CHANNELS + c] * bent[k]
-                to_right, to_left = moved[c]
-                around = lanes_sum(
-                    to_right[t], to_right[t - 1], to_left[t], to_left[(t + 1) % count], lane
-                )
+                around = tiles.around(c, t, lane)
                 around = around + (padded[row, c, :, cols(t)] + padded[row + 2, c, :, cols(t)])
                 stepped = (
-                    ((1.0 - 2.0 * KAPPA_V) * here[c] - 4.0 * scaled[c][t])
+                    ((1.0 - 2.0 * KAPPA_V) * here[c] - 4.0 * tiles.here(c, t))
                     + around
                     + levels_sum(here[c], masks)
                     + TIME_STEP * mixed

time: 170 us -> 170 us (level)
  no operation moved by 1% of the time
where the time goes in v8:
time: 170 us; the launch traced here: 168 us
  waiting for transfers between devices  63.5 us (37%)
  starting transfers between devices  58.1 us (34%)
  Pallas kernels  43.6 us (26%)
  local copies, waits for them, and re-layouts  1.88 us (1%)
    all_to_all x8, waiting for transfers between devices, exchange(): lax.all_to_all(split, 'horiz', split_axis=0, concat_axis=0, tiled=True)  57.1 us
    pallas_call x22, Pallas kernels, call(): pl.pallas_call(run, name=name, in_specs=[pl.BlockSpec(memory_space=item.s...  43.6 us
    all_to_all x8, starting transfers between devices, exchange(): lax.all_to_all(split, 'horiz', split_axis=0, concat_axis=0, tiled=True)  41.8 us
    ppermute x11, starting transfers between devices, swap(): lax.ppermute(second, 'horiz', outer)  7.25 us
    all_to_all x1, starting transfers between devices, body(): lax.all_to_all(sums, 'horiz', split_axis=0, concat_axis=0, tiled=True)  5.36 us
    all_to_all x1, waiting for transfers between devices, body(): lax.all_to_all(sums, 'horiz', split_axis=0, concat_axis=0, tiled=True)  4.68 us
    ppermute x11, starting transfers between devices, swap(): lax.ppermute(first, 'horiz', inner)  3.69 us
  transfers between devices with their start and end apart: 31, of which 13 were waited for; matrix products, arithmetic and copies ran while one was open for 1% of the time, Pallas kernels for 12%

profile of v8, /device:TPU:0, one launch (start us, length us, event | category | flops | bytes accessed | tf_op | source)
XLA Modules:
  0.0 167.9 jit_solution(2816987378661334025)
XLA Ops:
  0.0 1.6 edges.1
  1.6 0.5 collective-permute-start
  2.2 0.7 collective-permute-start.1
  3.1 2.0 %load.1.refs_6_ = f32[5,4,8,1920]{3,2,1,0:T(8,128)S(1)} custom-call(f32[8,5,4,1920]{3,2,1,0:T(4,128)} %refs_1_.6, f32[8,5,4,1920]{3,2,1,0:T(4,128)} %refs_1_.4), custom_call_target="tpu_custom_call" | custom-call | tf_op jit(solution)/shard_map/load/pallas_call | solution.py:978
  5.2 1.7 %setup.1 = (f32[16,8,128]{2,1,0:T(8,128)S(1)}, f32[5,1,1920]{2,1,0:T(1,128)S(1)}, s32[1,128]{1,0:T(1,128)}, f32[8,128]{1,0:T(8,128)}, f32[16,8,128]{2,1,0:T(8,128)}) custom-call(f32[2,128]{1,0:T(2,128)S(1)} %get-tuple-element.228.refs_0_, f32[2,128]{1,0:T(2,128)S(1)} %get-tuple-element.227.refs_1_, f32[16,8]{1,0:T(8,128)S(1)} %bitcast.55, f32[5,1920]{1,0:T(8,128)} %refs_0_.4), custom_call_target="tpu_custom_call" | custom-call | tf_op jit(solution)/shard_map/setup/pallas_call | solution.py:978
  7.0 2.6 %step.2 = (f32[5,4,8,1920]{3,2,1,0:T(8,128)}, f32[5,4,8,1920]{3,2,1,0:T(8,128)}, f32[304,128]{1,0:T(8,128)}, f32[320,128]{1,0:T(8,128)}, f32[40,128]{1,0:T(8,128...) custom-call(s32[1,128]{1,0:T(1,128)} %get-tuple-element.114.refs_0_.refs_7_.refs_5_, ...), custom_call_target="tpu_custom_call" | custom-call | tf_op jit(solution)/shard_map/step/pallas_call | solution.py:978
  9.6 11.6 %all-to-all-start = ((f32[16,5,4,128]{3,2,1,0:T(4,128)}), f32[16,5,4,128]{3,2,1,0:T(4,128)S(1)}, u32[]{:S(2)}, u32[]{:S(2)}) async-start(f32[16,5,4,128]{3,2,1,0:T(4,128)} %bitcast.62), calls=%async_computation | async-start | bytes 327680 | tf_op jit(solution)/shard_map/all_to_all | solution.py:1006
  21.2 0.4 collective-permute-start.2
  21.6 0.7 collective-permute-start.3
  22.3 0.4 collective-permute-done.2.refs_5_.refs_1_
  22.6 7.0 %all-to-all-done = f32[16,5,4,128]{3,2,1,0:T(4,128)S(1)} async-done(((f32[16,5,4,128]{3,2,1,0:T(4,128)}), f32[16,5,4,128]{3,2,1,0:T(4,128)S(1)}, u32[]{:S(2)}, u32[]{:S(2)}) %all-to-all-start) | async-done | bytes 163872 | tf_op jit(solution)/shard_map/all_to_all | solution.py:1006
  29.6 1.7 %owners.2 = (s32[3,128]{1,0:T(4,128)}, f32[24,128]{1,0:T(8,128)}, f32[480,128]{1,0:T(8,128)}, f32[4,80,128]{2,1,0:T(8,128)}, f32[4,80,128]{2,1,0:T(8,128)}) custom-call(f32[320,128]{1,0:T(8,128)S(1)} %bitcast.52, f32[80,80]{1,0:T(8,128)S(1)} %bitcast.46, f32[80,128]{1,0:T(8,128)S(1)} %get-tuple-element.229.refs_2_, ...), custom_call_target="tpu_custom_call" | custom-call | tf_op jit(solution)/shard_map/owners/pallas_call | solution.py:978
  31.3 3.5 %all-to-all-start.1 = ((f32[16,15,2,128]{3,2,1,0:T(2,128)}), f32[16,15,2,128]{3,2,1,0:T(2,128)S(1)}, u32[]{:S(2)}, u32[]{:S(2)}) async-start(f32[16,15,2,128]{3,2,1,0:T(2,128)} %bitcast.60), calls=%async_computation.1 | async-start | bytes 491520 | tf_op jit(solution)/shard_map/all_to_all | solution.py:1006
  34.9 0.4 collective-permute-start.4
  35.3 0.7 collective-permute-start.5
  35.9 2.3 %relayout.2.refs_5_ = f32[5,4,8,1920]{3,2,1,0:T(8,128)} custom-call(f32[8,5,4,1920]{3,2,1,0:T(4,128)} %refs_6_), custom_call_target="tpu_custom_call" | custom-call | tf_op jit(solution)/shard_map/relayout/pallas_call | solution.py:978
  38.2 1.7 %columns.1 = (f32[5,1,1920]{2,1,0:T(1,128)}, f32[5,1,1920]{2,1,0:T(1,128)}, f32[300,128]{1,0:T(8,128)}, f32[300,128]{1,0:T(8,128)}) custom-call(f32[5,1920]{1,0:T(8,128)} %refs_0_.4, f32[5,1920]{1,0:T(8,128)} %refs_1_.5), custom_call_target="tpu_custom_call" | custom-call | tf_op jit(solution)/shard_map/columns/pallas_call | solution.py:978
  40.0 4.7 %all-to-all-done.1 = f32[16,15,2,128]{3,2,1,0:T(2,128)S(1)} async-done(((f32[16,15,2,128]{3,2,1,0:T(2,128)}), f32[16,15,2,128]{3,2,1,0:T(2,128)S(1)}, u32[]{:S(2)}, u32[]{:S(2)}) %all-to-all-start.1) | async-done | bytes 245792 | tf_op jit(solution)/shard_map/all_to_all | solution.py:1006
  44.6 1.9 %surface.2 = (f32[304,128]{1,0:T(8,128)S(1)}, f32[60,128]{1,0:T(8,128)S(1)}, f32[60,128]{1,0:T(8,128)S(1)}, f32[64,128]{1,0:T(8,128)}) custom-call(f32[480,128]{1,0:T(8,128)S(1)} %bitcast.42, f32[40,128]{1,0:T(8,128)S(1)} %collective-permute-done.2.refs_5_.refs_1_, f32[40,128]{1,0:T(8,128)S(1)} %collective-permute-done.3.refs_6_.refs_2_, ...), custom_call_target="tpu_custom_call" | custom-call | tf_op jit(solution)/shard_map/surface/pallas_call | solution.py:978
  46.6 0.7 collective-permute-start.7
  47.3 1.9 %step_load.1 = (f32[16,8,128]{2,1,0:T(8,128)S(1)}, f32[5,1,1920]{2,1,0:T(1,128)S(1)}, f32[5,4,8,1920]{3,2,1,0:T(8,128)S(1)}, f32[5,1,1920]{2,1,0:T(1,128)S(1)}, f32[5,4,8,1920]{3,2,1,0:T(8,128)S(1)}) custom-call(f32[16,8,128]{2,1,0:T(8,128)} %get-tuple-element.144.refs_0_, f32[5,1,1920]{2,1,0:T(1,128)} %get-tuple-element.145.refs_1_, ...), custom_call_target="tpu_custom_call" | custom-call | tf_op jit(solution)/shard_map/step_load/pallas_call | solution.py:978
  49.3 2.7 %step.3 = (f32[5,4,8,1920]{3,2,1,0:T(8,128)}, f32[5,4,8,1920]{3,2,1,0:T(8,128)}, f32[304,128]{1,0:T(8,128)}, f32[320,128]{1,0:T(8,128)}, f32[32,128]{1,0:T(8,128...) custom-call(s32[1,128]{1,0:T(1,128)} %get-tuple-element.114.refs_0_.refs_7_.refs_5_, ...), custom_call_target="tpu_custom_call" | custom-call | tf_op jit(solution)/shard_map/step/pallas_call | solution.py:978
  52.0 6.6 %all-to-all-start.2 = ((f32[16,5,4,128]{3,2,1,0:T(4,128)}), f32[16,5,4,128]{3,2,1,0:T(4,128)S(1)}, u32[]{:S(2)}, u32[]{:S(2)}) async-start(f32[16,5,4,128]{3,2,1,0:T(4,128)} %bitcast.63), calls=%async_computation.2 | async-start | bytes 327680 | tf_op jit(solution)/shard_map/all_to_all | solution.py:1006
  58.5 0.4 collective-permute-start.8
  58.9 0.7 collective-permute-start.9
  59.6 0.4 collective-permute-done.8.refs_1_
  60.0 7.0 %all-to-all-done.2 = f32[16,5,4,128]{3,2,1,0:T(4,128)S(1)} async-done(((f32[16,5,4,128]{3,2,1,0:T(4,128)}), f32[16,5,4,128]{3,2,1,0:T(4,128)S(1)}, u32[]{:S(2)}, u32[]{:S(2)}) %all-to-all-start.2) | async-done | bytes 163872 | tf_op jit(solution)/shard_map/all_to_all | solution.py:1006
  67.0 1.7 %owners.3 = (f32[480,128]{1,0:T(8,128)}, f32[4,80,128]{2,1,0:T(8,128)}, f32[4,80,128]{2,1,0:T(8,128)}) custom-call(f32[320,128]{1,0:T(8,128)S(1)} %bitcast.53, f32[80,80]{1,0:T(8,128)S(1)} %bitcast.47, f32[80,128]{1,0:T(8,128)S(1)} %get-tuple-element.230.refs_2_, f32[80,128]{1,0:T(8,128)S(1)} %get-tuple-element.223.refs_3_, ...), custom_call_target="tpu_custom_call" | custom-call | tf_op jit(solution)/shard_map/owners/pallas_call | solution.py:978
  68.7 3.5 %all-to-all-start.3 = ((f32[16,15,2,128]{3,2,1,0:T(2,128)}), f32[16,15,2,128]{3,2,1,0:T(2,128)S(1)}, u32[]{:S(2)}, u32[]{:S(2)}) async-start(f32[16,15,2,128]{3,2,1,0:T(2,128)} %bitcast.61), calls=%async_computation.3 | async-start | bytes 491520 | tf_op jit(solution)/shard_map/all_to_all | solution.py:1006
  72.2 2.3 %relayout.3.refs_5_ = f32[5,4,8,1920]{3,2,1,0:T(8,128)} custom-call(f32[8,5,4,1920]{3,2,1,0:T(4,128)} %refs_1_.6), custom_call_target="tpu_custom_call" | custom-call | tf_op jit(solution)/shard_map/relayout/pallas_call | solution.py:978
  74.6 7.4 %all-to-all-done.3 = f32[16,15,2,128]{3,2,1,0:T(2,128)S(1)} async-done(((f32[16,15,2,128]{3,2,1,0:T(2,128)}), f32[16,15,2,128]{3,2,1,0:T(2,128)S(1)}, u32[]{:S(2)}, u32[]{:S(2)}) %all-to-all-start.3) | async-done | bytes 245792 | tf_op jit(solution)/shard_map/all_to_all | solution.py:1006
  82.0 2.3 %surface.3 = (f32[304,128]{1,0:T(8,128)}, f32[64,128]{1,0:T(8,128)}, f32[480,128]{1,0:T(8,128)}, f32[32,128]{1,0:T(8,128)}, f32[32,128]{1,0:T(8,128)}) custom-call(f32[480,128]{1,0:T(8,128)S(1)} %bitcast.45, f32[32,128]{1,0:T(8,128)S(1)} %collective-permute-done.8.refs_1_, f32[32,128]{1,0:T(8,128)S(1)} %collective-permute-done.9.refs_2_, ...), custom_call_target="tpu_custom_call" | custom-call | tf_op jit(solution)/shard_map/surface/pallas_call | solution.py:978
  84.4 3.7 %all-to-all-start.4 = ((f32[16,15,2,128]{3,2,1,0:T(2,128)}), f32[16,15,2,128]{3,2,1,0:T(2,128)S(1)}, u32[]{:S(2)}, u32[]{:S(2)}) async-start(f32[16,15,2,128]{3,2,1,0:T(2,128)} %bitcast.59), calls=%async_computation.4 | async-start | bytes 491520 | tf_op jit(solution)/shard_map/all_to_all | solution.py:1006
  88.0 0.3 collective-permute-start.12
  88.3 0.7 collective-permute-start.13
  89.0 0.5 collective-permute-done.12.refs_1_
  89.5 8.3 %all-to-all-done.4 = f32[16,15,2,128]{3,2,1,0:T(2,128)S(1)} async-done(((f32[16,15,2,128]{3,2,1,0:T(2,128)}), f32[16,15,2,128]{3,2,1,0:T(2,128)S(1)}, u32[]{:S(2)}, u32[]{:S(2)}) %all-to-all-start.4) | async-done | bytes 245792 | tf_op jit(solution)/shard_map/all_to_all | solution.py:1006
  97.8 2.0 %owners_back.2 = f32[320,128]{1,0:T(8,128)} custom-call(f32[480,128]{1,0:T(8,128)S(1)} %bitcast.43, f32[80,80]{1,0:T(8,128)S(1)} %bitcast.48, f32[4,80,128]{2,1,0:T(8,128)} %get-tuple-element.178.refs_2_, f32[4,80,128]{2,1,0:T(8,128)} %get-tuple-element.179.refs_3_, f32[8,128]{1,0:T(8,128)} %get-tuple-element.115.refs_1_.refs_7_.refs_4_.refs_8_.refs_6_), custom_call_target="tpu_custom_call" | custom-call | tf_op jit(solution)/shard_map/owners_back/pallas_call | solution.py:978
  99.8 3.5 %all-to-all-start.5 = ((f32[16,5,4,128]{3,2,1,0:T(4,128)}), f32[16,5,4,128]{3,2,1,0:T(4,128)S(1)}, u32[]{:S(2)}, u32[]{:S(2)}) async-start(f32[16,5,4,128]{3,2,1,0:T(4,128)} %bitcast.56), calls=%async_computation.5 | async-start | bytes 327680 | tf_op jit(solution)/shard_map/all_to_all | solution.py:1006
  103.4 0.4 collective-permute-start.10
  103.7 0.7 collective-permute-start.11
  104.4 7.4 %all-to-all-done.5 = f32[16,5,4,128]{3,2,1,0:T(4,128)S(1)} async-done(((f32[16,5,4,128]{3,2,1,0:T(4,128)}), f32[16,5,4,128]{3,2,1,0:T(4,128)S(1)}, u32[]{:S(2)}, u32[]{:S(2)}) %all-to-all-start.5) | async-done | bytes 163872 | tf_op jit(solution)/shard_map/all_to_all | solution.py:1006
  111.8 1.2 merge.2
  113.1 0.7 collective-permute-start.15
  113.7 2.0 %step_back_load.2 = (f32[16,8,128]{2,1,0:T(8,128)S(1)}, f32[5,1,1920]{2,1,0:T(1,128)S(1)}, f32[5,4,8,1920]{3,2,1,0:T(8,128)S(1)}, f32[5,4,8,1920]{3,2,1,0:T(8,128)S(1)}, f32[5,4,8,1920]{3,2,1,0:T(8,128)S(1)}) custom-call(f32[16,8,128]{2,1,0:T(8,128)} %get-tuple-element.144.refs_0_, f32[5,1,1920]{2,1,0:T(1,128)} %get-tuple-element.145.refs_1_, ...), custom_call_target="tpu_custom_call" | custom-call | tf_op jit(solution)/shard_map/step_back_load/pallas_call | solution.py:978
  115.8 2.7 %step_back.1 = (f32[5,4,8,1920]{3,2,1,0:T(8,128)}, f32[304,128]{1,0:T(8,128)}, f32[480,128]{1,0:T(8,128)}, f32[32,128]{1,0:T(8,128)}, f32[32,128]{1,0:T(8,128)}, /*index=5*/f32[480,128]{1,0:T(8,128)}, f32[480,128]{1,0:T(8,128)}) custom-call(s32[3,128]{1,0:T(4,128)} %get-tuple-element.126.refs_4_.refs_0_, f32[24,128]{1,0:T(8,128)} %get-tuple-element.127.refs_5_.refs_1_, ...), custom_call_target="tpu_custom_call" | custom-call | tf_op jit(solution)/shard_map/step_back/pallas_call | solution.py:978
  118.5 5.9 %all-to-all-start.6 = ((f32[16,15,2,128]{3,2,1,0:T(2,128)}), f32[16,15,2,128]{3,2,1,0:T(2,128)S(1)}, u32[]{:S(2)}, u32[]{:S(2)}) async-start(f32[16,15,2,128]{3,2,1,0:T(2,128)} %bitcast.58), calls=%async_computation.6 | async-start | bytes 491520 | tf_op jit(solution)/shard_map/all_to_all | solution.py:1006
  124.3 0.8 collective-permute-start.16
  125.1 0.7 collective-permute-start.17
  125.8 0.4 collective-permute-done.16.refs_1_
  126.2 7.9 %all-to-all-done.6 = f32[16,15,2,128]{3,2,1,0:T(2,128)S(1)} async-done(((f32[16,15,2,128]{3,2,1,0:T(2,128)}), f32[16,15,2,128]{3,2,1,0:T(2,128)S(1)}, u32[]{:S(2)}, u32[]{:S(2)}) %all-to-all-start.6) | async-done | bytes 245792 | tf_op jit(solution)/shard_map/all_to_all | solution.py:1006
  134.1 2.0 %owners_back.3 = f32[320,128]{1,0:T(8,128)} custom-call(f32[480,128]{1,0:T(8,128)S(1)} %bitcast.44, f32[80,80]{1,0:T(8,128)S(1)} %bitcast.49, f32[4,80,128]{2,1,0:T(8,128)} %get-tuple-element.199.refs_2_, f32[4,80,128]{2,1,0:T(8,128)} %get-tuple-element.200.refs_3_, f32[8,128]{1,0:T(8,128)} %get-tuple-element.115.refs_1_.refs_7_.refs_4_.refs_8_.refs_6_), custom_call_target="tpu_custom_call" | custom-call | tf_op jit(solution)/shard_map/owners_back/pallas_call | solution.py:978
  136.2 3.5 %all-to-all-start.7 = ((f32[16,5,4,128]{3,2,1,0:T(4,128)}), f32[16,5,4,128]{3,2,1,0:T(4,128)S(1)}, u32[]{:S(2)}, u32[]{:S(2)}) async-start(f32[16,5,4,128]{3,2,1,0:T(4,128)} %bitcast.57), calls=%async_computation.7 | async-start | bytes 327680 | tf_op jit(solution)/shard_map/all_to_all | solution.py:1006
  139.7 0.4 collective-permute-start.18
  140.1 0.7 collective-permute-start.19
  140.7 7.4 %all-to-all-done.7 = f32[16,5,4,128]{3,2,1,0:T(4,128)S(1)} async-done(((f32[16,5,4,128]{3,2,1,0:T(4,128)}), f32[16,5,4,128]{3,2,1,0:T(4,128)S(1)}, u32[]{:S(2)}, u32[]{:S(2)}) %all-to-all-start.7) | async-done | bytes 163872 | tf_op jit(solution)/shard_map/all_to_all | solution.py:1006
  148.1 1.2 merge.3
  149.4 0.7 collective-permute-start.21
  150.1 2.4 %step_back_load.3 = (f32[16,8,128]{2,1,0:T(8,128)S(1)}, f32[5,1,1920]{2,1,0:T(1,128)S(1)}, f32[5,4,8,1920]{3,2,1,0:T(8,128)S(1)}, f32[5,4,8,1920]{3,2,1,0:T(8,12...) custom-call(f32[16,8,128]{2,1,0:T(8,128)} %get-tuple-element.144.refs_0_, ...), custom_call_target="tpu_custom_call" | custom-call | tf_op jit(solution)/shard_map/step_back_load/pallas_call | solution.py:978
  152.5 2.4 %step_back_sums.1 = (f32[5,4,8,1920]{3,2,1,0:T(8,128)}, f32[16,128]{1,0:T(8,128)}) custom-call(f32[480,128]{1,0:T(8,128)S(1)} %collective-permute-done.18.refs_0_, f32[480,128]{1,0:T(8,128)S(1)} %collective-permute-done.19.refs_1_, f32[60,128]{1,0:T(8,128)S(1)} %collective-permute-done.20.refs_2_, f32[60,128]{1,0:T(8,128)S(1)} %collective-permute-done.21.refs_3_, ...), custom_call_target="tpu_custom_call" | custom-call | tf_op jit(solution)/shard_map/step_back_sums/pallas_call | solution.py:978
  154.9 5.4 %all-to-all-start.8 = ((f32[16,1,128]{2,1,0:T(1,128)}), f32[16,1,128]{2,1,0:T(1,128)S(1)}, u32[]{:S(2)}, u32[]{:S(2)}) async-start(f32[16,1,128]{2,1,0:T(1,128)} %bitcast.64), calls=%async_computation.8 | async-start | bytes 16384 | tf_op jit(solution)/shard_map/all_to_all | solution.py:1241
  160.3 1.7 %copy.20 = f32[5,4,8,1920]{3,1,0,2:T(4,128)S(1)} copy(f32[5,4,8,1920]{3,2,1,0:T(8,128)} %get-tuple-element.222) | data formatting | bytes 2457600 | tf_op jit(solution)/shard_map/step_back_sums/pallas_call | solution.py:978
  162.0 4.7 %all-to-all-done.8 = f32[16,1,128]{2,1,0:T(1,128)S(1)} async-done(((f32[16,1,128]{2,1,0:T(1,128)}), f32[16,1,128]{2,1,0:T(1,128)S(1)}, u32[]{:S(2)}, u32[]{:S(2)}) %all-to-all-start.8) | async-done | bytes 8224 | tf_op jit(solution)/shard_map/all_to_all | solution.py:1241
  166.7 1.2 finish.1
  (64 shorter events, 0.6 us)
Async XLA Ops:
  0.0 2.9 %copy-start.5 = (f32[4,4]{1,0:T(4,128)S(1)}, f32[4,4]{1,0:T(4,128)}, u32[]{:S(2)}) copy-start(f32[4,4]{1,0:T(4,128)} %param.21) | copy-start | bytes 196
  0.0 2.9 %copy-start.7 = (s32[15]{0:T(128)S(1)}, s32[15]{0:T(128)}, u32[]{:S(2)}) copy-start(s32[15]{0:T(128)} %param.28) | copy-start | bytes 184
  0.0 2.9 %copy-start.6 = (s32[15]{0:T(128)S(1)}, s32[15]{0:T(128)}, u32[]{:S(2)}) copy-start(s32[15]{0:T(128)} %param.27) | copy-start | bytes 184
  0.0 3.0 %copy-start.14 = (f32[15]{0:T(128)S(1)}, f32[15]{0:T(128)}, u32[]{:S(2)}) copy-start(f32[15]{0:T(128)} %param.29) | copy-start | bytes 184
  1.6 5.3 %collective-permute-start = (f32[480,128]{1,0:T(8,128)S(1)}, f32[480,128]{1,0:T(8,128)S(1)}, u32[]{:S(2)}, u32[]{:S(2)}) collective-permute-start(f32[480,128]{1,0:T(8,128)S(1)} %get-tuple-element.116), channel_id=1, source_target_pairs={{0,1},{1,0},{2,3},{3,2},{4,5},{5,4},{6,7},{7,6},{8,9},{9,8},{10,11... | collective-permute-start | bytes 737288 | tf_op jit(solution)/shard_map/ppermute | solution.py:999
  2.2 4.8 %collective-permute-start.1 = (f32[480,128]{1,0:T(8,128)S(1)}, f32[480,128]{1,0:T(8,128)S(1)}, u32[]{:S(2)}, u32[]{:S(2)}) collective-permute-start(f32[480,128]{1,0:T(8,128)S(1)} %get-tuple-element.117), channel_id=1, source_target_pairs={{1,2},{3,4},{5,6},{7,8},{9,10},{11,12},{13,14},{2,1},{4,3},{6,5},{... | collective-permute-start | bytes 737288 | tf_op jit(solution)/shard_map/ppermute | solution.py:999
  3.0 2.0 %copy-start.15 = (s32[1,75]{1,0:T(1,128)S(1)}, s32[1,75]{1,0:T(1,128)}, u32[]{:S(2)}) copy-start(s32[1,75]{1,0:T(1,128)} %param.25) | copy-start | bytes 904
  3.0 2.1 %copy-start.16 = (s32[1,75]{1,0:T(1,128)S(1)}, s32[1,75]{1,0:T(1,128)}, u32[]{:S(2)}) copy-start(s32[1,75]{1,0:T(1,128)} %param.26) | copy-start | bytes 904
  3.1 2.2 %copy-start.2 = (f32[8,4,4]{0,2,1:T(4,128)S(1)}, f32[8,4,4]{0,2,1:T(4,128)}, u32[]{:S(2)}) copy-start(f32[8,4,4]{0,2,1:T(4,128)} %param.20) | copy-start | bytes 1540
  5.1 17.2 %copy-start.3 = (f32[2,1,80,128]{3,2,1,0:T(8,128)S(1)}, f32[2,1,80,128]{3,2,1,0:T(8,128)}, u32[]{:S(2)}) copy-start(f32[2,1,80,128]{3,2,1,0:T(8,128)} %param.24) | copy-start | bytes 245764
  5.1 17.2 %copy-start.4 = (f32[2,1,80,128]{3,2,1,0:T(8,128)S(1)}, f32[2,1,80,128]{3,2,1,0:T(8,128)}, u32[]{:S(2)}) copy-start(f32[2,1,80,128]{3,2,1,0:T(8,128)} %param.23) | copy-start | bytes 245764
  6.9 22.7 %copy-start.1 = (f32[1,80,80]{2,1,0:T(8,128)S(1)}, f32[1,80,80]{2,1,0:T(8,128)}, u32[]{:S(2)}) copy-start(f32[1,80,80]{2,1,0:T(8,128)} %param.22) | copy-start | bytes 76804
  9.6 25.3 %copy-start.11 = (f32[480,128]{1,0:T(8,128)S(1)}, f32[480,128]{1,0:T(8,128)}, u32[]{:S(2)}) copy-start(f32[480,128]{1,0:T(8,128)} %get-tuple-element.142) | copy-start | bytes 737284
  9.6 25.7 %copy-start.10 = (f32[480,128]{1,0:T(8,128)S(1)}, f32[480,128]{1,0:T(8,128)}, u32[]{:S(2)}) copy-start(f32[480,128]{1,0:T(8,128)} %get-tuple-element.143) | copy-start | bytes 737284
  9.6 20.0 %all-to-all-start = ((f32[16,5,4,128]{3,2,1,0:T(4,128)}), f32[16,5,4,128]{3,2,1,0:T(4,128)S(1)}, u32[]{:S(2)}, u32[]{:S(2)}) async-start(f32[16,5,4,128]{3,2,1,0:T(4,128)} %bitcast.62), calls=%async_computation | async-start | bytes 327680 | tf_op jit(solution)/shard_map/all_to_all | solution.py:1006
  21.2 1.5 collective-permute-start.2
  21.6 1.1 collective-permute-start.3
  31.3 13.3 %all-to-all-start.1 = ((f32[16,15,2,128]{3,2,1,0:T(2,128)}), f32[16,15,2,128]{3,2,1,0:T(2,128)S(1)}, u32[]{:S(2)}, u32[]{:S(2)}) async-start(f32[16,15,2,128]{3,2,1,0:T(2,128)} %bitcast.60), calls=%async_computation.1 | async-start | bytes 491520 | tf_op jit(solution)/shard_map/all_to_all | solution.py:1006
  34.9 14.3 %collective-permute-start.4 = (f32[480,128]{1,0:T(8,128)S(1)}, f32[480,128]{1,0:T(8,128)S(1)}, u32[]{:S(2)}, u32[]{:S(2)}) collective-permute-start(f32[480,128]{1,0:T(8,128)S(1)} %copy-done.11), channel_id=1, source_target_pairs={{0,1},{1,0},{2,3},{3,2},{4,5},{5,4},{6,7},{7,6},{8,9},{9,8},{10,11... | collective-permute-start | bytes 737288 | tf_op jit(solution)/shard_map/ppermute | solution.py:999
  35.3 14.0 %collective-permute-start.5 = (f32[480,128]{1,0:T(8,128)S(1)}, f32[480,128]{1,0:T(8,128)S(1)}, u32[]{:S(2)}, u32[]{:S(2)}) collective-permute-start(f32[480,128]{1,0:T(8,128)S(1)} %copy-done.10), channel_id=1, source_target_pairs={{1,2},{3,4},{5,6},{7,8},{9,10},{11,12},{13,14},{2,1},{4,3},{6,5},{... | collective-permute-start | bytes 737288 | tf_op jit(solution)/shard_map/ppermute | solution.py:999
  46.5 2.7 %collective-permute-start.6 = (f32[60,128]{1,0:T(8,128)S(1)}, f32[60,128]{1,0:T(8,128)S(1)}, u32[]{:S(2)}, u32[]{:S(2)}) collective-permute-start(f32[60,128]{1,0:T(8,128)S(1)} %get-tuple-element.153), channel_id=1, source_target_pairs={{0,1},{1,0},{2,3},{3,2},{4,5},{5,4},{6,7},{7,6},{8,9},{9,8},{10,11... | collective-permute-start | bytes 92168 | tf_op jit(solution)/shard_map/ppermute | solution.py:999
  46.6 2.6 %collective-permute-start.7 = (f32[60,128]{1,0:T(8,128)S(1)}, f32[60,128]{1,0:T(8,128)S(1)}, u32[]{:S(2)}, u32[]{:S(2)}) collective-permute-start(f32[60,128]{1,0:T(8,128)S(1)} %get-tuple-element.154), channel_id=1, source_target_pairs={{1,2},{3,4},{5,6},{7,8},{9,10},{11,12},{13,14},{2,1},{4,3},{6,5},{... | collective-permute-start | bytes 92168 | tf_op jit(solution)/shard_map/ppermute | solution.py:999
  52.0 15.0 %all-to-all-start.2 = ((f32[16,5,4,128]{3,2,1,0:T(4,128)}), f32[16,5,4,128]{3,2,1,0:T(4,128)S(1)}, u32[]{:S(2)}, u32[]{:S(2)}) async-start(f32[16,5,4,128]{3,2,1,0:T(4,128)} %bitcast.63), calls=%async_computation.2 | async-start | bytes 327680 | tf_op jit(solution)/shard_map/all_to_all | solution.py:1006
  58.5 1.5 collective-permute-start.8
  58.9 1.1 collective-permute-start.9
  68.7 13.3 %all-to-all-start.3 = ((f32[16,15,2,128]{3,2,1,0:T(2,128)}), f32[16,15,2,128]{3,2,1,0:T(2,128)S(1)}, u32[]{:S(2)}, u32[]{:S(2)}) async-start(f32[16,15,2,128]{3,2,1,0:T(2,128)} %bitcast.61), calls=%async_computation.3 | async-start | bytes 491520 | tf_op jit(solution)/shard_map/all_to_all | solution.py:1006
  84.3 19.0 %copy-start.9 = (f32[480,128]{1,0:T(8,128)S(1)}, f32[480,128]{1,0:T(8,128)}, u32[]{:S(2)}) copy-start(f32[480,128]{1,0:T(8,128)} %get-tuple-element.164) | copy-start | bytes 737284
  84.4 19.4 %copy-start.8 = (f32[480,128]{1,0:T(8,128)S(1)}, f32[480,128]{1,0:T(8,128)}, u32[]{:S(2)}) copy-start(f32[480,128]{1,0:T(8,128)} %get-tuple-element.165) | copy-start | bytes 737284
  84.4 13.4 %all-to-all-start.4 = ((f32[16,15,2,128]{3,2,1,0:T(2,128)}), f32[16,15,2,128]{3,2,1,0:T(2,128)S(1)}, u32[]{:S(2)}, u32[]{:S(2)}) async-start(f32[16,15,2,128]{3,2,1,0:T(2,128)} %bitcast.59), calls=%async_computation.4 | async-start | bytes 491520 | tf_op jit(solution)/shard_map/all_to_all | solution.py:1006
  88.0 1.5 collective-permute-start.12
  88.3 1.2 collective-permute-start.13
  99.8 12.0 %all-to-all-start.5 = ((f32[16,5,4,128]{3,2,1,0:T(4,128)}), f32[16,5,4,128]{3,2,1,0:T(4,128)S(1)}, u32[]{:S(2)}, u32[]{:S(2)}) async-start(f32[16,5,4,128]{3,2,1,0:T(4,128)} %bitcast.56), calls=%async_computation.5 | async-start | bytes 327680 | tf_op jit(solution)/shard_map/all_to_all | solution.py:1006
  103.4 12.4 %collective-permute-start.10 = (f32[480,128]{1,0:T(8,128)S(1)}, f32[480,128]{1,0:T(8,128)S(1)}, u32[]{:S(2)}, u32[]{:S(2)}) collective-permute-start(f32[480,128]{1,0:T(8,128)S(1)} %copy-done.9), channel_id=1, source_target_pairs={{0,1},{1,0},{2,3},{3,2},{4,5},{5,4},{6,7},{7,6},{8,9},{9,8},{10,11... | collective-permute-start | bytes 737288 | tf_op jit(solution)/shard_map/ppermute | solution.py:999
  103.7 12.0 %collective-permute-start.11 = (f32[480,128]{1,0:T(8,128)S(1)}, f32[480,128]{1,0:T(8,128)S(1)}, u32[]{:S(2)}, u32[]{:S(2)}) collective-permute-start(f32[480,128]{1,0:T(8,128)S(1)} %copy-done.8), channel_id=1, source_target_pairs={{1,2},{3,4},{5,6},{7,8},{9,10},{11,12},{13,14},{2,1},{4,3},{6,5},{... | collective-permute-start | bytes 737288 | tf_op jit(solution)/shard_map/ppermute | solution.py:999
  113.0 2.8 %collective-permute-start.14 = (f32[60,128]{1,0:T(8,128)S(1)}, f32[60,128]{1,0:T(8,128)S(1)}, u32[]{:S(2)}, u32[]{:S(2)}) collective-permute-start(f32[60,128]{1,0:T(8,128)S(1)} %get-tuple-element.185), channel_id=1, source_target_pairs={{0,1},{1,0},{2,3},{3,2},{4,5},{5,4},{6,7},{7,6},{8,9},{9,8},{10,11... | collective-permute-start | bytes 92168 | tf_op jit(solution)/shard_map/ppermute | solution.py:999
  113.1 2.7 %collective-permute-start.15 = (f32[60,128]{1,0:T(8,128)S(1)}, f32[60,128]{1,0:T(8,128)S(1)}, u32[]{:S(2)}, u32[]{:S(2)}) collective-permute-start(f32[60,128]{1,0:T(8,128)S(1)} %get-tuple-element.186), channel_id=1, source_target_pairs={{1,2},{3,4},{5,6},{7,8},{9,10},{11,12},{13,14},{2,1},{4,3},{6,5},{... | collective-permute-start | bytes 92168 | tf_op jit(solution)/shard_map/ppermute | solution.py:999
  118.5 21.2 %copy-start.13 = (f32[480,128]{1,0:T(8,128)S(1)}, f32[480,128]{1,0:T(8,128)}, u32[]{:S(2)}) copy-start(f32[480,128]{1,0:T(8,128)} %get-tuple-element.203) | copy-start | bytes 737284
  118.5 21.6 %copy-start.12 = (f32[480,128]{1,0:T(8,128)S(1)}, f32[480,128]{1,0:T(8,128)}, u32[]{:S(2)}) copy-start(f32[480,128]{1,0:T(8,128)} %get-tuple-element.204) | copy-start | bytes 737284
  118.5 15.6 %all-to-all-start.6 = ((f32[16,15,2,128]{3,2,1,0:T(2,128)}), f32[16,15,2,128]{3,2,1,0:T(2,128)S(1)}, u32[]{:S(2)}, u32[]{:S(2)}) async-start(f32[16,15,2,128]{3,2,1,0:T(2,128)} %bitcast.58), calls=%async_computation.6 | async-start | bytes 491520 | tf_op jit(solution)/shard_map/all_to_all | solution.py:1006
  124.3 1.8 %collective-permute-start.16 = (f32[32,128]{1,0:T(8,128)}, f32[32,128]{1,0:T(8,128)S(1)}, u32[]{:S(2)}, u32[]{:S(2)}) collective-permute-start(f32[32,128]{1,0:T(8,128)} %get-tuple-element.196), channel_id=1, source_target_pairs={{0,1},{1,0},{2,3},{3,2},{4,5},{5,4},{6,7},{7,6},{8,9},{9,8},{10,11... | collective-permute-start | bytes 49160 | tf_op jit(solution)/shard_map/ppermute | solution.py:999
  125.1 1.1 collective-permute-start.17
  136.2 12.0 %all-to-all-start.7 = ((f32[16,5,4,128]{3,2,1,0:T(4,128)}), f32[16,5,4,128]{3,2,1,0:T(4,128)S(1)}, u32[]{:S(2)}, u32[]{:S(2)}) async-start(f32[16,5,4,128]{3,2,1,0:T(4,128)} %bitcast.57), calls=%async_computation.7 | async-start | bytes 327680 | tf_op jit(solution)/shard_map/all_to_all | solution.py:1006
  139.7 12.7 %collective-permute-start.18 = (f32[480,128]{1,0:T(8,128)S(1)}, f32[480,128]{1,0:T(8,128)S(1)}, u32[]{:S(2)}, u32[]{:S(2)}) collective-permute-start(f32[480,128]{1,0:T(8,128)S(1)} %copy-done.13), channel_id=1, source_target_pairs={{0,1},{1,0},{2,3},{3,2},{4,5},{5,4},{6,7},{7,6},{8,9},{9,8},{10,11... | collective-permute-start | bytes 737288 | tf_op jit(solution)/shard_map/ppermute | solution.py:999
  140.1 12.4 %collective-permute-start.19 = (f32[480,128]{1,0:T(8,128)S(1)}, f32[480,128]{1,0:T(8,128)S(1)}, u32[]{:S(2)}, u32[]{:S(2)}) collective-permute-start(f32[480,128]{1,0:T(8,128)S(1)} %copy-done.12), channel_id=1, source_target_pairs={{1,2},{3,4},{5,6},{7,8},{9,10},{11,12},{13,14},{2,1},{4,3},{6,5},{... | collective-permute-start | bytes 737288 | tf_op jit(solution)/shard_map/ppermute | solution.py:999
  149.3 3.1 %collective-permute-start.20 = (f32[60,128]{1,0:T(8,128)S(1)}, f32[60,128]{1,0:T(8,128)S(1)}, u32[]{:S(2)}, u32[]{:S(2)}) collective-permute-start(f32[60,128]{1,0:T(8,128)S(1)} %get-tuple-element.209), channel_id=1, source_target_pairs={{0,1},{1,0},{2,3},{3,2},{4,5},{5,4},{6,7},{7,6},{8,9},{9,8},{10,11... | collective-permute-start | bytes 92168 | tf_op jit(solution)/shard_map/ppermute | solution.py:999
  149.4 3.1 %collective-permute-start.21 = (f32[60,128]{1,0:T(8,128)S(1)}, f32[60,128]{1,0:T(8,128)S(1)}, u32[]{:S(2)}, u32[]{:S(2)}) collective-permute-start(f32[60,128]{1,0:T(8,128)S(1)} %get-tuple-element.210), channel_id=1, source_target_pairs={{1,2},{3,4},{5,6},{7,8},{9,10},{11,12},{13,14},{2,1},{4,3},{6,5},{... | collective-permute-start | bytes 92168 | tf_op jit(solution)/shard_map/ppermute | solution.py:999
  154.9 11.8 %all-to-all-start.8 = ((f32[16,1,128]{2,1,0:T(1,128)}), f32[16,1,128]{2,1,0:T(1,128)S(1)}, u32[]{:S(2)}, u32[]{:S(2)}) async-start(f32[16,1,128]{2,1,0:T(1,128)} %bitcast.64), calls=%async_computation.8 | async-start | bytes 16384 | tf_op jit(solution)/shard_map/all_to_all | solution.py:1241
  160.3 6.4 %copy-start = (f32[8,5,4,1920]{3,2,1,0:T(4,128)S(1)}, f32[8,5,4,1920]{3,2,1,0:T(4,128)}, u32[]{:S(2)}) copy-start(f32[8,5,4,1920]{3,2,1,0:T(4,128)} %refs_1_.6) | copy-start | bytes 3686404

commit v9 on v8

--- a/solution.py
+++ b/solution.py
@@ -51,7 +51,7 @@
         self.lats = (self.lat_lines, WIDTH)
         self.bulk_at = NEAR_LAT * rows
         self.tables = (3 * self.slot_lines, WIDTH)
-        self.weights = (3 * self.facts, WIDTH)
+        self.weights = (3, WIDTH)
         self.near = (-(-(self.tiles + 1) // SUBLANES) * SUBLANES, WIDTH)
         self.by_slot = (CHANNELS, self.slots, WIDTH)
 
@@ -172,7 +172,7 @@
 
 
 def setup_kernel(sz, entries, remap_entries, arrive, wet, remap, mix_rows, diffusivity, *outs):
-    first_mix, first_rows, table, facts, mix = outs
+    first_mix, first_rows, table, facts, line, mix = outs
     arrive_all(arrive)
     for row in range(sz.rows):
         first_rows[row] = diffusivity[row : row + 1, :]
@@ -190,18 +190,19 @@
     rank = jnp.sum(jnp.where(same, 1.0, 0.0), axis=1, keepdims=True)
     slot = jnp.where(owner_here >= 0.0, owner_here * sz.capacity + rank, -1.0)
     facts[...] = jnp.zeros((sz.facts, WIDTH), jnp.float32)
-    for line in range(sz.slot_lines):
-        place = lax.broadcasted_iota(jnp.int32, (size, WIDTH), 1) + line * WIDTH
+    for index in range(sz.slot_lines):
+        place = lax.broadcasted_iota(jnp.int32, (size, WIDTH), 1) + index * WIDTH
         match = slot.astype(jnp.int32) == place
         told = jnp.sum(jnp.where(match, sz.tiles - tile_here, 0.0), axis=0, keepdims=True)
-        facts[line : line + 1, :] = told
-        table[line : line + 1, :] = sz.tiles - told.astype(jnp.int32)
+        facts[index : index + 1, :] = told
+        table[index : index + 1, :] = sz.tiles - told.astype(jnp.int32)
     size = -(-remap_entries // SUBLANES) * SUBLANES
     at, amount = as_column(remap[0:1, :], size), as_column(remap[1:2, :], size)
     place = lax.broadcasted_iota(jnp.int32, (size, WIDTH), 1)
-    facts[sz.slot_lines : sz.slot_lines + 1, :] = jnp.sum(
+    line[...] = jnp.sum(
         jnp.where(at.astype(jnp.int32) == place, amount, 0.0), axis=0, keepdims=True
     )
+    facts[sz.slot_lines : sz.slot_lines + 1, :] = line[...]
 
 
 def columns_kernel(sz, arrive, diffusivity, weight, *outs):
@@ -293,8 +294,7 @@
         self.sz, self.weights = sz, weights
 
     def weight(self, which, lat, row):
-        line = which * self.sz.facts + self.sz.slot_lines
-        return self.weights[line, lat * self.sz.rows + row]
+        return self.weights[which, lat * self.sz.rows + row]
 
     def own(self, lat, row):
         return self.weight(0, lat, row)
@@ -512,8 +512,9 @@
         told_first, told_second, own_table, own_facts, tables, weights = refs[:6]
         refs = refs[6:]
     flux, mixed_slope, flux_slope, flat, first = refs
+
     def bulk(row, column):
-        return facts[sz.slot_lines, sz.bulk_at + row * CHANNELS + column]
+        return facts[0, sz.bulk_at + row * CHANNELS + column]
 
     values = [arrived[pl.ds(c, slots, stride=CHANNELS), :] for c in range(CHANNELS)]
     mixed = jnp.tanh(
@@ -534,13 +535,12 @@
     if decode:
         lines = sz.slot_lines
         tables[0:lines, :] = own_table[...]
-        weights[0 : sz.facts, :] = own_facts[...]
+        weights[0:1, :] = own_facts[...]
         both = sided(told_first[sz.lat_lines :, :], told_second[sz.lat_lines :, :])
         for which, told in ((1, both[0]), (2, both[1])):
             got = told[0:lines, :].astype(jnp.int32)
             tables[which * lines : (which + 1) * lines, :] = sz.tiles - got
-            at = which * sz.facts
-            weights[at : at + sz.facts, :] = told
+            weights[which : which + 1, :] = told[lines : lines + 1, :]
         tables.start()
         weights.start()
 
@@ -573,7 +573,7 @@
     slots, cap = sz.slots, sz.capacity
 
     def bulk(row, column):
-        return facts[sz.slot_lines, sz.bulk_at + row * CHANNELS + column]
+        return facts[0, sz.bulk_at + row * CHANNELS + column]
 
     for d in range(sz.devices):
         at = d * sz.chunk
@@ -1053,7 +1053,7 @@
     mix_rows = chan_mix.transpose(1, 2, 0).reshape(CHANNELS * CHANNELS, LEVELS)
     row_lines = (rows, 1, sz.cells)
     tiles_lines = (CHANNELS * sz.tiles, WIDTH)
-    first_mix, first_rows, table, facts, mix = call(
+    first_mix, first_rows, table, facts, line, mix = call(
         functools.partial(setup_kernel, sz, wet_list.shape[1], remap_at.shape[0] + places.shape[0]),
         "setup",
         near_by(lined(wet_list[0], wet_owner[0]), remap_lines, mix_rows)
@@ -1062,6 +1062,7 @@
         shipped=[
             jax.ShapeDtypeStruct((sz.slot_lines, WIDTH), jnp.int32),
             (sz.facts, WIDTH),
+            (1, WIDTH),
             (CHANNELS * CHANNELS, LEVELS, WIDTH),
         ],
     )
@@ -1095,7 +1096,7 @@
     by_slot = (sz.slots, WIDTH)
     for hour in range(hours):
         first, last = hour == 0, hour == hours - 1
-        inputs = scalars(table, facts)
+        inputs = scalars(table, line)
         if first:
             inputs += near_by(*edges, first_rows, first_mix, field) + fetched(facts)
             assert not last
@@ -1124,11 +1125,11 @@
         arrived, *got = lax.optimization_barrier((arrived, *got))
         inputs = (
             near_by(arrived, owner_mix[0], air_temp[hour, 0], wind_speed[hour, 0])
-            + scalars(facts)
+            + scalars(line)
         )
         decoded = []
         if first:
-            inputs += near_by(*got) + fetched(table, facts)
+            inputs += near_by(*got) + fetched(table, line)
             decoded = [jax.ShapeDtypeStruct(sz.tables, jnp.int32), sz.weights]
         *decoded, flux, mixed_slope, flux_slope = call(
             functools.partial(owner_kernel, sz, first),
@@ -1190,7 +1191,7 @@
         back = call(
             functools.partial(owner_back_kernel, sz),
             "owners_back",
-            near_by(arrived, owner_mix[0]) + fetched(mixed_slope, flux_slope) + scalars(facts),
+            near_by(arrived, owner_mix[0]) + fetched(mixed_slope, flux_slope) + scalars(line),
             shipped=[sz.narrow],
             scratch=[sz.narrow, by_slot],
         )[0]
@@ -1203,7 +1204,7 @@
             "merge",
             near_by(back, *got)
             + fetched(surface, slope)
-            + scalars(table, facts)
+            + scalars(table, line)
             + fetched(diffusivity_tiles),
             kept=[sz.surface, row_surface, row_surface],
         )

time: 170 us -> 169 us (level)
  no operation moved by 1% of the time
where the time goes in v9:
time: 169 us; the launch traced here: 168 us
  waiting for transfers between devices  63.5 us (38%)
  starting transfers between devices  58.1 us (34%)
  Pallas kernels  43.4 us (26%)
  local copies, waits for them, and re-layouts  1.88 us (1%)
    all_to_all x8, waiting for transfers between devices, exchange(): lax.all_to_all(split, 'horiz', split_axis=0, concat_axis=0, tiled=True)  57.1 us
    pallas_call x22, Pallas kernels, call(): pl.pallas_call(run, name=name, in_specs=[pl.BlockSpec(memory_space=item.s...  43.4 us
    all_to_all x8, starting transfers between devices, exchange(): lax.all_to_all(split, 'horiz', split_axis=0, concat_axis=0, tiled=True)  41.8 us
    ppermute x11, starting transfers between devices, swap(): lax.ppermute(second, 'horiz', outer)  7.25 us
    all_to_all x1, starting transfers between devices, body(): lax.all_to_all(sums, 'horiz', split_axis=0, concat_axis=0, tiled=True)  5.36 us
    all_to_all x1, waiting for transfers between devices, body(): lax.all_to_all(sums, 'horiz', split_axis=0, concat_axis=0, tiled=True)  4.68 us
    ppermute x11, starting transfers between devices, swap(): lax.ppermute(first, 'horiz', inner)  3.69 us
  transfers between devices with their start and end apart: 31, of which 13 were waited for; matrix products, arithmetic and copies ran while one was open for 1% of the time, Pallas kernels for 12%

profile of v9, /device:TPU:0, one launch (start us, length us, event | category | flops | bytes accessed | tf_op | source)
XLA Modules:
  0.0 167.7 jit_solution(12887002017403522317)
XLA Ops:
  0.0 1.6 edges.1
  1.6 0.5 collective-permute-start
  2.2 0.7 collective-permute-start.1
  3.1 2.0 %load.1.refs_6_ = f32[5,4,8,1920]{3,2,1,0:T(8,128)S(1)} custom-call(f32[8,5,4,1920]{3,2,1,0:T(4,128)} %refs_1_.6, f32[8,5,4,1920]{3,2,1,0:T(4,128)} %refs_1_.4), custom_call_target="tpu_custom_call" | custom-call | tf_op jit(solution)/shard_map/load/pallas_call | solution.py:978
  5.2 1.7 %setup.1 = (f32[16,8,128]{2,1,0:T(8,128)S(1)}, f32[5,1,1920]{2,1,0:T(1,128)S(1)}, s32[1,128]{1,0:T(1,128)}, f32[8,128]{1,0:T(8,128)}, f32[1,128]{1,0:T(1,128)}, /*index=5*/f32[16,8,128]{2,1,0:T(8,128)}) custom-call(f32[2,128]{1,0:T(2,128)S(1)} %get-tuple-element.230.refs_0_, f32[2,128]{1,0:T(2,128)S(1)} %get-tuple-element.229.refs_1_, f32[16,8]{1,0:T(8,128)S(1)} %bitcast.55, ...), custom_call_target="tpu_custom_call" | custom-call | tf_op jit(solution)/shard_map/setup/pallas_call | solution.py:978
  7.0 2.6 %step.2 = (f32[5,4,8,1920]{3,2,1,0:T(8,128)}, f32[5,4,8,1920]{3,2,1,0:T(8,128)}, f32[304,128]{1,0:T(8,128)}, f32[320,128]{1,0:T(8,128)}, f32[40,128]{1,0:T(8,128...) custom-call(s32[1,128]{1,0:T(1,128)} %get-tuple-element.115.refs_0_.refs_7_.refs_5_, ...), custom_call_target="tpu_custom_call" | custom-call | tf_op jit(solution)/shard_map/step/pallas_call | solution.py:978
  9.6 11.6 %all-to-all-start = ((f32[16,5,4,128]{3,2,1,0:T(4,128)}), f32[16,5,4,128]{3,2,1,0:T(4,128)S(1)}, u32[]{:S(2)}, u32[]{:S(2)}) async-start(f32[16,5,4,128]{3,2,1,0:T(4,128)} %bitcast.62), calls=%async_computation | async-start | bytes 327680 | tf_op jit(solution)/shard_map/all_to_all | solution.py:1006
  21.1 0.4 collective-permute-start.2
  21.5 0.7 collective-permute-start.3
  22.2 0.4 collective-permute-done.2.refs_5_.refs_1_
  22.6 7.0 %all-to-all-done = f32[16,5,4,128]{3,2,1,0:T(4,128)S(1)} async-done(((f32[16,5,4,128]{3,2,1,0:T(4,128)}), f32[16,5,4,128]{3,2,1,0:T(4,128)S(1)}, u32[]{:S(2)}, u32[]{:S(2)}) %all-to-all-start) | async-done | bytes 163872 | tf_op jit(solution)/shard_map/all_to_all | solution.py:1006
  29.6 1.7 %owners.2 = (s32[3,128]{1,0:T(4,128)}, f32[3,128]{1,0:T(4,128)}, f32[480,128]{1,0:T(8,128)}, f32[4,80,128]{2,1,0:T(8,128)}, f32[4,80,128]{2,1,0:T(8,128)}) custom-call(f32[320,128]{1,0:T(8,128)S(1)} %bitcast.46, f32[80,80]{1,0:T(8,128)S(1)} %bitcast.50, f32[80,128]{1,0:T(8,128)S(1)} %get-tuple-element.231.refs_2_, f32[80,128]{1,0:T(8,128)S(1)} %get-tuple-element.226.refs_3_, ...), custom_call_target="tpu_custom_call" | custom-call | tf_op jit(solution)/shard_map/owners/pallas_call | solution.py:978
  31.3 3.5 %all-to-all-start.1 = ((f32[16,15,2,128]{3,2,1,0:T(2,128)}), f32[16,15,2,128]{3,2,1,0:T(2,128)S(1)}, u32[]{:S(2)}, u32[]{:S(2)}) async-start(f32[16,15,2,128]{3,2,1,0:T(2,128)} %bitcast.60), calls=%async_computation.1 | async-start | bytes 491520 | tf_op jit(solution)/shard_map/all_to_all | solution.py:1006
  34.9 0.4 collective-permute-start.4
  35.2 0.7 collective-permute-start.5
  35.9 2.3 %relayout.2.refs_5_ = f32[5,4,8,1920]{3,2,1,0:T(8,128)} custom-call(f32[8,5,4,1920]{3,2,1,0:T(4,128)} %refs_6_), custom_call_target="tpu_custom_call" | custom-call | tf_op jit(solution)/shard_map/relayout/pallas_call | solution.py:978
  38.2 1.7 %columns.1 = (f32[5,1,1920]{2,1,0:T(1,128)}, f32[5,1,1920]{2,1,0:T(1,128)}, f32[300,128]{1,0:T(8,128)}, f32[300,128]{1,0:T(8,128)}) custom-call(f32[5,1920]{1,0:T(8,128)} %refs_0_.4, f32[5,1920]{1,0:T(8,128)} %refs_1_.5), custom_call_target="tpu_custom_call" | custom-call | tf_op jit(solution)/shard_map/columns/pallas_call | solution.py:978
  39.9 4.7 %all-to-all-done.1 = f32[16,15,2,128]{3,2,1,0:T(2,128)S(1)} async-done(((f32[16,15,2,128]{3,2,1,0:T(2,128)}), f32[16,15,2,128]{3,2,1,0:T(2,128)S(1)}, u32[]{:S(2)}, u32[]{:S(2)}) %all-to-all-start.1) | async-done | bytes 245792 | tf_op jit(solution)/shard_map/all_to_all | solution.py:1006
  44.6 1.8 %surface.2 = (f32[304,128]{1,0:T(8,128)S(1)}, f32[60,128]{1,0:T(8,128)S(1)}, f32[60,128]{1,0:T(8,128)S(1)}, f32[64,128]{1,0:T(8,128)}) custom-call(f32[480,128]{1,0:T(8,128)S(1)} %bitcast.43, f32[40,128]{1,0:T(8,128)S(1)} %collective-permute-done.2.refs_5_.refs_1_, f32[40,128]{1,0:T(8,128)S(1)} %collective-permute-done.3.refs_6_.refs_2_, ...), custom_call_target="tpu_custom_call" | custom-call | tf_op jit(solution)/shard_map/surface/pallas_call | solution.py:978
  46.5 0.7 collective-permute-start.7
  47.1 1.9 %step_load.1 = (f32[16,8,128]{2,1,0:T(8,128)S(1)}, f32[5,1,1920]{2,1,0:T(1,128)S(1)}, f32[5,4,8,1920]{3,2,1,0:T(8,128)S(1)}, f32[5,1,1920]{2,1,0:T(1,128)S(1)}, f32[5,4,8,1920]{3,2,1,0:T(8,128)S(1)}) custom-call(f32[16,8,128]{2,1,0:T(8,128)} %get-tuple-element.146.refs_0_, f32[5,1,1920]{2,1,0:T(1,128)} %get-tuple-element.147.refs_1_, ...), custom_call_target="tpu_custom_call" | custom-call | tf_op jit(solution)/shard_map/step_load/pallas_call | solution.py:978
  49.1 2.7 %step.3 = (f32[5,4,8,1920]{3,2,1,0:T(8,128)}, f32[5,4,8,1920]{3,2,1,0:T(8,128)}, f32[304,128]{1,0:T(8,128)}, f32[320,128]{1,0:T(8,128)}, f32[32,128]{1,0:T(8,128...) custom-call(s32[1,128]{1,0:T(1,128)} %get-tuple-element.115.refs_0_.refs_7_.refs_5_, ...), custom_call_target="tpu_custom_call" | custom-call | tf_op jit(solution)/shard_map/step/pallas_call | solution.py:978
  51.9 6.6 %all-to-all-start.2 = ((f32[16,5,4,128]{3,2,1,0:T(4,128)}), f32[16,5,4,128]{3,2,1,0:T(4,128)S(1)}, u32[]{:S(2)}, u32[]{:S(2)}) async-start(f32[16,5,4,128]{3,2,1,0:T(4,128)} %bitcast.63), calls=%async_computation.2 | async-start | bytes 327680 | tf_op jit(solution)/shard_map/all_to_all | solution.py:1006
  58.4 0.4 collective-permute-start.8
  58.8 0.7 collective-permute-start.9
  59.5 0.4 collective-permute-done.8.refs_1_
  59.9 7.0 %all-to-all-done.2 = f32[16,5,4,128]{3,2,1,0:T(4,128)S(1)} async-done(((f32[16,5,4,128]{3,2,1,0:T(4,128)}), f32[16,5,4,128]{3,2,1,0:T(4,128)S(1)}, u32[]{:S(2)}, u32[]{:S(2)}) %all-to-all-start.2) | async-done | bytes 163872 | tf_op jit(solution)/shard_map/all_to_all | solution.py:1006
  66.9 1.6 owners.3
  68.5 3.5 %all-to-all-start.3 = ((f32[16,15,2,128]{3,2,1,0:T(2,128)}), f32[16,15,2,128]{3,2,1,0:T(2,128)S(1)}, u32[]{:S(2)}, u32[]{:S(2)}) async-start(f32[16,15,2,128]{3,2,1,0:T(2,128)} %bitcast.61), calls=%async_computation.3 | async-start | bytes 491520 | tf_op jit(solution)/shard_map/all_to_all | solution.py:1006
  72.1 2.3 %relayout.3.refs_5_ = f32[5,4,8,1920]{3,2,1,0:T(8,128)} custom-call(f32[8,5,4,1920]{3,2,1,0:T(4,128)} %refs_1_.6), custom_call_target="tpu_custom_call" | custom-call | tf_op jit(solution)/shard_map/relayout/pallas_call | solution.py:978
  74.4 7.4 %all-to-all-done.3 = f32[16,15,2,128]{3,2,1,0:T(2,128)S(1)} async-done(((f32[16,15,2,128]{3,2,1,0:T(2,128)}), f32[16,15,2,128]{3,2,1,0:T(2,128)S(1)}, u32[]{:S(2)}, u32[]{:S(2)}) %all-to-all-start.3) | async-done | bytes 245792 | tf_op jit(solution)/shard_map/all_to_all | solution.py:1006
  81.8 2.3 %surface.3 = (f32[304,128]{1,0:T(8,128)}, f32[64,128]{1,0:T(8,128)}, f32[480,128]{1,0:T(8,128)}, f32[32,128]{1,0:T(8,128)}, f32[32,128]{1,0:T(8,128)}) custom-call(f32[480,128]{1,0:T(8,128)S(1)} %bitcast.42, f32[32,128]{1,0:T(8,128)S(1)} %collective-permute-done.8.refs_1_, f32[32,128]{1,0:T(8,128)S(1)} %collective-permute-done.9.refs_2_, ...), custom_call_target="tpu_custom_call" | custom-call | tf_op jit(solution)/shard_map/surface/pallas_call | solution.py:978
  84.2 3.7 %all-to-all-start.4 = ((f32[16,15,2,128]{3,2,1,0:T(2,128)}), f32[16,15,2,128]{3,2,1,0:T(2,128)S(1)}, u32[]{:S(2)}, u32[]{:S(2)}) async-start(f32[16,15,2,128]{3,2,1,0:T(2,128)} %bitcast.59), calls=%async_computation.4 | async-start | bytes 491520 | tf_op jit(solution)/shard_map/all_to_all | solution.py:1006
  87.9 0.3 collective-permute-start.12
  88.1 0.7 collective-permute-start.13
  88.8 0.5 collective-permute-done.12.refs_1_
  89.3 8.3 %all-to-all-done.4 = f32[16,15,2,128]{3,2,1,0:T(2,128)S(1)} async-done(((f32[16,15,2,128]{3,2,1,0:T(2,128)}), f32[16,15,2,128]{3,2,1,0:T(2,128)S(1)}, u32[]{:S(2)}, u32[]{:S(2)}) %all-to-all-start.4) | async-done | bytes 245792 | tf_op jit(solution)/shard_map/all_to_all | solution.py:1006
  97.6 2.0 %owners_back.2 = f32[320,128]{1,0:T(8,128)} custom-call(f32[480,128]{1,0:T(8,128)S(1)} %bitcast.44, f32[80,80]{1,0:T(8,128)S(1)} %bitcast.52, f32[4,80,128]{2,1,0:T(8,128)} %get-tuple-element.180.refs_2_, f32[4,80,128]{2,1,0:T(8,128)} %get-tuple-element.181.refs_3_, f32[1,128]{1,0:T(1,128)} %get-tuple-element.116.refs_1_.refs_4_.refs_8_.refs_6_), custom_call_target="tpu_custom_call" | custom-call | tf_op jit(solution)/shard_map/owners_back/pallas_call | solution.py:978
  99.6 3.5 %all-to-all-start.5 = ((f32[16,5,4,128]{3,2,1,0:T(4,128)}), f32[16,5,4,128]{3,2,1,0:T(4,128)S(1)}, u32[]{:S(2)}, u32[]{:S(2)}) async-start(f32[16,5,4,128]{3,2,1,0:T(4,128)} %bitcast.56), calls=%async_computation.5 | async-start | bytes 327680 | tf_op jit(solution)/shard_map/all_to_all | solution.py:1006
  103.2 0.4 collective-permute-start.10
  103.5 0.7 collective-permute-start.11
  104.2 7.4 %all-to-all-done.5 = f32[16,5,4,128]{3,2,1,0:T(4,128)S(1)} async-done(((f32[16,5,4,128]{3,2,1,0:T(4,128)}), f32[16,5,4,128]{3,2,1,0:T(4,128)S(1)}, u32[]{:S(2)}, u32[]{:S(2)}) %all-to-all-start.5) | async-done | bytes 163872 | tf_op jit(solution)/shard_map/all_to_all | solution.py:1006
  111.6 1.2 merge.2
  112.9 0.7 collective-permute-start.15
  113.6 2.0 %step_back_load.2 = (f32[16,8,128]{2,1,0:T(8,128)S(1)}, f32[5,1,1920]{2,1,0:T(1,128)S(1)}, f32[5,4,8,1920]{3,2,1,0:T(8,128)S(1)}, f32[5,4,8,1920]{3,2,1,0:T(8,128)S(1)}, f32[5,4,8,1920]{3,2,1,0:T(8,128)S(1)}) custom-call(f32[16,8,128]{2,1,0:T(8,128)} %get-tuple-element.146.refs_0_, f32[5,1,1920]{2,1,0:T(1,128)} %get-tuple-element.147.refs_1_, ...), custom_call_target="tpu_custom_call" | custom-call | tf_op jit(solution)/shard_map/step_back_load/pallas_call | solution.py:978
  115.6 2.7 %step_back.1 = (f32[5,4,8,1920]{3,2,1,0:T(8,128)}, f32[304,128]{1,0:T(8,128)}, f32[480,128]{1,0:T(8,128)}, f32[32,128]{1,0:T(8,128)}, f32[32,128]{1,0:T(8,128)}, /*index=5*/f32[480,128]{1,0:T(8,128)}, f32[480,128]{1,0:T(8,128)}) custom-call(s32[3,128]{1,0:T(4,128)} %get-tuple-element.128.refs_4_.refs_0_, f32[3,128]{1,0:T(4,128)} %get-tuple-element.129.refs_5_.refs_1_, ...), custom_call_target="tpu_custom_call" | custom-call | tf_op jit(solution)/shard_map/step_back/pallas_call | solution.py:978
  118.3 5.9 %all-to-all-start.6 = ((f32[16,15,2,128]{3,2,1,0:T(2,128)}), f32[16,15,2,128]{3,2,1,0:T(2,128)S(1)}, u32[]{:S(2)}, u32[]{:S(2)}) async-start(f32[16,15,2,128]{3,2,1,0:T(2,128)} %bitcast.58), calls=%async_computation.6 | async-start | bytes 491520 | tf_op jit(solution)/shard_map/all_to_all | solution.py:1006
  124.2 0.8 collective-permute-start.16
  124.9 0.7 collective-permute-start.17
  125.6 0.4 collective-permute-done.16.refs_1_
  126.0 7.9 %all-to-all-done.6 = f32[16,15,2,128]{3,2,1,0:T(2,128)S(1)} async-done(((f32[16,15,2,128]{3,2,1,0:T(2,128)}), f32[16,15,2,128]{3,2,1,0:T(2,128)S(1)}, u32[]{:S(2)}, u32[]{:S(2)}) %all-to-all-start.6) | async-done | bytes 245792 | tf_op jit(solution)/shard_map/all_to_all | solution.py:1006
  133.9 2.0 %owners_back.3 = f32[320,128]{1,0:T(8,128)} custom-call(f32[480,128]{1,0:T(8,128)S(1)} %bitcast.45, f32[80,80]{1,0:T(8,128)S(1)} %bitcast.53, f32[4,80,128]{2,1,0:T(8,128)} %get-tuple-element.201.refs_2_, f32[4,80,128]{2,1,0:T(8,128)} %get-tuple-element.202.refs_3_, f32[1,128]{1,0:T(1,128)} %get-tuple-element.116.refs_1_.refs_4_.refs_8_.refs_6_), custom_call_target="tpu_custom_call" | custom-call | tf_op jit(solution)/shard_map/owners_back/pallas_call | solution.py:978
  136.0 3.5 %all-to-all-start.7 = ((f32[16,5,4,128]{3,2,1,0:T(4,128)}), f32[16,5,4,128]{3,2,1,0:T(4,128)S(1)}, u32[]{:S(2)}, u32[]{:S(2)}) async-start(f32[16,5,4,128]{3,2,1,0:T(4,128)} %bitcast.57), calls=%async_computation.7 | async-start | bytes 327680 | tf_op jit(solution)/shard_map/all_to_all | solution.py:1006
  139.5 0.4 collective-permute-start.18
  139.9 0.7 collective-permute-start.19
  140.6 7.4 %all-to-all-done.7 = f32[16,5,4,128]{3,2,1,0:T(4,128)S(1)} async-done(((f32[16,5,4,128]{3,2,1,0:T(4,128)}), f32[16,5,4,128]{3,2,1,0:T(4,128)S(1)}, u32[]{:S(2)}, u32[]{:S(2)}) %all-to-all-start.7) | async-done | bytes 163872 | tf_op jit(solution)/shard_map/all_to_all | solution.py:1006
  148.0 1.2 merge.3
  149.2 0.7 collective-permute-start.21
  149.9 2.4 %step_back_load.3 = (f32[16,8,128]{2,1,0:T(8,128)S(1)}, f32[5,1,1920]{2,1,0:T(1,128)S(1)}, f32[5,4,8,1920]{3,2,1,0:T(8,128)S(1)}, f32[5,4,8,1920]{3,2,1,0:T(8,12...) custom-call(f32[16,8,128]{2,1,0:T(8,128)} %get-tuple-element.146.refs_0_, ...), custom_call_target="tpu_custom_call" | custom-call | tf_op jit(solution)/shard_map/step_back_load/pallas_call | solution.py:978
  152.3 2.4 %step_back_sums.1 = (f32[5,4,8,1920]{3,2,1,0:T(8,128)}, f32[16,128]{1,0:T(8,128)}) custom-call(f32[480,128]{1,0:T(8,128)S(1)} %collective-permute-done.18.refs_0_, f32[480,128]{1,0:T(8,128)S(1)} %collective-permute-done.19.refs_1_, f32[60,128]{1,0:T(8,128)S(1)} %collective-permute-done.20.refs_2_, f32[60,128]{1,0:T(8,128)S(1)} %collective-permute-done.21.refs_3_, ...), custom_call_target="tpu_custom_call" | custom-call | tf_op jit(solution)/shard_map/step_back_sums/pallas_call | solution.py:978
  154.7 5.4 %all-to-all-start.8 = ((f32[16,1,128]{2,1,0:T(1,128)}), f32[16,1,128]{2,1,0:T(1,128)S(1)}, u32[]{:S(2)}, u32[]{:S(2)}) async-start(f32[16,1,128]{2,1,0:T(1,128)} %bitcast.64), calls=%async_computation.8 | async-start | bytes 16384 | tf_op jit(solution)/shard_map/all_to_all | solution.py:1242
  160.1 1.7 %copy.20 = f32[5,4,8,1920]{3,1,0,2:T(4,128)S(1)} copy(f32[5,4,8,1920]{3,2,1,0:T(8,128)} %get-tuple-element.224) | data formatting | bytes 2457600 | tf_op jit(solution)/shard_map/step_back_sums/pallas_call | solution.py:978
  161.8 4.7 %all-to-all-done.8 = f32[16,1,128]{2,1,0:T(1,128)S(1)} async-done(((f32[16,1,128]{2,1,0:T(1,128)}), f32[16,1,128]{2,1,0:T(1,128)S(1)}, u32[]{:S(2)}, u32[]{:S(2)}) %all-to-all-start.8) | async-done | bytes 8224 | tf_op jit(solution)/shard_map/all_to_all | solution.py:1242
  166.5 1.2 finish.1
  (64 shorter events, 0.6 us)
Async XLA Ops:
  0.0 2.9 %copy-start.5 = (f32[4,4]{1,0:T(4,128)S(1)}, f32[4,4]{1,0:T(4,128)}, u32[]{:S(2)}) copy-start(f32[4,4]{1,0:T(4,128)} %param.21) | copy-start | bytes 196
  0.0 2.9 %copy-start.7 = (s32[15]{0:T(128)S(1)}, s32[15]{0:T(128)}, u32[]{:S(2)}) copy-start(s32[15]{0:T(128)} %param.28) | copy-start | bytes 184
  0.0 2.9 %copy-start.6 = (s32[15]{0:T(128)S(1)}, s32[15]{0:T(128)}, u32[]{:S(2)}) copy-start(s32[15]{0:T(128)} %param.27) | copy-start | bytes 184
  0.0 3.0 %copy-start.14 = (f32[15]{0:T(128)S(1)}, f32[15]{0:T(128)}, u32[]{:S(2)}) copy-start(f32[15]{0:T(128)} %param.29) | copy-start | bytes 184
  1.6 5.3 %collective-permute-start = (f32[480,128]{1,0:T(8,128)S(1)}, f32[480,128]{1,0:T(8,128)S(1)}, u32[]{:S(2)}, u32[]{:S(2)}) collective-permute-start(f32[480,128]{1,0:T(8,128)S(1)} %get-tuple-element.117), channel_id=1, source_target_pairs={{0,1},{1,0},{2,3},{3,2},{4,5},{5,4},{6,7},{7,6},{8,9},{9,8},{10,11... | collective-permute-start | bytes 737288 | tf_op jit(solution)/shard_map/ppermute | solution.py:999
  2.2 4.8 %collective-permute-start.1 = (f32[480,128]{1,0:T(8,128)S(1)}, f32[480,128]{1,0:T(8,128)S(1)}, u32[]{:S(2)}, u32[]{:S(2)}) collective-permute-start(f32[480,128]{1,0:T(8,128)S(1)} %get-tuple-element.118), channel_id=1, source_target_pairs={{1,2},{3,4},{5,6},{7,8},{9,10},{11,12},{13,14},{2,1},{4,3},{6,5},{... | collective-permute-start | bytes 737288 | tf_op jit(solution)/shard_map/ppermute | solution.py:999
  3.0 2.0 %copy-start.15 = (s32[1,75]{1,0:T(1,128)S(1)}, s32[1,75]{1,0:T(1,128)}, u32[]{:S(2)}) copy-start(s32[1,75]{1,0:T(1,128)} %param.25) | copy-start | bytes 904
  3.0 2.1 %copy-start.16 = (s32[1,75]{1,0:T(1,128)S(1)}, s32[1,75]{1,0:T(1,128)}, u32[]{:S(2)}) copy-start(s32[1,75]{1,0:T(1,128)} %param.26) | copy-start | bytes 904
  3.1 2.2 %copy-start.2 = (f32[8,4,4]{0,2,1:T(4,128)S(1)}, f32[8,4,4]{0,2,1:T(4,128)}, u32[]{:S(2)}) copy-start(f32[8,4,4]{0,2,1:T(4,128)} %param.20) | copy-start | bytes 1540
  5.1 17.1 %copy-start.3 = (f32[2,1,80,128]{3,2,1,0:T(8,128)S(1)}, f32[2,1,80,128]{3,2,1,0:T(8,128)}, u32[]{:S(2)}) copy-start(f32[2,1,80,128]{3,2,1,0:T(8,128)} %param.24) | copy-start | bytes 245764
  5.1 17.1 %copy-start.4 = (f32[2,1,80,128]{3,2,1,0:T(8,128)S(1)}, f32[2,1,80,128]{3,2,1,0:T(8,128)}, u32[]{:S(2)}) copy-start(f32[2,1,80,128]{3,2,1,0:T(8,128)} %param.23) | copy-start | bytes 245764
  6.9 22.6 %copy-start.1 = (f32[1,80,80]{2,1,0:T(8,128)S(1)}, f32[1,80,80]{2,1,0:T(8,128)}, u32[]{:S(2)}) copy-start(f32[1,80,80]{2,1,0:T(8,128)} %param.22) | copy-start | bytes 76804
  9.5 25.3 %copy-start.11 = (f32[480,128]{1,0:T(8,128)S(1)}, f32[480,128]{1,0:T(8,128)}, u32[]{:S(2)}) copy-start(f32[480,128]{1,0:T(8,128)} %get-tuple-element.144) | copy-start | bytes 737284
  9.5 25.7 %copy-start.10 = (f32[480,128]{1,0:T(8,128)S(1)}, f32[480,128]{1,0:T(8,128)}, u32[]{:S(2)}) copy-start(f32[480,128]{1,0:T(8,128)} %get-tuple-element.145) | copy-start | bytes 737284
  9.6 20.0 %all-to-all-start = ((f32[16,5,4,128]{3,2,1,0:T(4,128)}), f32[16,5,4,128]{3,2,1,0:T(4,128)S(1)}, u32[]{:S(2)}, u32[]{:S(2)}) async-start(f32[16,5,4,128]{3,2,1,0:T(4,128)} %bitcast.62), calls=%async_computation | async-start | bytes 327680 | tf_op jit(solution)/shard_map/all_to_all | solution.py:1006
  21.1 1.5 collective-permute-start.2
  21.5 1.1 collective-permute-start.3
  31.3 13.3 %all-to-all-start.1 = ((f32[16,15,2,128]{3,2,1,0:T(2,128)}), f32[16,15,2,128]{3,2,1,0:T(2,128)S(1)}, u32[]{:S(2)}, u32[]{:S(2)}) async-start(f32[16,15,2,128]{3,2,1,0:T(2,128)} %bitcast.60), calls=%async_computation.1 | async-start | bytes 491520 | tf_op jit(solution)/shard_map/all_to_all | solution.py:1006
  34.9 14.2 %collective-permute-start.4 = (f32[480,128]{1,0:T(8,128)S(1)}, f32[480,128]{1,0:T(8,128)S(1)}, u32[]{:S(2)}, u32[]{:S(2)}) collective-permute-start(f32[480,128]{1,0:T(8,128)S(1)} %copy-done.11), channel_id=1, source_target_pairs={{0,1},{1,0},{2,3},{3,2},{4,5},{5,4},{6,7},{7,6},{8,9},{9,8},{10,11... | collective-permute-start | bytes 737288 | tf_op jit(solution)/shard_map/ppermute | solution.py:999
  35.2 13.9 %collective-permute-start.5 = (f32[480,128]{1,0:T(8,128)S(1)}, f32[480,128]{1,0:T(8,128)S(1)}, u32[]{:S(2)}, u32[]{:S(2)}) collective-permute-start(f32[480,128]{1,0:T(8,128)S(1)} %copy-done.10), channel_id=1, source_target_pairs={{1,2},{3,4},{5,6},{7,8},{9,10},{11,12},{13,14},{2,1},{4,3},{6,5},{... | collective-permute-start | bytes 737288 | tf_op jit(solution)/shard_map/ppermute | solution.py:999
  46.4 2.7 %collective-permute-start.6 = (f32[60,128]{1,0:T(8,128)S(1)}, f32[60,128]{1,0:T(8,128)S(1)}, u32[]{:S(2)}, u32[]{:S(2)}) collective-permute-start(f32[60,128]{1,0:T(8,128)S(1)} %get-tuple-element.155), channel_id=1, source_target_pairs={{0,1},{1,0},{2,3},{3,2},{4,5},{5,4},{6,7},{7,6},{8,9},{9,8},{10,11... | collective-permute-start | bytes 92168 | tf_op jit(solution)/shard_map/ppermute | solution.py:999
  46.5 2.6 %collective-permute-start.7 = (f32[60,128]{1,0:T(8,128)S(1)}, f32[60,128]{1,0:T(8,128)S(1)}, u32[]{:S(2)}, u32[]{:S(2)}) collective-permute-start(f32[60,128]{1,0:T(8,128)S(1)} %get-tuple-element.156), channel_id=1, source_target_pairs={{1,2},{3,4},{5,6},{7,8},{9,10},{11,12},{13,14},{2,1},{4,3},{6,5},{... | collective-permute-start | bytes 92168 | tf_op jit(solution)/shard_map/ppermute | solution.py:999
  51.9 15.0 %all-to-all-start.2 = ((f32[16,5,4,128]{3,2,1,0:T(4,128)}), f32[16,5,4,128]{3,2,1,0:T(4,128)S(1)}, u32[]{:S(2)}, u32[]{:S(2)}) async-start(f32[16,5,4,128]{3,2,1,0:T(4,128)} %bitcast.63), calls=%async_computation.2 | async-start | bytes 327680 | tf_op jit(solution)/shard_map/all_to_all | solution.py:1006
  58.4 1.5 collective-permute-start.8
  58.8 1.1 collective-permute-start.9
  68.5 13.3 %all-to-all-start.3 = ((f32[16,15,2,128]{3,2,1,0:T(2,128)}), f32[16,15,2,128]{3,2,1,0:T(2,128)S(1)}, u32[]{:S(2)}, u32[]{:S(2)}) async-start(f32[16,15,2,128]{3,2,1,0:T(2,128)} %bitcast.61), calls=%async_computation.3 | async-start | bytes 491520 | tf_op jit(solution)/shard_map/all_to_all | solution.py:1006
  84.2 19.0 %copy-start.9 = (f32[480,128]{1,0:T(8,128)S(1)}, f32[480,128]{1,0:T(8,128)}, u32[]{:S(2)}) copy-start(f32[480,128]{1,0:T(8,128)} %get-tuple-element.166) | copy-start | bytes 737284
  84.2 19.4 %copy-start.8 = (f32[480,128]{1,0:T(8,128)S(1)}, f32[480,128]{1,0:T(8,128)}, u32[]{:S(2)}) copy-start(f32[480,128]{1,0:T(8,128)} %get-tuple-element.167) | copy-start | bytes 737284
  84.2 13.4 %all-to-all-start.4 = ((f32[16,15,2,128]{3,2,1,0:T(2,128)}), f32[16,15,2,128]{3,2,1,0:T(2,128)S(1)}, u32[]{:S(2)}, u32[]{:S(2)}) async-start(f32[16,15,2,128]{3,2,1,0:T(2,128)} %bitcast.59), calls=%async_computation.4 | async-start | bytes 491520 | tf_op jit(solution)/shard_map/all_to_all | solution.py:1006
  87.9 1.5 collective-permute-start.12
  88.1 1.2 collective-permute-start.13
  99.6 12.0 %all-to-all-start.5 = ((f32[16,5,4,128]{3,2,1,0:T(4,128)}), f32[16,5,4,128]{3,2,1,0:T(4,128)S(1)}, u32[]{:S(2)}, u32[]{:S(2)}) async-start(f32[16,5,4,128]{3,2,1,0:T(4,128)} %bitcast.56), calls=%async_computation.5 | async-start | bytes 327680 | tf_op jit(solution)/shard_map/all_to_all | solution.py:1006
  103.2 12.4 %collective-permute-start.10 = (f32[480,128]{1,0:T(8,128)S(1)}, f32[480,128]{1,0:T(8,128)S(1)}, u32[]{:S(2)}, u32[]{:S(2)}) collective-permute-start(f32[480,128]{1,0:T(8,128)S(1)} %copy-done.9), channel_id=1, source_target_pairs={{0,1},{1,0},{2,3},{3,2},{4,5},{5,4},{6,7},{7,6},{8,9},{9,8},{10,11... | collective-permute-start | bytes 737288 | tf_op jit(solution)/shard_map/ppermute | solution.py:999
  103.5 12.0 %collective-permute-start.11 = (f32[480,128]{1,0:T(8,128)S(1)}, f32[480,128]{1,0:T(8,128)S(1)}, u32[]{:S(2)}, u32[]{:S(2)}) collective-permute-start(f32[480,128]{1,0:T(8,128)S(1)} %copy-done.8), channel_id=1, source_target_pairs={{1,2},{3,4},{5,6},{7,8},{9,10},{11,12},{13,14},{2,1},{4,3},{6,5},{... | collective-permute-start | bytes 737288 | tf_op jit(solution)/shard_map/ppermute | solution.py:999
  112.8 2.8 %collective-permute-start.14 = (f32[60,128]{1,0:T(8,128)S(1)}, f32[60,128]{1,0:T(8,128)S(1)}, u32[]{:S(2)}, u32[]{:S(2)}) collective-permute-start(f32[60,128]{1,0:T(8,128)S(1)} %get-tuple-element.187), channel_id=1, source_target_pairs={{0,1},{1,0},{2,3},{3,2},{4,5},{5,4},{6,7},{7,6},{8,9},{9,8},{10,11... | collective-permute-start | bytes 92168 | tf_op jit(solution)/shard_map/ppermute | solution.py:999
  112.9 2.7 %collective-permute-start.15 = (f32[60,128]{1,0:T(8,128)S(1)}, f32[60,128]{1,0:T(8,128)S(1)}, u32[]{:S(2)}, u32[]{:S(2)}) collective-permute-start(f32[60,128]{1,0:T(8,128)S(1)} %get-tuple-element.188), channel_id=1, source_target_pairs={{1,2},{3,4},{5,6},{7,8},{9,10},{11,12},{13,14},{2,1},{4,3},{6,5},{... | collective-permute-start | bytes 92168 | tf_op jit(solution)/shard_map/ppermute | solution.py:999
  118.3 21.2 %copy-start.13 = (f32[480,128]{1,0:T(8,128)S(1)}, f32[480,128]{1,0:T(8,128)}, u32[]{:S(2)}) copy-start(f32[480,128]{1,0:T(8,128)} %get-tuple-element.205) | copy-start | bytes 737284
  118.3 21.6 %copy-start.12 = (f32[480,128]{1,0:T(8,128)S(1)}, f32[480,128]{1,0:T(8,128)}, u32[]{:S(2)}) copy-start(f32[480,128]{1,0:T(8,128)} %get-tuple-element.206) | copy-start | bytes 737284
  118.3 15.6 %all-to-all-start.6 = ((f32[16,15,2,128]{3,2,1,0:T(2,128)}), f32[16,15,2,128]{3,2,1,0:T(2,128)S(1)}, u32[]{:S(2)}, u32[]{:S(2)}) async-start(f32[16,15,2,128]{3,2,1,0:T(2,128)} %bitcast.58), calls=%async_computation.6 | async-start | bytes 491520 | tf_op jit(solution)/shard_map/all_to_all | solution.py:1006
  124.2 1.8 %collective-permute-start.16 = (f32[32,128]{1,0:T(8,128)}, f32[32,128]{1,0:T(8,128)S(1)}, u32[]{:S(2)}, u32[]{:S(2)}) collective-permute-start(f32[32,128]{1,0:T(8,128)} %get-tuple-element.198), channel_id=1, source_target_pairs={{0,1},{1,0},{2,3},{3,2},{4,5},{5,4},{6,7},{7,6},{8,9},{9,8},{10,11... | collective-permute-start | bytes 49160 | tf_op jit(solution)/shard_map/ppermute | solution.py:999
  124.9 1.1 collective-permute-start.17
  136.0 12.0 %all-to-all-start.7 = ((f32[16,5,4,128]{3,2,1,0:T(4,128)}), f32[16,5,4,128]{3,2,1,0:T(4,128)S(1)}, u32[]{:S(2)}, u32[]{:S(2)}) async-start(f32[16,5,4,128]{3,2,1,0:T(4,128)} %bitcast.57), calls=%async_computation.7 | async-start | bytes 327680 | tf_op jit(solution)/shard_map/all_to_all | solution.py:1006
  139.5 12.7 %collective-permute-start.18 = (f32[480,128]{1,0:T(8,128)S(1)}, f32[480,128]{1,0:T(8,128)S(1)}, u32[]{:S(2)}, u32[]{:S(2)}) collective-permute-start(f32[480,128]{1,0:T(8,128)S(1)} %copy-done.13), channel_id=1, source_target_pairs={{0,1},{1,0},{2,3},{3,2},{4,5},{5,4},{6,7},{7,6},{8,9},{9,8},{10,11... | collective-permute-start | bytes 737288 | tf_op jit(solution)/shard_map/ppermute | solution.py:999
  139.9 12.4 %collective-permute-start.19 = (f32[480,128]{1,0:T(8,128)S(1)}, f32[480,128]{1,0:T(8,128)S(1)}, u32[]{:S(2)}, u32[]{:S(2)}) collective-permute-start(f32[480,128]{1,0:T(8,128)S(1)} %copy-done.12), channel_id=1, source_target_pairs={{1,2},{3,4},{5,6},{7,8},{9,10},{11,12},{13,14},{2,1},{4,3},{6,5},{... | collective-permute-start | bytes 737288 | tf_op jit(solution)/shard_map/ppermute | solution.py:999
  149.1 3.1 %collective-permute-start.20 = (f32[60,128]{1,0:T(8,128)S(1)}, f32[60,128]{1,0:T(8,128)S(1)}, u32[]{:S(2)}, u32[]{:S(2)}) collective-permute-start(f32[60,128]{1,0:T(8,128)S(1)} %get-tuple-element.211), channel_id=1, source_target_pairs={{0,1},{1,0},{2,3},{3,2},{4,5},{5,4},{6,7},{7,6},{8,9},{9,8},{10,11... | collective-permute-start | bytes 92168 | tf_op jit(solution)/shard_map/ppermute | solution.py:999
  149.2 3.1 %collective-permute-start.21 = (f32[60,128]{1,0:T(8,128)S(1)}, f32[60,128]{1,0:T(8,128)S(1)}, u32[]{:S(2)}, u32[]{:S(2)}) collective-permute-start(f32[60,128]{1,0:T(8,128)S(1)} %get-tuple-element.212), channel_id=1, source_target_pairs={{1,2},{3,4},{5,6},{7,8},{9,10},{11,12},{13,14},{2,1},{4,3},{6,5},{... | collective-permute-start | bytes 92168 | tf_op jit(solution)/shard_map/ppermute | solution.py:999
  154.7 11.8 %all-to-all-start.8 = ((f32[16,1,128]{2,1,0:T(1,128)}), f32[16,1,128]{2,1,0:T(1,128)S(1)}, u32[]{:S(2)}, u32[]{:S(2)}) async-start(f32[16,1,128]{2,1,0:T(1,128)} %bitcast.64), calls=%async_computation.8 | async-start | bytes 16384 | tf_op jit(solution)/shard_map/all_to_all | solution.py:1242
  160.1 6.4 %copy-start = (f32[8,5,4,1920]{3,2,1,0:T(4,128)S(1)}, f32[8,5,4,1920]{3,2,1,0:T(4,128)}, u32[]{:S(2)}) copy-start(f32[8,5,4,1920]{3,2,1,0:T(4,128)} %refs_1_.6) | copy-start | bytes 3686404

commit v10 on v9

--- a/solution.py
+++ b/solution.py
@@ -74,6 +74,11 @@
         return pltpu.make_async_copy(
             self.block.at[index], self.home.at[index], self.sems.at[index]
         )
+
+    def row_from(self, block, index):
+        self.by_row = True
+        self.started = True
+        return pltpu.make_async_copy(block.at[index], self.home.at[index], self.sems.at[index])
 
     def all(self):
         return pltpu.make_async_copy(self.block, self.home, self.sems.at[0])
@@ -347,15 +352,19 @@
     return lows + highs
 
 
+def place_edge(sz, padded, at, edge, surface=None):
+    for channel in range(CHANNELS):
+        for tile in range(sz.row_tiles):
+            line = (channel * sz.row_tiles + tile) * LEVELS
+            padded[at, channel, :, cols(tile)] = edge[line : line + LEVELS, :]
+    if surface is not None:
+        load_surface_row(sz, padded, at, surface, 0)
+
+
 def place_edges(sz, padded, first, second, first_surface=None, second_surface=None):
     side = high_first() * (sz.rows + 1)
-    for at, edge, surface in ((side, first, first_surface), (sz.rows + 1 - side, second, second_surface)):
-        for channel in range(CHANNELS):
-            for tile in range(sz.row_tiles):
-                line = (channel * sz.row_tiles + tile) * LEVELS
-                padded[at, channel, :, cols(tile)] = edge[line : line + LEVELS, :]
-        if surface is not None:
-            load_surface_row(sz, padded, at, surface, 0)
+    place_edge(sz, padded, side, first, first_surface)
+    place_edge(sz, padded, sz.rows + 1 - side, second, second_surface)
 
 
 def store_rows(sz, surface, send_first, send_second, factor=None):
@@ -410,12 +419,18 @@
     lax.fori_loop(0, sz.rows, one_row, 0)
 
 
-def forward_kernel(sz, first, last, arrive, *refs):
+def forward_kernel(sz, first, last, part, arrive, *refs):
     refs = list(refs)
-    tables, facts, low, high, diffusivity, mix, field = refs[:7]
-    refs = refs[7:]
-    if first:
-        facts_block = refs.pop(0)
+    if part != 1:
+        tables, facts = refs[:2]
+        refs = refs[2:]
+    edges = refs[: 1 if part else 2]
+    refs = refs[len(edges) :]
+    diffusivity, mix, field = refs[:3]
+    refs = refs[3:]
+    if part == 2:
+        facts_block, out_before, drive_before, surface_before = refs[:4]
+        refs = refs[4:]
     surfaces = ()
     if not first:
         surfaces = refs[:2]
@@ -423,22 +438,43 @@
     if last:
         weight, target = refs[:2]
         refs = refs[2:]
-    out, drive, new_surface, packed, tell_first, tell_second, edge_first, edge_second, padded = refs
-    remap = Remap(sz, facts)
-    place_edges(sz, padded, low, high, *surfaces)
+    out, drive, new_surface, *refs = refs
+    if part != 1:
+        packed, tell_first, tell_second, edge_first, edge_second = refs[:5]
+        refs = refs[5:]
+        remap = Remap(sz, facts)
+    padded = refs[0]
+    flag = high_first()
+    near_side = flag * (sz.rows + 1)
+    if part == 0:
+        place_edges(sz, padded, *edges, *surfaces)
+    else:
+        place_edge(sz, padded, near_side if part == 1 else sz.rows + 1 - near_side, edges[0])
+    if part == 2:
+        new_surface[...] = surface_before[...]
+        for index in range(sz.rows - 1):
+            row = index + flag
+            out.row_from(out_before, row).start()
+            drive.row_from(drive_before, row).start()
 
     def ready(row):
         padded[row + 1] = field[row]
 
-    ready(0)
+    if part == 0:
+        ready(0)
+    else:
+        for row in range(sz.rows):
+            ready(row)
     lane = lax.broadcasted_iota(jnp.int32, (LEVELS, WIDTH), 1)
     masks = level_masks()
     count = sz.row_tiles
 
     def one_row(row, carry):
-        @pl.when(row < sz.rows - 1)
-        def _():
-            ready(row + 1)
+        if part == 0:
+
+            @pl.when(row < sz.rows - 1)
+            def _():
+                ready(row + 1)
 
         tiles = RowTiles(count, lambda c, t: padded[row + 1, c, :, cols(t)])
         for t in range(count):
@@ -466,11 +502,19 @@
                 if last:
                     stepped = scale * (stepped - target[row, c, :, cols(t)])
                 out[row, c, :, cols(t)] = stepped
-        drive.row(row).start()
-        out.row(row).start()
+        if part != 1:
+            drive.row(row).start()
+            out.row(row).start()
         return carry
 
-    lax.fori_loop(0, sz.rows, one_row, 0)
+    if part == 0:
+        lax.fori_loop(0, sz.rows, one_row, 0)
+    elif part == 1:
+        lax.fori_loop(0, sz.rows - 1, lambda index, carry: one_row(index + flag, carry), 0)
+        return
+    else:
+        one_row((1 - flag) * (sz.rows - 1), 0)
+        out[flag * (sz.rows - 1)] = out_before[flag * (sz.rows - 1)]
     new_surface[CHANNELS * sz.tiles :, :] = jnp.zeros((CHANNELS, WIDTH), jnp.float32)
     new_surface.start()
     arrive_all(arrive)
@@ -479,7 +523,7 @@
     own = [row_tiles_of(sz, new_surface.block, row) for row in range(sz.rows)]
     send_sums(sz, own_sums(sz, remap, own, 1.0), tell_first, tell_second)
     for tell in (tell_first, tell_second):
-        if first:
+        if part == 2:
             tell[sz.lat_lines :, :] = facts_block[...]
         tell.start()
     store_edges(sz, out, diffusivity if last else None, edge_first, edge_second)
@@ -1096,10 +1140,18 @@
     by_slot = (sz.slots, WIDTH)
     for hour in range(hours):
         first, last = hour == 0, hour == hours - 1
+        assert not (first and last)
         inputs = scalars(table, line)
         if first:
-            inputs += near_by(*edges, first_rows, first_mix, field) + fetched(facts)
-            assert not last
+            same = near_by(first_rows, first_mix, field)
+            before = call(
+                functools.partial(forward_kernel, sz, True, False, 1),
+                "step_near",
+                near_by(edges[0]) + same,
+                kept=[sz.whole, sz.whole, sz.surface],
+                scratch=[wider],
+            )
+            inputs += near_by(edges[1]) + same + fetched(facts) + near_by(*before)
         else:
             loads = fetched(mix, diffusivity_rows, *([weight_rows] if last else []))
             loads += far_off(field) + near_by(surface) + (far_off(target) if last else [])
@@ -1112,7 +1164,7 @@
             )
             inputs += near_by(*edges, rows_here, mix_here, field, *surface_edges, *more)
         field, drive, surface, packed, *sends = call(
-            functools.partial(forward_kernel, sz, first, last),
+            functools.partial(forward_kernel, sz, first, last, 2 if first else 0),
             "step",
             inputs,
             shipped=[sz.whole, sz.whole, sz.surface, sz.narrow]

time: 169 us -> 169 us (level)
    all_to_all x8, starting transfers between devices: 41.8 us -> 36.6 us  [exchange(): lax.all_to_all(split, 'horiz', split_axis=0, concat_axis=0, tiled=True)]
    ppermute x11, starting transfers between devices: 3.69 us -> 7.55 us  [swap(): lax.ppermute(first, 'horiz', inner)]
    pallas_call x22 -> x23, Pallas kernels: 43.4 us -> 44.1 us  [call(): pl.pallas_call(run, name=name, in_specs=[pl.BlockSpec(memory_space=item.s...]
  transfers between devices with their start and end apart: 31 -> 31, of which waited for: 13 -> 13; matrix products, arithmetic and copies ran while one was open for 1% -> 1% of each run, Pallas kernels for 12% -> 13%
where the time goes in v10:
time: 169 us; the launch traced here: 167 us
  waiting for transfers between devices  63.5 us (38%)
  starting transfers between devices  56.8 us (34%)
  Pallas kernels  44.1 us (26%)
  local copies, waits for them, and re-layouts  1.88 us (1%)
    all_to_all x8, waiting for transfers between devices, exchange(): lax.all_to_all(split, 'horiz', split_axis=0, concat_axis=0, tiled=True)  57.1 us
    pallas_call x23, Pallas kernels, call(): pl.pallas_call(run, name=name, in_specs=[pl.BlockSpec(memory_space=item.s...  44.1 us
    all_to_all x8, starting transfers between devices, exchange(): lax.all_to_all(split, 'horiz', split_axis=0, concat_axis=0, tiled=True)  36.6 us
    ppermute x11, starting transfers between devices, swap(): lax.ppermute(first, 'horiz', inner)  7.55 us
    ppermute x11, starting transfers between devices, swap(): lax.ppermute(second, 'horiz', outer)  7.26 us
    all_to_all x1, starting transfers between devices, body(): lax.all_to_all(sums, 'horiz', split_axis=0, concat_axis=0, tiled=True)  5.35 us
    all_to_all x1, waiting for transfers between devices, body(): lax.all_to_all(sums, 'horiz', split_axis=0, concat_axis=0, tiled=True)  4.68 us
  transfers between devices with their start and end apart: 31, of which 13 were waited for; matrix products, arithmetic and copies ran while one was open for 1% of the time, Pallas kernels for 13%

profile of v10, /device:TPU:0, one launch (start us, length us, event | category | flops | bytes accessed | tf_op | source)
XLA Modules:
  0.0 167.1 jit_solution(16719169645562306923)
XLA Ops:
  0.0 1.6 edges.1
  1.6 0.7 collective-permute-start
  2.3 4.4 %collective-permute-start.1 = (f32[480,128]{1,0:T(8,128)S(1)}, f32[480,128]{1,0:T(8,128)S(1)}, u32[]{:S(2)}, u32[]{:S(2)}) collective-permute-start(f32[480,128]{1,0:T(8,128)S(1)} %get-tuple-element.124), channel_id=1, source_target_pairs={{0,1},{1,0},{2,3},{3,2},{4,5},{5,4},{6,7},{7,6},{8,9},{9,8},{10,11... | collective-permute-start | bytes 737288 | tf_op jit(solution)/shard_map/ppermute | solution.py:1043
  6.9 2.0 %load.1.refs_3_.refs_5_ = f32[5,4,8,1920]{3,2,1,0:T(8,128)S(1)} custom-call(f32[8,5,4,1920]{3,2,1,0:T(4,128)} %refs_1_.6, f32[8,5,4,1920]{3,2,1,0:T(4,128)} %refs_1_.4), custom_call_target="tpu_custom_call" | custom-call | tf_op jit(solution)/shard_map/load/pallas_call | solution.py:1022
  9.0 1.7 %setup.1 = (f32[16,8,128]{2,1,0:T(8,128)S(1)}, f32[5,1,1920]{2,1,0:T(1,128)S(1)}, s32[1,128]{1,0:T(1,128)}, f32[8,128]{1,0:T(8,128)}, f32[1,128]{1,0:T(1,128)}, /*index=5*/f32[16,8,128]{2,1,0:T(8,128)}) custom-call(f32[2,128]{1,0:T(2,128)S(1)} %get-tuple-element.236.refs_0_, f32[2,128]{1,0:T(2,128)S(1)} %get-tuple-element.235.refs_1_, f32[16,8]{1,0:T(8,128)S(1)} %bitcast.55, ...), custom_call_target="tpu_custom_call" | custom-call | tf_op jit(solution)/shard_map/setup/pallas_call | solution.py:1022
  10.8 1.1 step_near.1
  11.9 2.2 %step.2 = (f32[5,4,8,1920]{3,2,1,0:T(8,128)}, f32[5,4,8,1920]{3,2,1,0:T(8,128)}, f32[304,128]{1,0:T(8,128)}, f32[320,128]{1,0:T(8,128)}, f32[40,128]{1,0:T(8,128...) custom-call(s32[1,128]{1,0:T(1,128)} %get-tuple-element.118.refs_0_.refs_7_.refs_5_, ...), custom_call_target="tpu_custom_call" | custom-call | tf_op jit(solution)/shard_map/step/pallas_call | solution.py:1022
  14.1 6.4 %all-to-all-start = ((f32[16,5,4,128]{3,2,1,0:T(4,128)}), f32[16,5,4,128]{3,2,1,0:T(4,128)S(1)}, u32[]{:S(2)}, u32[]{:S(2)}) async-start(f32[16,5,4,128]{3,2,1,0:T(4,128)} %bitcast.62), calls=%async_computation | async-start | bytes 327680 | tf_op jit(solution)/shard_map/all_to_all | solution.py:1050
  20.6 0.4 collective-permute-start.2
  21.0 0.7 collective-permute-start.3
  21.7 0.4 collective-permute-done.2.refs_5_.refs_1_
  22.0 7.0 %all-to-all-done = f32[16,5,4,128]{3,2,1,0:T(4,128)S(1)} async-done(((f32[16,5,4,128]{3,2,1,0:T(4,128)}), f32[16,5,4,128]{3,2,1,0:T(4,128)S(1)}, u32[]{:S(2)}, u32[]{:S(2)}) %all-to-all-start) | async-done | bytes 163872 | tf_op jit(solution)/shard_map/all_to_all | solution.py:1050
  29.0 1.7 owners.2
  30.7 3.5 %all-to-all-start.1 = ((f32[16,15,2,128]{3,2,1,0:T(2,128)}), f32[16,15,2,128]{3,2,1,0:T(2,128)S(1)}, u32[]{:S(2)}, u32[]{:S(2)}) async-start(f32[16,15,2,128]{3,2,1,0:T(2,128)} %bitcast.60), calls=%async_computation.1 | async-start | bytes 491520 | tf_op jit(solution)/shard_map/all_to_all | solution.py:1050
  34.3 0.4 collective-permute-start.4
  34.6 0.7 collective-permute-start.5
  35.3 2.3 %relayout.2.refs_5_ = f32[5,4,8,1920]{3,2,1,0:T(8,128)} custom-call(f32[8,5,4,1920]{3,2,1,0:T(4,128)} %refs_6_), custom_call_target="tpu_custom_call" | custom-call | tf_op jit(solution)/shard_map/relayout/pallas_call | solution.py:1022
  37.6 1.7 %columns.1 = (f32[5,1,1920]{2,1,0:T(1,128)}, f32[5,1,1920]{2,1,0:T(1,128)}, f32[300,128]{1,0:T(8,128)}, f32[300,128]{1,0:T(8,128)}) custom-call(f32[5,1920]{1,0:T(8,128)} %refs_0_.4, f32[5,1920]{1,0:T(8,128)} %refs_1_.5), custom_call_target="tpu_custom_call" | custom-call | tf_op jit(solution)/shard_map/columns/pallas_call | solution.py:1022
  39.3 4.7 %all-to-all-done.1 = f32[16,15,2,128]{3,2,1,0:T(2,128)S(1)} async-done(((f32[16,15,2,128]{3,2,1,0:T(2,128)}), f32[16,15,2,128]{3,2,1,0:T(2,128)S(1)}, u32[]{:S(2)}, u32[]{:S(2)}) %all-to-all-start.1) | async-done | bytes 245792 | tf_op jit(solution)/shard_map/all_to_all | solution.py:1050
  44.0 1.8 %surface.2 = (f32[304,128]{1,0:T(8,128)S(1)}, f32[60,128]{1,0:T(8,128)S(1)}, f32[60,128]{1,0:T(8,128)S(1)}, f32[64,128]{1,0:T(8,128)}) custom-call(f32[480,128]{1,0:T(8,128)S(1)} %bitcast.43, f32[40,128]{1,0:T(8,128)S(1)} %collective-permute-done.2.refs_5_.refs_1_, f32[40,128]{1,0:T(8,128)S(1)} %collective-permute-done.3.refs_6_.refs_2_, ...), custom_call_target="tpu_custom_call" | custom-call | tf_op jit(solution)/shard_map/surface/pallas_call | solution.py:1022
  45.9 0.7 collective-permute-start.7
  46.6 1.9 %step_load.1 = (f32[16,8,128]{2,1,0:T(8,128)S(1)}, f32[5,1,1920]{2,1,0:T(1,128)S(1)}, f32[5,4,8,1920]{3,2,1,0:T(8,128)S(1)}, f32[5,1,1920]{2,1,0:T(1,128)S(1)}, f32[5,4,8,1920]{3,2,1,0:T(8,128)S(1)}) custom-call(f32[16,8,128]{2,1,0:T(8,128)} %get-tuple-element.152.refs_0_, f32[5,1,1920]{2,1,0:T(1,128)} %get-tuple-element.153.refs_1_, ...), custom_call_target="tpu_custom_call" | custom-call | tf_op jit(solution)/shard_map/step_load/pallas_call | solution.py:1022
  48.5 2.7 %step.3 = (f32[5,4,8,1920]{3,2,1,0:T(8,128)}, f32[5,4,8,1920]{3,2,1,0:T(8,128)}, f32[304,128]{1,0:T(8,128)}, f32[320,128]{1,0:T(8,128)}, f32[32,128]{1,0:T(8,128...) custom-call(s32[1,128]{1,0:T(1,128)} %get-tuple-element.118.refs_0_.refs_7_.refs_5_, ...), custom_call_target="tpu_custom_call" | custom-call | tf_op jit(solution)/shard_map/step/pallas_call | solution.py:1022
  51.3 6.5 %all-to-all-start.2 = ((f32[16,5,4,128]{3,2,1,0:T(4,128)}), f32[16,5,4,128]{3,2,1,0:T(4,128)S(1)}, u32[]{:S(2)}, u32[]{:S(2)}) async-start(f32[16,5,4,128]{3,2,1,0:T(4,128)} %bitcast.63), calls=%async_computation.2 | async-start | bytes 327680 | tf_op jit(solution)/shard_map/all_to_all | solution.py:1050
  57.8 0.4 collective-permute-start.8
  58.2 0.7 collective-permute-start.9
  58.9 0.4 collective-permute-done.8.refs_1_
  59.3 7.0 %all-to-all-done.2 = f32[16,5,4,128]{3,2,1,0:T(4,128)S(1)} async-done(((f32[16,5,4,128]{3,2,1,0:T(4,128)}), f32[16,5,4,128]{3,2,1,0:T(4,128)S(1)}, u32[]{:S(2)}, u32[]{:S(2)}) %all-to-all-start.2) | async-done | bytes 163872 | tf_op jit(solution)/shard_map/all_to_all | solution.py:1050
  66.3 1.6 owners.3
  67.9 3.5 %all-to-all-start.3 = ((f32[16,15,2,128]{3,2,1,0:T(2,128)}), f32[16,15,2,128]{3,2,1,0:T(2,128)S(1)}, u32[]{:S(2)}, u32[]{:S(2)}) async-start(f32[16,15,2,128]{3,2,1,0:T(2,128)} %bitcast.61), calls=%async_computation.3 | async-start | bytes 491520 | tf_op jit(solution)/shard_map/all_to_all | solution.py:1050
  71.5 2.3 %relayout.3.refs_5_ = f32[5,4,8,1920]{3,2,1,0:T(8,128)} custom-call(f32[8,5,4,1920]{3,2,1,0:T(4,128)} %refs_1_.6), custom_call_target="tpu_custom_call" | custom-call | tf_op jit(solution)/shard_map/relayout/pallas_call | solution.py:1022
  73.8 7.4 %all-to-all-done.3 = f32[16,15,2,128]{3,2,1,0:T(2,128)S(1)} async-done(((f32[16,15,2,128]{3,2,1,0:T(2,128)}), f32[16,15,2,128]{3,2,1,0:T(2,128)S(1)}, u32[]{:S(2)}, u32[]{:S(2)}) %all-to-all-start.3) | async-done | bytes 245792 | tf_op jit(solution)/shard_map/all_to_all | solution.py:1050
  81.2 2.3 %surface.3 = (f32[304,128]{1,0:T(8,128)}, f32[64,128]{1,0:T(8,128)}, f32[480,128]{1,0:T(8,128)}, f32[32,128]{1,0:T(8,128)}, f32[32,128]{1,0:T(8,128)}) custom-call(f32[480,128]{1,0:T(8,128)S(1)} %bitcast.42, f32[32,128]{1,0:T(8,128)S(1)} %collective-permute-done.8.refs_1_, f32[32,128]{1,0:T(8,128)S(1)} %collective-permute-done.9.refs_2_, ...), custom_call_target="tpu_custom_call" | custom-call | tf_op jit(solution)/shard_map/surface/pallas_call | solution.py:1022
  83.6 3.7 %all-to-all-start.4 = ((f32[16,15,2,128]{3,2,1,0:T(2,128)}), f32[16,15,2,128]{3,2,1,0:T(2,128)S(1)}, u32[]{:S(2)}, u32[]{:S(2)}) async-start(f32[16,15,2,128]{3,2,1,0:T(2,128)} %bitcast.59), calls=%async_computation.4 | async-start | bytes 491520 | tf_op jit(solution)/shard_map/all_to_all | solution.py:1050
  87.5 0.7 collective-permute-start.13
  88.2 0.5 collective-permute-done.12.refs_1_
  88.7 8.3 %all-to-all-done.4 = f32[16,15,2,128]{3,2,1,0:T(2,128)S(1)} async-done(((f32[16,15,2,128]{3,2,1,0:T(2,128)}), f32[16,15,2,128]{3,2,1,0:T(2,128)S(1)}, u32[]{:S(2)}, u32[]{:S(2)}) %all-to-all-start.4) | async-done | bytes 245792 | tf_op jit(solution)/shard_map/all_to_all | solution.py:1050
  97.0 2.0 %owners_back.2 = f32[320,128]{1,0:T(8,128)} custom-call(f32[480,128]{1,0:T(8,128)S(1)} %bitcast.44, f32[80,80]{1,0:T(8,128)S(1)} %bitcast.52, f32[4,80,128]{2,1,0:T(8,128)} %get-tuple-element.186.refs_2_, f32[4,80,128]{2,1,0:T(8,128)} %get-tuple-element.187.refs_3_, f32[1,128]{1,0:T(1,128)} %get-tuple-element.119.refs_1_.refs_4_.refs_8_.refs_6_), custom_call_target="tpu_custom_call" | custom-call | tf_op jit(solution)/shard_map/owners_back/pallas_call | solution.py:1022
  99.0 3.5 %all-to-all-start.5 = ((f32[16,5,4,128]{3,2,1,0:T(4,128)}), f32[16,5,4,128]{3,2,1,0:T(4,128)S(1)}, u32[]{:S(2)}, u32[]{:S(2)}) async-start(f32[16,5,4,128]{3,2,1,0:T(4,128)} %bitcast.56), calls=%async_computation.5 | async-start | bytes 327680 | tf_op jit(solution)/shard_map/all_to_all | solution.py:1050
  102.6 0.4 collective-permute-start.10
  102.9 0.7 collective-permute-start.11
  103.6 7.4 %all-to-all-done.5 = f32[16,5,4,128]{3,2,1,0:T(4,128)S(1)} async-done(((f32[16,5,4,128]{3,2,1,0:T(4,128)}), f32[16,5,4,128]{3,2,1,0:T(4,128)S(1)}, u32[]{:S(2)}, u32[]{:S(2)}) %all-to-all-start.5) | async-done | bytes 163872 | tf_op jit(solution)/shard_map/all_to_all | solution.py:1050
  111.0 1.2 merge.2
  112.3 0.7 collective-permute-start.15
  113.0 2.0 %step_back_load.2 = (f32[16,8,128]{2,1,0:T(8,128)S(1)}, f32[5,1,1920]{2,1,0:T(1,128)S(1)}, f32[5,4,8,1920]{3,2,1,0:T(8,128)S(1)}, f32[5,4,8,1920]{3,2,1,0:T(8,128)S(1)}, f32[5,4,8,1920]{3,2,1,0:T(8,128)S(1)}) custom-call(f32[16,8,128]{2,1,0:T(8,128)} %get-tuple-element.152.refs_0_, f32[5,1,1920]{2,1,0:T(1,128)} %get-tuple-element.153.refs_1_, ...), custom_call_target="tpu_custom_call" | custom-call | tf_op jit(solution)/shard_map/step_back_load/pallas_call | solution.py:1022
  115.0 2.7 %step_back.1 = (f32[5,4,8,1920]{3,2,1,0:T(8,128)}, f32[304,128]{1,0:T(8,128)}, f32[480,128]{1,0:T(8,128)}, f32[32,128]{1,0:T(8,128)}, f32[32,128]{1,0:T(8,128)}, /*index=5*/f32[480,128]{1,0:T(8,128)}, f32[480,128]{1,0:T(8,128)}) custom-call(s32[3,128]{1,0:T(4,128)} %get-tuple-element.134.refs_4_.refs_0_, f32[3,128]{1,0:T(4,128)} %get-tuple-element.135.refs_5_.refs_1_, ...), custom_call_target="tpu_custom_call" | custom-call | tf_op jit(solution)/shard_map/step_back/pallas_call | solution.py:1022
  117.7 5.9 %all-to-all-start.6 = ((f32[16,15,2,128]{3,2,1,0:T(2,128)}), f32[16,15,2,128]{3,2,1,0:T(2,128)S(1)}, u32[]{:S(2)}, u32[]{:S(2)}) async-start(f32[16,15,2,128]{3,2,1,0:T(2,128)} %bitcast.58), calls=%async_computation.6 | async-start | bytes 491520 | tf_op jit(solution)/shard_map/all_to_all | solution.py:1050
  123.5 0.8 collective-permute-start.16
  124.3 0.7 collective-permute-start.17
  125.0 0.4 collective-permute-done.16.refs_1_
  125.4 7.9 %all-to-all-done.6 = f32[16,15,2,128]{3,2,1,0:T(2,128)S(1)} async-done(((f32[16,15,2,128]{3,2,1,0:T(2,128)}), f32[16,15,2,128]{3,2,1,0:T(2,128)S(1)}, u32[]{:S(2)}, u32[]{:S(2)}) %all-to-all-start.6) | async-done | bytes 245792 | tf_op jit(solution)/shard_map/all_to_all | solution.py:1050
  133.3 2.0 %owners_back.3 = f32[320,128]{1,0:T(8,128)} custom-call(f32[480,128]{1,0:T(8,128)S(1)} %bitcast.45, f32[80,80]{1,0:T(8,128)S(1)} %bitcast.53, f32[4,80,128]{2,1,0:T(8,128)} %get-tuple-element.207.refs_2_, f32[4,80,128]{2,1,0:T(8,128)} %get-tuple-element.208.refs_3_, f32[1,128]{1,0:T(1,128)} %get-tuple-element.119.refs_1_.refs_4_.refs_8_.refs_6_), custom_call_target="tpu_custom_call" | custom-call | tf_op jit(solution)/shard_map/owners_back/pallas_call | solution.py:1022
  135.4 3.5 %all-to-all-start.7 = ((f32[16,5,4,128]{3,2,1,0:T(4,128)}), f32[16,5,4,128]{3,2,1,0:T(4,128)S(1)}, u32[]{:S(2)}, u32[]{:S(2)}) async-start(f32[16,5,4,128]{3,2,1,0:T(4,128)} %bitcast.57), calls=%async_computation.7 | async-start | bytes 327680 | tf_op jit(solution)/shard_map/all_to_all | solution.py:1050
  138.9 0.4 collective-permute-start.18
  139.3 0.7 collective-permute-start.19
  139.9 7.4 %all-to-all-done.7 = f32[16,5,4,128]{3,2,1,0:T(4,128)S(1)} async-done(((f32[16,5,4,128]{3,2,1,0:T(4,128)}), f32[16,5,4,128]{3,2,1,0:T(4,128)S(1)}, u32[]{:S(2)}, u32[]{:S(2)}) %all-to-all-start.7) | async-done | bytes 163872 | tf_op jit(solution)/shard_map/all_to_all | solution.py:1050
  147.3 1.2 merge.3
  148.6 0.7 collective-permute-start.21
  149.3 2.4 %step_back_load.3 = (f32[16,8,128]{2,1,0:T(8,128)S(1)}, f32[5,1,1920]{2,1,0:T(1,128)S(1)}, f32[5,4,8,1920]{3,2,1,0:T(8,128)S(1)}, f32[5,4,8,1920]{3,2,1,0:T(8,12...) custom-call(f32[16,8,128]{2,1,0:T(8,128)} %get-tuple-element.152.refs_0_, ...), custom_call_target="tpu_custom_call" | custom-call | tf_op jit(solution)/shard_map/step_back_load/pallas_call | solution.py:1022
  151.7 2.4 %step_back_sums.1 = (f32[5,4,8,1920]{3,2,1,0:T(8,128)}, f32[16,128]{1,0:T(8,128)}) custom-call(f32[480,128]{1,0:T(8,128)S(1)} %collective-permute-done.18.refs_0_, f32[480,128]{1,0:T(8,128)S(1)} %collective-permute-done.19.refs_1_, f32[60,128]{1,0:T(8,128)S(1)} %collective-permute-done.20.refs_2_, f32[60,128]{1,0:T(8,128)S(1)} %collective-permute-done.21.refs_3_, ...), custom_call_target="tpu_custom_call" | custom-call | tf_op jit(solution)/shard_map/step_back_sums/pallas_call | solution.py:1022
  154.1 5.4 %all-to-all-start.8 = ((f32[16,1,128]{2,1,0:T(1,128)}), f32[16,1,128]{2,1,0:T(1,128)S(1)}, u32[]{:S(2)}, u32[]{:S(2)}) async-start(f32[16,1,128]{2,1,0:T(1,128)} %bitcast.64), calls=%async_computation.8 | async-start | bytes 16384 | tf_op jit(solution)/shard_map/all_to_all | solution.py:1294
  159.5 1.7 %copy.20 = f32[5,4,8,1920]{3,1,0,2:T(4,128)S(1)} copy(f32[5,4,8,1920]{3,2,1,0:T(8,128)} %get-tuple-element.230) | data formatting | bytes 2457600 | tf_op jit(solution)/shard_map/step_back_sums/pallas_call | solution.py:1022
  161.2 4.7 %all-to-all-done.8 = f32[16,1,128]{2,1,0:T(1,128)S(1)} async-done(((f32[16,1,128]{2,1,0:T(1,128)}), f32[16,1,128]{2,1,0:T(1,128)S(1)}, u32[]{:S(2)}, u32[]{:S(2)}) %all-to-all-start.8) | async-done | bytes 8224 | tf_op jit(solution)/shard_map/all_to_all | solution.py:1294
  165.9 1.2 finish.1
  (65 shorter events, 0.9 us)
Async XLA Ops:
  0.0 6.7 %copy-start.5 = (f32[4,4]{1,0:T(4,128)S(1)}, f32[4,4]{1,0:T(4,128)}, u32[]{:S(2)}) copy-start(f32[4,4]{1,0:T(4,128)} %param.21) | copy-start | bytes 196
  0.0 6.8 %copy-start.7 = (s32[15]{0:T(128)S(1)}, s32[15]{0:T(128)}, u32[]{:S(2)}) copy-start(s32[15]{0:T(128)} %param.28) | copy-start | bytes 184
  0.0 6.8 %copy-start.6 = (s32[15]{0:T(128)S(1)}, s32[15]{0:T(128)}, u32[]{:S(2)}) copy-start(s32[15]{0:T(128)} %param.27) | copy-start | bytes 184
  0.0 6.8 %copy-start.14 = (f32[15]{0:T(128)S(1)}, f32[15]{0:T(128)}, u32[]{:S(2)}) copy-start(f32[15]{0:T(128)} %param.29) | copy-start | bytes 184
  1.6 10.2 %collective-permute-start = (f32[480,128]{1,0:T(8,128)S(1)}, f32[480,128]{1,0:T(8,128)S(1)}, u32[]{:S(2)}, u32[]{:S(2)}) collective-permute-start(f32[480,128]{1,0:T(8,128)S(1)} %get-tuple-element.120), channel_id=1, source_target_pairs={{1,2},{3,4},{5,6},{7,8},{9,10},{11,12},{13,14},{2,1},{4,3},{6,5},{... | collective-permute-start | bytes 737288 | tf_op jit(solution)/shard_map/ppermute | solution.py:1043
  2.3 8.4 %collective-permute-start.1 = (f32[480,128]{1,0:T(8,128)S(1)}, f32[480,128]{1,0:T(8,128)S(1)}, u32[]{:S(2)}, u32[]{:S(2)}) collective-permute-start(f32[480,128]{1,0:T(8,128)S(1)} %get-tuple-element.124), channel_id=1, source_target_pairs={{0,1},{1,0},{2,3},{3,2},{4,5},{5,4},{6,7},{7,6},{8,9},{9,8},{10,11... | collective-permute-start | bytes 737288 | tf_op jit(solution)/shard_map/ppermute | solution.py:1043
  6.9 2.0 %copy-start.15 = (s32[1,75]{1,0:T(1,128)S(1)}, s32[1,75]{1,0:T(1,128)}, u32[]{:S(2)}) copy-start(s32[1,75]{1,0:T(1,128)} %param.25) | copy-start | bytes 904
  6.9 2.0 %copy-start.16 = (s32[1,75]{1,0:T(1,128)S(1)}, s32[1,75]{1,0:T(1,128)}, u32[]{:S(2)}) copy-start(s32[1,75]{1,0:T(1,128)} %param.26) | copy-start | bytes 904
  6.9 2.1 %copy-start.2 = (f32[8,4,4]{0,2,1:T(4,128)S(1)}, f32[8,4,4]{0,2,1:T(4,128)}, u32[]{:S(2)}) copy-start(f32[8,4,4]{0,2,1:T(4,128)} %param.20) | copy-start | bytes 1540
  11.8 9.8 %copy-start.3 = (f32[2,1,80,128]{3,2,1,0:T(8,128)S(1)}, f32[2,1,80,128]{3,2,1,0:T(8,128)}, u32[]{:S(2)}) copy-start(f32[2,1,80,128]{3,2,1,0:T(8,128)} %param.24) | copy-start | bytes 245764
  11.9 9.8 %copy-start.4 = (f32[2,1,80,128]{3,2,1,0:T(8,128)S(1)}, f32[2,1,80,128]{3,2,1,0:T(8,128)}, u32[]{:S(2)}) copy-start(f32[2,1,80,128]{3,2,1,0:T(8,128)} %param.23) | copy-start | bytes 245764
  11.9 17.2 %copy-start.1 = (f32[1,80,80]{2,1,0:T(8,128)S(1)}, f32[1,80,80]{2,1,0:T(8,128)}, u32[]{:S(2)}) copy-start(f32[1,80,80]{2,1,0:T(8,128)} %param.22) | copy-start | bytes 76804
  14.1 20.1 %copy-start.11 = (f32[480,128]{1,0:T(8,128)S(1)}, f32[480,128]{1,0:T(8,128)}, u32[]{:S(2)}) copy-start(f32[480,128]{1,0:T(8,128)} %get-tuple-element.150) | copy-start | bytes 737284
  14.1 20.5 %copy-start.10 = (f32[480,128]{1,0:T(8,128)S(1)}, f32[480,128]{1,0:T(8,128)}, u32[]{:S(2)}) copy-start(f32[480,128]{1,0:T(8,128)} %get-tuple-element.151) | copy-start | bytes 737284
  14.1 14.9 %all-to-all-start = ((f32[16,5,4,128]{3,2,1,0:T(4,128)}), f32[16,5,4,128]{3,2,1,0:T(4,128)S(1)}, u32[]{:S(2)}, u32[]{:S(2)}) async-start(f32[16,5,4,128]{3,2,1,0:T(4,128)} %bitcast.62), calls=%async_computation | async-start | bytes 327680 | tf_op jit(solution)/shard_map/all_to_all | solution.py:1050
  20.6 1.5 collective-permute-start.2
  21.0 1.1 collective-permute-start.3
  30.7 13.3 %all-to-all-start.1 = ((f32[16,15,2,128]{3,2,1,0:T(2,128)}), f32[16,15,2,128]{3,2,1,0:T(2,128)S(1)}, u32[]{:S(2)}, u32[]{:S(2)}) async-start(f32[16,15,2,128]{3,2,1,0:T(2,128)} %bitcast.60), calls=%async_computation.1 | async-start | bytes 491520 | tf_op jit(solution)/shard_map/all_to_all | solution.py:1050
  34.3 14.2 %collective-permute-start.4 = (f32[480,128]{1,0:T(8,128)S(1)}, f32[480,128]{1,0:T(8,128)S(1)}, u32[]{:S(2)}, u32[]{:S(2)}) collective-permute-start(f32[480,128]{1,0:T(8,128)S(1)} %copy-done.11), channel_id=1, source_target_pairs={{0,1},{1,0},{2,3},{3,2},{4,5},{5,4},{6,7},{7,6},{8,9},{9,8},{10,11... | collective-permute-start | bytes 737288 | tf_op jit(solution)/shard_map/ppermute | solution.py:1043
  34.6 13.9 %collective-permute-start.5 = (f32[480,128]{1,0:T(8,128)S(1)}, f32[480,128]{1,0:T(8,128)S(1)}, u32[]{:S(2)}, u32[]{:S(2)}) collective-permute-start(f32[480,128]{1,0:T(8,128)S(1)} %copy-done.10), channel_id=1, source_target_pairs={{1,2},{3,4},{5,6},{7,8},{9,10},{11,12},{13,14},{2,1},{4,3},{6,5},{... | collective-permute-start | bytes 737288 | tf_op jit(solution)/shard_map/ppermute | solution.py:1043
  45.8 2.7 %collective-permute-start.6 = (f32[60,128]{1,0:T(8,128)S(1)}, f32[60,128]{1,0:T(8,128)S(1)}, u32[]{:S(2)}, u32[]{:S(2)}) collective-permute-start(f32[60,128]{1,0:T(8,128)S(1)} %get-tuple-element.161), channel_id=1, source_target_pairs={{0,1},{1,0},{2,3},{3,2},{4,5},{5,4},{6,7},{7,6},{8,9},{9,8},{10,11... | collective-permute-start | bytes 92168 | tf_op jit(solution)/shard_map/ppermute | solution.py:1043
  45.9 2.6 %collective-permute-start.7 = (f32[60,128]{1,0:T(8,128)S(1)}, f32[60,128]{1,0:T(8,128)S(1)}, u32[]{:S(2)}, u32[]{:S(2)}) collective-permute-start(f32[60,128]{1,0:T(8,128)S(1)} %get-tuple-element.162), channel_id=1, source_target_pairs={{1,2},{3,4},{5,6},{7,8},{9,10},{11,12},{13,14},{2,1},{4,3},{6,5},{... | collective-permute-start | bytes 92168 | tf_op jit(solution)/shard_map/ppermute | solution.py:1043
  51.3 15.0 %all-to-all-start.2 = ((f32[16,5,4,128]{3,2,1,0:T(4,128)}), f32[16,5,4,128]{3,2,1,0:T(4,128)S(1)}, u32[]{:S(2)}, u32[]{:S(2)}) async-start(f32[16,5,4,128]{3,2,1,0:T(4,128)} %bitcast.63), calls=%async_computation.2 | async-start | bytes 327680 | tf_op jit(solution)/shard_map/all_to_all | solution.py:1050
  57.8 1.5 collective-permute-start.8
  58.2 1.1 collective-permute-start.9
  67.9 13.3 %all-to-all-start.3 = ((f32[16,15,2,128]{3,2,1,0:T(2,128)}), f32[16,15,2,128]{3,2,1,0:T(2,128)S(1)}, u32[]{:S(2)}, u32[]{:S(2)}) async-start(f32[16,15,2,128]{3,2,1,0:T(2,128)} %bitcast.61), calls=%async_computation.3 | async-start | bytes 491520 | tf_op jit(solution)/shard_map/all_to_all | solution.py:1050
  83.5 19.0 %copy-start.9 = (f32[480,128]{1,0:T(8,128)S(1)}, f32[480,128]{1,0:T(8,128)}, u32[]{:S(2)}) copy-start(f32[480,128]{1,0:T(8,128)} %get-tuple-element.172) | copy-start | bytes 737284
  83.6 19.4 %copy-start.8 = (f32[480,128]{1,0:T(8,128)S(1)}, f32[480,128]{1,0:T(8,128)}, u32[]{:S(2)}) copy-start(f32[480,128]{1,0:T(8,128)} %get-tuple-element.173) | copy-start | bytes 737284
  83.6 13.4 %all-to-all-start.4 = ((f32[16,15,2,128]{3,2,1,0:T(2,128)}), f32[16,15,2,128]{3,2,1,0:T(2,128)S(1)}, u32[]{:S(2)}, u32[]{:S(2)}) async-start(f32[16,15,2,128]{3,2,1,0:T(2,128)} %bitcast.59), calls=%async_computation.4 | async-start | bytes 491520 | tf_op jit(solution)/shard_map/all_to_all | solution.py:1050
  87.2 1.5 collective-permute-start.12
  87.5 1.2 collective-permute-start.13
  99.0 12.0 %all-to-all-start.5 = ((f32[16,5,4,128]{3,2,1,0:T(4,128)}), f32[16,5,4,128]{3,2,1,0:T(4,128)S(1)}, u32[]{:S(2)}, u32[]{:S(2)}) async-start(f32[16,5,4,128]{3,2,1,0:T(4,128)} %bitcast.56), calls=%async_computation.5 | async-start | bytes 327680 | tf_op jit(solution)/shard_map/all_to_all | solution.py:1050
  102.6 12.4 %collective-permute-start.10 = (f32[480,128]{1,0:T(8,128)S(1)}, f32[480,128]{1,0:T(8,128)S(1)}, u32[]{:S(2)}, u32[]{:S(2)}) collective-permute-start(f32[480,128]{1,0:T(8,128)S(1)} %copy-done.9), channel_id=1, source_target_pairs={{0,1},{1,0},{2,3},{3,2},{4,5},{5,4},{6,7},{7,6},{8,9},{9,8},{10,11... | collective-permute-start | bytes 737288 | tf_op jit(solution)/shard_map/ppermute | solution.py:1043
  102.9 12.0 %collective-permute-start.11 = (f32[480,128]{1,0:T(8,128)S(1)}, f32[480,128]{1,0:T(8,128)S(1)}, u32[]{:S(2)}, u32[]{:S(2)}) collective-permute-start(f32[480,128]{1,0:T(8,128)S(1)} %copy-done.8), channel_id=1, source_target_pairs={{1,2},{3,4},{5,6},{7,8},{9,10},{11,12},{13,14},{2,1},{4,3},{6,5},{... | collective-permute-start | bytes 737288 | tf_op jit(solution)/shard_map/ppermute | solution.py:1043
  112.2 2.8 %collective-permute-start.14 = (f32[60,128]{1,0:T(8,128)S(1)}, f32[60,128]{1,0:T(8,128)S(1)}, u32[]{:S(2)}, u32[]{:S(2)}) collective-permute-start(f32[60,128]{1,0:T(8,128)S(1)} %get-tuple-element.193), channel_id=1, source_target_pairs={{0,1},{1,0},{2,3},{3,2},{4,5},{5,4},{6,7},{7,6},{8,9},{9,8},{10,11... | collective-permute-start | bytes 92168 | tf_op jit(solution)/shard_map/ppermute | solution.py:1043
  112.3 2.7 %collective-permute-start.15 = (f32[60,128]{1,0:T(8,128)S(1)}, f32[60,128]{1,0:T(8,128)S(1)}, u32[]{:S(2)}, u32[]{:S(2)}) collective-permute-start(f32[60,128]{1,0:T(8,128)S(1)} %get-tuple-element.194), channel_id=1, source_target_pairs={{1,2},{3,4},{5,6},{7,8},{9,10},{11,12},{13,14},{2,1},{4,3},{6,5},{... | collective-permute-start | bytes 92168 | tf_op jit(solution)/shard_map/ppermute | solution.py:1043
  117.7 21.3 %copy-start.13 = (f32[480,128]{1,0:T(8,128)S(1)}, f32[480,128]{1,0:T(8,128)}, u32[]{:S(2)}) copy-start(f32[480,128]{1,0:T(8,128)} %get-tuple-element.211) | copy-start | bytes 737284
  117.7 21.6 %copy-start.12 = (f32[480,128]{1,0:T(8,128)S(1)}, f32[480,128]{1,0:T(8,128)}, u32[]{:S(2)}) copy-start(f32[480,128]{1,0:T(8,128)} %get-tuple-element.212) | copy-start | bytes 737284
  117.7 15.6 %all-to-all-start.6 = ((f32[16,15,2,128]{3,2,1,0:T(2,128)}), f32[16,15,2,128]{3,2,1,0:T(2,128)S(1)}, u32[]{:S(2)}, u32[]{:S(2)}) async-start(f32[16,15,2,128]{3,2,1,0:T(2,128)} %bitcast.58), calls=%async_computation.6 | async-start | bytes 491520 | tf_op jit(solution)/shard_map/all_to_all | solution.py:1050
  123.5 1.8 %collective-permute-start.16 = (f32[32,128]{1,0:T(8,128)}, f32[32,128]{1,0:T(8,128)S(1)}, u32[]{:S(2)}, u32[]{:S(2)}) collective-permute-start(f32[32,128]{1,0:T(8,128)} %get-tuple-element.204), channel_id=1, source_target_pairs={{0,1},{1,0},{2,3},{3,2},{4,5},{5,4},{6,7},{7,6},{8,9},{9,8},{10,11... | collective-permute-start | bytes 49160 | tf_op jit(solution)/shard_map/ppermute | solution.py:1043
  124.3 1.1 collective-permute-start.17
  135.4 12.0 %all-to-all-start.7 = ((f32[16,5,4,128]{3,2,1,0:T(4,128)}), f32[16,5,4,128]{3,2,1,0:T(4,128)S(1)}, u32[]{:S(2)}, u32[]{:S(2)}) async-start(f32[16,5,4,128]{3,2,1,0:T(4,128)} %bitcast.57), calls=%async_computation.7 | async-start | bytes 327680 | tf_op jit(solution)/shard_map/all_to_all | solution.py:1050
  138.9 12.7 %collective-permute-start.18 = (f32[480,128]{1,0:T(8,128)S(1)}, f32[480,128]{1,0:T(8,128)S(1)}, u32[]{:S(2)}, u32[]{:S(2)}) collective-permute-start(f32[480,128]{1,0:T(8,128)S(1)} %copy-done.13), channel_id=1, source_target_pairs={{0,1},{1,0},{2,3},{3,2},{4,5},{5,4},{6,7},{7,6},{8,9},{9,8},{10,11... | collective-permute-start | bytes 737288 | tf_op jit(solution)/shard_map/ppermute | solution.py:1043
  139.3 12.4 %collective-permute-start.19 = (f32[480,128]{1,0:T(8,128)S(1)}, f32[480,128]{1,0:T(8,128)S(1)}, u32[]{:S(2)}, u32[]{:S(2)}) collective-permute-start(f32[480,128]{1,0:T(8,128)S(1)} %copy-done.12), channel_id=1, source_target_pairs={{1,2},{3,4},{5,6},{7,8},{9,10},{11,12},{13,14},{2,1},{4,3},{6,5},{... | collective-permute-start | bytes 737288 | tf_op jit(solution)/shard_map/ppermute | solution.py:1043
  148.5 3.1 %collective-permute-start.20 = (f32[60,128]{1,0:T(8,128)S(1)}, f32[60,128]{1,0:T(8,128)S(1)}, u32[]{:S(2)}, u32[]{:S(2)}) collective-permute-start(f32[60,128]{1,0:T(8,128)S(1)} %get-tuple-element.217), channel_id=1, source_target_pairs={{0,1},{1,0},{2,3},{3,2},{4,5},{5,4},{6,7},{7,6},{8,9},{9,8},{10,11... | collective-permute-start | bytes 92168 | tf_op jit(solution)/shard_map/ppermute | solution.py:1043
  148.6 3.1 %collective-permute-start.21 = (f32[60,128]{1,0:T(8,128)S(1)}, f32[60,128]{1,0:T(8,128)S(1)}, u32[]{:S(2)}, u32[]{:S(2)}) collective-permute-start(f32[60,128]{1,0:T(8,128)S(1)} %get-tuple-element.218), channel_id=1, source_target_pairs={{1,2},{3,4},{5,6},{7,8},{9,10},{11,12},{13,14},{2,1},{4,3},{6,5},{... | collective-permute-start | bytes 92168 | tf_op jit(solution)/shard_map/ppermute | solution.py:1043
  154.1 11.8 %all-to-all-start.8 = ((f32[16,1,128]{2,1,0:T(1,128)}), f32[16,1,128]{2,1,0:T(1,128)S(1)}, u32[]{:S(2)}, u32[]{:S(2)}) async-start(f32[16,1,128]{2,1,0:T(1,128)} %bitcast.64), calls=%async_computation.8 | async-start | bytes 16384 | tf_op jit(solution)/shard_map/all_to_all | solution.py:1294
  159.5 6.4 %copy-start = (f32[8,5,4,1920]{3,2,1,0:T(4,128)S(1)}, f32[8,5,4,1920]{3,2,1,0:T(4,128)}, u32[]{:S(2)}) copy-start(f32[8,5,4,1920]{3,2,1,0:T(4,128)} %refs_1_.6) | copy-start | bytes 3686404

commit v11 on v10

--- a/solution.py
+++ b/solution.py
@@ -462,9 +462,12 @@
 
     if part == 0:
         ready(0)
-    else:
+    elif part == 1:
         for row in range(sz.rows):
             ready(row)
+    else:
+        ready((1 - flag) * (sz.rows - 1))
+        ready((1 - flag) * (sz.rows - 1) + 2 * flag - 1)
     lane = lax.broadcasted_iota(jnp.int32, (LEVELS, WIDTH), 1)
     masks = level_masks()
     count = sz.row_tiles

time: 169 us -> 169 us (level)
  no operation moved by 1% of the time
where the time goes in v11:
time: 169 us; the launch traced here: 167 us
  waiting for transfers between devices  63.5 us (38%)
  starting transfers between devices  56.8 us (34%)
  Pallas kernels  44 us (26%)
  local copies, waits for them, and re-layouts  1.88 us (1%)
    all_to_all x8, waiting for transfers between devices, exchange(): lax.all_to_all(split, 'horiz', split_axis=0, concat_axis=0, tiled=True)  57.1 us
    pallas_call x23, Pallas kernels, call(): pl.pallas_call(run, name=name, in_specs=[pl.BlockSpec(memory_space=item.s...  44 us
    all_to_all x8, starting transfers between devices, exchange(): lax.all_to_all(split, 'horiz', split_axis=0, concat_axis=0, tiled=True)  36.6 us
    ppermute x11, starting transfers between devices, swap(): lax.ppermute(first, 'horiz', inner)  7.55 us
    ppermute x11, starting transfers between devices, swap(): lax.ppermute(second, 'horiz', outer)  7.26 us
    all_to_all x1, starting transfers between devices, body(): lax.all_to_all(sums, 'horiz', split_axis=0, concat_axis=0, tiled=True)  5.36 us
    all_to_all x1, waiting for transfers between devices, body(): lax.all_to_all(sums, 'horiz', split_axis=0, concat_axis=0, tiled=True)  4.68 us
  transfers between devices with their start and end apart: 31, of which 13 were waited for; matrix products, arithmetic and copies ran while one was open for 1% of the time, Pallas kernels for 13%

profile of v11, /device:TPU:0, one launch (start us, length us, event | category | flops | bytes accessed | tf_op | source)
XLA Modules:
  0.0 167.0 jit_solution(7369644966316397174)
XLA Ops:
  0.0 1.6 edges.1
  1.6 0.7 collective-permute-start
  2.3 4.4 %collective-permute-start.1 = (f32[480,128]{1,0:T(8,128)S(1)}, f32[480,128]{1,0:T(8,128)S(1)}, u32[]{:S(2)}, u32[]{:S(2)}) collective-permute-start(f32[480,128]{1,0:T(8,128)S(1)} %get-tuple-element.124), channel_id=1, source_target_pairs={{0,1},{1,0},{2,3},{3,2},{4,5},{5,4},{6,7},{7,6},{8,9},{9,8},{10,11... | collective-permute-start | bytes 737288 | tf_op jit(solution)/shard_map/ppermute | solution.py:1046
  6.9 2.0 %load.1.refs_3_.refs_5_ = f32[5,4,8,1920]{3,2,1,0:T(8,128)S(1)} custom-call(f32[8,5,4,1920]{3,2,1,0:T(4,128)} %refs_1_.6, f32[8,5,4,1920]{3,2,1,0:T(4,128)} %refs_1_.4), custom_call_target="tpu_custom_call" | custom-call | tf_op jit(solution)/shard_map/load/pallas_call | solution.py:1025
  9.0 1.7 %setup.1 = (f32[16,8,128]{2,1,0:T(8,128)S(1)}, f32[5,1,1920]{2,1,0:T(1,128)S(1)}, s32[1,128]{1,0:T(1,128)}, f32[8,128]{1,0:T(8,128)}, f32[1,128]{1,0:T(1,128)}, /*index=5*/f32[16,8,128]{2,1,0:T(8,128)}) custom-call(f32[2,128]{1,0:T(2,128)S(1)} %get-tuple-element.236.refs_0_, f32[2,128]{1,0:T(2,128)S(1)} %get-tuple-element.235.refs_1_, f32[16,8]{1,0:T(8,128)S(1)} %bitcast.55, ...), custom_call_target="tpu_custom_call" | custom-call | tf_op jit(solution)/shard_map/setup/pallas_call | solution.py:1025
  10.8 1.1 step_near.1
  11.9 2.2 %step.2 = (f32[5,4,8,1920]{3,2,1,0:T(8,128)}, f32[5,4,8,1920]{3,2,1,0:T(8,128)}, f32[304,128]{1,0:T(8,128)}, f32[320,128]{1,0:T(8,128)}, f32[40,128]{1,0:T(8,128...) custom-call(s32[1,128]{1,0:T(1,128)} %get-tuple-element.118.refs_0_.refs_7_.refs_5_, ...), custom_call_target="tpu_custom_call" | custom-call | tf_op jit(solution)/shard_map/step/pallas_call | solution.py:1025
  14.1 6.4 %all-to-all-start = ((f32[16,5,4,128]{3,2,1,0:T(4,128)}), f32[16,5,4,128]{3,2,1,0:T(4,128)S(1)}, u32[]{:S(2)}, u32[]{:S(2)}) async-start(f32[16,5,4,128]{3,2,1,0:T(4,128)} %bitcast.62), calls=%async_computation | async-start | bytes 327680 | tf_op jit(solution)/shard_map/all_to_all | solution.py:1053
  20.5 0.4 collective-permute-start.2
  20.9 0.7 collective-permute-start.3
  21.6 0.4 collective-permute-done.2.refs_5_.refs_1_
  22.0 7.0 %all-to-all-done = f32[16,5,4,128]{3,2,1,0:T(4,128)S(1)} async-done(((f32[16,5,4,128]{3,2,1,0:T(4,128)}), f32[16,5,4,128]{3,2,1,0:T(4,128)S(1)}, u32[]{:S(2)}, u32[]{:S(2)}) %all-to-all-start) | async-done | bytes 163872 | tf_op jit(solution)/shard_map/all_to_all | solution.py:1053
  29.0 1.7 owners.2
  30.7 3.5 %all-to-all-start.1 = ((f32[16,15,2,128]{3,2,1,0:T(2,128)}), f32[16,15,2,128]{3,2,1,0:T(2,128)S(1)}, u32[]{:S(2)}, u32[]{:S(2)}) async-start(f32[16,15,2,128]{3,2,1,0:T(2,128)} %bitcast.60), calls=%async_computation.1 | async-start | bytes 491520 | tf_op jit(solution)/shard_map/all_to_all | solution.py:1053
  34.2 0.4 collective-permute-start.4
  34.6 0.7 collective-permute-start.5
  35.2 2.3 %relayout.2.refs_5_ = f32[5,4,8,1920]{3,2,1,0:T(8,128)} custom-call(f32[8,5,4,1920]{3,2,1,0:T(4,128)} %refs_6_), custom_call_target="tpu_custom_call" | custom-call | tf_op jit(solution)/shard_map/relayout/pallas_call | solution.py:1025
  37.5 1.7 %columns.1 = (f32[5,1,1920]{2,1,0:T(1,128)}, f32[5,1,1920]{2,1,0:T(1,128)}, f32[300,128]{1,0:T(8,128)}, f32[300,128]{1,0:T(8,128)}) custom-call(f32[5,1920]{1,0:T(8,128)} %refs_0_.4, f32[5,1920]{1,0:T(8,128)} %refs_1_.5), custom_call_target="tpu_custom_call" | custom-call | tf_op jit(solution)/shard_map/columns/pallas_call | solution.py:1025
  39.3 4.7 %all-to-all-done.1 = f32[16,15,2,128]{3,2,1,0:T(2,128)S(1)} async-done(((f32[16,15,2,128]{3,2,1,0:T(2,128)}), f32[16,15,2,128]{3,2,1,0:T(2,128)S(1)}, u32[]{:S(2)}, u32[]{:S(2)}) %all-to-all-start.1) | async-done | bytes 245792 | tf_op jit(solution)/shard_map/all_to_all | solution.py:1053
  43.9 1.8 %surface.2 = (f32[304,128]{1,0:T(8,128)S(1)}, f32[60,128]{1,0:T(8,128)S(1)}, f32[60,128]{1,0:T(8,128)S(1)}, f32[64,128]{1,0:T(8,128)}) custom-call(f32[480,128]{1,0:T(8,128)S(1)} %bitcast.43, f32[40,128]{1,0:T(8,128)S(1)} %collective-permute-done.2.refs_5_.refs_1_, f32[40,128]{1,0:T(8,128)S(1)} %collective-permute-done.3.refs_6_.refs_2_, ...), custom_call_target="tpu_custom_call" | custom-call | tf_op jit(solution)/shard_map/surface/pallas_call | solution.py:1025
  45.8 0.7 collective-permute-start.7
  46.5 1.9 %step_load.1 = (f32[16,8,128]{2,1,0:T(8,128)S(1)}, f32[5,1,1920]{2,1,0:T(1,128)S(1)}, f32[5,4,8,1920]{3,2,1,0:T(8,128)S(1)}, f32[5,1,1920]{2,1,0:T(1,128)S(1)}, f32[5,4,8,1920]{3,2,1,0:T(8,128)S(1)}) custom-call(f32[16,8,128]{2,1,0:T(8,128)} %get-tuple-element.152.refs_0_, f32[5,1,1920]{2,1,0:T(1,128)} %get-tuple-element.153.refs_1_, ...), custom_call_target="tpu_custom_call" | custom-call | tf_op jit(solution)/shard_map/step_load/pallas_call | solution.py:1025
  48.5 2.7 %step.3 = (f32[5,4,8,1920]{3,2,1,0:T(8,128)}, f32[5,4,8,1920]{3,2,1,0:T(8,128)}, f32[304,128]{1,0:T(8,128)}, f32[320,128]{1,0:T(8,128)}, f32[32,128]{1,0:T(8,128...) custom-call(s32[1,128]{1,0:T(1,128)} %get-tuple-element.118.refs_0_.refs_7_.refs_5_, ...), custom_call_target="tpu_custom_call" | custom-call | tf_op jit(solution)/shard_map/step/pallas_call | solution.py:1025
  51.2 6.5 %all-to-all-start.2 = ((f32[16,5,4,128]{3,2,1,0:T(4,128)}), f32[16,5,4,128]{3,2,1,0:T(4,128)S(1)}, u32[]{:S(2)}, u32[]{:S(2)}) async-start(f32[16,5,4,128]{3,2,1,0:T(4,128)} %bitcast.63), calls=%async_computation.2 | async-start | bytes 327680 | tf_op jit(solution)/shard_map/all_to_all | solution.py:1053
  57.8 0.4 collective-permute-start.8
  58.2 0.7 collective-permute-start.9
  58.8 0.4 collective-permute-done.8.refs_1_
  59.2 7.0 %all-to-all-done.2 = f32[16,5,4,128]{3,2,1,0:T(4,128)S(1)} async-done(((f32[16,5,4,128]{3,2,1,0:T(4,128)}), f32[16,5,4,128]{3,2,1,0:T(4,128)S(1)}, u32[]{:S(2)}, u32[]{:S(2)}) %all-to-all-start.2) | async-done | bytes 163872 | tf_op jit(solution)/shard_map/all_to_all | solution.py:1053
  66.2 1.6 owners.3
  67.9 3.5 %all-to-all-start.3 = ((f32[16,15,2,128]{3,2,1,0:T(2,128)}), f32[16,15,2,128]{3,2,1,0:T(2,128)S(1)}, u32[]{:S(2)}, u32[]{:S(2)}) async-start(f32[16,15,2,128]{3,2,1,0:T(2,128)} %bitcast.61), calls=%async_computation.3 | async-start | bytes 491520 | tf_op jit(solution)/shard_map/all_to_all | solution.py:1053
  71.4 2.3 %relayout.3.refs_5_ = f32[5,4,8,1920]{3,2,1,0:T(8,128)} custom-call(f32[8,5,4,1920]{3,2,1,0:T(4,128)} %refs_1_.6), custom_call_target="tpu_custom_call" | custom-call | tf_op jit(solution)/shard_map/relayout/pallas_call | solution.py:1025
  73.7 7.4 %all-to-all-done.3 = f32[16,15,2,128]{3,2,1,0:T(2,128)S(1)} async-done(((f32[16,15,2,128]{3,2,1,0:T(2,128)}), f32[16,15,2,128]{3,2,1,0:T(2,128)S(1)}, u32[]{:S(2)}, u32[]{:S(2)}) %all-to-all-start.3) | async-done | bytes 245792 | tf_op jit(solution)/shard_map/all_to_all | solution.py:1053
  81.2 2.3 %surface.3 = (f32[304,128]{1,0:T(8,128)}, f32[64,128]{1,0:T(8,128)}, f32[480,128]{1,0:T(8,128)}, f32[32,128]{1,0:T(8,128)}, f32[32,128]{1,0:T(8,128)}) custom-call(f32[480,128]{1,0:T(8,128)S(1)} %bitcast.42, f32[32,128]{1,0:T(8,128)S(1)} %collective-permute-done.8.refs_1_, f32[32,128]{1,0:T(8,128)S(1)} %collective-permute-done.9.refs_2_, ...), custom_call_target="tpu_custom_call" | custom-call | tf_op jit(solution)/shard_map/surface/pallas_call | solution.py:1025
  83.5 3.7 %all-to-all-start.4 = ((f32[16,15,2,128]{3,2,1,0:T(2,128)}), f32[16,15,2,128]{3,2,1,0:T(2,128)S(1)}, u32[]{:S(2)}, u32[]{:S(2)}) async-start(f32[16,15,2,128]{3,2,1,0:T(2,128)} %bitcast.59), calls=%async_computation.4 | async-start | bytes 491520 | tf_op jit(solution)/shard_map/all_to_all | solution.py:1053
  87.5 0.7 collective-permute-start.13
  88.1 0.5 collective-permute-done.12.refs_1_
  88.7 8.3 %all-to-all-done.4 = f32[16,15,2,128]{3,2,1,0:T(2,128)S(1)} async-done(((f32[16,15,2,128]{3,2,1,0:T(2,128)}), f32[16,15,2,128]{3,2,1,0:T(2,128)S(1)}, u32[]{:S(2)}, u32[]{:S(2)}) %all-to-all-start.4) | async-done | bytes 245792 | tf_op jit(solution)/shard_map/all_to_all | solution.py:1053
  96.9 2.0 %owners_back.2 = f32[320,128]{1,0:T(8,128)} custom-call(f32[480,128]{1,0:T(8,128)S(1)} %bitcast.44, f32[80,80]{1,0:T(8,128)S(1)} %bitcast.52, f32[4,80,128]{2,1,0:T(8,128)} %get-tuple-element.186.refs_2_, f32[4,80,128]{2,1,0:T(8,128)} %get-tuple-element.187.refs_3_, f32[1,128]{1,0:T(1,128)} %get-tuple-element.119.refs_1_.refs_4_.refs_8_.refs_6_), custom_call_target="tpu_custom_call" | custom-call | tf_op jit(solution)/shard_map/owners_back/pallas_call | solution.py:1025
  99.0 3.5 %all-to-all-start.5 = ((f32[16,5,4,128]{3,2,1,0:T(4,128)}), f32[16,5,4,128]{3,2,1,0:T(4,128)S(1)}, u32[]{:S(2)}, u32[]{:S(2)}) async-start(f32[16,5,4,128]{3,2,1,0:T(4,128)} %bitcast.56), calls=%async_computation.5 | async-start | bytes 327680 | tf_op jit(solution)/shard_map/all_to_all | solution.py:1053
  102.5 0.4 collective-permute-start.10
  102.9 0.7 collective-permute-start.11
  103.6 7.4 %all-to-all-done.5 = f32[16,5,4,128]{3,2,1,0:T(4,128)S(1)} async-done(((f32[16,5,4,128]{3,2,1,0:T(4,128)}), f32[16,5,4,128]{3,2,1,0:T(4,128)S(1)}, u32[]{:S(2)}, u32[]{:S(2)}) %all-to-all-start.5) | async-done | bytes 163872 | tf_op jit(solution)/shard_map/all_to_all | solution.py:1053
  111.0 1.2 merge.2
  112.2 0.7 collective-permute-start.15
  112.9 2.0 %step_back_load.2 = (f32[16,8,128]{2,1,0:T(8,128)S(1)}, f32[5,1,1920]{2,1,0:T(1,128)S(1)}, f32[5,4,8,1920]{3,2,1,0:T(8,128)S(1)}, f32[5,4,8,1920]{3,2,1,0:T(8,128)S(1)}, f32[5,4,8,1920]{3,2,1,0:T(8,128)S(1)}) custom-call(f32[16,8,128]{2,1,0:T(8,128)} %get-tuple-element.152.refs_0_, f32[5,1,1920]{2,1,0:T(1,128)} %get-tuple-element.153.refs_1_, ...), custom_call_target="tpu_custom_call" | custom-call | tf_op jit(solution)/shard_map/step_back_load/pallas_call | solution.py:1025
  114.9 2.7 %step_back.1 = (f32[5,4,8,1920]{3,2,1,0:T(8,128)}, f32[304,128]{1,0:T(8,128)}, f32[480,128]{1,0:T(8,128)}, f32[32,128]{1,0:T(8,128)}, f32[32,128]{1,0:T(8,128)}, /*index=5*/f32[480,128]{1,0:T(8,128)}, f32[480,128]{1,0:T(8,128)}) custom-call(s32[3,128]{1,0:T(4,128)} %get-tuple-element.134.refs_4_.refs_0_, f32[3,128]{1,0:T(4,128)} %get-tuple-element.135.refs_5_.refs_1_, ...), custom_call_target="tpu_custom_call" | custom-call | tf_op jit(solution)/shard_map/step_back/pallas_call | solution.py:1025
  117.6 5.9 %all-to-all-start.6 = ((f32[16,15,2,128]{3,2,1,0:T(2,128)}), f32[16,15,2,128]{3,2,1,0:T(2,128)S(1)}, u32[]{:S(2)}, u32[]{:S(2)}) async-start(f32[16,15,2,128]{3,2,1,0:T(2,128)} %bitcast.58), calls=%async_computation.6 | async-start | bytes 491520 | tf_op jit(solution)/shard_map/all_to_all | solution.py:1053
  123.5 0.8 collective-permute-start.16
  124.3 0.7 collective-permute-start.17
  124.9 0.4 collective-permute-done.16.refs_1_
  125.3 7.9 %all-to-all-done.6 = f32[16,15,2,128]{3,2,1,0:T(2,128)S(1)} async-done(((f32[16,15,2,128]{3,2,1,0:T(2,128)}), f32[16,15,2,128]{3,2,1,0:T(2,128)S(1)}, u32[]{:S(2)}, u32[]{:S(2)}) %all-to-all-start.6) | async-done | bytes 245792 | tf_op jit(solution)/shard_map/all_to_all | solution.py:1053
  133.3 2.0 %owners_back.3 = f32[320,128]{1,0:T(8,128)} custom-call(f32[480,128]{1,0:T(8,128)S(1)} %bitcast.45, f32[80,80]{1,0:T(8,128)S(1)} %bitcast.53, f32[4,80,128]{2,1,0:T(8,128)} %get-tuple-element.207.refs_2_, f32[4,80,128]{2,1,0:T(8,128)} %get-tuple-element.208.refs_3_, f32[1,128]{1,0:T(1,128)} %get-tuple-element.119.refs_1_.refs_4_.refs_8_.refs_6_), custom_call_target="tpu_custom_call" | custom-call | tf_op jit(solution)/shard_map/owners_back/pallas_call | solution.py:1025
  135.3 3.5 %all-to-all-start.7 = ((f32[16,5,4,128]{3,2,1,0:T(4,128)}), f32[16,5,4,128]{3,2,1,0:T(4,128)S(1)}, u32[]{:S(2)}, u32[]{:S(2)}) async-start(f32[16,5,4,128]{3,2,1,0:T(4,128)} %bitcast.57), calls=%async_computation.7 | async-start | bytes 327680 | tf_op jit(solution)/shard_map/all_to_all | solution.py:1053
  138.8 0.4 collective-permute-start.18
  139.2 0.7 collective-permute-start.19
  139.9 7.4 %all-to-all-done.7 = f32[16,5,4,128]{3,2,1,0:T(4,128)S(1)} async-done(((f32[16,5,4,128]{3,2,1,0:T(4,128)}), f32[16,5,4,128]{3,2,1,0:T(4,128)S(1)}, u32[]{:S(2)}, u32[]{:S(2)}) %all-to-all-start.7) | async-done | bytes 163872 | tf_op jit(solution)/shard_map/all_to_all | solution.py:1053
  147.3 1.2 merge.3
  148.5 0.7 collective-permute-start.21
  149.2 2.4 %step_back_load.3 = (f32[16,8,128]{2,1,0:T(8,128)S(1)}, f32[5,1,1920]{2,1,0:T(1,128)S(1)}, f32[5,4,8,1920]{3,2,1,0:T(8,128)S(1)}, f32[5,4,8,1920]{3,2,1,0:T(8,12...) custom-call(f32[16,8,128]{2,1,0:T(8,128)} %get-tuple-element.152.refs_0_, ...), custom_call_target="tpu_custom_call" | custom-call | tf_op jit(solution)/shard_map/step_back_load/pallas_call | solution.py:1025
  151.6 2.4 %step_back_sums.1 = (f32[5,4,8,1920]{3,2,1,0:T(8,128)}, f32[16,128]{1,0:T(8,128)}) custom-call(f32[480,128]{1,0:T(8,128)S(1)} %collective-permute-done.18.refs_0_, f32[480,128]{1,0:T(8,128)S(1)} %collective-permute-done.19.refs_1_, f32[60,128]{1,0:T(8,128)S(1)} %collective-permute-done.20.refs_2_, f32[60,128]{1,0:T(8,128)S(1)} %collective-permute-done.21.refs_3_, ...), custom_call_target="tpu_custom_call" | custom-call | tf_op jit(solution)/shard_map/step_back_sums/pallas_call | solution.py:1025
  154.0 5.4 %all-to-all-start.8 = ((f32[16,1,128]{2,1,0:T(1,128)}), f32[16,1,128]{2,1,0:T(1,128)S(1)}, u32[]{:S(2)}, u32[]{:S(2)}) async-start(f32[16,1,128]{2,1,0:T(1,128)} %bitcast.64), calls=%async_computation.8 | async-start | bytes 16384 | tf_op jit(solution)/shard_map/all_to_all | solution.py:1297
  159.4 1.7 %copy.20 = f32[5,4,8,1920]{3,1,0,2:T(4,128)S(1)} copy(f32[5,4,8,1920]{3,2,1,0:T(8,128)} %get-tuple-element.230) | data formatting | bytes 2457600 | tf_op jit(solution)/shard_map/step_back_sums/pallas_call | solution.py:1025
  161.1 4.7 %all-to-all-done.8 = f32[16,1,128]{2,1,0:T(1,128)S(1)} async-done(((f32[16,1,128]{2,1,0:T(1,128)}), f32[16,1,128]{2,1,0:T(1,128)S(1)}, u32[]{:S(2)}, u32[]{:S(2)}) %all-to-all-start.8) | async-done | bytes 8224 | tf_op jit(solution)/shard_map/all_to_all | solution.py:1297
  165.8 1.2 finish.1
  (65 shorter events, 0.9 us)
Async XLA Ops:
  0.0 6.7 %copy-start.5 = (f32[4,4]{1,0:T(4,128)S(1)}, f32[4,4]{1,0:T(4,128)}, u32[]{:S(2)}) copy-start(f32[4,4]{1,0:T(4,128)} %param.21) | copy-start | bytes 196
  0.0 6.8 %copy-start.7 = (s32[15]{0:T(128)S(1)}, s32[15]{0:T(128)}, u32[]{:S(2)}) copy-start(s32[15]{0:T(128)} %param.28) | copy-start | bytes 184
  0.0 6.8 %copy-start.6 = (s32[15]{0:T(128)S(1)}, s32[15]{0:T(128)}, u32[]{:S(2)}) copy-start(s32[15]{0:T(128)} %param.27) | copy-start | bytes 184
  0.0 6.8 %copy-start.14 = (f32[15]{0:T(128)S(1)}, f32[15]{0:T(128)}, u32[]{:S(2)}) copy-start(f32[15]{0:T(128)} %param.29) | copy-start | bytes 184
  1.6 10.2 %collective-permute-start = (f32[480,128]{1,0:T(8,128)S(1)}, f32[480,128]{1,0:T(8,128)S(1)}, u32[]{:S(2)}, u32[]{:S(2)}) collective-permute-start(f32[480,128]{1,0:T(8,128)S(1)} %get-tuple-element.120), channel_id=1, source_target_pairs={{1,2},{3,4},{5,6},{7,8},{9,10},{11,12},{13,14},{2,1},{4,3},{6,5},{... | collective-permute-start | bytes 737288 | tf_op jit(solution)/shard_map/ppermute | solution.py:1046
  2.3 8.4 %collective-permute-start.1 = (f32[480,128]{1,0:T(8,128)S(1)}, f32[480,128]{1,0:T(8,128)S(1)}, u32[]{:S(2)}, u32[]{:S(2)}) collective-permute-start(f32[480,128]{1,0:T(8,128)S(1)} %get-tuple-element.124), channel_id=1, source_target_pairs={{0,1},{1,0},{2,3},{3,2},{4,5},{5,4},{6,7},{7,6},{8,9},{9,8},{10,11... | collective-permute-start | bytes 737288 | tf_op jit(solution)/shard_map/ppermute | solution.py:1046
  6.9 2.0 %copy-start.15 = (s32[1,75]{1,0:T(1,128)S(1)}, s32[1,75]{1,0:T(1,128)}, u32[]{:S(2)}) copy-start(s32[1,75]{1,0:T(1,128)} %param.25) | copy-start | bytes 904
  6.9 2.0 %copy-start.16 = (s32[1,75]{1,0:T(1,128)S(1)}, s32[1,75]{1,0:T(1,128)}, u32[]{:S(2)}) copy-start(s32[1,75]{1,0:T(1,128)} %param.26) | copy-start | bytes 904
  6.9 2.1 %copy-start.2 = (f32[8,4,4]{0,2,1:T(4,128)S(1)}, f32[8,4,4]{0,2,1:T(4,128)}, u32[]{:S(2)}) copy-start(f32[8,4,4]{0,2,1:T(4,128)} %param.20) | copy-start | bytes 1540
  11.8 9.8 %copy-start.3 = (f32[2,1,80,128]{3,2,1,0:T(8,128)S(1)}, f32[2,1,80,128]{3,2,1,0:T(8,128)}, u32[]{:S(2)}) copy-start(f32[2,1,80,128]{3,2,1,0:T(8,128)} %param.24) | copy-start | bytes 245764
  11.9 9.7 %copy-start.4 = (f32[2,1,80,128]{3,2,1,0:T(8,128)S(1)}, f32[2,1,80,128]{3,2,1,0:T(8,128)}, u32[]{:S(2)}) copy-start(f32[2,1,80,128]{3,2,1,0:T(8,128)} %param.23) | copy-start | bytes 245764
  11.9 17.1 %copy-start.1 = (f32[1,80,80]{2,1,0:T(8,128)S(1)}, f32[1,80,80]{2,1,0:T(8,128)}, u32[]{:S(2)}) copy-start(f32[1,80,80]{2,1,0:T(8,128)} %param.22) | copy-start | bytes 76804
  14.1 20.1 %copy-start.11 = (f32[480,128]{1,0:T(8,128)S(1)}, f32[480,128]{1,0:T(8,128)}, u32[]{:S(2)}) copy-start(f32[480,128]{1,0:T(8,128)} %get-tuple-element.150) | copy-start | bytes 737284
  14.1 20.5 %copy-start.10 = (f32[480,128]{1,0:T(8,128)S(1)}, f32[480,128]{1,0:T(8,128)}, u32[]{:S(2)}) copy-start(f32[480,128]{1,0:T(8,128)} %get-tuple-element.151) | copy-start | bytes 737284
  14.1 14.9 %all-to-all-start = ((f32[16,5,4,128]{3,2,1,0:T(4,128)}), f32[16,5,4,128]{3,2,1,0:T(4,128)S(1)}, u32[]{:S(2)}, u32[]{:S(2)}) async-start(f32[16,5,4,128]{3,2,1,0:T(4,128)} %bitcast.62), calls=%async_computation | async-start | bytes 327680 | tf_op jit(solution)/shard_map/all_to_all | solution.py:1053
  20.5 1.5 collective-permute-start.2
  20.9 1.1 collective-permute-start.3
  30.7 13.3 %all-to-all-start.1 = ((f32[16,15,2,128]{3,2,1,0:T(2,128)}), f32[16,15,2,128]{3,2,1,0:T(2,128)S(1)}, u32[]{:S(2)}, u32[]{:S(2)}) async-start(f32[16,15,2,128]{3,2,1,0:T(2,128)} %bitcast.60), calls=%async_computation.1 | async-start | bytes 491520 | tf_op jit(solution)/shard_map/all_to_all | solution.py:1053
  34.2 14.2 %collective-permute-start.4 = (f32[480,128]{1,0:T(8,128)S(1)}, f32[480,128]{1,0:T(8,128)S(1)}, u32[]{:S(2)}, u32[]{:S(2)}) collective-permute-start(f32[480,128]{1,0:T(8,128)S(1)} %copy-done.11), channel_id=1, source_target_pairs={{0,1},{1,0},{2,3},{3,2},{4,5},{5,4},{6,7},{7,6},{8,9},{9,8},{10,11... | collective-permute-start | bytes 737288 | tf_op jit(solution)/shard_map/ppermute | solution.py:1046
  34.6 13.9 %collective-permute-start.5 = (f32[480,128]{1,0:T(8,128)S(1)}, f32[480,128]{1,0:T(8,128)S(1)}, u32[]{:S(2)}, u32[]{:S(2)}) collective-permute-start(f32[480,128]{1,0:T(8,128)S(1)} %copy-done.10), channel_id=1, source_target_pairs={{1,2},{3,4},{5,6},{7,8},{9,10},{11,12},{13,14},{2,1},{4,3},{6,5},{... | collective-permute-start | bytes 737288 | tf_op jit(solution)/shard_map/ppermute | solution.py:1046
  45.7 2.7 %collective-permute-start.6 = (f32[60,128]{1,0:T(8,128)S(1)}, f32[60,128]{1,0:T(8,128)S(1)}, u32[]{:S(2)}, u32[]{:S(2)}) collective-permute-start(f32[60,128]{1,0:T(8,128)S(1)} %get-tuple-element.161), channel_id=1, source_target_pairs={{0,1},{1,0},{2,3},{3,2},{4,5},{5,4},{6,7},{7,6},{8,9},{9,8},{10,11... | collective-permute-start | bytes 92168 | tf_op jit(solution)/shard_map/ppermute | solution.py:1046
  45.8 2.6 %collective-permute-start.7 = (f32[60,128]{1,0:T(8,128)S(1)}, f32[60,128]{1,0:T(8,128)S(1)}, u32[]{:S(2)}, u32[]{:S(2)}) collective-permute-start(f32[60,128]{1,0:T(8,128)S(1)} %get-tuple-element.162), channel_id=1, source_target_pairs={{1,2},{3,4},{5,6},{7,8},{9,10},{11,12},{13,14},{2,1},{4,3},{6,5},{... | collective-permute-start | bytes 92168 | tf_op jit(solution)/shard_map/ppermute | solution.py:1046
  51.2 15.0 %all-to-all-start.2 = ((f32[16,5,4,128]{3,2,1,0:T(4,128)}), f32[16,5,4,128]{3,2,1,0:T(4,128)S(1)}, u32[]{:S(2)}, u32[]{:S(2)}) async-start(f32[16,5,4,128]{3,2,1,0:T(4,128)} %bitcast.63), calls=%async_computation.2 | async-start | bytes 327680 | tf_op jit(solution)/shard_map/all_to_all | solution.py:1053
  57.8 1.5 collective-permute-start.8
  58.2 1.1 collective-permute-start.9
  67.9 13.3 %all-to-all-start.3 = ((f32[16,15,2,128]{3,2,1,0:T(2,128)}), f32[16,15,2,128]{3,2,1,0:T(2,128)S(1)}, u32[]{:S(2)}, u32[]{:S(2)}) async-start(f32[16,15,2,128]{3,2,1,0:T(2,128)} %bitcast.61), calls=%async_computation.3 | async-start | bytes 491520 | tf_op jit(solution)/shard_map/all_to_all | solution.py:1053
  83.5 19.0 %copy-start.9 = (f32[480,128]{1,0:T(8,128)S(1)}, f32[480,128]{1,0:T(8,128)}, u32[]{:S(2)}) copy-start(f32[480,128]{1,0:T(8,128)} %get-tuple-element.172) | copy-start | bytes 737284
  83.5 19.4 %copy-start.8 = (f32[480,128]{1,0:T(8,128)S(1)}, f32[480,128]{1,0:T(8,128)}, u32[]{:S(2)}) copy-start(f32[480,128]{1,0:T(8,128)} %get-tuple-element.173) | copy-start | bytes 737284
  83.5 13.4 %all-to-all-start.4 = ((f32[16,15,2,128]{3,2,1,0:T(2,128)}), f32[16,15,2,128]{3,2,1,0:T(2,128)S(1)}, u32[]{:S(2)}, u32[]{:S(2)}) async-start(f32[16,15,2,128]{3,2,1,0:T(2,128)} %bitcast.59), calls=%async_computation.4 | async-start | bytes 491520 | tf_op jit(solution)/shard_map/all_to_all | solution.py:1053
  87.2 1.5 collective-permute-start.12
  87.5 1.2 collective-permute-start.13
  99.0 12.0 %all-to-all-start.5 = ((f32[16,5,4,128]{3,2,1,0:T(4,128)}), f32[16,5,4,128]{3,2,1,0:T(4,128)S(1)}, u32[]{:S(2)}, u32[]{:S(2)}) async-start(f32[16,5,4,128]{3,2,1,0:T(4,128)} %bitcast.56), calls=%async_computation.5 | async-start | bytes 327680 | tf_op jit(solution)/shard_map/all_to_all | solution.py:1053
  102.5 12.4 %collective-permute-start.10 = (f32[480,128]{1,0:T(8,128)S(1)}, f32[480,128]{1,0:T(8,128)S(1)}, u32[]{:S(2)}, u32[]{:S(2)}) collective-permute-start(f32[480,128]{1,0:T(8,128)S(1)} %copy-done.9), channel_id=1, source_target_pairs={{0,1},{1,0},{2,3},{3,2},{4,5},{5,4},{6,7},{7,6},{8,9},{9,8},{10,11... | collective-permute-start | bytes 737288 | tf_op jit(solution)/shard_map/ppermute | solution.py:1046
  102.9 12.0 %collective-permute-start.11 = (f32[480,128]{1,0:T(8,128)S(1)}, f32[480,128]{1,0:T(8,128)S(1)}, u32[]{:S(2)}, u32[]{:S(2)}) collective-permute-start(f32[480,128]{1,0:T(8,128)S(1)} %copy-done.8), channel_id=1, source_target_pairs={{1,2},{3,4},{5,6},{7,8},{9,10},{11,12},{13,14},{2,1},{4,3},{6,5},{... | collective-permute-start | bytes 737288 | tf_op jit(solution)/shard_map/ppermute | solution.py:1046
  112.1 2.8 %collective-permute-start.14 = (f32[60,128]{1,0:T(8,128)S(1)}, f32[60,128]{1,0:T(8,128)S(1)}, u32[]{:S(2)}, u32[]{:S(2)}) collective-permute-start(f32[60,128]{1,0:T(8,128)S(1)} %get-tuple-element.193), channel_id=1, source_target_pairs={{0,1},{1,0},{2,3},{3,2},{4,5},{5,4},{6,7},{7,6},{8,9},{9,8},{10,11... | collective-permute-start | bytes 92168 | tf_op jit(solution)/shard_map/ppermute | solution.py:1046
  112.2 2.7 %collective-permute-start.15 = (f32[60,128]{1,0:T(8,128)S(1)}, f32[60,128]{1,0:T(8,128)S(1)}, u32[]{:S(2)}, u32[]{:S(2)}) collective-permute-start(f32[60,128]{1,0:T(8,128)S(1)} %get-tuple-element.194), channel_id=1, source_target_pairs={{1,2},{3,4},{5,6},{7,8},{9,10},{11,12},{13,14},{2,1},{4,3},{6,5},{... | collective-permute-start | bytes 92168 | tf_op jit(solution)/shard_map/ppermute | solution.py:1046
  117.6 21.2 %copy-start.13 = (f32[480,128]{1,0:T(8,128)S(1)}, f32[480,128]{1,0:T(8,128)}, u32[]{:S(2)}) copy-start(f32[480,128]{1,0:T(8,128)} %get-tuple-element.211) | copy-start | bytes 737284
  117.6 21.6 %copy-start.12 = (f32[480,128]{1,0:T(8,128)S(1)}, f32[480,128]{1,0:T(8,128)}, u32[]{:S(2)}) copy-start(f32[480,128]{1,0:T(8,128)} %get-tuple-element.212) | copy-start | bytes 737284
  117.6 15.6 %all-to-all-start.6 = ((f32[16,15,2,128]{3,2,1,0:T(2,128)}), f32[16,15,2,128]{3,2,1,0:T(2,128)S(1)}, u32[]{:S(2)}, u32[]{:S(2)}) async-start(f32[16,15,2,128]{3,2,1,0:T(2,128)} %bitcast.58), calls=%async_computation.6 | async-start | bytes 491520 | tf_op jit(solution)/shard_map/all_to_all | solution.py:1053
  123.5 1.8 %collective-permute-start.16 = (f32[32,128]{1,0:T(8,128)}, f32[32,128]{1,0:T(8,128)S(1)}, u32[]{:S(2)}, u32[]{:S(2)}) collective-permute-start(f32[32,128]{1,0:T(8,128)} %get-tuple-element.204), channel_id=1, source_target_pairs={{0,1},{1,0},{2,3},{3,2},{4,5},{5,4},{6,7},{7,6},{8,9},{9,8},{10,11... | collective-permute-start | bytes 49160 | tf_op jit(solution)/shard_map/ppermute | solution.py:1046
  124.3 1.1 collective-permute-start.17
  135.3 12.0 %all-to-all-start.7 = ((f32[16,5,4,128]{3,2,1,0:T(4,128)}), f32[16,5,4,128]{3,2,1,0:T(4,128)S(1)}, u32[]{:S(2)}, u32[]{:S(2)}) async-start(f32[16,5,4,128]{3,2,1,0:T(4,128)} %bitcast.57), calls=%async_computation.7 | async-start | bytes 327680 | tf_op jit(solution)/shard_map/all_to_all | solution.py:1053
  138.8 12.7 %collective-permute-start.18 = (f32[480,128]{1,0:T(8,128)S(1)}, f32[480,128]{1,0:T(8,128)S(1)}, u32[]{:S(2)}, u32[]{:S(2)}) collective-permute-start(f32[480,128]{1,0:T(8,128)S(1)} %copy-done.13), channel_id=1, source_target_pairs={{0,1},{1,0},{2,3},{3,2},{4,5},{5,4},{6,7},{7,6},{8,9},{9,8},{10,11... | collective-permute-start | bytes 737288 | tf_op jit(solution)/shard_map/ppermute | solution.py:1046
  139.2 12.4 %collective-permute-start.19 = (f32[480,128]{1,0:T(8,128)S(1)}, f32[480,128]{1,0:T(8,128)S(1)}, u32[]{:S(2)}, u32[]{:S(2)}) collective-permute-start(f32[480,128]{1,0:T(8,128)S(1)} %copy-done.12), channel_id=1, source_target_pairs={{1,2},{3,4},{5,6},{7,8},{9,10},{11,12},{13,14},{2,1},{4,3},{6,5},{... | collective-permute-start | bytes 737288 | tf_op jit(solution)/shard_map/ppermute | solution.py:1046
  148.5 3.1 %collective-permute-start.20 = (f32[60,128]{1,0:T(8,128)S(1)}, f32[60,128]{1,0:T(8,128)S(1)}, u32[]{:S(2)}, u32[]{:S(2)}) collective-permute-start(f32[60,128]{1,0:T(8,128)S(1)} %get-tuple-element.217), channel_id=1, source_target_pairs={{0,1},{1,0},{2,3},{3,2},{4,5},{5,4},{6,7},{7,6},{8,9},{9,8},{10,11... | collective-permute-start | bytes 92168 | tf_op jit(solution)/shard_map/ppermute | solution.py:1046
  148.5 3.1 %collective-permute-start.21 = (f32[60,128]{1,0:T(8,128)S(1)}, f32[60,128]{1,0:T(8,128)S(1)}, u32[]{:S(2)}, u32[]{:S(2)}) collective-permute-start(f32[60,128]{1,0:T(8,128)S(1)} %get-tuple-element.218), channel_id=1, source_target_pairs={{1,2},{3,4},{5,6},{7,8},{9,10},{11,12},{13,14},{2,1},{4,3},{6,5},{... | collective-permute-start | bytes 92168 | tf_op jit(solution)/shard_map/ppermute | solution.py:1046
  154.0 11.8 %all-to-all-start.8 = ((f32[16,1,128]{2,1,0:T(1,128)}), f32[16,1,128]{2,1,0:T(1,128)S(1)}, u32[]{:S(2)}, u32[]{:S(2)}) async-start(f32[16,1,128]{2,1,0:T(1,128)} %bitcast.64), calls=%async_computation.8 | async-start | bytes 16384 | tf_op jit(solution)/shard_map/all_to_all | solution.py:1297
  159.4 6.4 %copy-start = (f32[8,5,4,1920]{3,2,1,0:T(4,128)S(1)}, f32[8,5,4,1920]{3,2,1,0:T(4,128)}, u32[]{:S(2)}) copy-start(f32[8,5,4,1920]{3,2,1,0:T(4,128)} %refs_1_.6) | copy-start | bytes 3686404
